TPU v7x, 32 devices: a whole 2x2x4 slice. The times are simulated.
32 devices in a mesh: section: 4 (over y, x), ctx: 8 (over z, core).
Axes of the slice: x: 2, y: 2, z: 4, core: 2. Of those that a mesh axis runs over, the one named last changes fastest.
Arguments:
- queries: bfloat16 [2, 4, 1024, 1024], P(None, 'section', 'ctx'), may hold values from -8 to 8
- out_grad: bfloat16 [2, 4, 1024, 1024], P(None, 'section', 'ctx'), may hold values from -6 to 6
- keys: bfloat16 [4, 1024, 128], P('section', 'ctx'), may hold values from -4 to 4
- values: bfloat16 [4, 1024, 128], P('section', 'ctx'), may hold values from -6 to 6
- entering_keys: bfloat16 [1024, 128], P('ctx'), may hold values from -4 to 4
- entering_values: bfloat16 [1024, 128], P('ctx'), may hold values from -6 to 6
- key_grads_in: float32 [4, 1024, 128], P('section', 'ctx'), may hold values from -4 to 4
- value_grads_in: float32 [4, 1024, 128], P('section', 'ctx'), may hold values from -4 to 4
- group_order: int32 [8], replicated, may hold values from 0 to 7, each once
Outputs:
- query_grads: bfloat16 [2, 4, 1024, 1024], P(None, 'section', 'ctx')
- key_grads: float32 [2, 4, 1024, 128], P(None, 'section', 'ctx')
- value_grads: float32 [2, 4, 1024, 128], P(None, 'section', 'ctx')
Inputs may be any that keep to these rules, and one draw needn't show every extreme that they name: `group_order`: each number 0 to 7 appears once.
All inputs are finite; a program needn't handle non-finite values.
Results may differ from a plain program's by a relative error of at most 0.0062.
Values may be sent and summed in bfloat16 or wider, within the bound.
No kernel may reach another device: no remote copies, remote signals or barrier semaphores. Data moves between devices by JAX's collectives and lax.ppermute only.
A program may use at most 128 MiB of HBM per device.

v0:
```python
import math

import jax
import jax.numpy as jnp
from jax import lax
from jax.experimental import pallas as pl
from jax.experimental.pallas import tpu as pltpu
from jax.sharding import PartitionSpec as P

MASK_FILL = -1e30
CONTRACT_LAST = (((1,), (1,)), ((), ()))


def stack_kernel(q_ref, g_ref, q_out_ref, g_out_ref):
    ticks, _, local_rows, model = q_ref.shape
    head_dim = q_out_ref.shape[1]
    heads = model // head_dim
    for tick in range(ticks):
        for head in range(heads):
            rows = pl.ds((tick * heads + head) * local_rows, local_rows)
            cols = pl.ds(head * head_dim, head_dim)
            q_out_ref[rows, :] = q_ref[tick, 0, :, cols]
            g_out_ref[rows, :] = g_ref[tick, 0, :, cols]


def stacked_heads(queries, out_grad, head_dim):
    rows = queries.size // head_dim
    in_vmem = pl.BlockSpec(memory_space=pltpu.VMEM)
    return pl.pallas_call(
        stack_kernel,
        out_shape=(jax.ShapeDtypeStruct((rows, head_dim), queries.dtype),) * 2,
        in_specs=[in_vmem, in_vmem],
        out_specs=(in_vmem, in_vmem),
        compiler_params=pltpu.CompilerParams(vmem_limit_bytes=8 * 2**20),
        cost_estimate=pl.CostEstimate(
            flops=queries.size, bytes_accessed=8 * queries.size, transcendentals=0
        ),
    )(queries, out_grad)


def tick_kernel(tick, blocks, aliased, *refs):
    order_ref, q_ref, g_ref = refs[:3]
    kv_refs = refs[3 : 3 + blocks]
    outs = refs[3 + blocks + aliased :]
    dq_ref = outs[0]
    term_refs = outs[1 : 1 + blocks]
    e_ref, dp_ref, p_ref, ds_ref, acc_ref, kt_ref, dq_held, dq_sem = outs[1 + blocks :]
    local_rows, head_dim = kv_refs[0].shape[0], kv_refs[0].shape[1] // 2
    heads = dq_held.shape[1] // head_dim
    pairs = heads // 2
    width = 2 * local_rows
    chips = blocks // 2
    scale = 1.0 / math.sqrt(head_dim)
    exp_scale = scale * math.log2(math.e)

    core = lax.axis_index("core")
    chip = lax.axis_index("z")
    own_group = order_ref[2 * chip + core]

    def allowed(slot):
        source = jnp.bitwise_xor(chip, slot % chips)
        parity = core if slot < chips else 1 - core
        return order_ref[2 * source + parity] < own_group

    for slot in range(blocks):
        kt_ref[:, slot * local_rows : (slot + 1) * local_rows] = kv_refs[slot][:, :head_dim].T

    def pair_of(ref, pair):
        return ref[pl.ds((tick * pairs + pair) * width, width), :]

    def rows_of(slot):
        return slice(slot * local_rows, (slot + 1) * local_rows)

    def front(pair):
        q_pair = pair_of(q_ref, pair)
        g_pair = pair_of(g_ref, pair)
        peaks, totals, weights = [], [], []
        for slot in range(blocks):
            scores = lax.dot_general(
                kv_refs[slot][:, :head_dim],
                q_pair,
                CONTRACT_LAST,
                preferred_element_type=jnp.float32,
            )
            if slot == 0:
                key_row = lax.broadcasted_iota(jnp.int32, (local_rows, width), 0)
                query_row = lax.rem(
                    lax.broadcasted_iota(jnp.int32, (local_rows, width), 1), local_rows
                )
                scores = jnp.where(key_row <= query_row, scores, MASK_FILL)
            peak = jnp.max(scores, axis=0, keepdims=True) * exp_scale
            expo = jnp.exp2(scores * exp_scale - peak)
            prob_grads = lax.dot_general(
                kv_refs[slot][:, head_dim:],
                g_pair,
                CONTRACT_LAST,
                preferred_element_type=jnp.float32,
            )
            e_ref[pair, rows_of(slot)] = expo
            dp_ref[pair, rows_of(slot)] = prob_grads
            peaks.append(peak if slot == 0 else jnp.where(allowed(slot), peak, MASK_FILL))
            totals.append(jnp.sum(expo, axis=0, keepdims=True))
            weights.append(jnp.sum(expo * prob_grads, axis=0, keepdims=True))
        biggest = peaks[0]
        for peak in peaks[1:]:
            biggest = jnp.maximum(biggest, peak)
        factors = [jnp.exp2(peak - biggest) for peak in peaks]
        total = sum(part * factor for part, factor in zip(totals, factors))
        weighted = sum(part * factor for part, factor in zip(weights, factors))
        inverse = 1.0 / total
        return [factor * inverse for factor in factors], weighted * inverse

    def back(pair, factors, delta):
        q_pair = pair_of(q_ref, pair)
        g_pair = pair_of(g_ref, pair)
        for slot in range(blocks):
            probs = e_ref[pair, rows_of(slot)] * factors[slot]
            p_ref[pair, rows_of(slot)] = probs.astype(jnp.bfloat16)
            ds_ref[pair, rows_of(slot)] = (
                probs * (dp_ref[pair, rows_of(slot)] - delta)
            ).astype(jnp.bfloat16)
        score_grad = ds_ref[pair]
        key_terms = jnp.dot(score_grad, q_pair, preferred_element_type=jnp.float32)
        value_terms = jnp.dot(p_ref[pair], g_pair, preferred_element_type=jnp.float32)
        if pair > 0:
            key_terms += acc_ref[:, :head_dim]
            value_terms += acc_ref[:, head_dim:]
        if pair < pairs - 1:
            acc_ref[:, :head_dim] = key_terms
            acc_ref[:, head_dim:] = value_terms
        else:
            for slot, out in enumerate(term_refs):
                out[:, :head_dim] = (key_terms[rows_of(slot)] * scale).astype(out.dtype)
                out[:, head_dim:] = value_terms[rows_of(slot)].astype(out.dtype)
        query_t = jnp.dot(kt_ref[...], score_grad, preferred_element_type=jnp.float32) * scale
        for half in range(2):
            lo = (2 * pair + half) * head_dim
            dq_held[:, lo : lo + head_dim] = query_t[
                :, half * local_rows : (half + 1) * local_rows
            ].T.astype(dq_held.dtype)
        cols = pl.ds(2 * pair * head_dim, 2 * head_dim)
        copy = pltpu.make_async_copy(
            dq_held.at[:, cols], dq_ref.at[tick, 0, :, cols], dq_sem.at[pair]
        )
        copy.start()
        return copy

    copies = []
    held = front(0)
    for pair in range(pairs):
        following = front(pair + 1) if pair + 1 < pairs else None
        copies.append(back(pair, *held))
        held = following
    for copy in copies:
        copy.wait()


def attend_back(tick, group_order, queries, q_stack, g_stack, near, far, query_grads):
    local_rows, model = queries.shape[2:]
    kv_blocks = [*near, *far]
    blocks = len(kv_blocks)
    width = kv_blocks[0].shape[1]
    key_rows = blocks * local_rows
    head_dim = width // 2
    pairs = model // head_dim // 2
    in_vmem = pl.BlockSpec(memory_space=pltpu.VMEM)
    operands = [group_order, q_stack, g_stack, *kv_blocks]
    in_specs = [pl.BlockSpec(memory_space=pltpu.SMEM), *[in_vmem] * (2 + blocks)]
    aliases = {}
    if query_grads is not None:
        aliases = {len(operands): 0}
        operands.append(query_grads)
        in_specs.append(pl.BlockSpec(memory_space=pl.ANY))
    tile = (pairs, key_rows, 2 * local_rows)

    def kernel(*refs):
        tick_kernel(tick, blocks, len(aliases), *refs)

    kinds = [jnp.float32] * len(near) + [jnp.bfloat16] * len(far)
    query_grads, *terms = pl.pallas_call(
        kernel,
        out_shape=(
            jax.ShapeDtypeStruct(queries.shape, jnp.bfloat16),
            *[jax.ShapeDtypeStruct((local_rows, width), kind) for kind in kinds],
        ),
        in_specs=in_specs,
        out_specs=(pl.BlockSpec(memory_space=pl.ANY), *[in_vmem] * blocks),
        scratch_shapes=[
            pltpu.VMEM(tile, jnp.float32),
            pltpu.VMEM(tile, jnp.float32),
            pltpu.VMEM(tile, jnp.bfloat16),
            pltpu.VMEM(tile, jnp.bfloat16),
            pltpu.VMEM((key_rows, width), jnp.float32),
            pltpu.VMEM((head_dim, key_rows), jnp.bfloat16),
            pltpu.VMEM((local_rows, model), jnp.bfloat16),
            pltpu.SemaphoreType.DMA((pairs,)),
        ],
        input_output_aliases=aliases,
        compiler_params=pltpu.CompilerParams(vmem_limit_bytes=44 * 2**20),
        cost_estimate=pl.CostEstimate(
            flops=40 * model * key_rows * local_rows,
            bytes_accessed=6 * local_rows * model + 5 * key_rows * width,
            transcendentals=model // head_dim * key_rows * local_rows,
        ),
    )(*operands)
    return query_grads, terms[: len(near)], terms[len(near) :]


def other_core(block):
    return lax.ppermute(block, "core", [(0, 1), (1, 0)])


def across_chips(block, k):
    return lax.ppermute(block, "z", [(chip, chip ^ k) for chip in range(lax.axis_size("z"))])


def body(
    queries,
    out_grad,
    keys,
    values,
    entering_keys,
    entering_values,
    key_grads_in,
    value_grads_in,
    group_order,
):
    head_dim = keys.shape[2]
    chips = lax.axis_size("z")
    sections = lax.axis_size("section")
    section = lax.axis_index("section")

    own_pair = jnp.concatenate([keys[0], values[0]], axis=1)
    entering_pair = jnp.concatenate([entering_keys, entering_values], axis=1)
    leaving_pair = jnp.where(section == 0, entering_pair, own_pair)

    near = [across_chips(own_pair, k) for k in range(1, chips)]
    own_far = other_core(own_pair)
    next_pair = lax.ppermute(
        leaving_pair, "section", [(i, (i - 1) % sections) for i in range(sections)]
    )
    stacks = stacked_heads(queries, out_grad, head_dim)
    near, next_pair, stacks = lax.optimization_barrier((near, next_pair, stacks))
    far = [own_far] + [other_core(block) for block in near]
    next_near = [next_pair] + [across_chips(next_pair, k) for k in range(1, chips)]
    query_grads, near_terms, far_terms = attend_back(
        0, group_order, queries, *stacks, [own_pair, *near], far, None
    )
    query_grads, far_terms, next_near = lax.optimization_barrier(
        (query_grads, far_terms, next_near)
    )
    next_far = [other_core(block) for block in next_near]

    def chip_sums(near_terms, far_terms):
        sums = [
            mine + other_core(theirs).astype(jnp.float32)
            for mine, theirs in zip(near_terms, far_terms)
        ]
        return sums[0], [block.astype(jnp.bfloat16) for block in sums[1:]]

    def reduced(own_sum, leaving):
        for k, block in enumerate(leaving, 1):
            own_sum = own_sum + across_chips(block, k).astype(jnp.float32)
        return own_sum

    own_sum, leaving = chip_sums(near_terms, far_terms)
    query_grads, leaving = lax.optimization_barrier((query_grads, leaving))
    first_acc = jnp.concatenate([key_grads_in[0], value_grads_in[0]], axis=1) + reduced(
        own_sum, leaving
    )
    query_grads, near_terms, far_terms = attend_back(
        1, group_order, queries, *stacks, next_near, next_far, query_grads
    )
    first_acc, far_terms = lax.optimization_barrier((first_acc, far_terms))
    own_sum, leaving = chip_sums(near_terms, far_terms)
    first_acc, leaving = lax.optimization_barrier((first_acc, leaving))
    moved_acc = lax.ppermute(first_acc, "section", [(i, i - 1) for i in range(1, sections)])
    second_acc = moved_acc + reduced(own_sum, leaving)
    key_grads = jnp.stack([first_acc[:, :head_dim], second_acc[:, :head_dim]], axis=0)[:, None]
    value_grads = jnp.stack([first_acc[:, head_dim:], second_acc[:, head_dim:]], axis=0)[:, None]
    return (query_grads, key_grads, value_grads)


def solution(mesh):
    sections, ctx_count = mesh.shape["section"], mesh.shape["ctx"]
    chip_mesh = jax.sharding.Mesh(
        mesh.devices.reshape(sections, ctx_count // 2, 2), ("section", "z", "core")
    )
    tokens = ("z", "core")
    return jax.shard_map(
        body,
        mesh=chip_mesh,
        in_specs=(
            P(None, "section", tokens, None),
            P(None, "section", tokens, None),
            P("section", tokens, None),
            P("section", tokens, None),
            P(tokens, None),
            P(tokens, None),
            P("section", tokens, None),
            P("section", tokens, None),
            P(),
        ),
        out_specs=(
            P(None, "section", tokens, None),
            P(None, "section", tokens, None),
            P(None, "section", tokens, None),
        ),
        check_vma=False,
    )
```

profile of v0, /device:TPU:0, one launch (start us, length us, event | category | flops | bytes accessed | tf_op | source)
XLA Modules:
  0.0 49.9 jit_solution(5950495463936877275)
XLA Ops:
  0.6 0.8 %maximum_select_fusion = (bf16[128,256]{1,0:T(8,128)(2,1)S(1)}, bf16[128,256]{1,0:T(8,128)(2,1)S(1)}) fusion(bf16[128,128]{1,0:T(8,128)(2,1)} %param.14, bf16[128,128]{1,0:T(8,128)(2,1)} %param.13, pred[]{:T(512)S(6)} %eq.3, bf16[128,128]{1,0:T(8,128)(2,1)} %bitcast.22, bf16[128,128]{1,0:T(8,128)(2,1)} %bitcast.23), kind=kLoop, calls=%fused_computation.13 | loop fusion | flops 294912 | bytes 262145 | tf_op jit(solution)/shard_map/jit(_where)/select_n | solution.py:235
  1.5 3.9 %collective-permute-start.3 = (bf16[128,256]{1,0:T(8,128)(2,1)S(1)}, bf16[128,256]{1,0:T(8,128)(2,1)S(1)}, u32[]{:S(2)}, u32[]{:S(2)}) collective-permute-start(bf16[128,256]{1,0:T(8,128)(2,1)S(1)} %get-tuple-element.106), channel_id=1, source_target_pairs={{0,24},{8,0},{16,8},{24,16},{1,25},{9,1},{17,9},{25,17},{2,26},{10... | collective-permute-start | bytes 196616 | tf_op jit(solution)/shard_map/ppermute | solution.py:239
  5.4 3.6 %collective-permute-start.2 = (bf16[128,256]{1,0:T(8,128)(2,1)S(1)}, bf16[128,256]{1,0:T(8,128)(2,1)S(1)}, u32[]{:S(2)}, u32[]{:S(2)}) collective-permute-start(bf16[128,256]{1,0:T(8,128)(2,1)S(1)} %get-tuple-element.107.refs_3_), channel_id=1, source_target_pairs={{0,6},{2,4},{4,2},{6,0},{1,7},{3,5},{5,3},{7,1},{8,14},{10,12},{12... | collective-permute-start | bytes 196616 | tf_op jit(solution)/shard_map/ppermute | solution.py:214
  9.0 0.8 %collective-permute-start = (bf16[128,256]{1,0:T(8,128)(2,1)S(1)}, bf16[128,256]{1,0:T(8,128)(2,1)S(1)}, u32[]{:S(2)}, u32[]{:S(2)}) collective-permute-start(bf16[128,256]{1,0:T(8,128)(2,1)S(1)} %get-tuple-element.107.refs_3_), channel_id=1, source_target_pairs={{0,2},{2,0},{4,6},{6,4},{1,3},{3,1},{5,7},{7,5},{8,10},{10,8},{12,... | collective-permute-start | bytes 196616 | tf_op jit(solution)/shard_map/ppermute | solution.py:214
  9.8 1.0 %copy-done = bf16[2,1,128,1024]{3,2,1,0:T(8,128)(2,1)S(1)} copy-done((bf16[2,1,128,1024]{3,2,1,0:T(8,128)(2,1)S(1)}, bf16[2,1,128,1024]{3,2,1,0:T(8,128)(2,1)}, u32[]{:S(2)}) %copy-start) | copy-done | bytes 524312
  10.9 1.0 %copy-done.1 = bf16[2,1,128,1024]{3,2,1,0:T(8,128)(2,1)S(1)} copy-done((bf16[2,1,128,1024]{3,2,1,0:T(8,128)(2,1)S(1)}, bf16[2,1,128,1024]{3,2,1,0:T(8,128)(2,1)}, u32[]{:S(2)}) %copy-start.1) | copy-done | bytes 524312
  12.3 2.1 %collective-permute-done.1.refs_5_ = bf16[128,256]{1,0:T(8,128)(2,1)S(1)} collective-permute-done((bf16[128,256]{1,0:T(8,128)(2,1)S(1)}, bf16[128,256]{1,0:T(8,128)(2,1)S(1)}, u32[]{:S(2)}, u32[]{:S(2)}) %collective-permute-start.1) | collective-permute-done | bytes 65568 | tf_op jit(solution)/shard_map/ppermute | solution.py:214
  14.5 0.5 %collective-permute-start.6 = (bf16[128,256]{1,0:T(8,128)(2,1)S(1)}, bf16[128,256]{1,0:T(8,128)(2,1)S(1)}, u32[]{:S(2)}, u32[]{:S(2)}) collective-permute-start(bf16[128,256]{1,0:T(8,128)(2,1)S(1)} %collective-permute-done.1.refs_5_), channel_id=1, source_target_pairs={{0,1},{1,0},{2,3},{3,2},{4,5},{5,4},{6,7},{7,6},{8,9},{9,8},{10,11... | collective-permute-start | bytes 196616 | tf_op jit(solution)/shard_map/ppermute | solution.py:210
  15.0 2.6 %collective-permute-start.10 = (bf16[128,256]{1,0:T(8,128)(2,1)S(1)}, bf16[128,256]{1,0:T(8,128)(2,1)S(1)}, u32[]{:S(2)}, u32[]{:S(2)}) collective-permute-start(bf16[128,256]{1,0:T(8,128)(2,1)S(1)} %collective-permute-done.3.refs_3_), channel_id=1, source_target_pairs={{0,6},{2,4},{4,2},{6,0},{1,7},{3,5},{5,3},{7,1},{8,14},{10,12},{12... | collective-permute-start | bytes 196616 | tf_op jit(solution)/shard_map/ppermute | solution.py:214
  17.6 1.8 %collective-permute-start.8 = (bf16[128,256]{1,0:T(8,128)(2,1)S(1)}, bf16[128,256]{1,0:T(8,128)(2,1)S(1)}, u32[]{:S(2)}, u32[]{:S(2)}) collective-permute-start(bf16[128,256]{1,0:T(8,128)(2,1)S(1)} %collective-permute-done.3.refs_3_), channel_id=1, source_target_pairs={{0,2},{2,0},{4,6},{6,4},{1,3},{3,1},{5,7},{7,5},{8,10},{10,8},{12,... | collective-permute-start | bytes 196616 | tf_op jit(solution)/shard_map/ppermute | solution.py:214
  19.4 4.7 %shard_map.113 = (bf16[2,1,128,1024]{3,2,1,0:T(8,128)(2,1)}, f32[128,256]{1,0:T(8,128)S(1)}, f32[128,256]{1,0:T(8,128)S(1)}, f32[128,256]{1,0:T(8,128)S(1)}, f32...) custom-call(s32[8]{0:T(128)S(1)} %copy-done.2, ...), custom_call_target="tpu_custom_call" | custom-call | flops 5368709120 | bytes 2097152 | tf_op jit(solution)/shard_map/pallas_call | solution.py:180
  24.2 0.5 collective-permute-start.16
  26.5 0.7 %collective-permute-start.19 = (bf16[128,256]{1,0:T(8,128)(2,1)S(1)}, bf16[128,256]{1,0:T(8,128)(2,1)S(1)}, u32[]{:S(2)}, u32[]{:S(2)}) collective-permute-start(bf16[128,256]{1,0:T(8,128)(2,1)S(1)} %add_convert_fusion.5), channel_id=1, source_target_pairs={{0,2},{2,0},{4,6},{6,4},{1,3},{3,1},{5,7},{7,5},{8,10},{10,8},{12,... | collective-permute-start | bytes 196616 | tf_op jit(solution)/shard_map/ppermute | solution.py:214
  27.2 2.5 %collective-permute-start.20 = (bf16[128,256]{1,0:T(8,128)(2,1)S(1)}, bf16[128,256]{1,0:T(8,128)(2,1)S(1)}, u32[]{:S(2)}, u32[]{:S(2)}) collective-permute-start(bf16[128,256]{1,0:T(8,128)(2,1)S(1)} %add_convert_fusion.4), channel_id=1, source_target_pairs={{0,4},{2,6},{4,0},{6,2},{1,5},{3,7},{5,1},{7,3},{8,12},{10,14},{12... | collective-permute-start | bytes 196616 | tf_op jit(solution)/shard_map/ppermute | solution.py:214
  29.7 1.2 %collective-permute-start.21 = (bf16[128,256]{1,0:T(8,128)(2,1)S(1)}, bf16[128,256]{1,0:T(8,128)(2,1)S(1)}, u32[]{:S(2)}, u32[]{:S(2)}) collective-permute-start(bf16[128,256]{1,0:T(8,128)(2,1)S(1)} %add_convert_fusion.3), channel_id=1, source_target_pairs={{0,6},{2,4},{4,2},{6,0},{1,7},{3,5},{5,3},{7,1},{8,14},{10,12},{12... | collective-permute-start | bytes 196616 | tf_op jit(solution)/shard_map/ppermute | solution.py:214
  30.9 4.7 %shard_map.114 = (bf16[2,1,128,1024]{3,2,1,0:T(8,128)(2,1)}, f32[128,256]{1,0:T(8,128)S(1)}, f32[128,256]{1,0:T(8,128)S(1)}, f32[128,256]{1,0:T(8,128)S(1)}, f32...) custom-call(s32[8]{0:T(128)S(1)} %copy-done.2, ...), custom_call_target="tpu_custom_call", output_to_operand_aliasing={{0}: (11, {})} | custom-call | flops 5368709120 | bytes 2097152 | tf_op jit(solution)/shard_map/pallas_call | solution.py:180
  36.0 0.5 collective-permute-start.23
  37.8 1.2 %collective-permute-start.27 = (bf16[128,256]{1,0:T(8,128)(2,1)S(1)}, bf16[128,256]{1,0:T(8,128)(2,1)S(1)}, u32[]{:S(2)}, u32[]{:S(2)}) collective-permute-start(bf16[128,256]{1,0:T(8,128)(2,1)S(1)} %add_convert_fusion.2), channel_id=1, source_target_pairs={{0,2},{2,0},{4,6},{6,4},{1,3},{3,1},{5,7},{7,5},{8,10},{10,8},{12,... | collective-permute-start | bytes 196616 | tf_op jit(solution)/shard_map/ppermute | solution.py:214
  39.0 1.8 %collective-permute-start.28 = (bf16[128,256]{1,0:T(8,128)(2,1)S(1)}, bf16[128,256]{1,0:T(8,128)(2,1)S(1)}, u32[]{:S(2)}, u32[]{:S(2)}) collective-permute-start(bf16[128,256]{1,0:T(8,128)(2,1)S(1)} %add_convert_fusion.1), channel_id=1, source_target_pairs={{0,4},{2,6},{4,0},{6,2},{1,5},{3,7},{5,1},{7,3},{8,12},{10,14},{12... | collective-permute-start | bytes 196616 | tf_op jit(solution)/shard_map/ppermute | solution.py:214
  40.8 1.4 %collective-permute-start.29 = (bf16[128,256]{1,0:T(8,128)(2,1)S(1)}, bf16[128,256]{1,0:T(8,128)(2,1)S(1)}, u32[]{:S(2)}, u32[]{:S(2)}) collective-permute-start(bf16[128,256]{1,0:T(8,128)(2,1)S(1)} %add_convert_fusion), channel_id=1, source_target_pairs={{0,6},{2,4},{4,2},{6,0},{1,7},{3,5},{5,3},{7,1},{8,14},{10,12},{12... | collective-permute-start | bytes 196616 | tf_op jit(solution)/shard_map/ppermute | solution.py:214
  42.2 1.3 %collective-permute-start.25 = (f32[128,256]{1,0:T(8,128)S(1)}, f32[128,256]{1,0:T(8,128)S(1)}, u32[]{:S(2)}, u32[]{:S(2)}) collective-permute-start(f32[128,256]{1,0:T(8,128)S(1)} %maximum_add_fusion), channel_id=1, source_target_pairs={{8,0},{16,8},{24,16},{9,1},{17,9},{25,17},{10,2},{18,10},{26,18},{... | collective-permute-start | bytes 393224 | tf_op jit(solution)/shard_map/ppermute | solution.py:277
  43.6 3.7 %collective-permute-done.28 = bf16[128,256]{1,0:T(8,128)(2,1)S(1)} collective-permute-done((bf16[128,256]{1,0:T(8,128)(2,1)S(1)}, bf16[128,256]{1,0:T(8,128)(2,1)S(1)}, u32[]{:S(2)}, u32[]{:S(2)}) %collective-permute-start.28) | collective-permute-done | bytes 65568 | tf_op jit(solution)/shard_map/ppermute | solution.py:214
  47.3 1.8 %collective-permute-done.25 = f32[128,256]{1,0:T(8,128)S(1)} collective-permute-done((f32[128,256]{1,0:T(8,128)S(1)}, f32[128,256]{1,0:T(8,128)S(1)}, u32[]{:S(2)}, u32[]{:S(2)}) %collective-permute-start.25) | collective-permute-done | bytes 131104 | tf_op jit(solution)/shard_map/ppermute | solution.py:277
  49.2 0.7 %maximum_bitcast_fusion = (f32[2,1,128,128]{3,2,1,0:T(8,128)}, f32[2,1,128,128]{3,2,1,0:T(8,128)}) fusion(f32[1,128,128]{2,1,0:T(8,128)S(1)} %get-tuple-element.105, f32[1,128,128]{2,1,0:T(8,128)S(1)} %get-tuple-element.103, f32[1,128,128]{2,1,0:T(8,128)S(1)} %get-tuple-element.104, f32[1,128,128]{2,1,0:T(8,128)S(1)} %get-tuple-element.102), kind=kLoop, calls=%fused_computation.1 | loop fusion | flops 65536 | bytes 524288
  (61 shorter events, 4.0 us)
Async XLA Ops:
  1.5 10.6 %collective-permute-start.3 = (bf16[128,256]{1,0:T(8,128)(2,1)S(1)}, bf16[128,256]{1,0:T(8,128)(2,1)S(1)}, u32[]{:S(2)}, u32[]{:S(2)}) collective-permute-start(bf16[128,256]{1,0:T(8,128)(2,1)S(1)} %get-tuple-element.106), channel_id=1, source_target_pairs={{0,24},{8,0},{16,8},{24,16},{1,25},{9,1},{17,9},{25,17},{2,26},{10... | collective-permute-start | bytes 196616 | tf_op jit(solution)/shard_map/ppermute | solution.py:239
  5.4 6.9 %collective-permute-start.2 = (bf16[128,256]{1,0:T(8,128)(2,1)S(1)}, bf16[128,256]{1,0:T(8,128)(2,1)S(1)}, u32[]{:S(2)}, u32[]{:S(2)}) collective-permute-start(bf16[128,256]{1,0:T(8,128)(2,1)S(1)} %get-tuple-element.107.refs_3_), channel_id=1, source_target_pairs={{0,6},{2,4},{4,2},{6,0},{1,7},{3,5},{5,3},{7,1},{8,14},{10,12},{12... | collective-permute-start | bytes 196616 | tf_op jit(solution)/shard_map/ppermute | solution.py:214
  9.0 5.4 %collective-permute-start.1 = (bf16[128,256]{1,0:T(8,128)(2,1)S(1)}, bf16[128,256]{1,0:T(8,128)(2,1)S(1)}, u32[]{:S(2)}, u32[]{:S(2)}) collective-permute-start(bf16[128,256]{1,0:T(8,128)(2,1)S(1)} %get-tuple-element.107.refs_3_), channel_id=1, source_target_pairs={{0,4},{2,6},{4,0},{6,2},{1,5},{3,7},{5,1},{7,3},{8,12},{10,14},{12... | collective-permute-start | bytes 196616 | tf_op jit(solution)/shard_map/ppermute | solution.py:214
  9.0 5.4 %collective-permute-start = (bf16[128,256]{1,0:T(8,128)(2,1)S(1)}, bf16[128,256]{1,0:T(8,128)(2,1)S(1)}, u32[]{:S(2)}, u32[]{:S(2)}) collective-permute-start(bf16[128,256]{1,0:T(8,128)(2,1)S(1)} %get-tuple-element.107.refs_3_), channel_id=1, source_target_pairs={{0,2},{2,0},{4,6},{6,4},{1,3},{3,1},{5,7},{7,5},{8,10},{10,8},{12,... | collective-permute-start | bytes 196616 | tf_op jit(solution)/shard_map/ppermute | solution.py:214
  9.8 7.8 %collective-permute-start.4 = (bf16[128,256]{1,0:T(8,128)(2,1)S(1)}, bf16[128,256]{1,0:T(8,128)(2,1)S(1)}, u32[]{:S(2)}, u32[]{:S(2)}) collective-permute-start(bf16[128,256]{1,0:T(8,128)(2,1)S(1)} %get-tuple-element.107.refs_3_), channel_id=1, source_target_pairs={{0,1},{1,0},{2,3},{3,2},{4,5},{5,4},{6,7},{7,6},{8,9},{9,8},{10,11... | collective-permute-start | bytes 196616 | tf_op jit(solution)/shard_map/ppermute | solution.py:210
  14.5 3.1 %collective-permute-start.5 = (bf16[128,256]{1,0:T(8,128)(2,1)S(1)}, bf16[128,256]{1,0:T(8,128)(2,1)S(1)}, u32[]{:S(2)}, u32[]{:S(2)}) collective-permute-start(bf16[128,256]{1,0:T(8,128)(2,1)S(1)} %collective-permute-done.refs_4_), channel_id=1, source_target_pairs={{0,1},{1,0},{2,3},{3,2},{4,5},{5,4},{6,7},{7,6},{8,9},{9,8},{10,11... | collective-permute-start | bytes 196616 | tf_op jit(solution)/shard_map/ppermute | solution.py:210
  14.5 4.9 %collective-permute-start.6 = (bf16[128,256]{1,0:T(8,128)(2,1)S(1)}, bf16[128,256]{1,0:T(8,128)(2,1)S(1)}, u32[]{:S(2)}, u32[]{:S(2)}) collective-permute-start(bf16[128,256]{1,0:T(8,128)(2,1)S(1)} %collective-permute-done.1.refs_5_), channel_id=1, source_target_pairs={{0,1},{1,0},{2,3},{3,2},{4,5},{5,4},{6,7},{7,6},{8,9},{9,8},{10,11... | collective-permute-start | bytes 196616 | tf_op jit(solution)/shard_map/ppermute | solution.py:210
  15.0 4.4 %collective-permute-start.7 = (bf16[128,256]{1,0:T(8,128)(2,1)S(1)}, bf16[128,256]{1,0:T(8,128)(2,1)S(1)}, u32[]{:S(2)}, u32[]{:S(2)}) collective-permute-start(bf16[128,256]{1,0:T(8,128)(2,1)S(1)} %collective-permute-done.2.refs_6_), channel_id=1, source_target_pairs={{0,1},{1,0},{2,3},{3,2},{4,5},{5,4},{6,7},{7,6},{8,9},{9,8},{10,11... | collective-permute-start | bytes 196616 | tf_op jit(solution)/shard_map/ppermute | solution.py:210
  15.0 9.1 %collective-permute-start.10 = (bf16[128,256]{1,0:T(8,128)(2,1)S(1)}, bf16[128,256]{1,0:T(8,128)(2,1)S(1)}, u32[]{:S(2)}, u32[]{:S(2)}) collective-permute-start(bf16[128,256]{1,0:T(8,128)(2,1)S(1)} %collective-permute-done.3.refs_3_), channel_id=1, source_target_pairs={{0,6},{2,4},{4,2},{6,0},{1,7},{3,5},{5,3},{7,1},{8,14},{10,12},{12... | collective-permute-start | bytes 196616 | tf_op jit(solution)/shard_map/ppermute | solution.py:214
  17.6 6.5 %collective-permute-start.9 = (bf16[128,256]{1,0:T(8,128)(2,1)S(1)}, bf16[128,256]{1,0:T(8,128)(2,1)S(1)}, u32[]{:S(2)}, u32[]{:S(2)}) collective-permute-start(bf16[128,256]{1,0:T(8,128)(2,1)S(1)} %collective-permute-done.3.refs_3_), channel_id=1, source_target_pairs={{0,4},{2,6},{4,0},{6,2},{1,5},{3,7},{5,1},{7,3},{8,12},{10,14},{12... | collective-permute-start | bytes 196616 | tf_op jit(solution)/shard_map/ppermute | solution.py:214
  17.6 6.5 %collective-permute-start.8 = (bf16[128,256]{1,0:T(8,128)(2,1)S(1)}, bf16[128,256]{1,0:T(8,128)(2,1)S(1)}, u32[]{:S(2)}, u32[]{:S(2)}) collective-permute-start(bf16[128,256]{1,0:T(8,128)(2,1)S(1)} %collective-permute-done.3.refs_3_), channel_id=1, source_target_pairs={{0,2},{2,0},{4,6},{6,4},{1,3},{3,1},{5,7},{7,5},{8,10},{10,8},{12,... | collective-permute-start | bytes 196616 | tf_op jit(solution)/shard_map/ppermute | solution.py:214
  24.2 1.5 %collective-permute-start.16 = (bf16[128,256]{1,0:T(8,128)(2,1)S(1)}, bf16[128,256]{1,0:T(8,128)(2,1)S(1)}, u32[]{:S(2)}, u32[]{:S(2)}) collective-permute-start(bf16[128,256]{1,0:T(8,128)(2,1)S(1)} %get-tuple-element.72), channel_id=1, source_target_pairs={{0,1},{1,0},{2,3},{3,2},{4,5},{5,4},{6,7},{7,6},{8,9},{9,8},{10,11... | collective-permute-start | bytes 196616 | tf_op jit(solution)/shard_map/ppermute | solution.py:210
  24.8 10.8 %collective-permute-start.18 = (bf16[128,256]{1,0:T(8,128)(2,1)S(1)}, bf16[128,256]{1,0:T(8,128)(2,1)S(1)}, u32[]{:S(2)}, u32[]{:S(2)}) collective-permute-start(bf16[128,256]{1,0:T(8,128)(2,1)S(1)} %get-tuple-element.78), channel_id=1, source_target_pairs={{0,1},{1,0},{2,3},{3,2},{4,5},{5,4},{6,7},{7,6},{8,9},{9,8},{10,11... | collective-permute-start | bytes 196616 | tf_op jit(solution)/shard_map/ppermute | solution.py:210
  25.4 1.8 %collective-permute-start.12 = (bf16[128,256]{1,0:T(8,128)(2,1)S(1)}, bf16[128,256]{1,0:T(8,128)(2,1)S(1)}, u32[]{:S(2)}, u32[]{:S(2)}) collective-permute-start(bf16[128,256]{1,0:T(8,128)(2,1)S(1)} %collective-permute-done.8.refs_4_), channel_id=1, source_target_pairs={{0,1},{1,0},{2,3},{3,2},{4,5},{5,4},{6,7},{7,6},{8,9},{9,8},{10,11... | collective-permute-start | bytes 196616 | tf_op jit(solution)/shard_map/ppermute | solution.py:210
  25.8 3.9 %collective-permute-start.13 = (bf16[128,256]{1,0:T(8,128)(2,1)S(1)}, bf16[128,256]{1,0:T(8,128)(2,1)S(1)}, u32[]{:S(2)}, u32[]{:S(2)}) collective-permute-start(bf16[128,256]{1,0:T(8,128)(2,1)S(1)} %collective-permute-done.9.refs_5_), channel_id=1, source_target_pairs={{0,1},{1,0},{2,3},{3,2},{4,5},{5,4},{6,7},{7,6},{8,9},{9,8},{10,11... | collective-permute-start | bytes 196616 | tf_op jit(solution)/shard_map/ppermute | solution.py:210
  26.1 4.9 %collective-permute-start.14 = (bf16[128,256]{1,0:T(8,128)(2,1)S(1)}, bf16[128,256]{1,0:T(8,128)(2,1)S(1)}, u32[]{:S(2)}, u32[]{:S(2)}) collective-permute-start(bf16[128,256]{1,0:T(8,128)(2,1)S(1)} %collective-permute-done.10.refs_6_), channel_id=1, source_target_pairs={{0,1},{1,0},{2,3},{3,2},{4,5},{5,4},{6,7},{7,6},{8,9},{9,8},{10,11... | collective-permute-start | bytes 196616 | tf_op jit(solution)/shard_map/ppermute | solution.py:210
  26.5 9.1 %collective-permute-start.19 = (bf16[128,256]{1,0:T(8,128)(2,1)S(1)}, bf16[128,256]{1,0:T(8,128)(2,1)S(1)}, u32[]{:S(2)}, u32[]{:S(2)}) collective-permute-start(bf16[128,256]{1,0:T(8,128)(2,1)S(1)} %add_convert_fusion.5), channel_id=1, source_target_pairs={{0,2},{2,0},{4,6},{6,4},{1,3},{3,1},{5,7},{7,5},{8,10},{10,8},{12,... | collective-permute-start | bytes 196616 | tf_op jit(solution)/shard_map/ppermute | solution.py:214
  27.2 8.4 %collective-permute-start.20 = (bf16[128,256]{1,0:T(8,128)(2,1)S(1)}, bf16[128,256]{1,0:T(8,128)(2,1)S(1)}, u32[]{:S(2)}, u32[]{:S(2)}) collective-permute-start(bf16[128,256]{1,0:T(8,128)(2,1)S(1)} %add_convert_fusion.4), channel_id=1, source_target_pairs={{0,4},{2,6},{4,0},{6,2},{1,5},{3,7},{5,1},{7,3},{8,12},{10,14},{12... | collective-permute-start | bytes 196616 | tf_op jit(solution)/shard_map/ppermute | solution.py:214
  29.7 6.2 %collective-permute-start.21 = (bf16[128,256]{1,0:T(8,128)(2,1)S(1)}, bf16[128,256]{1,0:T(8,128)(2,1)S(1)}, u32[]{:S(2)}, u32[]{:S(2)}) collective-permute-start(bf16[128,256]{1,0:T(8,128)(2,1)S(1)} %add_convert_fusion.3), channel_id=1, source_target_pairs={{0,6},{2,4},{4,2},{6,0},{1,7},{3,5},{5,3},{7,1},{8,14},{10,12},{12... | collective-permute-start | bytes 196616 | tf_op jit(solution)/shard_map/ppermute | solution.py:214
  36.6 7.0 %collective-permute-start.26 = (bf16[128,256]{1,0:T(8,128)(2,1)S(1)}, bf16[128,256]{1,0:T(8,128)(2,1)S(1)}, u32[]{:S(2)}, u32[]{:S(2)}) collective-permute-start(bf16[128,256]{1,0:T(8,128)(2,1)S(1)} %get-tuple-element.95), channel_id=1, source_target_pairs={{0,1},{1,0},{2,3},{3,2},{4,5},{5,4},{6,7},{7,6},{8,9},{9,8},{10,11... | collective-permute-start | bytes 196616 | tf_op jit(solution)/shard_map/ppermute | solution.py:210
  37.8 5.8 %collective-permute-start.27 = (bf16[128,256]{1,0:T(8,128)(2,1)S(1)}, bf16[128,256]{1,0:T(8,128)(2,1)S(1)}, u32[]{:S(2)}, u32[]{:S(2)}) collective-permute-start(bf16[128,256]{1,0:T(8,128)(2,1)S(1)} %add_convert_fusion.2), channel_id=1, source_target_pairs={{0,2},{2,0},{4,6},{6,4},{1,3},{3,1},{5,7},{7,5},{8,10},{10,8},{12,... | collective-permute-start | bytes 196616 | tf_op jit(solution)/shard_map/ppermute | solution.py:214
  39.0 8.3 %collective-permute-start.28 = (bf16[128,256]{1,0:T(8,128)(2,1)S(1)}, bf16[128,256]{1,0:T(8,128)(2,1)S(1)}, u32[]{:S(2)}, u32[]{:S(2)}) collective-permute-start(bf16[128,256]{1,0:T(8,128)(2,1)S(1)} %add_convert_fusion.1), channel_id=1, source_target_pairs={{0,4},{2,6},{4,0},{6,2},{1,5},{3,7},{5,1},{7,3},{8,12},{10,14},{12... | collective-permute-start | bytes 196616 | tf_op jit(solution)/shard_map/ppermute | solution.py:214
  40.8 6.5 %collective-permute-start.29 = (bf16[128,256]{1,0:T(8,128)(2,1)S(1)}, bf16[128,256]{1,0:T(8,128)(2,1)S(1)}, u32[]{:S(2)}, u32[]{:S(2)}) collective-permute-start(bf16[128,256]{1,0:T(8,128)(2,1)S(1)} %add_convert_fusion), channel_id=1, source_target_pairs={{0,6},{2,4},{4,2},{6,0},{1,7},{3,5},{5,3},{7,1},{8,14},{10,12},{12... | collective-permute-start | bytes 196616 | tf_op jit(solution)/shard_map/ppermute | solution.py:214
  42.2 6.8 %collective-permute-start.25 = (f32[128,256]{1,0:T(8,128)S(1)}, f32[128,256]{1,0:T(8,128)S(1)}, u32[]{:S(2)}, u32[]{:S(2)}) collective-permute-start(f32[128,256]{1,0:T(8,128)S(1)} %maximum_add_fusion), channel_id=1, source_target_pairs={{8,0},{16,8},{24,16},{9,1},{17,9},{25,17},{10,2},{18,10},{26,18},{... | collective-permute-start | bytes 393224 | tf_op jit(solution)/shard_map/ppermute | solution.py:277
  (11 other events, 33.8 us)
where the time goes:
time: 50.2 us; the launch traced here: 49.9 us
  starting transfers between devices  26.6 us (53%)
  Pallas kernels  9.53 us (19%)
  waiting for transfers between devices  9.03 us (18%)
  local copies, waits for them, and re-layouts  2.12 us (4%)
  other arithmetic  1.73 us (3%)
  between operations  0.87 us (2%)
    ppermute x12, starting transfers between devices, across_chips(): lax.ppermute(block, 'z', [(chip, chip ^ k) for chip in range(lax.axis_siz...  17.7 us
    pallas_call x2, Pallas kernels, attend_back(): pl.pallas_call(kernel, out_shape=(jax.ShapeDtypeStruct(queries.shape, jnp...  9.35 us
    ppermute x12, waiting for transfers between devices, across_chips(): lax.ppermute(block, 'z', [(chip, chip ^ k) for chip in range(lax.axis_siz...  6.3 us
    ppermute x1, starting transfers between devices, body(): lax.ppermute(leaving_pair, 'section', [(i, (i - 1) % sections) for i in r...  3.95 us
    ppermute x16, starting transfers between devices, other_core(): return lax.ppermute(block, 'core', [(0, 1), (1, 0)])  3.69 us
    unnamed x10, local copies, waits for them, and re-layouts  2.1 us
    ppermute x1, waiting for transfers between devices, body(): lax.ppermute(first_acc, 'section', [(i, i - 1) for i in range(1, sections)])  1.83 us
    ppermute x1, starting transfers between devices, body(): lax.ppermute(first_acc, 'section', [(i, i - 1) for i in range(1, sections)])  1.28 us
  transfers between devices with their start and end apart: 30, of which 10 were waited for; matrix products, arithmetic and copies ran while one was open for 0% of the time, Pallas kernels for 19%

commit v1 on v0

--- a/solution.py
+++ b/solution.py
@@ -38,15 +38,21 @@
     )(queries, out_grad)
 
 
-def tick_kernel(tick, blocks, aliased, *refs):
+def tick_kernel(tick, arrays, aliased, *refs):
     order_ref, q_ref, g_ref = refs[:3]
-    kv_refs = refs[3 : 3 + blocks]
-    outs = refs[3 + blocks + aliased :]
-    dq_ref = outs[0]
-    term_refs = outs[1 : 1 + blocks]
-    e_ref, dp_ref, p_ref, ds_ref, acc_ref, kt_ref, dq_held, dq_sem = outs[1 + blocks :]
-    local_rows, head_dim = kv_refs[0].shape[0], kv_refs[0].shape[1] // 2
-    heads = dq_held.shape[1] // head_dim
+    outs = refs[3 + arrays + aliased :]
+    dq_ref, near_out_ref, far_out_ref = outs[:3]
+    e_ref, dp_ref, p_ref, ds_ref, acc_ref, kt_ref, dq_held, dq_sem = outs[3:]
+    local_rows, model = dq_held.shape
+    head_dim = near_out_ref.shape[1] // 2
+    half_rows = near_out_ref.shape[0]
+    kv_refs = [
+        ref.at[pl.ds(row, local_rows)]
+        for ref in refs[3 : 3 + arrays]
+        for row in range(0, ref.shape[0], local_rows)
+    ]
+    blocks = len(kv_refs)
+    heads = model // head_dim
     pairs = heads // 2
     width = 2 * local_rows
     chips = blocks // 2
@@ -129,9 +135,11 @@
             acc_ref[:, :head_dim] = key_terms
             acc_ref[:, head_dim:] = value_terms
         else:
-            for slot, out in enumerate(term_refs):
-                out[:, :head_dim] = (key_terms[rows_of(slot)] * scale).astype(out.dtype)
-                out[:, head_dim:] = value_terms[rows_of(slot)].astype(out.dtype)
+            key_terms = key_terms * scale
+            near_out_ref[:, :head_dim] = key_terms[:half_rows]
+            near_out_ref[:, head_dim:] = value_terms[:half_rows]
+            far_out_ref[:, :head_dim] = key_terms[half_rows:].astype(far_out_ref.dtype)
+            far_out_ref[:, head_dim:] = value_terms[half_rows:].astype(far_out_ref.dtype)
         query_t = jnp.dot(kt_ref[...], score_grad, preferred_element_type=jnp.float32) * scale
         for half in range(2):
             lo = (2 * pair + half) * head_dim
@@ -155,17 +163,15 @@
         copy.wait()
 
 
-def attend_back(tick, group_order, queries, q_stack, g_stack, near, far, query_grads):
+def attend_back(tick, group_order, queries, q_stack, g_stack, kv_arrays, query_grads):
     local_rows, model = queries.shape[2:]
-    kv_blocks = [*near, *far]
-    blocks = len(kv_blocks)
-    width = kv_blocks[0].shape[1]
-    key_rows = blocks * local_rows
+    width = kv_arrays[0].shape[1]
+    key_rows = sum(array.shape[0] for array in kv_arrays)
     head_dim = width // 2
     pairs = model // head_dim // 2
     in_vmem = pl.BlockSpec(memory_space=pltpu.VMEM)
-    operands = [group_order, q_stack, g_stack, *kv_blocks]
-    in_specs = [pl.BlockSpec(memory_space=pltpu.SMEM), *[in_vmem] * (2 + blocks)]
+    operands = [group_order, q_stack, g_stack, *kv_arrays]
+    in_specs = [pl.BlockSpec(memory_space=pltpu.SMEM), *[in_vmem] * (2 + len(kv_arrays))]
     aliases = {}
     if query_grads is not None:
         aliases = {len(operands): 0}
@@ -174,17 +180,17 @@
     tile = (pairs, key_rows, 2 * local_rows)
 
     def kernel(*refs):
-        tick_kernel(tick, blocks, len(aliases), *refs)
-
-    kinds = [jnp.float32] * len(near) + [jnp.bfloat16] * len(far)
-    query_grads, *terms = pl.pallas_call(
+        tick_kernel(tick, len(kv_arrays), len(aliases), *refs)
+
+    return pl.pallas_call(
         kernel,
         out_shape=(
             jax.ShapeDtypeStruct(queries.shape, jnp.bfloat16),
-            *[jax.ShapeDtypeStruct((local_rows, width), kind) for kind in kinds],
+            jax.ShapeDtypeStruct((key_rows // 2, width), jnp.float32),
+            jax.ShapeDtypeStruct((key_rows // 2, width), jnp.bfloat16),
         ),
         in_specs=in_specs,
-        out_specs=(pl.BlockSpec(memory_space=pl.ANY), *[in_vmem] * blocks),
+        out_specs=(pl.BlockSpec(memory_space=pl.ANY), in_vmem, in_vmem),
         scratch_shapes=[
             pltpu.VMEM(tile, jnp.float32),
             pltpu.VMEM(tile, jnp.float32),
@@ -203,7 +209,6 @@
             transcendentals=model // head_dim * key_rows * local_rows,
         ),
     )(*operands)
-    return query_grads, terms[: len(near)], terms[len(near) :]
 
 
 def other_core(block):
@@ -225,7 +230,8 @@
     value_grads_in,
     group_order,
 ):
-    head_dim = keys.shape[2]
+    local_rows, head_dim = keys.shape[1:]
+    width = 2 * head_dim
     chips = lax.axis_size("z")
     sections = lax.axis_size("section")
     section = lax.axis_index("section")
@@ -234,7 +240,8 @@
     entering_pair = jnp.concatenate([entering_keys, entering_values], axis=1)
     leaving_pair = jnp.where(section == 0, entering_pair, own_pair)
 
-    near = [across_chips(own_pair, k) for k in range(1, chips)]
+    partners = range(chips - 1, 0, -1)
+    near = [across_chips(own_pair, k) for k in partners][::-1]
     own_far = other_core(own_pair)
     next_pair = lax.ppermute(
         leaving_pair, "section", [(i, (i - 1) % sections) for i in range(sections)]
@@ -242,25 +249,24 @@
     stacks = stacked_heads(queries, out_grad, head_dim)
     near, next_pair, stacks = lax.optimization_barrier((near, next_pair, stacks))
     far = [own_far] + [other_core(block) for block in near]
-    next_near = [next_pair] + [across_chips(next_pair, k) for k in range(1, chips)]
+    next_far = other_core(next_pair)
+    next_near = [across_chips(next_pair, k) for k in partners][::-1]
     query_grads, near_terms, far_terms = attend_back(
-        0, group_order, queries, *stacks, [own_pair, *near], far, None
+        0, group_order, queries, *stacks, [own_pair, *near, *far], None
     )
     query_grads, far_terms, next_near = lax.optimization_barrier(
         (query_grads, far_terms, next_near)
     )
-    next_far = [other_core(block) for block in next_near]
+    next_kv = [next_pair, *next_near, next_far, other_core(jnp.concatenate(next_near, axis=0))]
 
     def chip_sums(near_terms, far_terms):
-        sums = [
-            mine + other_core(theirs).astype(jnp.float32)
-            for mine, theirs in zip(near_terms, far_terms)
-        ]
-        return sums[0], [block.astype(jnp.bfloat16) for block in sums[1:]]
+        sums = near_terms + other_core(far_terms).astype(jnp.float32)
+        sums = sums.reshape(chips, local_rows, width)
+        return sums[0], [sums[k].astype(jnp.bfloat16) for k in range(1, chips)]
 
     def reduced(own_sum, leaving):
-        for k, block in enumerate(leaving, 1):
-            own_sum = own_sum + across_chips(block, k).astype(jnp.float32)
+        for k in partners:
+            own_sum = own_sum + across_chips(leaving[k - 1], k).astype(jnp.float32)
         return own_sum
 
     own_sum, leaving = chip_sums(near_terms, far_terms)
@@ -269,13 +275,11 @@
         own_sum, leaving
     )
     query_grads, near_terms, far_terms = attend_back(
-        1, group_order, queries, *stacks, next_near, next_far, query_grads
+        1, group_order, queries, *stacks, next_kv, query_grads
     )
     first_acc, far_terms = lax.optimization_barrier((first_acc, far_terms))
-    own_sum, leaving = chip_sums(near_terms, far_terms)
-    first_acc, leaving = lax.optimization_barrier((first_acc, leaving))
     moved_acc = lax.ppermute(first_acc, "section", [(i, i - 1) for i in range(1, sections)])
-    second_acc = moved_acc + reduced(own_sum, leaving)
+    second_acc = moved_acc + reduced(*chip_sums(near_terms, far_terms))
     key_grads = jnp.stack([first_acc[:, :head_dim], second_acc[:, :head_dim]], axis=0)[:, None]
     value_grads = jnp.stack([first_acc[:, head_dim:], second_acc[:, head_dim:]], axis=0)[:, None]
     return (query_grads, key_grads, value_grads)

time: 50.2 us -> 46.4 us (0.924)
  the two profiles are of different devices: /device:TPU:0 before, /device:TPU:5 now
where the time goes in v1:
time: 46.4 us; the launch traced here: 46.1 us
  starting transfers between devices  25.6 us (55%)
  Pallas kernels  9.53 us (21%)
  waiting for transfers between devices  6.27 us (14%)
  local copies, waits for them, and re-layouts  2.15 us (5%)
  other arithmetic  1.79 us (4%)
  between operations  0.83 us (2%)
    ppermute x12, starting transfers between devices, across_chips(): lax.ppermute(block, 'z', [(chip, chip ^ k) for chip in range(lax.axis_siz...  14.4 us
    pallas_call x2, Pallas kernels, attend_back(): pl.pallas_call(kernel, out_shape=(jax.ShapeDtypeStruct(queries.shape, jnp...  9.35 us
    ppermute x8, starting transfers between devices, other_core(): return lax.ppermute(block, 'core', [(0, 1), (1, 0)])  6.6 us
    ppermute x12, waiting for transfers between devices, across_chips(): lax.ppermute(block, 'z', [(chip, chip ^ k) for chip in range(lax.axis_siz...  5.68 us
    ppermute x1, starting transfers between devices, body(): lax.ppermute(first_acc, 'section', [(i, i - 1) for i in range(1, sections)])  3.35 us
    unnamed x10, local copies, waits for them, and re-layouts  2.1 us
    ppermute x1, starting transfers between devices, body(): lax.ppermute(leaving_pair, 'section', [(i, (i - 1) % sections) for i in r...  1.15 us
  transfers between devices with their start and end apart: 22, of which 5 were waited for; matrix products, arithmetic and copies ran while one was open for 0% of the time, Pallas kernels for 21%

profile of v1, /device:TPU:5, one launch (start us, length us, event | category | flops | bytes accessed | tf_op | source)
XLA Modules:
  0.0 46.1 jit_solution(9263496180421169989)
XLA Ops:
  0.6 0.8 %maximum_select_fusion = (bf16[128,256]{1,0:T(8,128)(2,1)S(1)}, bf16[128,256]{1,0:T(8,128)(2,1)S(1)}) fusion(bf16[128,128]{1,0:T(8,128)(2,1)} %param.14, bf16[128,128]{1,0:T(8,128)(2,1)} %param.13, pred[]{:T(512)S(6)} %eq.3, bf16[128,128]{1,0:T(8,128)(2,1)} %bitcast.22, bf16[128,128]{1,0:T(8,128)(2,1)} %bitcast.23), kind=kLoop, calls=%fused_computation.16 | loop fusion | flops 294912 | bytes 262145 | tf_op jit(solution)/shard_map/jit(_where)/select_n | solution.py:241
  1.5 1.4 %collective-permute-start = (bf16[128,256]{1,0:T(8,128)(2,1)S(1)}, bf16[128,256]{1,0:T(8,128)(2,1)S(1)}, u32[]{:S(2)}, u32[]{:S(2)}) collective-permute-start(bf16[128,256]{1,0:T(8,128)(2,1)S(1)} %get-tuple-element.71.refs_3_), channel_id=1, source_target_pairs={{0,2},{2,0},{4,6},{6,4},{1,3},{3,1},{5,7},{7,5},{8,10},{10,8},{12,... | collective-permute-start | bytes 196616 | tf_op jit(solution)/shard_map/ppermute | solution.py:219
  2.8 2.3 %collective-permute-start.1 = (bf16[128,256]{1,0:T(8,128)(2,1)S(1)}, bf16[128,256]{1,0:T(8,128)(2,1)S(1)}, u32[]{:S(2)}, u32[]{:S(2)}) collective-permute-start(bf16[128,256]{1,0:T(8,128)(2,1)S(1)} %get-tuple-element.71.refs_3_), channel_id=1, source_target_pairs={{0,4},{2,6},{4,0},{6,2},{1,5},{3,7},{5,1},{7,3},{8,12},{10,14},{12... | collective-permute-start | bytes 196616 | tf_op jit(solution)/shard_map/ppermute | solution.py:219
  5.1 1.2 %collective-permute-start.3 = (bf16[128,256]{1,0:T(8,128)(2,1)S(1)}, bf16[128,256]{1,0:T(8,128)(2,1)S(1)}, u32[]{:S(2)}, u32[]{:S(2)}) collective-permute-start(bf16[128,256]{1,0:T(8,128)(2,1)S(1)} %get-tuple-element.70), channel_id=1, source_target_pairs={{0,24},{8,0},{16,8},{24,16},{1,25},{9,1},{17,9},{25,17},{2,26},{10... | collective-permute-start | bytes 196616 | tf_op jit(solution)/shard_map/ppermute | solution.py:246
  6.3 1.7 %collective-permute-start.4 = (bf16[128,256]{1,0:T(8,128)(2,1)S(1)}, bf16[128,256]{1,0:T(8,128)(2,1)S(1)}, u32[]{:S(2)}, u32[]{:S(2)}) collective-permute-start(bf16[128,256]{1,0:T(8,128)(2,1)S(1)} %get-tuple-element.71.refs_3_), channel_id=1, source_target_pairs={{0,1},{1,0},{2,3},{3,2},{4,5},{5,4},{6,7},{7,6},{8,9},{9,8},{10,11... | collective-permute-start | bytes 196616 | tf_op jit(solution)/shard_map/ppermute | solution.py:215
  8.0 1.0 %copy-done = bf16[2,1,128,1024]{3,2,1,0:T(8,128)(2,1)S(1)} copy-done((bf16[2,1,128,1024]{3,2,1,0:T(8,128)(2,1)S(1)}, bf16[2,1,128,1024]{3,2,1,0:T(8,128)(2,1)}, u32[]{:S(2)}) %copy-start) | copy-done | bytes 524312
  9.1 1.0 %copy-done.1 = bf16[2,1,128,1024]{3,2,1,0:T(8,128)(2,1)S(1)} copy-done((bf16[2,1,128,1024]{3,2,1,0:T(8,128)(2,1)S(1)}, bf16[2,1,128,1024]{3,2,1,0:T(8,128)(2,1)}, u32[]{:S(2)}) %copy-start.1) | copy-done | bytes 524312
  10.4 2.1 %collective-permute-start.5 = (bf16[128,256]{1,0:T(8,128)(2,1)S(1)}, bf16[128,256]{1,0:T(8,128)(2,1)S(1)}, u32[]{:S(2)}, u32[]{:S(2)}) collective-permute-start(bf16[128,256]{1,0:T(8,128)(2,1)S(1)} %collective-permute-done.refs_4_), channel_id=1, source_target_pairs={{0,1},{1,0},{2,3},{3,2},{4,5},{5,4},{6,7},{7,6},{8,9},{9,8},{10,11... | collective-permute-start | bytes 196616 | tf_op jit(solution)/shard_map/ppermute | solution.py:215
  13.0 1.7 %collective-permute-start.10 = (bf16[128,256]{1,0:T(8,128)(2,1)S(1)}, bf16[128,256]{1,0:T(8,128)(2,1)S(1)}, u32[]{:S(2)}, u32[]{:S(2)}) collective-permute-start(bf16[128,256]{1,0:T(8,128)(2,1)S(1)} %collective-permute-done.3.refs_3_), channel_id=1, source_target_pairs={{0,6},{2,4},{4,2},{6,0},{1,7},{3,5},{5,3},{7,1},{8,14},{10,12},{12... | collective-permute-start | bytes 196616 | tf_op jit(solution)/shard_map/ppermute | solution.py:219
  14.7 1.8 %collective-permute-start.9 = (bf16[128,256]{1,0:T(8,128)(2,1)S(1)}, bf16[128,256]{1,0:T(8,128)(2,1)S(1)}, u32[]{:S(2)}, u32[]{:S(2)}) collective-permute-start(bf16[128,256]{1,0:T(8,128)(2,1)S(1)} %collective-permute-done.3.refs_3_), channel_id=1, source_target_pairs={{0,4},{2,6},{4,0},{6,2},{1,5},{3,7},{5,1},{7,3},{8,12},{10,14},{12... | collective-permute-start | bytes 196616 | tf_op jit(solution)/shard_map/ppermute | solution.py:219
  16.5 4.7 %shard_map.113 = (bf16[2,1,128,1024]{3,2,1,0:T(8,128)(2,1)}, f32[512,256]{1,0:T(8,128)S(1)}, bf16[512,256]{1,0:T(8,128)(2,1)S(1)}) custom-call(s32[8]{0:T(128)S(1)} %copy-done.2, bf16[2048,128]{1,0:T(8,128)(2,1)S(1)} %get-tuple-element.30.refs_1_, bf16[2048,128]{1,0:T(8,128)(2,1)S(1)} %get-tuple-element.31.refs_2_, ...), custom_call_target="tpu_custom_call" | custom-call | flops 5368709120 | bytes 2097152 | tf_op jit(solution)/shard_map/pallas_call | solution.py:185
  21.5 0.8 %collective-permute-start.13 = (bf16[512,256]{1,0:T(8,128)(2,1)S(1)}, bf16[512,256]{1,0:T(8,128)(2,1)S(1)}, u32[]{:S(2)}, u32[]{:S(2)}) collective-permute-start(bf16[512,256]{1,0:T(8,128)(2,1)S(1)} %get-tuple-element.43), channel_id=1, source_target_pairs={{0,1},{1,0},{2,3},{3,2},{4,5},{5,4},{6,7},{7,6},{8,9},{9,8},{10,11... | collective-permute-start | bytes 786440 | tf_op jit(solution)/shard_map/ppermute | solution.py:215
  22.3 0.5 %collective-permute-start.12 = (bf16[384,256]{1,0:T(8,128)(2,1)S(1)}, bf16[384,256]{1,0:T(8,128)(2,1)S(1)}, u32[]{:S(2)}, u32[]{:S(2)}) collective-permute-start(bf16[384,256]{1,0:T(8,128)(2,1)S(1)} %pad_maximum_fusion), channel_id=1, source_target_pairs={{0,1},{1,0},{2,3},{3,2},{4,5},{5,4},{6,7},{7,6},{8,9},{9,8},{10,11... | collective-permute-start | bytes 589832 | tf_op jit(solution)/shard_map/ppermute | solution.py:215
  22.8 0.6 %collective-permute-done.13 = bf16[512,256]{1,0:T(8,128)(2,1)S(1)} collective-permute-done((bf16[512,256]{1,0:T(8,128)(2,1)S(1)}, bf16[512,256]{1,0:T(8,128)(2,1)S(1)}, u32[]{:S(2)}, u32[]{:S(2)}) %collective-permute-start.13) | collective-permute-done | bytes 262176 | tf_op jit(solution)/shard_map/ppermute | solution.py:215
  23.5 1.8 %collective-permute-start.14 = (bf16[128,256]{1,0:T(8,128)(2,1)S(1)}, bf16[128,256]{1,0:T(8,128)(2,1)S(1)}, u32[]{:S(2)}, u32[]{:S(2)}) collective-permute-start(bf16[128,256]{1,0:T(8,128)(2,1)S(1)} %get-tuple-element.46), channel_id=1, source_target_pairs={{0,6},{2,4},{4,2},{6,0},{1,7},{3,5},{5,3},{7,1},{8,14},{10,12},{12... | collective-permute-start | bytes 196616 | tf_op jit(solution)/shard_map/ppermute | solution.py:219
  25.3 1.8 %collective-permute-start.16 = (bf16[128,256]{1,0:T(8,128)(2,1)S(1)}, bf16[128,256]{1,0:T(8,128)(2,1)S(1)}, u32[]{:S(2)}, u32[]{:S(2)}) collective-permute-start(bf16[128,256]{1,0:T(8,128)(2,1)S(1)} %get-tuple-element.48), channel_id=1, source_target_pairs={{0,2},{2,0},{4,6},{6,4},{1,3},{3,1},{5,7},{7,5},{8,10},{10,8},{12,... | collective-permute-start | bytes 196616 | tf_op jit(solution)/shard_map/ppermute | solution.py:219
  27.1 4.7 %shard_map.114 = (bf16[2,1,128,1024]{3,2,1,0:T(8,128)(2,1)}, f32[512,256]{1,0:T(8,128)S(1)}, bf16[512,256]{1,0:T(8,128)(2,1)S(1)}) custom-call(s32[8]{0:T(128)S(1)} %copy-done.2, bf16[2048,128]{1,0:T(8,128)(2,1)S(1)} %get-tuple-element.30.refs_1_, bf16[2048,128]{1,0:T(8,128)(2,1)S(1)} %get-tuple-element.31.refs_2_, ...), custom_call_target="tpu_custom_call", output_to_operand_aliasing={{0}: (9, {})} | custom-call | flops 5368709120 | bytes 2097152 | tf_op jit(solution)/shard_map/pallas_call | solution.py:185
  32.3 0.9 %collective-permute-start.18 = (bf16[512,256]{1,0:T(8,128)(2,1)S(1)}, bf16[512,256]{1,0:T(8,128)(2,1)S(1)}, u32[]{:S(2)}, u32[]{:S(2)}) collective-permute-start(bf16[512,256]{1,0:T(8,128)(2,1)S(1)} %get-tuple-element.52), channel_id=1, source_target_pairs={{0,1},{1,0},{2,3},{3,2},{4,5},{5,4},{6,7},{7,6},{8,9},{9,8},{10,11... | collective-permute-start | bytes 786440 | tf_op jit(solution)/shard_map/ppermute | solution.py:215
  33.2 3.4 %collective-permute-start.17 = (f32[128,256]{1,0:T(8,128)S(1)}, f32[128,256]{1,0:T(8,128)S(1)}, u32[]{:S(2)}, u32[]{:S(2)}) collective-permute-start(f32[128,256]{1,0:T(8,128)S(1)} %fusion.5), channel_id=1, source_target_pairs={{8,0},{16,8},{24,16},{9,1},{17,9},{25,17},{10,2},{18,10},{26,18},{... | collective-permute-start | bytes 393224 | tf_op jit(solution)/shard_map/ppermute | solution.py:281
  36.7 2.3 %collective-permute-start.19 = (bf16[128,256]{1,0:T(8,128)(2,1)S(1)}, bf16[128,256]{1,0:T(8,128)(2,1)S(1)}, u32[]{:S(2)}, u32[]{:S(2)}) collective-permute-start(bf16[128,256]{1,0:T(8,128)(2,1)S(1)} %get-tuple-element.60), channel_id=1, source_target_pairs={{0,6},{2,4},{4,2},{6,0},{1,7},{3,5},{5,3},{7,1},{8,14},{10,12},{12... | collective-permute-start | bytes 196616 | tf_op jit(solution)/shard_map/ppermute | solution.py:219
  39.0 1.3 %collective-permute-start.21 = (bf16[128,256]{1,0:T(8,128)(2,1)S(1)}, bf16[128,256]{1,0:T(8,128)(2,1)S(1)}, u32[]{:S(2)}, u32[]{:S(2)}) collective-permute-start(bf16[128,256]{1,0:T(8,128)(2,1)S(1)} %get-tuple-element.61), channel_id=1, source_target_pairs={{0,2},{2,0},{4,6},{6,4},{1,3},{3,1},{5,7},{7,5},{8,10},{10,8},{12,... | collective-permute-start | bytes 196616 | tf_op jit(solution)/shard_map/ppermute | solution.py:219
  40.3 1.4 %collective-permute-done.19 = bf16[128,256]{1,0:T(8,128)(2,1)S(1)} collective-permute-done((bf16[128,256]{1,0:T(8,128)(2,1)S(1)}, bf16[128,256]{1,0:T(8,128)(2,1)S(1)}, u32[]{:S(2)}, u32[]{:S(2)}) %collective-permute-start.19) | collective-permute-done | bytes 65568 | tf_op jit(solution)/shard_map/ppermute | solution.py:219
  41.7 3.7 %collective-permute-done.20 = bf16[128,256]{1,0:T(8,128)(2,1)S(1)} collective-permute-done((bf16[128,256]{1,0:T(8,128)(2,1)S(1)}, bf16[128,256]{1,0:T(8,128)(2,1)S(1)}, u32[]{:S(2)}, u32[]{:S(2)}) %collective-permute-start.20) | collective-permute-done | bytes 65568 | tf_op jit(solution)/shard_map/ppermute | solution.py:219
  45.4 0.7 %maximum_bitcast_fusion = (f32[2,1,128,128]{3,2,1,0:T(8,128)}, f32[2,1,128,128]{3,2,1,0:T(8,128)}) fusion(f32[1,128,128]{2,1,0:T(8,128)S(1)} %get-tuple-element.69, f32[1,128,128]{2,1,0:T(8,128)S(1)} %get-tuple-element.67, f32[1,128,128]{2,1,0:T(8,128)S(1)} %get-tuple-element.68, f32[1,128,128]{2,1,0:T(8,128)S(1)} %get-tuple-element.66), kind=kLoop, calls=%fused_computation.11 | loop fusion | flops 65536 | bytes 524288
  (44 shorter events, 1.7 us)
Async XLA Ops:
  1.5 8.8 %collective-permute-start = (bf16[128,256]{1,0:T(8,128)(2,1)S(1)}, bf16[128,256]{1,0:T(8,128)(2,1)S(1)}, u32[]{:S(2)}, u32[]{:S(2)}) collective-permute-start(bf16[128,256]{1,0:T(8,128)(2,1)S(1)} %get-tuple-element.71.refs_3_), channel_id=1, source_target_pairs={{0,2},{2,0},{4,6},{6,4},{1,3},{3,1},{5,7},{7,5},{8,10},{10,8},{12,... | collective-permute-start | bytes 196616 | tf_op jit(solution)/shard_map/ppermute | solution.py:219
  2.8 7.5 %collective-permute-start.1 = (bf16[128,256]{1,0:T(8,128)(2,1)S(1)}, bf16[128,256]{1,0:T(8,128)(2,1)S(1)}, u32[]{:S(2)}, u32[]{:S(2)}) collective-permute-start(bf16[128,256]{1,0:T(8,128)(2,1)S(1)} %get-tuple-element.71.refs_3_), channel_id=1, source_target_pairs={{0,4},{2,6},{4,0},{6,2},{1,5},{3,7},{5,1},{7,3},{8,12},{10,14},{12... | collective-permute-start | bytes 196616 | tf_op jit(solution)/shard_map/ppermute | solution.py:219
  5.1 5.2 %collective-permute-start.2 = (bf16[128,256]{1,0:T(8,128)(2,1)S(1)}, bf16[128,256]{1,0:T(8,128)(2,1)S(1)}, u32[]{:S(2)}, u32[]{:S(2)}) collective-permute-start(bf16[128,256]{1,0:T(8,128)(2,1)S(1)} %get-tuple-element.71.refs_3_), channel_id=1, source_target_pairs={{0,6},{2,4},{4,2},{6,0},{1,7},{3,5},{5,3},{7,1},{8,14},{10,12},{12... | collective-permute-start | bytes 196616 | tf_op jit(solution)/shard_map/ppermute | solution.py:219
  5.1 5.2 %collective-permute-start.3 = (bf16[128,256]{1,0:T(8,128)(2,1)S(1)}, bf16[128,256]{1,0:T(8,128)(2,1)S(1)}, u32[]{:S(2)}, u32[]{:S(2)}) collective-permute-start(bf16[128,256]{1,0:T(8,128)(2,1)S(1)} %get-tuple-element.70), channel_id=1, source_target_pairs={{0,24},{8,0},{16,8},{24,16},{1,25},{9,1},{17,9},{25,17},{2,26},{10... | collective-permute-start | bytes 196616 | tf_op jit(solution)/shard_map/ppermute | solution.py:246
  6.3 8.4 %collective-permute-start.4 = (bf16[128,256]{1,0:T(8,128)(2,1)S(1)}, bf16[128,256]{1,0:T(8,128)(2,1)S(1)}, u32[]{:S(2)}, u32[]{:S(2)}) collective-permute-start(bf16[128,256]{1,0:T(8,128)(2,1)S(1)} %get-tuple-element.71.refs_3_), channel_id=1, source_target_pairs={{0,1},{1,0},{2,3},{3,2},{4,5},{5,4},{6,7},{7,6},{8,9},{9,8},{10,11... | collective-permute-start | bytes 196616 | tf_op jit(solution)/shard_map/ppermute | solution.py:215
  10.4 4.4 %collective-permute-start.5 = (bf16[128,256]{1,0:T(8,128)(2,1)S(1)}, bf16[128,256]{1,0:T(8,128)(2,1)S(1)}, u32[]{:S(2)}, u32[]{:S(2)}) collective-permute-start(bf16[128,256]{1,0:T(8,128)(2,1)S(1)} %collective-permute-done.refs_4_), channel_id=1, source_target_pairs={{0,1},{1,0},{2,3},{3,2},{4,5},{5,4},{6,7},{7,6},{8,9},{9,8},{10,11... | collective-permute-start | bytes 196616 | tf_op jit(solution)/shard_map/ppermute | solution.py:215
  12.5 4.1 %collective-permute-start.6 = (bf16[128,256]{1,0:T(8,128)(2,1)S(1)}, bf16[128,256]{1,0:T(8,128)(2,1)S(1)}, u32[]{:S(2)}, u32[]{:S(2)}) collective-permute-start(bf16[128,256]{1,0:T(8,128)(2,1)S(1)} %collective-permute-done.1.refs_5_), channel_id=1, source_target_pairs={{0,1},{1,0},{2,3},{3,2},{4,5},{5,4},{6,7},{7,6},{8,9},{9,8},{10,11... | collective-permute-start | bytes 196616 | tf_op jit(solution)/shard_map/ppermute | solution.py:215
  12.5 4.0 %collective-permute-start.7 = (bf16[128,256]{1,0:T(8,128)(2,1)S(1)}, bf16[128,256]{1,0:T(8,128)(2,1)S(1)}, u32[]{:S(2)}, u32[]{:S(2)}) collective-permute-start(bf16[128,256]{1,0:T(8,128)(2,1)S(1)} %collective-permute-done.2.refs_6_), channel_id=1, source_target_pairs={{0,1},{1,0},{2,3},{3,2},{4,5},{5,4},{6,7},{7,6},{8,9},{9,8},{10,11... | collective-permute-start | bytes 196616 | tf_op jit(solution)/shard_map/ppermute | solution.py:215
  13.0 8.3 %collective-permute-start.10 = (bf16[128,256]{1,0:T(8,128)(2,1)S(1)}, bf16[128,256]{1,0:T(8,128)(2,1)S(1)}, u32[]{:S(2)}, u32[]{:S(2)}) collective-permute-start(bf16[128,256]{1,0:T(8,128)(2,1)S(1)} %collective-permute-done.3.refs_3_), channel_id=1, source_target_pairs={{0,6},{2,4},{4,2},{6,0},{1,7},{3,5},{5,3},{7,1},{8,14},{10,12},{12... | collective-permute-start | bytes 196616 | tf_op jit(solution)/shard_map/ppermute | solution.py:219
  14.7 6.8 %collective-permute-start.8 = (bf16[128,256]{1,0:T(8,128)(2,1)S(1)}, bf16[128,256]{1,0:T(8,128)(2,1)S(1)}, u32[]{:S(2)}, u32[]{:S(2)}) collective-permute-start(bf16[128,256]{1,0:T(8,128)(2,1)S(1)} %collective-permute-done.3.refs_3_), channel_id=1, source_target_pairs={{0,2},{2,0},{4,6},{6,4},{1,3},{3,1},{5,7},{7,5},{8,10},{10,8},{12,... | collective-permute-start | bytes 196616 | tf_op jit(solution)/shard_map/ppermute | solution.py:219
  14.7 6.8 %collective-permute-start.9 = (bf16[128,256]{1,0:T(8,128)(2,1)S(1)}, bf16[128,256]{1,0:T(8,128)(2,1)S(1)}, u32[]{:S(2)}, u32[]{:S(2)}) collective-permute-start(bf16[128,256]{1,0:T(8,128)(2,1)S(1)} %collective-permute-done.3.refs_3_), channel_id=1, source_target_pairs={{0,4},{2,6},{4,0},{6,2},{1,5},{3,7},{5,1},{7,3},{8,12},{10,14},{12... | collective-permute-start | bytes 196616 | tf_op jit(solution)/shard_map/ppermute | solution.py:219
  21.5 1.9 %collective-permute-start.13 = (bf16[512,256]{1,0:T(8,128)(2,1)S(1)}, bf16[512,256]{1,0:T(8,128)(2,1)S(1)}, u32[]{:S(2)}, u32[]{:S(2)}) collective-permute-start(bf16[512,256]{1,0:T(8,128)(2,1)S(1)} %get-tuple-element.43), channel_id=1, source_target_pairs={{0,1},{1,0},{2,3},{3,2},{4,5},{5,4},{6,7},{7,6},{8,9},{9,8},{10,11... | collective-permute-start | bytes 786440 | tf_op jit(solution)/shard_map/ppermute | solution.py:215
  22.2 4.9 %collective-permute-start.11 = (bf16[128,256]{1,0:T(8,128)(2,1)S(1)}, bf16[128,256]{1,0:T(8,128)(2,1)S(1)}, u32[]{:S(2)}, u32[]{:S(2)}) collective-permute-start(bf16[128,256]{1,0:T(8,128)(2,1)S(1)} %collective-permute-done.3.refs_3_), channel_id=1, source_target_pairs={{0,1},{1,0},{2,3},{3,2},{4,5},{5,4},{6,7},{7,6},{8,9},{9,8},{10,11... | collective-permute-start | bytes 196616 | tf_op jit(solution)/shard_map/ppermute | solution.py:215
  22.3 4.8 %collective-permute-start.12 = (bf16[384,256]{1,0:T(8,128)(2,1)S(1)}, bf16[384,256]{1,0:T(8,128)(2,1)S(1)}, u32[]{:S(2)}, u32[]{:S(2)}) collective-permute-start(bf16[384,256]{1,0:T(8,128)(2,1)S(1)} %pad_maximum_fusion), channel_id=1, source_target_pairs={{0,1},{1,0},{2,3},{3,2},{4,5},{5,4},{6,7},{7,6},{8,9},{9,8},{10,11... | collective-permute-start | bytes 589832 | tf_op jit(solution)/shard_map/ppermute | solution.py:215
  23.5 8.7 %copy-start.3 = (f32[1,128,128]{2,1,0:T(8,128)S(1)}, f32[1,128,128]{2,1,0:T(8,128)}, u32[]{:S(2)}) copy-start(f32[1,128,128]{2,1,0:T(8,128)} %param.16) | copy-start | bytes 196612
  23.5 8.7 %copy-start.4 = (f32[1,128,128]{2,1,0:T(8,128)S(1)}, f32[1,128,128]{2,1,0:T(8,128)}, u32[]{:S(2)}) copy-start(f32[1,128,128]{2,1,0:T(8,128)} %param.15) | copy-start | bytes 196612
  23.5 8.3 %collective-permute-start.14 = (bf16[128,256]{1,0:T(8,128)(2,1)S(1)}, bf16[128,256]{1,0:T(8,128)(2,1)S(1)}, u32[]{:S(2)}, u32[]{:S(2)}) collective-permute-start(bf16[128,256]{1,0:T(8,128)(2,1)S(1)} %get-tuple-element.46), channel_id=1, source_target_pairs={{0,6},{2,4},{4,2},{6,0},{1,7},{3,5},{5,3},{7,1},{8,14},{10,12},{12... | collective-permute-start | bytes 196616 | tf_op jit(solution)/shard_map/ppermute | solution.py:219
  25.3 6.9 %collective-permute-start.15 = (bf16[128,256]{1,0:T(8,128)(2,1)S(1)}, bf16[128,256]{1,0:T(8,128)(2,1)S(1)}, u32[]{:S(2)}, u32[]{:S(2)}) collective-permute-start(bf16[128,256]{1,0:T(8,128)(2,1)S(1)} %get-tuple-element.47), channel_id=1, source_target_pairs={{0,4},{2,6},{4,0},{6,2},{1,5},{3,7},{5,1},{7,3},{8,12},{10,14},{12... | collective-permute-start | bytes 196616 | tf_op jit(solution)/shard_map/ppermute | solution.py:219
  25.3 6.9 %collective-permute-start.16 = (bf16[128,256]{1,0:T(8,128)(2,1)S(1)}, bf16[128,256]{1,0:T(8,128)(2,1)S(1)}, u32[]{:S(2)}, u32[]{:S(2)}) collective-permute-start(bf16[128,256]{1,0:T(8,128)(2,1)S(1)} %get-tuple-element.48), channel_id=1, source_target_pairs={{0,2},{2,0},{4,6},{6,4},{1,3},{3,1},{5,7},{7,5},{8,10},{10,8},{12,... | collective-permute-start | bytes 196616 | tf_op jit(solution)/shard_map/ppermute | solution.py:219
  32.3 4.3 %collective-permute-start.18 = (bf16[512,256]{1,0:T(8,128)(2,1)S(1)}, bf16[512,256]{1,0:T(8,128)(2,1)S(1)}, u32[]{:S(2)}, u32[]{:S(2)}) collective-permute-start(bf16[512,256]{1,0:T(8,128)(2,1)S(1)} %get-tuple-element.52), channel_id=1, source_target_pairs={{0,1},{1,0},{2,3},{3,2},{4,5},{5,4},{6,7},{7,6},{8,9},{9,8},{10,11... | collective-permute-start | bytes 786440 | tf_op jit(solution)/shard_map/ppermute | solution.py:215
  33.2 7.1 %collective-permute-start.17 = (f32[128,256]{1,0:T(8,128)S(1)}, f32[128,256]{1,0:T(8,128)S(1)}, u32[]{:S(2)}, u32[]{:S(2)}) collective-permute-start(f32[128,256]{1,0:T(8,128)S(1)} %fusion.5), channel_id=1, source_target_pairs={{8,0},{16,8},{24,16},{9,1},{17,9},{25,17},{10,2},{18,10},{26,18},{... | collective-permute-start | bytes 393224 | tf_op jit(solution)/shard_map/ppermute | solution.py:281
  36.7 5.0 %collective-permute-start.19 = (bf16[128,256]{1,0:T(8,128)(2,1)S(1)}, bf16[128,256]{1,0:T(8,128)(2,1)S(1)}, u32[]{:S(2)}, u32[]{:S(2)}) collective-permute-start(bf16[128,256]{1,0:T(8,128)(2,1)S(1)} %get-tuple-element.60), channel_id=1, source_target_pairs={{0,6},{2,4},{4,2},{6,0},{1,7},{3,5},{5,3},{7,1},{8,14},{10,12},{12... | collective-permute-start | bytes 196616 | tf_op jit(solution)/shard_map/ppermute | solution.py:219
  39.0 6.4 %collective-permute-start.20 = (bf16[128,256]{1,0:T(8,128)(2,1)S(1)}, bf16[128,256]{1,0:T(8,128)(2,1)S(1)}, u32[]{:S(2)}, u32[]{:S(2)}) collective-permute-start(bf16[128,256]{1,0:T(8,128)(2,1)S(1)} %get-tuple-element.62), channel_id=1, source_target_pairs={{0,4},{2,6},{4,0},{6,2},{1,5},{3,7},{5,1},{7,3},{8,12},{10,14},{12... | collective-permute-start | bytes 196616 | tf_op jit(solution)/shard_map/ppermute | solution.py:219
  39.0 6.4 %collective-permute-start.21 = (bf16[128,256]{1,0:T(8,128)(2,1)S(1)}, bf16[128,256]{1,0:T(8,128)(2,1)S(1)}, u32[]{:S(2)}, u32[]{:S(2)}) collective-permute-start(bf16[128,256]{1,0:T(8,128)(2,1)S(1)} %get-tuple-element.61), channel_id=1, source_target_pairs={{0,2},{2,0},{4,6},{6,4},{1,3},{3,1},{5,7},{7,5},{8,10},{10,8},{12,... | collective-permute-start | bytes 196616 | tf_op jit(solution)/shard_map/ppermute | solution.py:219
  (3 other events, 8.3 us)

commit v2 on v1

--- a/solution.py
+++ b/solution.py
@@ -45,7 +45,6 @@
     e_ref, dp_ref, p_ref, ds_ref, acc_ref, kt_ref, dq_held, dq_sem = outs[3:]
     local_rows, model = dq_held.shape
     head_dim = near_out_ref.shape[1] // 2
-    half_rows = near_out_ref.shape[0]
     kv_refs = [
         ref.at[pl.ds(row, local_rows)]
         for ref in refs[3 : 3 + arrays]
@@ -63,9 +62,18 @@
     chip = lax.axis_index("z")
     own_group = order_ref[2 * chip + core]
 
+    half = chips // 2 - 1
+    mine = [1 + core * half + j for j in range(half)]
+    partners = [1 + (1 - core) * half + j for j in range(half)]
+    places = [(0, True), (0, False), (chips - 1, True)]
+    places += [(k, same) for k in mine for same in (True, False)]
+    places += [(chips - 1, False)]
+    places += [(k, same) for k in partners for same in (False, True)]
+
     def allowed(slot):
-        source = jnp.bitwise_xor(chip, slot % chips)
-        parity = core if slot < chips else 1 - core
+        k, same = places[slot]
+        source = jnp.bitwise_xor(chip, k)
+        parity = core if same else 1 - core
         return order_ref[2 * source + parity] < own_group
 
     for slot in range(blocks):
@@ -135,11 +143,11 @@
             acc_ref[:, :head_dim] = key_terms
             acc_ref[:, head_dim:] = value_terms
         else:
-            key_terms = key_terms * scale
-            near_out_ref[:, :head_dim] = key_terms[:half_rows]
-            near_out_ref[:, head_dim:] = value_terms[:half_rows]
-            far_out_ref[:, :head_dim] = key_terms[half_rows:].astype(far_out_ref.dtype)
-            far_out_ref[:, head_dim:] = value_terms[half_rows:].astype(far_out_ref.dtype)
+            for slot, (k, same) in enumerate(places):
+                out = near_out_ref if same else far_out_ref
+                rows = pl.ds(pl.multiple_of(k * local_rows, local_rows), local_rows)
+                out[rows, :head_dim] = (key_terms[rows_of(slot)] * scale).astype(out.dtype)
+                out[rows, head_dim:] = value_terms[rows_of(slot)].astype(out.dtype)
         query_t = jnp.dot(kt_ref[...], score_grad, preferred_element_type=jnp.float32) * scale
         for half in range(2):
             lo = (2 * pair + half) * head_dim
@@ -219,6 +227,23 @@
     return lax.ppermute(block, "z", [(chip, chip ^ k) for chip in range(lax.axis_size("z"))])
 
 
+def across_pairs(blocks, j):
+    chips = lax.axis_size("z")
+    route = [
+        (2 * chip + core, 2 * (chip ^ (1 + core * (chips // 2 - 1) + j)) + core)
+        for chip in range(chips)
+        for core in range(2)
+    ]
+    return lax.ppermute(blocks, ("z", "core"), route)
+
+
+def gathered(own, own_far):
+    chips = lax.axis_size("z")
+    shared = across_chips(own, chips - 1)
+    both = jnp.concatenate([own, own_far], axis=0)
+    return [shared, *[across_pairs(both, j) for j in range(chips // 2 - 1)]]
+
+
 def body(
     queries,
     out_grad,
@@ -240,24 +265,29 @@
     entering_pair = jnp.concatenate([entering_keys, entering_values], axis=1)
     leaving_pair = jnp.where(section == 0, entering_pair, own_pair)
 
-    partners = range(chips - 1, 0, -1)
-    near = [across_chips(own_pair, k) for k in partners][::-1]
     own_far = other_core(own_pair)
+    shared, *pairs = gathered(own_pair, own_far)
     next_pair = lax.ppermute(
         leaving_pair, "section", [(i, (i - 1) % sections) for i in range(sections)]
     )
     stacks = stacked_heads(queries, out_grad, head_dim)
-    near, next_pair, stacks = lax.optimization_barrier((near, next_pair, stacks))
-    far = [own_far] + [other_core(block) for block in near]
+    pairs, next_pair, stacks = lax.optimization_barrier((pairs, next_pair, stacks))
     next_far = other_core(next_pair)
-    next_near = [across_chips(next_pair, k) for k in partners][::-1]
+    partner_blocks = [other_core(block) for block in (shared, *pairs)]
+    next_blocks = gathered(next_pair, next_far)
     query_grads, near_terms, far_terms = attend_back(
-        0, group_order, queries, *stacks, [own_pair, *near, *far], None
-    )
-    query_grads, far_terms, next_near = lax.optimization_barrier(
-        (query_grads, far_terms, next_near)
-    )
-    next_kv = [next_pair, *next_near, next_far, other_core(jnp.concatenate(next_near, axis=0))]
+        0,
+        group_order,
+        queries,
+        *stacks,
+        [own_pair, own_far, shared, *pairs, *partner_blocks],
+        None,
+    )
+    query_grads, far_terms, next_blocks = lax.optimization_barrier(
+        (query_grads, far_terms, next_blocks)
+    )
+    partner_blocks = other_core(jnp.concatenate(next_blocks, axis=0))
+    next_kv = [next_pair, next_far, *next_blocks, partner_blocks]
 
     def chip_sums(near_terms, far_terms):
         sums = near_terms + other_core(far_terms).astype(jnp.float32)
@@ -265,7 +295,7 @@
         return sums[0], [sums[k].astype(jnp.bfloat16) for k in range(1, chips)]
 
     def reduced(own_sum, leaving):
-        for k in partners:
+        for k in range(chips - 1, 0, -1):
             own_sum = own_sum + across_chips(leaving[k - 1], k).astype(jnp.float32)
         return own_sum
 
@@ -278,8 +308,12 @@
         1, group_order, queries, *stacks, next_kv, query_grads
     )
     first_acc, far_terms = lax.optimization_barrier((first_acc, far_terms))
-    moved_acc = lax.ppermute(first_acc, "section", [(i, i - 1) for i in range(1, sections)])
-    second_acc = moved_acc + reduced(*chip_sums(near_terms, far_terms))
+    odd_acc = lax.ppermute(first_acc, "section", [(i, i - 1) for i in range(1, sections, 2)])
+    own_sum, leaving = chip_sums(near_terms, far_terms)
+    late_acc, leaving = lax.optimization_barrier((first_acc.astype(jnp.bfloat16), leaving))
+    second_acc = reduced(own_sum + odd_acc, leaving)
+    even_acc = lax.ppermute(late_acc, "section", [(i, i - 1) for i in range(2, sections, 2)])
+    second_acc = second_acc + even_acc.astype(jnp.float32)
     key_grads = jnp.stack([first_acc[:, :head_dim], second_acc[:, :head_dim]], axis=0)[:, None]
     value_grads = jnp.stack([first_acc[:, head_dim:], second_acc[:, head_dim:]], axis=0)[:, None]
     return (query_grads, key_grads, value_grads)

time: 46.4 us -> 49.1 us (1.058)
  the two profiles are of different devices: /device:TPU:5 before, /device:TPU:2 now
where the time goes in v2:
time: 49.1 us; the launch traced here: 48.8 us
  starting transfers between devices  23 us (47%)
  waiting for transfers between devices  11.7 us (24%)
  Pallas kernels  9.58 us (20%)
  other arithmetic  2.65 us (5%)
  local copies, waits for them, and re-layouts  1.11 us (2%)
  between operations  0.86 us (2%)
    ppermute x8, starting transfers between devices, across_chips(): lax.ppermute(block, 'z', [(chip, chip ^ k) for chip in range(lax.axis_siz...  14.5 us
    pallas_call x2, Pallas kernels, attend_back(): pl.pallas_call(kernel, out_shape=(jax.ShapeDtypeStruct(queries.shape, jnp...  9.4 us
    ppermute x8, waiting for transfers between devices, across_chips(): lax.ppermute(block, 'z', [(chip, chip ^ k) for chip in range(lax.axis_siz...  4.22 us
    ppermute x1, starting transfers between devices, body(): lax.ppermute(first_acc, 'section', [(i, i - 1) for i in range(1, sections...  3.53 us
    ppermute x1, waiting for transfers between devices, body(): lax.ppermute(late_acc, 'section', [(i, i - 1) for i in range(2, sections,...  2.62 us
    ppermute x7, waiting for transfers between devices, other_core(): return lax.ppermute(block, 'core', [(0, 1), (1, 0)])  2.2 us
    ppermute x2, starting transfers between devices, across_pairs(): return lax.ppermute(blocks, ('z', 'core'), route)  1.88 us
    ppermute x1, waiting for transfers between devices, body(): lax.ppermute(leaving_pair, 'section', [(i, (i - 1) % sections) for i in r...  1.54 us
  transfers between devices with their start and end apart: 20, of which 8 were waited for; matrix products, arithmetic and copies ran while one was open for 0% of the time, Pallas kernels for 20%

profile of v2, /device:TPU:2, one launch (start us, length us, event | category | flops | bytes accessed | tf_op | source)
XLA Modules:
  0.0 48.8 jit_solution(810696196147871063)
XLA Ops:
  0.6 0.9 %maximum_select_fusion = (bf16[128,256]{1,0:T(8,128)(2,1)S(1)}, bf16[128,256]{1,0:T(8,128)(2,1)S(1)}) fusion(bf16[128,128]{1,0:T(8,128)(2,1)} %param.14, bf16[128,128]{1,0:T(8,128)(2,1)} %param.13, pred[]{:T(512)S(6)} %eq.3, bf16[128,128]{1,0:T(8,128)(2,1)} %bitcast.20, bf16[128,128]{1,0:T(8,128)(2,1)} %bitcast.22), kind=kLoop, calls=%fused_computation.19 | loop fusion | flops 294912 | bytes 262145 | tf_op jit(solution)/shard_map/jit(_where)/select_n | solution.py:266
  1.6 1.2 %collective-permute-done.refs_4_ = bf16[128,256]{1,0:T(8,128)(2,1)S(1)} collective-permute-done((bf16[128,256]{1,0:T(8,128)(2,1)S(1)}, bf16[128,256]{1,0:T(8,128)(2,1)S(1)}, u32[]{:S(2)}, u32[]{:S(2)}) %collective-permute-start) | collective-permute-done | bytes 65568 | tf_op jit(solution)/shard_map/ppermute | solution.py:223
  2.9 0.8 %pad_maximum_fusion.1 = bf16[256,256]{1,0:T(8,128)(2,1)S(1)} fusion(bf16[128,256]{1,0:T(8,128)(2,1)S(1)} %collective-permute-done.refs_4_, bf16[128,128]{1,0:T(8,128)(2,1)} %bitcast.21, bf16[128,128]{1,0:T(8,128)(2,1)} %bitcast.23), kind=kLoop, calls=%fused_computation.12 | loop fusion | flops 393216 | bytes 262144 | tf_op jit(solution)/shard_map/concatenate | solution.py:243
  3.6 1.6 %collective-permute-start.1 = (bf16[256,256]{1,0:T(8,128)(2,1)S(1)}, bf16[256,256]{1,0:T(8,128)(2,1)S(1)}, u32[]{:S(2)}, u32[]{:S(2)}) collective-permute-start(bf16[256,256]{1,0:T(8,128)(2,1)S(1)} %pad_maximum_fusion.1), channel_id=1, source_target_pairs={{0,2},{1,5},{2,0},{3,7},{4,6},{5,1},{6,4},{7,3},{8,10},{9,13},{10,... | collective-permute-start | bytes 393224 | tf_op jit(solution)/shard_map/ppermute | solution.py:237
  5.3 0.5 %collective-permute-start.2 = (bf16[128,256]{1,0:T(8,128)(2,1)S(1)}, bf16[128,256]{1,0:T(8,128)(2,1)S(1)}, u32[]{:S(2)}, u32[]{:S(2)}) collective-permute-start(bf16[128,256]{1,0:T(8,128)(2,1)S(1)} %get-tuple-element.72), channel_id=1, source_target_pairs={{0,24},{8,0},{16,8},{24,16},{1,25},{9,1},{17,9},{25,17},{2,26},{10... | collective-permute-start | bytes 196616 | tf_op jit(solution)/shard_map/ppermute | solution.py:270
  5.8 2.5 %collective-permute-start.4 = (bf16[128,256]{1,0:T(8,128)(2,1)S(1)}, bf16[128,256]{1,0:T(8,128)(2,1)S(1)}, u32[]{:S(2)}, u32[]{:S(2)}) collective-permute-start(bf16[128,256]{1,0:T(8,128)(2,1)S(1)} %get-tuple-element.73.refs_3_), channel_id=1, source_target_pairs={{0,6},{2,4},{4,2},{6,0},{1,7},{3,5},{5,3},{7,1},{8,14},{10,12},{12... | collective-permute-start | bytes 196616 | tf_op jit(solution)/shard_map/ppermute | solution.py:227
  8.3 1.0 %copy-done.1 = bf16[2,1,128,1024]{3,2,1,0:T(8,128)(2,1)S(1)} copy-done((bf16[2,1,128,1024]{3,2,1,0:T(8,128)(2,1)S(1)}, bf16[2,1,128,1024]{3,2,1,0:T(8,128)(2,1)}, u32[]{:S(2)}) %copy-start.1) | copy-done | bytes 524312
  9.5 1.5 %collective-permute-done.2.refs_3_ = bf16[128,256]{1,0:T(8,128)(2,1)S(1)} collective-permute-done((bf16[128,256]{1,0:T(8,128)(2,1)S(1)}, bf16[128,256]{1,0:T(8,128)(2,1)S(1)}, u32[]{:S(2)}, u32[]{:S(2)}) %collective-permute-start.2) | collective-permute-done | bytes 65568 | tf_op jit(solution)/shard_map/ppermute | solution.py:270
  11.6 1.1 %collective-permute-done.4.refs_5_ = bf16[128,256]{1,0:T(8,128)(2,1)S(1)} collective-permute-done((bf16[128,256]{1,0:T(8,128)(2,1)S(1)}, bf16[128,256]{1,0:T(8,128)(2,1)S(1)}, u32[]{:S(2)}, u32[]{:S(2)}) %collective-permute-start.4) | collective-permute-done | bytes 65568 | tf_op jit(solution)/shard_map/ppermute | solution.py:227
  12.7 3.1 %collective-permute-start.7 = (bf16[128,256]{1,0:T(8,128)(2,1)S(1)}, bf16[128,256]{1,0:T(8,128)(2,1)S(1)}, u32[]{:S(2)}, u32[]{:S(2)}) collective-permute-start(bf16[128,256]{1,0:T(8,128)(2,1)S(1)} %collective-permute-done.2.refs_3_), channel_id=1, source_target_pairs={{0,6},{2,4},{4,2},{6,0},{1,7},{3,5},{5,3},{7,1},{8,14},{10,12},{12... | collective-permute-start | bytes 196616 | tf_op jit(solution)/shard_map/ppermute | solution.py:227
  16.1 4.7 %shard_map.113 = (bf16[2,1,128,1024]{3,2,1,0:T(8,128)(2,1)}, f32[512,256]{1,0:T(8,128)S(1)}, bf16[512,256]{1,0:T(8,128)(2,1)S(1)}) custom-call(s32[8]{0:T(128)S(1)} %copy-done.2, bf16[2048,128]{1,0:T(8,128)(2,1)S(1)} %get-tuple-element.31.refs_1_, bf16[2048,128]{1,0:T(8,128)(2,1)S(1)} %get-tuple-element.32.refs_2_, ...), custom_call_target="tpu_custom_call" | custom-call | flops 5368709120 | bytes 2097152 | tf_op jit(solution)/shard_map/pallas_call | solution.py:193
  20.8 1.1 %collective-permute-done.8.refs_6_ = bf16[256,256]{1,0:T(8,128)(2,1)S(1)} collective-permute-done((bf16[256,256]{1,0:T(8,128)(2,1)S(1)}, bf16[256,256]{1,0:T(8,128)(2,1)S(1)}, u32[]{:S(2)}, u32[]{:S(2)}) %collective-permute-start.8) | collective-permute-done | bytes 131104 | tf_op jit(solution)/shard_map/ppermute | solution.py:237
  22.5 0.9 %collective-permute-done.10 = bf16[512,256]{1,0:T(8,128)(2,1)S(1)} collective-permute-done((bf16[512,256]{1,0:T(8,128)(2,1)S(1)}, bf16[512,256]{1,0:T(8,128)(2,1)S(1)}, u32[]{:S(2)}, u32[]{:S(2)}) %collective-permute-start.10) | collective-permute-done | bytes 262176 | tf_op jit(solution)/shard_map/ppermute | solution.py:223
  23.5 2.5 %collective-permute-start.11 = (bf16[128,256]{1,0:T(8,128)(2,1)S(1)}, bf16[128,256]{1,0:T(8,128)(2,1)S(1)}, u32[]{:S(2)}, u32[]{:S(2)}) collective-permute-start(bf16[128,256]{1,0:T(8,128)(2,1)S(1)} %get-tuple-element.44), channel_id=1, source_target_pairs={{0,6},{2,4},{4,2},{6,0},{1,7},{3,5},{5,3},{7,1},{8,14},{10,12},{12... | collective-permute-start | bytes 196616 | tf_op jit(solution)/shard_map/ppermute | solution.py:227
  26.0 2.0 %collective-permute-start.13 = (bf16[128,256]{1,0:T(8,128)(2,1)S(1)}, bf16[128,256]{1,0:T(8,128)(2,1)S(1)}, u32[]{:S(2)}, u32[]{:S(2)}) collective-permute-start(bf16[128,256]{1,0:T(8,128)(2,1)S(1)} %get-tuple-element.46), channel_id=1, source_target_pairs={{0,2},{2,0},{4,6},{6,4},{1,3},{3,1},{5,7},{7,5},{8,10},{10,8},{12,... | collective-permute-start | bytes 196616 | tf_op jit(solution)/shard_map/ppermute | solution.py:227
  28.0 4.7 %shard_map.114 = (bf16[2,1,128,1024]{3,2,1,0:T(8,128)(2,1)}, f32[512,256]{1,0:T(8,128)S(1)}, bf16[512,256]{1,0:T(8,128)(2,1)S(1)}) custom-call(s32[8]{0:T(128)S(1)} %copy-done.2, bf16[2048,128]{1,0:T(8,128)(2,1)S(1)} %get-tuple-element.31.refs_1_, bf16[2048,128]{1,0:T(8,128)(2,1)S(1)} %get-tuple-element.32.refs_2_, ...), custom_call_target="tpu_custom_call", output_to_operand_aliasing={{0}: (8, {})} | custom-call | flops 5368709120 | bytes 2097152 | tf_op jit(solution)/shard_map/pallas_call | solution.py:193
  32.9 3.5 %collective-permute-start.15 = (f32[128,256]{1,0:T(8,128)S(1)}, f32[128,256]{1,0:T(8,128)S(1)}, u32[]{:S(2)}, u32[]{:S(2)}) collective-permute-start(f32[128,256]{1,0:T(8,128)S(1)} %fusion.6), channel_id=1, source_target_pairs={{8,0},{24,16},{9,1},{25,17},{10,2},{26,18},{11,3},{27,19},{12,4},{... | collective-permute-start | bytes 393224 | tf_op jit(solution)/shard_map/ppermute | solution.py:311
  36.5 2.2 %collective-permute-start.16 = (bf16[128,256]{1,0:T(8,128)(2,1)S(1)}, bf16[128,256]{1,0:T(8,128)(2,1)S(1)}, u32[]{:S(2)}, u32[]{:S(2)}) collective-permute-start(bf16[128,256]{1,0:T(8,128)(2,1)S(1)} %get-tuple-element.51), channel_id=1, source_target_pairs={{0,6},{2,4},{4,2},{6,0},{1,7},{3,5},{5,3},{7,1},{8,14},{10,12},{12... | collective-permute-start | bytes 196616 | tf_op jit(solution)/shard_map/ppermute | solution.py:227
  38.7 2.3 %collective-permute-start.18 = (bf16[128,256]{1,0:T(8,128)(2,1)S(1)}, bf16[128,256]{1,0:T(8,128)(2,1)S(1)}, u32[]{:S(2)}, u32[]{:S(2)}) collective-permute-start(bf16[128,256]{1,0:T(8,128)(2,1)S(1)} %get-tuple-element.53), channel_id=1, source_target_pairs={{0,2},{2,0},{4,6},{6,4},{1,3},{3,1},{5,7},{7,5},{8,10},{10,8},{12,... | collective-permute-start | bytes 196616 | tf_op jit(solution)/shard_map/ppermute | solution.py:227
  41.0 1.3 %collective-permute-start.19 = (bf16[128,256]{1,0:T(8,128)(2,1)S(1)}, bf16[128,256]{1,0:T(8,128)(2,1)S(1)}, u32[]{:S(2)}, u32[]{:S(2)}) collective-permute-start(bf16[128,256]{1,0:T(8,128)(2,1)S(1)} %convert_element_type.41), channel_id=1, source_target_pairs={{16,8},{17,9},{18,10},{19,11},{20,12},{21,13},{22,14},{23,15}} | collective-permute-start | bytes 196616 | tf_op jit(solution)/shard_map/ppermute | solution.py:315
  42.3 1.1 %collective-permute-done.16 = bf16[128,256]{1,0:T(8,128)(2,1)S(1)} collective-permute-done((bf16[128,256]{1,0:T(8,128)(2,1)S(1)}, bf16[128,256]{1,0:T(8,128)(2,1)S(1)}, u32[]{:S(2)}, u32[]{:S(2)}) %collective-permute-start.16) | collective-permute-done | bytes 65568 | tf_op jit(solution)/shard_map/ppermute | solution.py:227
  43.4 2.0 %collective-permute-done.17 = bf16[128,256]{1,0:T(8,128)(2,1)S(1)} collective-permute-done((bf16[128,256]{1,0:T(8,128)(2,1)S(1)}, bf16[128,256]{1,0:T(8,128)(2,1)S(1)}, u32[]{:S(2)}, u32[]{:S(2)}) %collective-permute-start.17) | collective-permute-done | bytes 65568 | tf_op jit(solution)/shard_map/ppermute | solution.py:227
  45.4 2.6 %collective-permute-done.19 = bf16[128,256]{1,0:T(8,128)(2,1)S(1)} collective-permute-done((bf16[128,256]{1,0:T(8,128)(2,1)S(1)}, bf16[128,256]{1,0:T(8,128)(2,1)S(1)}, u32[]{:S(2)}, u32[]{:S(2)}) %collective-permute-start.19) | collective-permute-done | bytes 65568 | tf_op jit(solution)/shard_map/ppermute | solution.py:315
  48.1 0.7 %maximum_bitcast_fusion = (f32[2,1,128,128]{3,2,1,0:T(8,128)}, f32[2,1,128,128]{3,2,1,0:T(8,128)}) fusion(f32[1,128,128]{2,1,0:T(8,128)S(1)} %get-tuple-element.71, f32[1,128,128]{2,1,0:T(8,128)S(1)} %get-tuple-element.69, f32[1,128,128]{2,1,0:T(8,128)S(1)} %get-tuple-element.70, f32[1,128,128]{2,1,0:T(8,128)S(1)} %get-tuple-element.68), kind=kLoop, calls=%fused_computation.14 | loop fusion | flops 65536 | bytes 524288
  (43 shorter events, 2.0 us)
Async XLA Ops:
  0.6 7.7 %copy-start = (bf16[2,1,128,1024]{3,2,1,0:T(8,128)(2,1)S(1)}, bf16[2,1,128,1024]{3,2,1,0:T(8,128)(2,1)}, u32[]{:S(2)}) copy-start(bf16[2,1,128,1024]{3,2,1,0:T(8,128)(2,1)} %q_ref.1) | copy-start | bytes 1572868
  1.5 1.3 %collective-permute-start = (bf16[128,256]{1,0:T(8,128)(2,1)S(1)}, bf16[128,256]{1,0:T(8,128)(2,1)S(1)}, u32[]{:S(2)}, u32[]{:S(2)}) collective-permute-start(bf16[128,256]{1,0:T(8,128)(2,1)S(1)} %get-tuple-element.73.refs_3_), channel_id=1, source_target_pairs={{0,1},{1,0},{2,3},{3,2},{4,5},{5,4},{6,7},{7,6},{8,9},{9,8},{10,11... | collective-permute-start | bytes 196616 | tf_op jit(solution)/shard_map/ppermute | solution.py:223
  3.6 7.4 %collective-permute-start.1 = (bf16[256,256]{1,0:T(8,128)(2,1)S(1)}, bf16[256,256]{1,0:T(8,128)(2,1)S(1)}, u32[]{:S(2)}, u32[]{:S(2)}) collective-permute-start(bf16[256,256]{1,0:T(8,128)(2,1)S(1)} %pad_maximum_fusion.1), channel_id=1, source_target_pairs={{0,2},{1,5},{2,0},{3,7},{4,6},{5,1},{6,4},{7,3},{8,10},{9,13},{10,... | collective-permute-start | bytes 393224 | tf_op jit(solution)/shard_map/ppermute | solution.py:237
  5.3 5.8 %collective-permute-start.2 = (bf16[128,256]{1,0:T(8,128)(2,1)S(1)}, bf16[128,256]{1,0:T(8,128)(2,1)S(1)}, u32[]{:S(2)}, u32[]{:S(2)}) collective-permute-start(bf16[128,256]{1,0:T(8,128)(2,1)S(1)} %get-tuple-element.72), channel_id=1, source_target_pairs={{0,24},{8,0},{16,8},{24,16},{1,25},{9,1},{17,9},{25,17},{2,26},{10... | collective-permute-start | bytes 196616 | tf_op jit(solution)/shard_map/ppermute | solution.py:270
  5.8 6.9 %collective-permute-start.4 = (bf16[128,256]{1,0:T(8,128)(2,1)S(1)}, bf16[128,256]{1,0:T(8,128)(2,1)S(1)}, u32[]{:S(2)}, u32[]{:S(2)}) collective-permute-start(bf16[128,256]{1,0:T(8,128)(2,1)S(1)} %get-tuple-element.73.refs_3_), channel_id=1, source_target_pairs={{0,6},{2,4},{4,2},{6,0},{1,7},{3,5},{5,3},{7,1},{8,14},{10,12},{12... | collective-permute-start | bytes 196616 | tf_op jit(solution)/shard_map/ppermute | solution.py:227
  11.1 5.0 %copy-start.2 = (s32[8]{0:T(128)S(1)}, s32[8]{0:T(128)}, u32[]{:S(2)}) copy-start(s32[8]{0:T(128)} %refs_0_.3) | copy-start | bytes 100
  11.1 4.8 %collective-permute-start.3 = (bf16[128,256]{1,0:T(8,128)(2,1)S(1)}, bf16[128,256]{1,0:T(8,128)(2,1)S(1)}, u32[]{:S(2)}, u32[]{:S(2)}) collective-permute-start(bf16[128,256]{1,0:T(8,128)(2,1)S(1)} %collective-permute-done.2.refs_3_), channel_id=1, source_target_pairs={{0,1},{1,0},{2,3},{3,2},{4,5},{5,4},{6,7},{7,6},{8,9},{9,8},{10,11... | collective-permute-start | bytes 196616 | tf_op jit(solution)/shard_map/ppermute | solution.py:223
  11.1 5.0 %collective-permute-start.6 = (bf16[256,256]{1,0:T(8,128)(2,1)S(1)}, bf16[256,256]{1,0:T(8,128)(2,1)S(1)}, u32[]{:S(2)}, u32[]{:S(2)}) collective-permute-start(bf16[256,256]{1,0:T(8,128)(2,1)S(1)} %collective-permute-done.1.refs_6_), channel_id=1, source_target_pairs={{0,1},{1,0},{2,3},{3,2},{4,5},{5,4},{6,7},{7,6},{8,9},{9,8},{10,11... | collective-permute-start | bytes 393224 | tf_op jit(solution)/shard_map/ppermute | solution.py:223
  12.7 3.4 %collective-permute-start.5 = (bf16[128,256]{1,0:T(8,128)(2,1)S(1)}, bf16[128,256]{1,0:T(8,128)(2,1)S(1)}, u32[]{:S(2)}, u32[]{:S(2)}) collective-permute-start(bf16[128,256]{1,0:T(8,128)(2,1)S(1)} %collective-permute-done.4.refs_5_), channel_id=1, source_target_pairs={{0,1},{1,0},{2,3},{3,2},{4,5},{5,4},{6,7},{7,6},{8,9},{9,8},{10,11... | collective-permute-start | bytes 196616 | tf_op jit(solution)/shard_map/ppermute | solution.py:223
  12.7 8.1 %collective-permute-start.7 = (bf16[128,256]{1,0:T(8,128)(2,1)S(1)}, bf16[128,256]{1,0:T(8,128)(2,1)S(1)}, u32[]{:S(2)}, u32[]{:S(2)}) collective-permute-start(bf16[128,256]{1,0:T(8,128)(2,1)S(1)} %collective-permute-done.2.refs_3_), channel_id=1, source_target_pairs={{0,6},{2,4},{4,2},{6,0},{1,7},{3,5},{5,3},{7,1},{8,14},{10,12},{12... | collective-permute-start | bytes 196616 | tf_op jit(solution)/shard_map/ppermute | solution.py:227
  15.9 6.0 %collective-permute-start.8 = (bf16[256,256]{1,0:T(8,128)(2,1)S(1)}, bf16[256,256]{1,0:T(8,128)(2,1)S(1)}, u32[]{:S(2)}, u32[]{:S(2)}) collective-permute-start(bf16[256,256]{1,0:T(8,128)(2,1)S(1)} %pad_maximum_fusion.2), channel_id=1, source_target_pairs={{0,2},{1,5},{2,0},{3,7},{4,6},{5,1},{6,4},{7,3},{8,10},{9,13},{10,... | collective-permute-start | bytes 393224 | tf_op jit(solution)/shard_map/ppermute | solution.py:237
  21.9 1.5 %collective-permute-start.10 = (bf16[512,256]{1,0:T(8,128)(2,1)S(1)}, bf16[512,256]{1,0:T(8,128)(2,1)S(1)}, u32[]{:S(2)}, u32[]{:S(2)}) collective-permute-start(bf16[512,256]{1,0:T(8,128)(2,1)S(1)} %get-tuple-element.41), channel_id=1, source_target_pairs={{0,1},{1,0},{2,3},{3,2},{4,5},{5,4},{6,7},{7,6},{8,9},{9,8},{10,11... | collective-permute-start | bytes 786440 | tf_op jit(solution)/shard_map/ppermute | solution.py:223
  22.1 5.9 %collective-permute-start.9 = (bf16[384,256]{1,0:T(8,128)(2,1)S(1)}, bf16[384,256]{1,0:T(8,128)(2,1)S(1)}, u32[]{:S(2)}, u32[]{:S(2)}) collective-permute-start(bf16[384,256]{1,0:T(8,128)(2,1)S(1)} %pad_maximum_fusion), channel_id=1, source_target_pairs={{0,1},{1,0},{2,3},{3,2},{4,5},{5,4},{6,7},{7,6},{8,9},{9,8},{10,11... | collective-permute-start | bytes 589832 | tf_op jit(solution)/shard_map/ppermute | solution.py:223
  23.5 9.2 %copy-start.3 = (f32[1,128,128]{2,1,0:T(8,128)S(1)}, f32[1,128,128]{2,1,0:T(8,128)}, u32[]{:S(2)}) copy-start(f32[1,128,128]{2,1,0:T(8,128)} %param.16) | copy-start | bytes 196612
  23.5 9.2 %copy-start.4 = (f32[1,128,128]{2,1,0:T(8,128)S(1)}, f32[1,128,128]{2,1,0:T(8,128)}, u32[]{:S(2)}) copy-start(f32[1,128,128]{2,1,0:T(8,128)} %param.15) | copy-start | bytes 196612
  23.5 9.2 %collective-permute-start.11 = (bf16[128,256]{1,0:T(8,128)(2,1)S(1)}, bf16[128,256]{1,0:T(8,128)(2,1)S(1)}, u32[]{:S(2)}, u32[]{:S(2)}) collective-permute-start(bf16[128,256]{1,0:T(8,128)(2,1)S(1)} %get-tuple-element.44), channel_id=1, source_target_pairs={{0,6},{2,4},{4,2},{6,0},{1,7},{3,5},{5,3},{7,1},{8,14},{10,12},{12... | collective-permute-start | bytes 196616 | tf_op jit(solution)/shard_map/ppermute | solution.py:227
  26.0 6.7 %collective-permute-start.12 = (bf16[128,256]{1,0:T(8,128)(2,1)S(1)}, bf16[128,256]{1,0:T(8,128)(2,1)S(1)}, u32[]{:S(2)}, u32[]{:S(2)}) collective-permute-start(bf16[128,256]{1,0:T(8,128)(2,1)S(1)} %get-tuple-element.45), channel_id=1, source_target_pairs={{0,4},{2,6},{4,0},{6,2},{1,5},{3,7},{5,1},{7,3},{8,12},{10,14},{12... | collective-permute-start | bytes 196616 | tf_op jit(solution)/shard_map/ppermute | solution.py:227
  26.0 6.7 %collective-permute-start.13 = (bf16[128,256]{1,0:T(8,128)(2,1)S(1)}, bf16[128,256]{1,0:T(8,128)(2,1)S(1)}, u32[]{:S(2)}, u32[]{:S(2)}) collective-permute-start(bf16[128,256]{1,0:T(8,128)(2,1)S(1)} %get-tuple-element.46), channel_id=1, source_target_pairs={{0,2},{2,0},{4,6},{6,4},{1,3},{3,1},{5,7},{7,5},{8,10},{10,8},{12,... | collective-permute-start | bytes 196616 | tf_op jit(solution)/shard_map/ppermute | solution.py:227
  32.8 3.6 %collective-permute-start.14 = (bf16[512,256]{1,0:T(8,128)(2,1)S(1)}, bf16[512,256]{1,0:T(8,128)(2,1)S(1)}, u32[]{:S(2)}, u32[]{:S(2)}) collective-permute-start(bf16[512,256]{1,0:T(8,128)(2,1)S(1)} %get-tuple-element.50), channel_id=1, source_target_pairs={{0,1},{1,0},{2,3},{3,2},{4,5},{5,4},{6,7},{7,6},{8,9},{9,8},{10,11... | collective-permute-start | bytes 786440 | tf_op jit(solution)/shard_map/ppermute | solution.py:223
  32.9 9.4 %collective-permute-start.15 = (f32[128,256]{1,0:T(8,128)S(1)}, f32[128,256]{1,0:T(8,128)S(1)}, u32[]{:S(2)}, u32[]{:S(2)}) collective-permute-start(f32[128,256]{1,0:T(8,128)S(1)} %fusion.6), channel_id=1, source_target_pairs={{8,0},{24,16},{9,1},{25,17},{10,2},{26,18},{11,3},{27,19},{12,4},{... | collective-permute-start | bytes 393224 | tf_op jit(solution)/shard_map/ppermute | solution.py:311
  36.5 6.9 %collective-permute-start.16 = (bf16[128,256]{1,0:T(8,128)(2,1)S(1)}, bf16[128,256]{1,0:T(8,128)(2,1)S(1)}, u32[]{:S(2)}, u32[]{:S(2)}) collective-permute-start(bf16[128,256]{1,0:T(8,128)(2,1)S(1)} %get-tuple-element.51), channel_id=1, source_target_pairs={{0,6},{2,4},{4,2},{6,0},{1,7},{3,5},{5,3},{7,1},{8,14},{10,12},{12... | collective-permute-start | bytes 196616 | tf_op jit(solution)/shard_map/ppermute | solution.py:227
  38.7 6.7 %collective-permute-start.17 = (bf16[128,256]{1,0:T(8,128)(2,1)S(1)}, bf16[128,256]{1,0:T(8,128)(2,1)S(1)}, u32[]{:S(2)}, u32[]{:S(2)}) collective-permute-start(bf16[128,256]{1,0:T(8,128)(2,1)S(1)} %get-tuple-element.52), channel_id=1, source_target_pairs={{0,4},{2,6},{4,0},{6,2},{1,5},{3,7},{5,1},{7,3},{8,12},{10,14},{12... | collective-permute-start | bytes 196616 | tf_op jit(solution)/shard_map/ppermute | solution.py:227
  38.7 6.7 %collective-permute-start.18 = (bf16[128,256]{1,0:T(8,128)(2,1)S(1)}, bf16[128,256]{1,0:T(8,128)(2,1)S(1)}, u32[]{:S(2)}, u32[]{:S(2)}) collective-permute-start(bf16[128,256]{1,0:T(8,128)(2,1)S(1)} %get-tuple-element.53), channel_id=1, source_target_pairs={{0,2},{2,0},{4,6},{6,4},{1,3},{3,1},{5,7},{7,5},{8,10},{10,8},{12,... | collective-permute-start | bytes 196616 | tf_op jit(solution)/shard_map/ppermute | solution.py:227
  41.0 7.0 %collective-permute-start.19 = (bf16[128,256]{1,0:T(8,128)(2,1)S(1)}, bf16[128,256]{1,0:T(8,128)(2,1)S(1)}, u32[]{:S(2)}, u32[]{:S(2)}) collective-permute-start(bf16[128,256]{1,0:T(8,128)(2,1)S(1)} %convert_element_type.41), channel_id=1, source_target_pairs={{16,8},{17,9},{18,10},{19,11},{20,12},{21,13},{22,14},{23,15}} | collective-permute-start | bytes 196616 | tf_op jit(solution)/shard_map/ppermute | solution.py:315
  (1 other events, 1.0 us)

commit v3 on v1

--- a/solution.py
+++ b/solution.py
@@ -219,6 +219,15 @@
     return lax.ppermute(block, "z", [(chip, chip ^ k) for chip in range(lax.axis_size("z"))])
 
 
+def section_swap(block, first):
+    sections = lax.axis_size("section")
+    route = []
+    for low in range(first, sections, 2):
+        high = (low + 1) % sections
+        route += [(low, high), (high, low)]
+    return lax.ppermute(block, "section", route)
+
+
 def body(
     queries,
     out_grad,
@@ -278,8 +287,13 @@
         1, group_order, queries, *stacks, next_kv, query_grads
     )
     first_acc, far_terms = lax.optimization_barrier((first_acc, far_terms))
-    moved_acc = lax.ppermute(first_acc, "section", [(i, i - 1) for i in range(1, sections)])
-    second_acc = moved_acc + reduced(*chip_sums(near_terms, far_terms))
+    early_acc = section_swap(first_acc, 0)
+    own_sum, leaving = chip_sums(near_terms, far_terms)
+    late_acc, leaving = lax.optimization_barrier((first_acc.astype(jnp.bfloat16), leaving))
+    second_acc = reduced(own_sum, leaving)
+    late_acc = section_swap(late_acc, 1).astype(jnp.float32)
+    moved_acc = jnp.where(section % 2 == 0, early_acc, late_acc)
+    second_acc = second_acc + jnp.where(section == sections - 1, 0.0, moved_acc)
     key_grads = jnp.stack([first_acc[:, :head_dim], second_acc[:, :head_dim]], axis=0)[:, None]
     value_grads = jnp.stack([first_acc[:, head_dim:], second_acc[:, head_dim:]], axis=0)[:, None]
     return (query_grads, key_grads, value_grads)

time: 46.4 us -> 46.7 us (level)
  the two profiles are of different devices: /device:TPU:5 before, /device:TPU:0 now
where the time goes in v3:
time: 46.7 us; the launch traced here: 46.4 us
  starting transfers between devices  27.2 us (58%)
  Pallas kernels  9.52 us (20%)
  waiting for transfers between devices  4.78 us (10%)
  local copies, waits for them, and re-layouts  2.15 us (5%)
  other arithmetic  1.81 us (4%)
  between operations  0.88 us (2%)
    ppermute x12, starting transfers between devices, across_chips(): lax.ppermute(block, 'z', [(chip, chip ^ k) for chip in range(lax.axis_siz...  19 us
    pallas_call x2, Pallas kernels, attend_back(): pl.pallas_call(kernel, out_shape=(jax.ShapeDtypeStruct(queries.shape, jnp...  9.34 us
    ppermute x2, starting transfers between devices, section_swap(): return lax.ppermute(block, 'section', route)  4.24 us
    ppermute x12, waiting for transfers between devices, across_chips(): lax.ppermute(block, 'z', [(chip, chip ^ k) for chip in range(lax.axis_siz...  3.14 us
    ppermute x1, starting transfers between devices, body(): lax.ppermute(leaving_pair, 'section', [(i, (i - 1) % sections) for i in r...  2.67 us
    unnamed x10, local copies, waits for them, and re-layouts  2.1 us
    ppermute x8, starting transfers between devices, other_core(): return lax.ppermute(block, 'core', [(0, 1), (1, 0)])  1.36 us
  transfers between devices with their start and end apart: 23, of which 4 were waited for; matrix products, arithmetic and copies ran while one was open for 0% of the time, Pallas kernels for 21%

profile of v3, /device:TPU:0, one launch (start us, length us, event | category | flops | bytes accessed | tf_op | source)
XLA Modules:
  0.0 46.4 jit_solution(8835182532454485008)
XLA Ops:
  0.6 0.8 %maximum_select_fusion = (bf16[128,256]{1,0:T(8,128)(2,1)S(1)}, bf16[128,256]{1,0:T(8,128)(2,1)S(1)}) fusion(bf16[128,128]{1,0:T(8,128)(2,1)} %param.14, bf16[128,128]{1,0:T(8,128)(2,1)} %param.13, pred[]{:T(512)S(6)} %eq.11, bf16[128,128]{1,0:T(8,128)(2,1)} %bitcast.22, bf16[128,128]{1,0:T(8,128)(2,1)} %bitcast.23), kind=kLoop, calls=%fused_computation.16 | loop fusion | flops 294912 | bytes 262145 | tf_op jit(solution)/shard_map/jit(_where)/select_n | solution.py:250
  1.5 3.1 %collective-permute-start = (bf16[128,256]{1,0:T(8,128)(2,1)S(1)}, bf16[128,256]{1,0:T(8,128)(2,1)S(1)}, u32[]{:S(2)}, u32[]{:S(2)}) collective-permute-start(bf16[128,256]{1,0:T(8,128)(2,1)S(1)} %get-tuple-element.79.refs_3_), channel_id=1, source_target_pairs={{0,2},{2,0},{4,6},{6,4},{1,3},{3,1},{5,7},{7,5},{8,10},{10,8},{12,... | collective-permute-start | bytes 196616 | tf_op jit(solution)/shard_map/ppermute | solution.py:219
  4.6 2.6 %collective-permute-start.1 = (bf16[128,256]{1,0:T(8,128)(2,1)S(1)}, bf16[128,256]{1,0:T(8,128)(2,1)S(1)}, u32[]{:S(2)}, u32[]{:S(2)}) collective-permute-start(bf16[128,256]{1,0:T(8,128)(2,1)S(1)} %get-tuple-element.79.refs_3_), channel_id=1, source_target_pairs={{0,4},{2,6},{4,0},{6,2},{1,5},{3,7},{5,1},{7,3},{8,12},{10,14},{12... | collective-permute-start | bytes 196616 | tf_op jit(solution)/shard_map/ppermute | solution.py:219
  7.2 2.7 %collective-permute-start.3 = (bf16[128,256]{1,0:T(8,128)(2,1)S(1)}, bf16[128,256]{1,0:T(8,128)(2,1)S(1)}, u32[]{:S(2)}, u32[]{:S(2)}) collective-permute-start(bf16[128,256]{1,0:T(8,128)(2,1)S(1)} %get-tuple-element.78), channel_id=1, source_target_pairs={{0,24},{8,0},{16,8},{24,16},{1,25},{9,1},{17,9},{25,17},{2,26},{10... | collective-permute-start | bytes 196616 | tf_op jit(solution)/shard_map/ppermute | solution.py:255
  9.8 1.0 %copy-done = bf16[2,1,128,1024]{3,2,1,0:T(8,128)(2,1)S(1)} copy-done((bf16[2,1,128,1024]{3,2,1,0:T(8,128)(2,1)S(1)}, bf16[2,1,128,1024]{3,2,1,0:T(8,128)(2,1)}, u32[]{:S(2)}) %copy-start) | copy-done | bytes 524312
  10.9 1.0 %copy-done.1 = bf16[2,1,128,1024]{3,2,1,0:T(8,128)(2,1)S(1)} copy-done((bf16[2,1,128,1024]{3,2,1,0:T(8,128)(2,1)S(1)}, bf16[2,1,128,1024]{3,2,1,0:T(8,128)(2,1)}, u32[]{:S(2)}) %copy-start.1) | copy-done | bytes 524312
  11.9 0.2 shard_map.112
  12.1 1.1 %collective-permute-done.2.refs_6_ = bf16[128,256]{1,0:T(8,128)(2,1)S(1)} collective-permute-done((bf16[128,256]{1,0:T(8,128)(2,1)S(1)}, bf16[128,256]{1,0:T(8,128)(2,1)S(1)}, u32[]{:S(2)}, u32[]{:S(2)}) %collective-permute-start.2) | collective-permute-done | bytes 65568 | tf_op jit(solution)/shard_map/ppermute | solution.py:219
  13.2 0.5 %collective-permute-start.6 = (bf16[128,256]{1,0:T(8,128)(2,1)S(1)}, bf16[128,256]{1,0:T(8,128)(2,1)S(1)}, u32[]{:S(2)}, u32[]{:S(2)}) collective-permute-start(bf16[128,256]{1,0:T(8,128)(2,1)S(1)} %collective-permute-done.1.refs_5_), channel_id=1, source_target_pairs={{0,1},{1,0},{2,3},{3,2},{4,5},{5,4},{6,7},{7,6},{8,9},{9,8},{10,11... | collective-permute-start | bytes 196616 | tf_op jit(solution)/shard_map/ppermute | solution.py:215
  13.8 3.0 %collective-permute-start.10 = (bf16[128,256]{1,0:T(8,128)(2,1)S(1)}, bf16[128,256]{1,0:T(8,128)(2,1)S(1)}, u32[]{:S(2)}, u32[]{:S(2)}) collective-permute-start(bf16[128,256]{1,0:T(8,128)(2,1)S(1)} %collective-permute-done.3.refs_3_), channel_id=1, source_target_pairs={{0,6},{2,4},{4,2},{6,0},{1,7},{3,5},{5,3},{7,1},{8,14},{10,12},{12... | collective-permute-start | bytes 196616 | tf_op jit(solution)/shard_map/ppermute | solution.py:219
  16.9 1.4 %collective-permute-start.9 = (bf16[128,256]{1,0:T(8,128)(2,1)S(1)}, bf16[128,256]{1,0:T(8,128)(2,1)S(1)}, u32[]{:S(2)}, u32[]{:S(2)}) collective-permute-start(bf16[128,256]{1,0:T(8,128)(2,1)S(1)} %collective-permute-done.3.refs_3_), channel_id=1, source_target_pairs={{0,4},{2,6},{4,0},{6,2},{1,5},{3,7},{5,1},{7,3},{8,12},{10,14},{12... | collective-permute-start | bytes 196616 | tf_op jit(solution)/shard_map/ppermute | solution.py:219
  18.2 4.7 %shard_map.113 = (bf16[2,1,128,1024]{3,2,1,0:T(8,128)(2,1)}, f32[512,256]{1,0:T(8,128)S(1)}, bf16[512,256]{1,0:T(8,128)(2,1)S(1)}) custom-call(s32[8]{0:T(128)S(1)} %copy-done.2, bf16[2048,128]{1,0:T(8,128)(2,1)S(1)} %get-tuple-element.34.refs_1_, bf16[2048,128]{1,0:T(8,128)(2,1)S(1)} %get-tuple-element.35.refs_2_, ...), custom_call_target="tpu_custom_call" | custom-call | flops 5368709120 | bytes 2097152 | tf_op jit(solution)/shard_map/pallas_call | solution.py:185
  23.0 0.5 %collective-permute-start.11 = (bf16[128,256]{1,0:T(8,128)(2,1)S(1)}, bf16[128,256]{1,0:T(8,128)(2,1)S(1)}, u32[]{:S(2)}, u32[]{:S(2)}) collective-permute-start(bf16[128,256]{1,0:T(8,128)(2,1)S(1)} %collective-permute-done.3.refs_3_), channel_id=1, source_target_pairs={{0,1},{1,0},{2,3},{3,2},{4,5},{5,4},{6,7},{7,6},{8,9},{9,8},{10,11... | collective-permute-start | bytes 196616 | tf_op jit(solution)/shard_map/ppermute | solution.py:215
  23.7 0.9 %collective-permute-done.13 = bf16[512,256]{1,0:T(8,128)(2,1)S(1)} collective-permute-done((bf16[512,256]{1,0:T(8,128)(2,1)S(1)}, bf16[512,256]{1,0:T(8,128)(2,1)S(1)}, u32[]{:S(2)}, u32[]{:S(2)}) %collective-permute-start.13) | collective-permute-done | bytes 262176 | tf_op jit(solution)/shard_map/ppermute | solution.py:215
  24.7 3.1 %collective-permute-start.14 = (bf16[128,256]{1,0:T(8,128)(2,1)S(1)}, bf16[128,256]{1,0:T(8,128)(2,1)S(1)}, u32[]{:S(2)}, u32[]{:S(2)}) collective-permute-start(bf16[128,256]{1,0:T(8,128)(2,1)S(1)} %get-tuple-element.50), channel_id=1, source_target_pairs={{0,6},{2,4},{4,2},{6,0},{1,7},{3,5},{5,3},{7,1},{8,14},{10,12},{12... | collective-permute-start | bytes 196616 | tf_op jit(solution)/shard_map/ppermute | solution.py:219
  27.8 1.4 %collective-permute-start.16 = (bf16[128,256]{1,0:T(8,128)(2,1)S(1)}, bf16[128,256]{1,0:T(8,128)(2,1)S(1)}, u32[]{:S(2)}, u32[]{:S(2)}) collective-permute-start(bf16[128,256]{1,0:T(8,128)(2,1)S(1)} %get-tuple-element.52), channel_id=1, source_target_pairs={{0,2},{2,0},{4,6},{6,4},{1,3},{3,1},{5,7},{7,5},{8,10},{10,8},{12,... | collective-permute-start | bytes 196616 | tf_op jit(solution)/shard_map/ppermute | solution.py:219
  29.1 4.7 %shard_map.114 = (bf16[2,1,128,1024]{3,2,1,0:T(8,128)(2,1)}, f32[512,256]{1,0:T(8,128)S(1)}, bf16[512,256]{1,0:T(8,128)(2,1)S(1)}) custom-call(s32[8]{0:T(128)S(1)} %copy-done.2, bf16[2048,128]{1,0:T(8,128)(2,1)S(1)} %get-tuple-element.34.refs_1_, bf16[2048,128]{1,0:T(8,128)(2,1)S(1)} %get-tuple-element.35.refs_2_, ...), custom_call_target="tpu_custom_call", output_to_operand_aliasing={{0}: (9, {})} | custom-call | flops 5368709120 | bytes 2097152 | tf_op jit(solution)/shard_map/pallas_call | solution.py:185
  34.0 1.9 %collective-permute-start.21 = (f32[128,256]{1,0:T(8,128)S(1)}, f32[128,256]{1,0:T(8,128)S(1)}, u32[]{:S(2)}, u32[]{:S(2)}) collective-permute-start(f32[128,256]{1,0:T(8,128)S(1)} %fusion.5), channel_id=1, source_target_pairs={{0,8},{8,0},{16,24},{24,16},{1,9},{9,1},{17,25},{25,17},{2,10},{10... | collective-permute-start | bytes 393224 | tf_op jit(solution)/shard_map/ppermute | solution.py:228
  36.0 2.7 %collective-permute-start.18 = (bf16[128,256]{1,0:T(8,128)(2,1)S(1)}, bf16[128,256]{1,0:T(8,128)(2,1)S(1)}, u32[]{:S(2)}, u32[]{:S(2)}) collective-permute-start(bf16[128,256]{1,0:T(8,128)(2,1)S(1)} %get-tuple-element.57), channel_id=1, source_target_pairs={{0,6},{2,4},{4,2},{6,0},{1,7},{3,5},{5,3},{7,1},{8,14},{10,12},{12... | collective-permute-start | bytes 196616 | tf_op jit(solution)/shard_map/ppermute | solution.py:219
  38.7 1.7 %collective-permute-start.20 = (bf16[128,256]{1,0:T(8,128)(2,1)S(1)}, bf16[128,256]{1,0:T(8,128)(2,1)S(1)}, u32[]{:S(2)}, u32[]{:S(2)}) collective-permute-start(bf16[128,256]{1,0:T(8,128)(2,1)S(1)} %get-tuple-element.59), channel_id=1, source_target_pairs={{0,2},{2,0},{4,6},{6,4},{1,3},{3,1},{5,7},{7,5},{8,10},{10,8},{12,... | collective-permute-start | bytes 196616 | tf_op jit(solution)/shard_map/ppermute | solution.py:219
  40.4 2.4 %collective-permute-start.22 = (bf16[128,256]{1,0:T(8,128)(2,1)S(1)}, bf16[128,256]{1,0:T(8,128)(2,1)S(1)}, u32[]{:S(2)}, u32[]{:S(2)}) collective-permute-start(bf16[128,256]{1,0:T(8,128)(2,1)S(1)} %convert_element_type.41), channel_id=1, source_target_pairs={{8,16},{16,8},{24,0},{0,24},{9,17},{17,9},{25,1},{1,25},{10,18},{1... | collective-permute-start | bytes 196616 | tf_op jit(solution)/shard_map/ppermute | solution.py:228
  42.8 2.0 %collective-permute-done.19 = bf16[128,256]{1,0:T(8,128)(2,1)S(1)} collective-permute-done((bf16[128,256]{1,0:T(8,128)(2,1)S(1)}, bf16[128,256]{1,0:T(8,128)(2,1)S(1)}, u32[]{:S(2)}, u32[]{:S(2)}) %collective-permute-start.19) | collective-permute-done | bytes 65568 | tf_op jit(solution)/shard_map/ppermute | solution.py:219
  44.8 0.7 %collective-permute-done.22 = bf16[128,256]{1,0:T(8,128)(2,1)S(1)} collective-permute-done((bf16[128,256]{1,0:T(8,128)(2,1)S(1)}, bf16[128,256]{1,0:T(8,128)(2,1)S(1)}, u32[]{:S(2)}, u32[]{:S(2)}) %collective-permute-start.22) | collective-permute-done | bytes 65568 | tf_op jit(solution)/shard_map/ppermute | solution.py:228
  45.7 0.7 %maximum_bitcast_fusion = (f32[2,1,128,128]{3,2,1,0:T(8,128)}, f32[2,1,128,128]{3,2,1,0:T(8,128)}) fusion(f32[1,128,128]{2,1,0:T(8,128)S(1)} %get-tuple-element.77, f32[1,128,128]{2,1,0:T(8,128)S(1)} %get-tuple-element.75, f32[1,128,128]{2,1,0:T(8,128)S(1)} %get-tuple-element.76, f32[1,128,128]{2,1,0:T(8,128)S(1)} %get-tuple-element.74), kind=kLoop, calls=%fused_computation.11 | loop fusion | flops 65536 | bytes 524288
  (47 shorter events, 0.7 us)
Async XLA Ops:
  1.5 10.6 %collective-permute-start = (bf16[128,256]{1,0:T(8,128)(2,1)S(1)}, bf16[128,256]{1,0:T(8,128)(2,1)S(1)}, u32[]{:S(2)}, u32[]{:S(2)}) collective-permute-start(bf16[128,256]{1,0:T(8,128)(2,1)S(1)} %get-tuple-element.79.refs_3_), channel_id=1, source_target_pairs={{0,2},{2,0},{4,6},{6,4},{1,3},{3,1},{5,7},{7,5},{8,10},{10,8},{12,... | collective-permute-start | bytes 196616 | tf_op jit(solution)/shard_map/ppermute | solution.py:219
  4.6 7.5 %collective-permute-start.1 = (bf16[128,256]{1,0:T(8,128)(2,1)S(1)}, bf16[128,256]{1,0:T(8,128)(2,1)S(1)}, u32[]{:S(2)}, u32[]{:S(2)}) collective-permute-start(bf16[128,256]{1,0:T(8,128)(2,1)S(1)} %get-tuple-element.79.refs_3_), channel_id=1, source_target_pairs={{0,4},{2,6},{4,0},{6,2},{1,5},{3,7},{5,1},{7,3},{8,12},{10,14},{12... | collective-permute-start | bytes 196616 | tf_op jit(solution)/shard_map/ppermute | solution.py:219
  7.2 6.1 %collective-permute-start.2 = (bf16[128,256]{1,0:T(8,128)(2,1)S(1)}, bf16[128,256]{1,0:T(8,128)(2,1)S(1)}, u32[]{:S(2)}, u32[]{:S(2)}) collective-permute-start(bf16[128,256]{1,0:T(8,128)(2,1)S(1)} %get-tuple-element.79.refs_3_), channel_id=1, source_target_pairs={{0,6},{2,4},{4,2},{6,0},{1,7},{3,5},{5,3},{7,1},{8,14},{10,12},{12... | collective-permute-start | bytes 196616 | tf_op jit(solution)/shard_map/ppermute | solution.py:219
  7.2 6.1 %collective-permute-start.3 = (bf16[128,256]{1,0:T(8,128)(2,1)S(1)}, bf16[128,256]{1,0:T(8,128)(2,1)S(1)}, u32[]{:S(2)}, u32[]{:S(2)}) collective-permute-start(bf16[128,256]{1,0:T(8,128)(2,1)S(1)} %get-tuple-element.78), channel_id=1, source_target_pairs={{0,24},{8,0},{16,8},{24,16},{1,25},{9,1},{17,9},{25,17},{2,26},{10... | collective-permute-start | bytes 196616 | tf_op jit(solution)/shard_map/ppermute | solution.py:255
  9.8 7.0 %collective-permute-start.4 = (bf16[128,256]{1,0:T(8,128)(2,1)S(1)}, bf16[128,256]{1,0:T(8,128)(2,1)S(1)}, u32[]{:S(2)}, u32[]{:S(2)}) collective-permute-start(bf16[128,256]{1,0:T(8,128)(2,1)S(1)} %get-tuple-element.79.refs_3_), channel_id=1, source_target_pairs={{0,1},{1,0},{2,3},{3,2},{4,5},{5,4},{6,7},{7,6},{8,9},{9,8},{10,11... | collective-permute-start | bytes 196616 | tf_op jit(solution)/shard_map/ppermute | solution.py:215
  13.2 3.6 %collective-permute-start.5 = (bf16[128,256]{1,0:T(8,128)(2,1)S(1)}, bf16[128,256]{1,0:T(8,128)(2,1)S(1)}, u32[]{:S(2)}, u32[]{:S(2)}) collective-permute-start(bf16[128,256]{1,0:T(8,128)(2,1)S(1)} %collective-permute-done.refs_4_), channel_id=1, source_target_pairs={{0,1},{1,0},{2,3},{3,2},{4,5},{5,4},{6,7},{7,6},{8,9},{9,8},{10,11... | collective-permute-start | bytes 196616 | tf_op jit(solution)/shard_map/ppermute | solution.py:215
  13.2 5.0 %collective-permute-start.6 = (bf16[128,256]{1,0:T(8,128)(2,1)S(1)}, bf16[128,256]{1,0:T(8,128)(2,1)S(1)}, u32[]{:S(2)}, u32[]{:S(2)}) collective-permute-start(bf16[128,256]{1,0:T(8,128)(2,1)S(1)} %collective-permute-done.1.refs_5_), channel_id=1, source_target_pairs={{0,1},{1,0},{2,3},{3,2},{4,5},{5,4},{6,7},{7,6},{8,9},{9,8},{10,11... | collective-permute-start | bytes 196616 | tf_op jit(solution)/shard_map/ppermute | solution.py:215
  13.7 4.5 %collective-permute-start.7 = (bf16[128,256]{1,0:T(8,128)(2,1)S(1)}, bf16[128,256]{1,0:T(8,128)(2,1)S(1)}, u32[]{:S(2)}, u32[]{:S(2)}) collective-permute-start(bf16[128,256]{1,0:T(8,128)(2,1)S(1)} %collective-permute-done.2.refs_6_), channel_id=1, source_target_pairs={{0,1},{1,0},{2,3},{3,2},{4,5},{5,4},{6,7},{7,6},{8,9},{9,8},{10,11... | collective-permute-start | bytes 196616 | tf_op jit(solution)/shard_map/ppermute | solution.py:215
  13.8 9.1 %collective-permute-start.10 = (bf16[128,256]{1,0:T(8,128)(2,1)S(1)}, bf16[128,256]{1,0:T(8,128)(2,1)S(1)}, u32[]{:S(2)}, u32[]{:S(2)}) collective-permute-start(bf16[128,256]{1,0:T(8,128)(2,1)S(1)} %collective-permute-done.3.refs_3_), channel_id=1, source_target_pairs={{0,6},{2,4},{4,2},{6,0},{1,7},{3,5},{5,3},{7,1},{8,14},{10,12},{12... | collective-permute-start | bytes 196616 | tf_op jit(solution)/shard_map/ppermute | solution.py:219
  16.8 6.1 %collective-permute-start.8 = (bf16[128,256]{1,0:T(8,128)(2,1)S(1)}, bf16[128,256]{1,0:T(8,128)(2,1)S(1)}, u32[]{:S(2)}, u32[]{:S(2)}) collective-permute-start(bf16[128,256]{1,0:T(8,128)(2,1)S(1)} %collective-permute-done.3.refs_3_), channel_id=1, source_target_pairs={{0,2},{2,0},{4,6},{6,4},{1,3},{3,1},{5,7},{7,5},{8,10},{10,8},{12,... | collective-permute-start | bytes 196616 | tf_op jit(solution)/shard_map/ppermute | solution.py:219
  16.9 6.1 %collective-permute-start.9 = (bf16[128,256]{1,0:T(8,128)(2,1)S(1)}, bf16[128,256]{1,0:T(8,128)(2,1)S(1)}, u32[]{:S(2)}, u32[]{:S(2)}) collective-permute-start(bf16[128,256]{1,0:T(8,128)(2,1)S(1)} %collective-permute-done.3.refs_3_), channel_id=1, source_target_pairs={{0,4},{2,6},{4,0},{6,2},{1,5},{3,7},{5,1},{7,3},{8,12},{10,14},{12... | collective-permute-start | bytes 196616 | tf_op jit(solution)/shard_map/ppermute | solution.py:219
  22.9 1.6 %collective-permute-start.13 = (bf16[512,256]{1,0:T(8,128)(2,1)S(1)}, bf16[512,256]{1,0:T(8,128)(2,1)S(1)}, u32[]{:S(2)}, u32[]{:S(2)}) collective-permute-start(bf16[512,256]{1,0:T(8,128)(2,1)S(1)} %get-tuple-element.47), channel_id=1, source_target_pairs={{0,1},{1,0},{2,3},{3,2},{4,5},{5,4},{6,7},{7,6},{8,9},{9,8},{10,11... | collective-permute-start | bytes 786440 | tf_op jit(solution)/shard_map/ppermute | solution.py:215
  23.0 6.1 %collective-permute-start.11 = (bf16[128,256]{1,0:T(8,128)(2,1)S(1)}, bf16[128,256]{1,0:T(8,128)(2,1)S(1)}, u32[]{:S(2)}, u32[]{:S(2)}) collective-permute-start(bf16[128,256]{1,0:T(8,128)(2,1)S(1)} %collective-permute-done.3.refs_3_), channel_id=1, source_target_pairs={{0,1},{1,0},{2,3},{3,2},{4,5},{5,4},{6,7},{7,6},{8,9},{9,8},{10,11... | collective-permute-start | bytes 196616 | tf_op jit(solution)/shard_map/ppermute | solution.py:215
  23.5 5.6 %collective-permute-start.12 = (bf16[384,256]{1,0:T(8,128)(2,1)S(1)}, bf16[384,256]{1,0:T(8,128)(2,1)S(1)}, u32[]{:S(2)}, u32[]{:S(2)}) collective-permute-start(bf16[384,256]{1,0:T(8,128)(2,1)S(1)} %pad_maximum_fusion), channel_id=1, source_target_pairs={{0,1},{1,0},{2,3},{3,2},{4,5},{5,4},{6,7},{7,6},{8,9},{9,8},{10,11... | collective-permute-start | bytes 589832 | tf_op jit(solution)/shard_map/ppermute | solution.py:215
  24.6 9.2 %copy-start.3 = (f32[1,128,128]{2,1,0:T(8,128)S(1)}, f32[1,128,128]{2,1,0:T(8,128)}, u32[]{:S(2)}) copy-start(f32[1,128,128]{2,1,0:T(8,128)} %param.16) | copy-start | bytes 196612
  24.7 9.1 %collective-permute-start.14 = (bf16[128,256]{1,0:T(8,128)(2,1)S(1)}, bf16[128,256]{1,0:T(8,128)(2,1)S(1)}, u32[]{:S(2)}, u32[]{:S(2)}) collective-permute-start(bf16[128,256]{1,0:T(8,128)(2,1)S(1)} %get-tuple-element.50), channel_id=1, source_target_pairs={{0,6},{2,4},{4,2},{6,0},{1,7},{3,5},{5,3},{7,1},{8,14},{10,12},{12... | collective-permute-start | bytes 196616 | tf_op jit(solution)/shard_map/ppermute | solution.py:219
  27.8 6.1 %collective-permute-start.15 = (bf16[128,256]{1,0:T(8,128)(2,1)S(1)}, bf16[128,256]{1,0:T(8,128)(2,1)S(1)}, u32[]{:S(2)}, u32[]{:S(2)}) collective-permute-start(bf16[128,256]{1,0:T(8,128)(2,1)S(1)} %get-tuple-element.51), channel_id=1, source_target_pairs={{0,4},{2,6},{4,0},{6,2},{1,5},{3,7},{5,1},{7,3},{8,12},{10,14},{12... | collective-permute-start | bytes 196616 | tf_op jit(solution)/shard_map/ppermute | solution.py:219
  27.8 6.1 %collective-permute-start.16 = (bf16[128,256]{1,0:T(8,128)(2,1)S(1)}, bf16[128,256]{1,0:T(8,128)(2,1)S(1)}, u32[]{:S(2)}, u32[]{:S(2)}) collective-permute-start(bf16[128,256]{1,0:T(8,128)(2,1)S(1)} %get-tuple-element.52), channel_id=1, source_target_pairs={{0,2},{2,0},{4,6},{6,4},{1,3},{3,1},{5,7},{7,5},{8,10},{10,8},{12,... | collective-permute-start | bytes 196616 | tf_op jit(solution)/shard_map/ppermute | solution.py:219
  33.9 2.0 %collective-permute-start.17 = (bf16[512,256]{1,0:T(8,128)(2,1)S(1)}, bf16[512,256]{1,0:T(8,128)(2,1)S(1)}, u32[]{:S(2)}, u32[]{:S(2)}) collective-permute-start(bf16[512,256]{1,0:T(8,128)(2,1)S(1)} %get-tuple-element.56), channel_id=1, source_target_pairs={{0,1},{1,0},{2,3},{3,2},{4,5},{5,4},{6,7},{7,6},{8,9},{9,8},{10,11... | collective-permute-start | bytes 786440 | tf_op jit(solution)/shard_map/ppermute | solution.py:215
  34.0 8.8 %collective-permute-start.21 = (f32[128,256]{1,0:T(8,128)S(1)}, f32[128,256]{1,0:T(8,128)S(1)}, u32[]{:S(2)}, u32[]{:S(2)}) collective-permute-start(f32[128,256]{1,0:T(8,128)S(1)} %fusion.5), channel_id=1, source_target_pairs={{0,8},{8,0},{16,24},{24,16},{1,9},{9,1},{17,25},{25,17},{2,10},{10... | collective-permute-start | bytes 393224 | tf_op jit(solution)/shard_map/ppermute | solution.py:228
  36.0 6.9 %collective-permute-start.18 = (bf16[128,256]{1,0:T(8,128)(2,1)S(1)}, bf16[128,256]{1,0:T(8,128)(2,1)S(1)}, u32[]{:S(2)}, u32[]{:S(2)}) collective-permute-start(bf16[128,256]{1,0:T(8,128)(2,1)S(1)} %get-tuple-element.57), channel_id=1, source_target_pairs={{0,6},{2,4},{4,2},{6,0},{1,7},{3,5},{5,3},{7,1},{8,14},{10,12},{12... | collective-permute-start | bytes 196616 | tf_op jit(solution)/shard_map/ppermute | solution.py:219
  38.7 6.2 %collective-permute-start.19 = (bf16[128,256]{1,0:T(8,128)(2,1)S(1)}, bf16[128,256]{1,0:T(8,128)(2,1)S(1)}, u32[]{:S(2)}, u32[]{:S(2)}) collective-permute-start(bf16[128,256]{1,0:T(8,128)(2,1)S(1)} %get-tuple-element.58), channel_id=1, source_target_pairs={{0,4},{2,6},{4,0},{6,2},{1,5},{3,7},{5,1},{7,3},{8,12},{10,14},{12... | collective-permute-start | bytes 196616 | tf_op jit(solution)/shard_map/ppermute | solution.py:219
  38.7 6.2 %collective-permute-start.20 = (bf16[128,256]{1,0:T(8,128)(2,1)S(1)}, bf16[128,256]{1,0:T(8,128)(2,1)S(1)}, u32[]{:S(2)}, u32[]{:S(2)}) collective-permute-start(bf16[128,256]{1,0:T(8,128)(2,1)S(1)} %get-tuple-element.59), channel_id=1, source_target_pairs={{0,2},{2,0},{4,6},{6,4},{1,3},{3,1},{5,7},{7,5},{8,10},{10,8},{12,... | collective-permute-start | bytes 196616 | tf_op jit(solution)/shard_map/ppermute | solution.py:219
  40.4 5.2 %collective-permute-start.22 = (bf16[128,256]{1,0:T(8,128)(2,1)S(1)}, bf16[128,256]{1,0:T(8,128)(2,1)S(1)}, u32[]{:S(2)}, u32[]{:S(2)}) collective-permute-start(bf16[128,256]{1,0:T(8,128)(2,1)S(1)} %convert_element_type.41), channel_id=1, source_target_pairs={{8,16},{16,8},{24,0},{0,24},{9,17},{17,9},{25,1},{1,25},{10,18},{1... | collective-permute-start | bytes 196616 | tf_op jit(solution)/shard_map/ppermute | solution.py:228
  (4 other events, 16.3 us)

commit v4 on v3

--- a/solution.py
+++ b/solution.py
@@ -42,7 +42,7 @@
     order_ref, q_ref, g_ref = refs[:3]
     outs = refs[3 + arrays + aliased :]
     dq_ref, near_out_ref, far_out_ref = outs[:3]
-    e_ref, dp_ref, p_ref, ds_ref, acc_ref, kt_ref, dq_held, dq_sem = outs[3:]
+    e_ref, dp_ref, p_ref, ds_ref, acc_ref, kv_ref, kt_ref, dq_held, dq_sem = outs[3:]
     local_rows, model = dq_held.shape
     head_dim = near_out_ref.shape[1] // 2
     half_rows = near_out_ref.shape[0]
@@ -68,26 +68,33 @@
         parity = core if slot < chips else 1 - core
         return order_ref[2 * source + parity] < own_group
 
-    for slot in range(blocks):
-        kt_ref[:, slot * local_rows : (slot + 1) * local_rows] = kv_refs[slot][:, :head_dim].T
-
-    def pair_of(ref, pair):
-        return ref[pl.ds((tick * pairs + pair) * width, width), :]
-
     def rows_of(slot):
         return slice(slot * local_rows, (slot + 1) * local_rows)
 
-    def front(pair):
-        q_pair = pair_of(q_ref, pair)
-        g_pair = pair_of(g_ref, pair)
-        peaks, totals, weights = [], [], []
-        for slot in range(blocks):
-            scores = lax.dot_general(
-                kv_refs[slot][:, :head_dim],
-                q_pair,
+    for slot in range(blocks):
+        block = kv_refs[slot][...]
+        kv_ref[rows_of(slot), :] = block
+        kt_ref[:, rows_of(slot)] = block[:, :head_dim].T
+
+    def stacked(ref, first, last):
+        return ref[pl.ds((tick * pairs + first) * width, (last - first) * width), :]
+
+    def products(pair):
+        for out, ref, cols in (
+            (e_ref, q_ref, slice(0, head_dim)),
+            (dp_ref, g_ref, slice(head_dim, 2 * head_dim)),
+        ):
+            out[pair] = lax.dot_general(
+                kv_ref[:, cols],
+                stacked(ref, pair, pair + 1),
                 CONTRACT_LAST,
                 preferred_element_type=jnp.float32,
             )
+
+    def softmax(pair):
+        peaks, totals, weights = [], [], []
+        for slot in range(blocks):
+            scores = e_ref[pair, rows_of(slot)]
             if slot == 0:
                 key_row = lax.broadcasted_iota(jnp.int32, (local_rows, width), 0)
                 query_row = lax.rem(
@@ -96,17 +103,10 @@
                 scores = jnp.where(key_row <= query_row, scores, MASK_FILL)
             peak = jnp.max(scores, axis=0, keepdims=True) * exp_scale
             expo = jnp.exp2(scores * exp_scale - peak)
-            prob_grads = lax.dot_general(
-                kv_refs[slot][:, head_dim:],
-                g_pair,
-                CONTRACT_LAST,
-                preferred_element_type=jnp.float32,
-            )
             e_ref[pair, rows_of(slot)] = expo
-            dp_ref[pair, rows_of(slot)] = prob_grads
             peaks.append(peak if slot == 0 else jnp.where(allowed(slot), peak, MASK_FILL))
             totals.append(jnp.sum(expo, axis=0, keepdims=True))
-            weights.append(jnp.sum(expo * prob_grads, axis=0, keepdims=True))
+            weights.append(jnp.sum(expo * dp_ref[pair, rows_of(slot)], axis=0, keepdims=True))
         biggest = peaks[0]
         for peak in peaks[1:]:
             biggest = jnp.maximum(biggest, peak)
@@ -114,38 +114,26 @@
         total = sum(part * factor for part, factor in zip(totals, factors))
         weighted = sum(part * factor for part, factor in zip(weights, factors))
         inverse = 1.0 / total
-        return [factor * inverse for factor in factors], weighted * inverse
-
-    def back(pair, factors, delta):
-        q_pair = pair_of(q_ref, pair)
-        g_pair = pair_of(g_ref, pair)
+        delta = weighted * inverse
+        cols = slice(pair * width, (pair + 1) * width)
         for slot in range(blocks):
-            probs = e_ref[pair, rows_of(slot)] * factors[slot]
-            p_ref[pair, rows_of(slot)] = probs.astype(jnp.bfloat16)
-            ds_ref[pair, rows_of(slot)] = (
+            probs = e_ref[pair, rows_of(slot)] * (factors[slot] * inverse)
+            p_ref[rows_of(slot), cols] = probs.astype(jnp.bfloat16)
+            ds_ref[rows_of(slot), cols] = (
                 probs * (dp_ref[pair, rows_of(slot)] - delta)
             ).astype(jnp.bfloat16)
-        score_grad = ds_ref[pair]
-        key_terms = jnp.dot(score_grad, q_pair, preferred_element_type=jnp.float32)
-        value_terms = jnp.dot(p_ref[pair], g_pair, preferred_element_type=jnp.float32)
-        if pair > 0:
-            key_terms += acc_ref[:, :head_dim]
-            value_terms += acc_ref[:, head_dim:]
-        if pair < pairs - 1:
-            acc_ref[:, :head_dim] = key_terms
-            acc_ref[:, head_dim:] = value_terms
-        else:
-            key_terms = key_terms * scale
-            near_out_ref[:, :head_dim] = key_terms[:half_rows]
-            near_out_ref[:, head_dim:] = value_terms[:half_rows]
-            far_out_ref[:, :head_dim] = key_terms[half_rows:].astype(far_out_ref.dtype)
-            far_out_ref[:, head_dim:] = value_terms[half_rows:].astype(far_out_ref.dtype)
-        query_t = jnp.dot(kt_ref[...], score_grad, preferred_element_type=jnp.float32) * scale
+
+    def query_grad(pair):
+        query_t = jnp.dot(
+            kt_ref[...],
+            ds_ref[:, pair * width : (pair + 1) * width],
+            preferred_element_type=jnp.float32,
+        )
         for half in range(2):
             lo = (2 * pair + half) * head_dim
-            dq_held[:, lo : lo + head_dim] = query_t[
-                :, half * local_rows : (half + 1) * local_rows
-            ].T.astype(dq_held.dtype)
+            dq_held[:, lo : lo + head_dim] = (
+                query_t[:, half * local_rows : (half + 1) * local_rows].T * scale
+            ).astype(dq_held.dtype)
         cols = pl.ds(2 * pair * head_dim, 2 * head_dim)
         copy = pltpu.make_async_copy(
             dq_held.at[:, cols], dq_ref.at[tick, 0, :, cols], dq_sem.at[pair]
@@ -153,12 +141,32 @@
         copy.start()
         return copy
 
+    def terms(first, last):
+        cols = slice(first * width, last * width)
+        return tuple(
+            jnp.dot(
+                held[:, cols], stacked(ref, first, last), preferred_element_type=jnp.float32
+            )
+            for held, ref in ((ds_ref, q_ref), (p_ref, g_ref))
+        )
+
     copies = []
-    held = front(0)
+    products(0)
     for pair in range(pairs):
-        following = front(pair + 1) if pair + 1 < pairs else None
-        copies.append(back(pair, *held))
-        held = following
+        if pair + 1 < pairs:
+            products(pair + 1)
+        if pair and pair + 1 == pairs:
+            acc_ref[:, :head_dim], acc_ref[:, head_dim:] = terms(0, pair)
+        softmax(pair)
+        copies.append(query_grad(pair))
+    key_terms, value_terms = terms(pairs - 1, pairs)
+    if pairs > 1:
+        key_terms += acc_ref[:, :head_dim]
+        value_terms += acc_ref[:, head_dim:]
+    near_out_ref[:, :head_dim] = key_terms[:half_rows] * scale
+    near_out_ref[:, head_dim:] = value_terms[:half_rows]
+    far_out_ref[:, :head_dim] = (key_terms[half_rows:] * scale).astype(far_out_ref.dtype)
+    far_out_ref[:, head_dim:] = value_terms[half_rows:].astype(far_out_ref.dtype)
     for copy in copies:
         copy.wait()
 
@@ -194,9 +202,10 @@
         scratch_shapes=[
             pltpu.VMEM(tile, jnp.float32),
             pltpu.VMEM(tile, jnp.float32),
-            pltpu.VMEM(tile, jnp.bfloat16),
-            pltpu.VMEM(tile, jnp.bfloat16),
+            pltpu.VMEM((key_rows, 2 * pairs * local_rows), jnp.bfloat16),
+            pltpu.VMEM((key_rows, 2 * pairs * local_rows), jnp.bfloat16),
             pltpu.VMEM((key_rows, width), jnp.float32),
+            pltpu.VMEM((key_rows, width), jnp.bfloat16),
             pltpu.VMEM((head_dim, key_rows), jnp.bfloat16),
             pltpu.VMEM((local_rows, model), jnp.bfloat16),
             pltpu.SemaphoreType.DMA((pairs,)),

time: 46.7 us -> 46.8 us (level)
  no operation moved by 1% of the time
where the time goes in v4:
time: 46.8 us; the launch traced here: 46.5 us
  starting transfers between devices  27.1 us (58%)
  Pallas kernels  9.74 us (21%)
  waiting for transfers between devices  4.77 us (10%)
  local copies, waits for them, and re-layouts  2.15 us (5%)
  other arithmetic  1.81 us (4%)
  between operations  0.88 us (2%)
    ppermute x12, starting transfers between devices, across_chips(): lax.ppermute(block, 'z', [(chip, chip ^ k) for chip in range(lax.axis_siz...  19 us
    pallas_call x2, Pallas kernels, attend_back(): pl.pallas_call(kernel, out_shape=(jax.ShapeDtypeStruct(queries.shape, jnp...  9.56 us
    ppermute x2, starting transfers between devices, section_swap(): return lax.ppermute(block, 'section', route)  4.13 us
    ppermute x12, waiting for transfers between devices, across_chips(): lax.ppermute(block, 'z', [(chip, chip ^ k) for chip in range(lax.axis_siz...  3.14 us
    ppermute x1, starting transfers between devices, body(): lax.ppermute(leaving_pair, 'section', [(i, (i - 1) % sections) for i in r...  2.67 us
    unnamed x10, local copies, waits for them, and re-layouts  2.1 us
    ppermute x8, starting transfers between devices, other_core(): return lax.ppermute(block, 'core', [(0, 1), (1, 0)])  1.36 us
  transfers between devices with their start and end apart: 23, of which 4 were waited for; matrix products, arithmetic and copies ran while one was open for 0% of the time, Pallas kernels for 21%

profile of v4, /device:TPU:0, one launch (start us, length us, event | category | flops | bytes accessed | tf_op | source)
XLA Modules:
  0.0 46.5 jit_solution(7486755846191094011)
XLA Ops:
  0.6 0.8 %maximum_select_fusion = (bf16[128,256]{1,0:T(8,128)(2,1)S(1)}, bf16[128,256]{1,0:T(8,128)(2,1)S(1)}) fusion(bf16[128,128]{1,0:T(8,128)(2,1)} %param.14, bf16[128,128]{1,0:T(8,128)(2,1)} %param.13, pred[]{:T(512)S(6)} %eq.11, bf16[128,128]{1,0:T(8,128)(2,1)} %bitcast.22, bf16[128,128]{1,0:T(8,128)(2,1)} %bitcast.23), kind=kLoop, calls=%fused_computation.16 | loop fusion | flops 294912 | bytes 262145 | tf_op jit(solution)/shard_map/jit(_where)/select_n | solution.py:259
  1.5 3.1 %collective-permute-start = (bf16[128,256]{1,0:T(8,128)(2,1)S(1)}, bf16[128,256]{1,0:T(8,128)(2,1)S(1)}, u32[]{:S(2)}, u32[]{:S(2)}) collective-permute-start(bf16[128,256]{1,0:T(8,128)(2,1)S(1)} %get-tuple-element.79.refs_3_), channel_id=1, source_target_pairs={{0,2},{2,0},{4,6},{6,4},{1,3},{3,1},{5,7},{7,5},{8,10},{10,8},{12,... | collective-permute-start | bytes 196616 | tf_op jit(solution)/shard_map/ppermute | solution.py:228
  4.6 2.6 %collective-permute-start.1 = (bf16[128,256]{1,0:T(8,128)(2,1)S(1)}, bf16[128,256]{1,0:T(8,128)(2,1)S(1)}, u32[]{:S(2)}, u32[]{:S(2)}) collective-permute-start(bf16[128,256]{1,0:T(8,128)(2,1)S(1)} %get-tuple-element.79.refs_3_), channel_id=1, source_target_pairs={{0,4},{2,6},{4,0},{6,2},{1,5},{3,7},{5,1},{7,3},{8,12},{10,14},{12... | collective-permute-start | bytes 196616 | tf_op jit(solution)/shard_map/ppermute | solution.py:228
  7.2 2.7 %collective-permute-start.3 = (bf16[128,256]{1,0:T(8,128)(2,1)S(1)}, bf16[128,256]{1,0:T(8,128)(2,1)S(1)}, u32[]{:S(2)}, u32[]{:S(2)}) collective-permute-start(bf16[128,256]{1,0:T(8,128)(2,1)S(1)} %get-tuple-element.78), channel_id=1, source_target_pairs={{0,24},{8,0},{16,8},{24,16},{1,25},{9,1},{17,9},{25,17},{2,26},{10... | collective-permute-start | bytes 196616 | tf_op jit(solution)/shard_map/ppermute | solution.py:264
  9.8 1.0 %copy-done = bf16[2,1,128,1024]{3,2,1,0:T(8,128)(2,1)S(1)} copy-done((bf16[2,1,128,1024]{3,2,1,0:T(8,128)(2,1)S(1)}, bf16[2,1,128,1024]{3,2,1,0:T(8,128)(2,1)}, u32[]{:S(2)}) %copy-start) | copy-done | bytes 524312
  10.9 1.0 %copy-done.1 = bf16[2,1,128,1024]{3,2,1,0:T(8,128)(2,1)S(1)} copy-done((bf16[2,1,128,1024]{3,2,1,0:T(8,128)(2,1)S(1)}, bf16[2,1,128,1024]{3,2,1,0:T(8,128)(2,1)}, u32[]{:S(2)}) %copy-start.1) | copy-done | bytes 524312
  11.9 0.2 shard_map.112
  12.1 1.1 %collective-permute-done.2.refs_6_ = bf16[128,256]{1,0:T(8,128)(2,1)S(1)} collective-permute-done((bf16[128,256]{1,0:T(8,128)(2,1)S(1)}, bf16[128,256]{1,0:T(8,128)(2,1)S(1)}, u32[]{:S(2)}, u32[]{:S(2)}) %collective-permute-start.2) | collective-permute-done | bytes 65568 | tf_op jit(solution)/shard_map/ppermute | solution.py:228
  13.2 0.5 %collective-permute-start.6 = (bf16[128,256]{1,0:T(8,128)(2,1)S(1)}, bf16[128,256]{1,0:T(8,128)(2,1)S(1)}, u32[]{:S(2)}, u32[]{:S(2)}) collective-permute-start(bf16[128,256]{1,0:T(8,128)(2,1)S(1)} %collective-permute-done.1.refs_5_), channel_id=1, source_target_pairs={{0,1},{1,0},{2,3},{3,2},{4,5},{5,4},{6,7},{7,6},{8,9},{9,8},{10,11... | collective-permute-start | bytes 196616 | tf_op jit(solution)/shard_map/ppermute | solution.py:224
  13.8 3.0 %collective-permute-start.10 = (bf16[128,256]{1,0:T(8,128)(2,1)S(1)}, bf16[128,256]{1,0:T(8,128)(2,1)S(1)}, u32[]{:S(2)}, u32[]{:S(2)}) collective-permute-start(bf16[128,256]{1,0:T(8,128)(2,1)S(1)} %collective-permute-done.3.refs_3_), channel_id=1, source_target_pairs={{0,6},{2,4},{4,2},{6,0},{1,7},{3,5},{5,3},{7,1},{8,14},{10,12},{12... | collective-permute-start | bytes 196616 | tf_op jit(solution)/shard_map/ppermute | solution.py:228
  16.9 1.4 %collective-permute-start.9 = (bf16[128,256]{1,0:T(8,128)(2,1)S(1)}, bf16[128,256]{1,0:T(8,128)(2,1)S(1)}, u32[]{:S(2)}, u32[]{:S(2)}) collective-permute-start(bf16[128,256]{1,0:T(8,128)(2,1)S(1)} %collective-permute-done.3.refs_3_), channel_id=1, source_target_pairs={{0,4},{2,6},{4,0},{6,2},{1,5},{3,7},{5,1},{7,3},{8,12},{10,14},{12... | collective-permute-start | bytes 196616 | tf_op jit(solution)/shard_map/ppermute | solution.py:228
  18.2 4.8 %shard_map.113 = (bf16[2,1,128,1024]{3,2,1,0:T(8,128)(2,1)}, f32[512,256]{1,0:T(8,128)S(1)}, bf16[512,256]{1,0:T(8,128)(2,1)S(1)}) custom-call(s32[8]{0:T(128)S(1)} %copy-done.2, bf16[2048,128]{1,0:T(8,128)(2,1)S(1)} %get-tuple-element.34.refs_1_, bf16[2048,128]{1,0:T(8,128)(2,1)S(1)} %get-tuple-element.35.refs_2_, ...), custom_call_target="tpu_custom_call" | custom-call | flops 5368709120 | bytes 2097152 | tf_op jit(solution)/shard_map/pallas_call | solution.py:193
  23.1 0.5 %collective-permute-start.11 = (bf16[128,256]{1,0:T(8,128)(2,1)S(1)}, bf16[128,256]{1,0:T(8,128)(2,1)S(1)}, u32[]{:S(2)}, u32[]{:S(2)}) collective-permute-start(bf16[128,256]{1,0:T(8,128)(2,1)S(1)} %collective-permute-done.3.refs_3_), channel_id=1, source_target_pairs={{0,1},{1,0},{2,3},{3,2},{4,5},{5,4},{6,7},{7,6},{8,9},{9,8},{10,11... | collective-permute-start | bytes 196616 | tf_op jit(solution)/shard_map/ppermute | solution.py:224
  23.8 0.9 %collective-permute-done.13 = bf16[512,256]{1,0:T(8,128)(2,1)S(1)} collective-permute-done((bf16[512,256]{1,0:T(8,128)(2,1)S(1)}, bf16[512,256]{1,0:T(8,128)(2,1)S(1)}, u32[]{:S(2)}, u32[]{:S(2)}) %collective-permute-start.13) | collective-permute-done | bytes 262176 | tf_op jit(solution)/shard_map/ppermute | solution.py:224
  24.8 3.1 %collective-permute-start.14 = (bf16[128,256]{1,0:T(8,128)(2,1)S(1)}, bf16[128,256]{1,0:T(8,128)(2,1)S(1)}, u32[]{:S(2)}, u32[]{:S(2)}) collective-permute-start(bf16[128,256]{1,0:T(8,128)(2,1)S(1)} %get-tuple-element.50), channel_id=1, source_target_pairs={{0,6},{2,4},{4,2},{6,0},{1,7},{3,5},{5,3},{7,1},{8,14},{10,12},{12... | collective-permute-start | bytes 196616 | tf_op jit(solution)/shard_map/ppermute | solution.py:228
  27.9 1.4 %collective-permute-start.16 = (bf16[128,256]{1,0:T(8,128)(2,1)S(1)}, bf16[128,256]{1,0:T(8,128)(2,1)S(1)}, u32[]{:S(2)}, u32[]{:S(2)}) collective-permute-start(bf16[128,256]{1,0:T(8,128)(2,1)S(1)} %get-tuple-element.52), channel_id=1, source_target_pairs={{0,2},{2,0},{4,6},{6,4},{1,3},{3,1},{5,7},{7,5},{8,10},{10,8},{12,... | collective-permute-start | bytes 196616 | tf_op jit(solution)/shard_map/ppermute | solution.py:228
  29.2 4.8 %shard_map.114 = (bf16[2,1,128,1024]{3,2,1,0:T(8,128)(2,1)}, f32[512,256]{1,0:T(8,128)S(1)}, bf16[512,256]{1,0:T(8,128)(2,1)S(1)}) custom-call(s32[8]{0:T(128)S(1)} %copy-done.2, bf16[2048,128]{1,0:T(8,128)(2,1)S(1)} %get-tuple-element.34.refs_1_, bf16[2048,128]{1,0:T(8,128)(2,1)S(1)} %get-tuple-element.35.refs_2_, ...), custom_call_target="tpu_custom_call", output_to_operand_aliasing={{0}: (9, {})} | custom-call | flops 5368709120 | bytes 2097152 | tf_op jit(solution)/shard_map/pallas_call | solution.py:193
  34.2 1.8 %collective-permute-start.21 = (f32[128,256]{1,0:T(8,128)S(1)}, f32[128,256]{1,0:T(8,128)S(1)}, u32[]{:S(2)}, u32[]{:S(2)}) collective-permute-start(f32[128,256]{1,0:T(8,128)S(1)} %fusion.5), channel_id=1, source_target_pairs={{0,8},{8,0},{16,24},{24,16},{1,9},{9,1},{17,25},{25,17},{2,10},{10... | collective-permute-start | bytes 393224 | tf_op jit(solution)/shard_map/ppermute | solution.py:237
  36.1 2.8 %collective-permute-start.18 = (bf16[128,256]{1,0:T(8,128)(2,1)S(1)}, bf16[128,256]{1,0:T(8,128)(2,1)S(1)}, u32[]{:S(2)}, u32[]{:S(2)}) collective-permute-start(bf16[128,256]{1,0:T(8,128)(2,1)S(1)} %get-tuple-element.57), channel_id=1, source_target_pairs={{0,6},{2,4},{4,2},{6,0},{1,7},{3,5},{5,3},{7,1},{8,14},{10,12},{12... | collective-permute-start | bytes 196616 | tf_op jit(solution)/shard_map/ppermute | solution.py:228
  38.9 1.6 %collective-permute-start.20 = (bf16[128,256]{1,0:T(8,128)(2,1)S(1)}, bf16[128,256]{1,0:T(8,128)(2,1)S(1)}, u32[]{:S(2)}, u32[]{:S(2)}) collective-permute-start(bf16[128,256]{1,0:T(8,128)(2,1)S(1)} %get-tuple-element.59), channel_id=1, source_target_pairs={{0,2},{2,0},{4,6},{6,4},{1,3},{3,1},{5,7},{7,5},{8,10},{10,8},{12,... | collective-permute-start | bytes 196616 | tf_op jit(solution)/shard_map/ppermute | solution.py:228
  40.5 2.4 %collective-permute-start.22 = (bf16[128,256]{1,0:T(8,128)(2,1)S(1)}, bf16[128,256]{1,0:T(8,128)(2,1)S(1)}, u32[]{:S(2)}, u32[]{:S(2)}) collective-permute-start(bf16[128,256]{1,0:T(8,128)(2,1)S(1)} %convert_element_type.41), channel_id=1, source_target_pairs={{8,16},{16,8},{24,0},{0,24},{9,17},{17,9},{25,1},{1,25},{10,18},{1... | collective-permute-start | bytes 196616 | tf_op jit(solution)/shard_map/ppermute | solution.py:237
  42.9 2.0 %collective-permute-done.19 = bf16[128,256]{1,0:T(8,128)(2,1)S(1)} collective-permute-done((bf16[128,256]{1,0:T(8,128)(2,1)S(1)}, bf16[128,256]{1,0:T(8,128)(2,1)S(1)}, u32[]{:S(2)}, u32[]{:S(2)}) %collective-permute-start.19) | collective-permute-done | bytes 65568 | tf_op jit(solution)/shard_map/ppermute | solution.py:228
  44.9 0.7 %collective-permute-done.22 = bf16[128,256]{1,0:T(8,128)(2,1)S(1)} collective-permute-done((bf16[128,256]{1,0:T(8,128)(2,1)S(1)}, bf16[128,256]{1,0:T(8,128)(2,1)S(1)}, u32[]{:S(2)}, u32[]{:S(2)}) %collective-permute-start.22) | collective-permute-done | bytes 65568 | tf_op jit(solution)/shard_map/ppermute | solution.py:237
  45.8 0.7 %maximum_bitcast_fusion = (f32[2,1,128,128]{3,2,1,0:T(8,128)}, f32[2,1,128,128]{3,2,1,0:T(8,128)}) fusion(f32[1,128,128]{2,1,0:T(8,128)S(1)} %get-tuple-element.77, f32[1,128,128]{2,1,0:T(8,128)S(1)} %get-tuple-element.75, f32[1,128,128]{2,1,0:T(8,128)S(1)} %get-tuple-element.76, f32[1,128,128]{2,1,0:T(8,128)S(1)} %get-tuple-element.74), kind=kLoop, calls=%fused_computation.11 | loop fusion | flops 65536 | bytes 524288
  (47 shorter events, 0.7 us)
Async XLA Ops:
  1.5 10.6 %collective-permute-start = (bf16[128,256]{1,0:T(8,128)(2,1)S(1)}, bf16[128,256]{1,0:T(8,128)(2,1)S(1)}, u32[]{:S(2)}, u32[]{:S(2)}) collective-permute-start(bf16[128,256]{1,0:T(8,128)(2,1)S(1)} %get-tuple-element.79.refs_3_), channel_id=1, source_target_pairs={{0,2},{2,0},{4,6},{6,4},{1,3},{3,1},{5,7},{7,5},{8,10},{10,8},{12,... | collective-permute-start | bytes 196616 | tf_op jit(solution)/shard_map/ppermute | solution.py:228
  4.6 7.5 %collective-permute-start.1 = (bf16[128,256]{1,0:T(8,128)(2,1)S(1)}, bf16[128,256]{1,0:T(8,128)(2,1)S(1)}, u32[]{:S(2)}, u32[]{:S(2)}) collective-permute-start(bf16[128,256]{1,0:T(8,128)(2,1)S(1)} %get-tuple-element.79.refs_3_), channel_id=1, source_target_pairs={{0,4},{2,6},{4,0},{6,2},{1,5},{3,7},{5,1},{7,3},{8,12},{10,14},{12... | collective-permute-start | bytes 196616 | tf_op jit(solution)/shard_map/ppermute | solution.py:228
  7.2 6.1 %collective-permute-start.2 = (bf16[128,256]{1,0:T(8,128)(2,1)S(1)}, bf16[128,256]{1,0:T(8,128)(2,1)S(1)}, u32[]{:S(2)}, u32[]{:S(2)}) collective-permute-start(bf16[128,256]{1,0:T(8,128)(2,1)S(1)} %get-tuple-element.79.refs_3_), channel_id=1, source_target_pairs={{0,6},{2,4},{4,2},{6,0},{1,7},{3,5},{5,3},{7,1},{8,14},{10,12},{12... | collective-permute-start | bytes 196616 | tf_op jit(solution)/shard_map/ppermute | solution.py:228
  7.2 6.1 %collective-permute-start.3 = (bf16[128,256]{1,0:T(8,128)(2,1)S(1)}, bf16[128,256]{1,0:T(8,128)(2,1)S(1)}, u32[]{:S(2)}, u32[]{:S(2)}) collective-permute-start(bf16[128,256]{1,0:T(8,128)(2,1)S(1)} %get-tuple-element.78), channel_id=1, source_target_pairs={{0,24},{8,0},{16,8},{24,16},{1,25},{9,1},{17,9},{25,17},{2,26},{10... | collective-permute-start | bytes 196616 | tf_op jit(solution)/shard_map/ppermute | solution.py:264
  9.8 7.0 %collective-permute-start.4 = (bf16[128,256]{1,0:T(8,128)(2,1)S(1)}, bf16[128,256]{1,0:T(8,128)(2,1)S(1)}, u32[]{:S(2)}, u32[]{:S(2)}) collective-permute-start(bf16[128,256]{1,0:T(8,128)(2,1)S(1)} %get-tuple-element.79.refs_3_), channel_id=1, source_target_pairs={{0,1},{1,0},{2,3},{3,2},{4,5},{5,4},{6,7},{7,6},{8,9},{9,8},{10,11... | collective-permute-start | bytes 196616 | tf_op jit(solution)/shard_map/ppermute | solution.py:224
  13.2 3.6 %collective-permute-start.5 = (bf16[128,256]{1,0:T(8,128)(2,1)S(1)}, bf16[128,256]{1,0:T(8,128)(2,1)S(1)}, u32[]{:S(2)}, u32[]{:S(2)}) collective-permute-start(bf16[128,256]{1,0:T(8,128)(2,1)S(1)} %collective-permute-done.refs_4_), channel_id=1, source_target_pairs={{0,1},{1,0},{2,3},{3,2},{4,5},{5,4},{6,7},{7,6},{8,9},{9,8},{10,11... | collective-permute-start | bytes 196616 | tf_op jit(solution)/shard_map/ppermute | solution.py:224
  13.2 5.0 %collective-permute-start.6 = (bf16[128,256]{1,0:T(8,128)(2,1)S(1)}, bf16[128,256]{1,0:T(8,128)(2,1)S(1)}, u32[]{:S(2)}, u32[]{:S(2)}) collective-permute-start(bf16[128,256]{1,0:T(8,128)(2,1)S(1)} %collective-permute-done.1.refs_5_), channel_id=1, source_target_pairs={{0,1},{1,0},{2,3},{3,2},{4,5},{5,4},{6,7},{7,6},{8,9},{9,8},{10,11... | collective-permute-start | bytes 196616 | tf_op jit(solution)/shard_map/ppermute | solution.py:224
  13.7 4.5 %collective-permute-start.7 = (bf16[128,256]{1,0:T(8,128)(2,1)S(1)}, bf16[128,256]{1,0:T(8,128)(2,1)S(1)}, u32[]{:S(2)}, u32[]{:S(2)}) collective-permute-start(bf16[128,256]{1,0:T(8,128)(2,1)S(1)} %collective-permute-done.2.refs_6_), channel_id=1, source_target_pairs={{0,1},{1,0},{2,3},{3,2},{4,5},{5,4},{6,7},{7,6},{8,9},{9,8},{10,11... | collective-permute-start | bytes 196616 | tf_op jit(solution)/shard_map/ppermute | solution.py:224
  13.8 9.2 %collective-permute-start.10 = (bf16[128,256]{1,0:T(8,128)(2,1)S(1)}, bf16[128,256]{1,0:T(8,128)(2,1)S(1)}, u32[]{:S(2)}, u32[]{:S(2)}) collective-permute-start(bf16[128,256]{1,0:T(8,128)(2,1)S(1)} %collective-permute-done.3.refs_3_), channel_id=1, source_target_pairs={{0,6},{2,4},{4,2},{6,0},{1,7},{3,5},{5,3},{7,1},{8,14},{10,12},{12... | collective-permute-start | bytes 196616 | tf_op jit(solution)/shard_map/ppermute | solution.py:228
  16.8 6.2 %collective-permute-start.8 = (bf16[128,256]{1,0:T(8,128)(2,1)S(1)}, bf16[128,256]{1,0:T(8,128)(2,1)S(1)}, u32[]{:S(2)}, u32[]{:S(2)}) collective-permute-start(bf16[128,256]{1,0:T(8,128)(2,1)S(1)} %collective-permute-done.3.refs_3_), channel_id=1, source_target_pairs={{0,2},{2,0},{4,6},{6,4},{1,3},{3,1},{5,7},{7,5},{8,10},{10,8},{12,... | collective-permute-start | bytes 196616 | tf_op jit(solution)/shard_map/ppermute | solution.py:228
  16.9 6.2 %collective-permute-start.9 = (bf16[128,256]{1,0:T(8,128)(2,1)S(1)}, bf16[128,256]{1,0:T(8,128)(2,1)S(1)}, u32[]{:S(2)}, u32[]{:S(2)}) collective-permute-start(bf16[128,256]{1,0:T(8,128)(2,1)S(1)} %collective-permute-done.3.refs_3_), channel_id=1, source_target_pairs={{0,4},{2,6},{4,0},{6,2},{1,5},{3,7},{5,1},{7,3},{8,12},{10,14},{12... | collective-permute-start | bytes 196616 | tf_op jit(solution)/shard_map/ppermute | solution.py:228
  23.0 1.6 %collective-permute-start.13 = (bf16[512,256]{1,0:T(8,128)(2,1)S(1)}, bf16[512,256]{1,0:T(8,128)(2,1)S(1)}, u32[]{:S(2)}, u32[]{:S(2)}) collective-permute-start(bf16[512,256]{1,0:T(8,128)(2,1)S(1)} %get-tuple-element.47), channel_id=1, source_target_pairs={{0,1},{1,0},{2,3},{3,2},{4,5},{5,4},{6,7},{7,6},{8,9},{9,8},{10,11... | collective-permute-start | bytes 786440 | tf_op jit(solution)/shard_map/ppermute | solution.py:224
  23.1 6.1 %collective-permute-start.11 = (bf16[128,256]{1,0:T(8,128)(2,1)S(1)}, bf16[128,256]{1,0:T(8,128)(2,1)S(1)}, u32[]{:S(2)}, u32[]{:S(2)}) collective-permute-start(bf16[128,256]{1,0:T(8,128)(2,1)S(1)} %collective-permute-done.3.refs_3_), channel_id=1, source_target_pairs={{0,1},{1,0},{2,3},{3,2},{4,5},{5,4},{6,7},{7,6},{8,9},{9,8},{10,11... | collective-permute-start | bytes 196616 | tf_op jit(solution)/shard_map/ppermute | solution.py:224
  23.6 5.6 %collective-permute-start.12 = (bf16[384,256]{1,0:T(8,128)(2,1)S(1)}, bf16[384,256]{1,0:T(8,128)(2,1)S(1)}, u32[]{:S(2)}, u32[]{:S(2)}) collective-permute-start(bf16[384,256]{1,0:T(8,128)(2,1)S(1)} %pad_maximum_fusion), channel_id=1, source_target_pairs={{0,1},{1,0},{2,3},{3,2},{4,5},{5,4},{6,7},{7,6},{8,9},{9,8},{10,11... | collective-permute-start | bytes 589832 | tf_op jit(solution)/shard_map/ppermute | solution.py:224
  24.7 9.3 %copy-start.3 = (f32[1,128,128]{2,1,0:T(8,128)S(1)}, f32[1,128,128]{2,1,0:T(8,128)}, u32[]{:S(2)}) copy-start(f32[1,128,128]{2,1,0:T(8,128)} %param.16) | copy-start | bytes 196612
  24.8 9.2 %collective-permute-start.14 = (bf16[128,256]{1,0:T(8,128)(2,1)S(1)}, bf16[128,256]{1,0:T(8,128)(2,1)S(1)}, u32[]{:S(2)}, u32[]{:S(2)}) collective-permute-start(bf16[128,256]{1,0:T(8,128)(2,1)S(1)} %get-tuple-element.50), channel_id=1, source_target_pairs={{0,6},{2,4},{4,2},{6,0},{1,7},{3,5},{5,3},{7,1},{8,14},{10,12},{12... | collective-permute-start | bytes 196616 | tf_op jit(solution)/shard_map/ppermute | solution.py:228
  27.9 6.2 %collective-permute-start.15 = (bf16[128,256]{1,0:T(8,128)(2,1)S(1)}, bf16[128,256]{1,0:T(8,128)(2,1)S(1)}, u32[]{:S(2)}, u32[]{:S(2)}) collective-permute-start(bf16[128,256]{1,0:T(8,128)(2,1)S(1)} %get-tuple-element.51), channel_id=1, source_target_pairs={{0,4},{2,6},{4,0},{6,2},{1,5},{3,7},{5,1},{7,3},{8,12},{10,14},{12... | collective-permute-start | bytes 196616 | tf_op jit(solution)/shard_map/ppermute | solution.py:228
  27.9 6.2 %collective-permute-start.16 = (bf16[128,256]{1,0:T(8,128)(2,1)S(1)}, bf16[128,256]{1,0:T(8,128)(2,1)S(1)}, u32[]{:S(2)}, u32[]{:S(2)}) collective-permute-start(bf16[128,256]{1,0:T(8,128)(2,1)S(1)} %get-tuple-element.52), channel_id=1, source_target_pairs={{0,2},{2,0},{4,6},{6,4},{1,3},{3,1},{5,7},{7,5},{8,10},{10,8},{12,... | collective-permute-start | bytes 196616 | tf_op jit(solution)/shard_map/ppermute | solution.py:228
  34.1 1.9 %collective-permute-start.17 = (bf16[512,256]{1,0:T(8,128)(2,1)S(1)}, bf16[512,256]{1,0:T(8,128)(2,1)S(1)}, u32[]{:S(2)}, u32[]{:S(2)}) collective-permute-start(bf16[512,256]{1,0:T(8,128)(2,1)S(1)} %get-tuple-element.56), channel_id=1, source_target_pairs={{0,1},{1,0},{2,3},{3,2},{4,5},{5,4},{6,7},{7,6},{8,9},{9,8},{10,11... | collective-permute-start | bytes 786440 | tf_op jit(solution)/shard_map/ppermute | solution.py:224
  34.2 8.7 %collective-permute-start.21 = (f32[128,256]{1,0:T(8,128)S(1)}, f32[128,256]{1,0:T(8,128)S(1)}, u32[]{:S(2)}, u32[]{:S(2)}) collective-permute-start(f32[128,256]{1,0:T(8,128)S(1)} %fusion.5), channel_id=1, source_target_pairs={{0,8},{8,0},{16,24},{24,16},{1,9},{9,1},{17,25},{25,17},{2,10},{10... | collective-permute-start | bytes 393224 | tf_op jit(solution)/shard_map/ppermute | solution.py:237
  36.1 6.9 %collective-permute-start.18 = (bf16[128,256]{1,0:T(8,128)(2,1)S(1)}, bf16[128,256]{1,0:T(8,128)(2,1)S(1)}, u32[]{:S(2)}, u32[]{:S(2)}) collective-permute-start(bf16[128,256]{1,0:T(8,128)(2,1)S(1)} %get-tuple-element.57), channel_id=1, source_target_pairs={{0,6},{2,4},{4,2},{6,0},{1,7},{3,5},{5,3},{7,1},{8,14},{10,12},{12... | collective-permute-start | bytes 196616 | tf_op jit(solution)/shard_map/ppermute | solution.py:228
  38.9 6.0 %collective-permute-start.19 = (bf16[128,256]{1,0:T(8,128)(2,1)S(1)}, bf16[128,256]{1,0:T(8,128)(2,1)S(1)}, u32[]{:S(2)}, u32[]{:S(2)}) collective-permute-start(bf16[128,256]{1,0:T(8,128)(2,1)S(1)} %get-tuple-element.58), channel_id=1, source_target_pairs={{0,4},{2,6},{4,0},{6,2},{1,5},{3,7},{5,1},{7,3},{8,12},{10,14},{12... | collective-permute-start | bytes 196616 | tf_op jit(solution)/shard_map/ppermute | solution.py:228
  38.9 6.0 %collective-permute-start.20 = (bf16[128,256]{1,0:T(8,128)(2,1)S(1)}, bf16[128,256]{1,0:T(8,128)(2,1)S(1)}, u32[]{:S(2)}, u32[]{:S(2)}) collective-permute-start(bf16[128,256]{1,0:T(8,128)(2,1)S(1)} %get-tuple-element.59), channel_id=1, source_target_pairs={{0,2},{2,0},{4,6},{6,4},{1,3},{3,1},{5,7},{7,5},{8,10},{10,8},{12,... | collective-permute-start | bytes 196616 | tf_op jit(solution)/shard_map/ppermute | solution.py:228
  40.5 5.2 %collective-permute-start.22 = (bf16[128,256]{1,0:T(8,128)(2,1)S(1)}, bf16[128,256]{1,0:T(8,128)(2,1)S(1)}, u32[]{:S(2)}, u32[]{:S(2)}) collective-permute-start(bf16[128,256]{1,0:T(8,128)(2,1)S(1)} %convert_element_type.41), channel_id=1, source_target_pairs={{8,16},{16,8},{24,0},{0,24},{9,17},{17,9},{25,1},{1,25},{10,18},{1... | collective-permute-start | bytes 196616 | tf_op jit(solution)/shard_map/ppermute | solution.py:237
  (4 other events, 16.4 us)

commit v5 on v3

v5 whole, which is shorter than its diff:
```python
import math

import jax
import jax.numpy as jnp
from jax import lax
from jax.experimental import pallas as pl
from jax.experimental.pallas import tpu as pltpu
from jax.sharding import PartitionSpec as P

MASK_FILL = -1e30
CONTRACT_LAST = (((1,), (1,)), ((), ()))


def stack_kernel(q_ref, g_ref, q_out_ref, g_out_ref):
    ticks, _, local_rows, model = q_ref.shape
    head_dim = q_out_ref.shape[1]
    heads = model // head_dim
    for tick in range(ticks):
        for head in range(heads):
            rows = pl.ds((tick * heads + head) * local_rows, local_rows)
            cols = pl.ds(head * head_dim, head_dim)
            q_out_ref[rows, :] = q_ref[tick, 0, :, cols]
            g_out_ref[rows, :] = g_ref[tick, 0, :, cols]


def stacked_heads(queries, out_grad, head_dim):
    rows = queries.size // head_dim
    in_vmem = pl.BlockSpec(memory_space=pltpu.VMEM)
    return pl.pallas_call(
        stack_kernel,
        out_shape=(jax.ShapeDtypeStruct((rows, head_dim), queries.dtype),) * 2,
        in_specs=[in_vmem, in_vmem],
        out_specs=(in_vmem, in_vmem),
        compiler_params=pltpu.CompilerParams(vmem_limit_bytes=8 * 2**20),
        cost_estimate=pl.CostEstimate(
            flops=queries.size, bytes_accessed=8 * queries.size, transcendentals=0
        ),
    )(queries, out_grad)


def tick_kernel(tick, arrays, *refs):
    order_ref, q_ref, g_ref = refs[:3]
    outs = refs[3 + arrays :]
    dq_ref, near_out_ref, far_out_ref, s_ref, e_ref, dp_ref, ds_ref, acc_ref, kt_ref = outs
    local_rows, model = dq_ref.shape
    head_dim = near_out_ref.shape[1] // 2
    half_rows = near_out_ref.shape[0]
    kv_refs = [
        ref.at[pl.ds(row, local_rows)]
        for ref in refs[3 : 3 + arrays]
        for row in range(0, ref.shape[0], local_rows)
    ]
    blocks = len(kv_refs)
    heads = model // head_dim
    pairs = heads // 2
    width = 2 * local_rows
    chips = blocks // 2
    scale = 1.0 / math.sqrt(head_dim)
    exp_scale = scale * math.log2(math.e)

    core = lax.axis_index("core")
    chip = lax.axis_index("z")
    own_group = order_ref[2 * chip + core]

    def allowed(slot):
        source = jnp.bitwise_xor(chip, slot % chips)
        parity = core if slot < chips else 1 - core
        return order_ref[2 * source + parity] < own_group

    for slot in range(blocks):
        kt_ref[:, slot * local_rows : (slot + 1) * local_rows] = kv_refs[slot][:, :head_dim].T

    def pair_of(ref, pair):
        return ref[pl.ds((tick * pairs + pair) * width, width), :]

    def rows_of(slot):
        return slice(slot * local_rows, (slot + 1) * local_rows)

    def products(pair, slot):
        for out, ref, lo in ((s_ref, q_ref, 0), (dp_ref, g_ref, head_dim)):
            out[pair, rows_of(slot)] = lax.dot_general(
                kv_refs[slot][:, lo : lo + head_dim],
                pair_of(ref, pair),
                CONTRACT_LAST,
                preferred_element_type=jnp.float32,
            )

    def exponentials(pair, slot):
        scores = s_ref[pair, rows_of(slot)]
        if slot == 0:
            key_row = lax.broadcasted_iota(jnp.int32, (local_rows, width), 0)
            query_row = lax.rem(
                lax.broadcasted_iota(jnp.int32, (local_rows, width), 1), local_rows
            )
            scores = jnp.where(key_row <= query_row, scores, MASK_FILL)
        peak = jnp.max(scores, axis=0, keepdims=True) * exp_scale
        expo = jnp.exp2(scores * exp_scale - peak)
        e_ref[pair, rows_of(slot)] = expo
        total = jnp.sum(expo, axis=0, keepdims=True)
        weighted = jnp.sum(expo * dp_ref[pair, rows_of(slot)], axis=0, keepdims=True)
        if slot > 0:
            peak = jnp.where(allowed(slot), peak, MASK_FILL)
        return peak, total, weighted

    def combined(parts):
        biggest = parts[0][0]
        for peak, _, _ in parts[1:]:
            biggest = jnp.maximum(biggest, peak)
        factors = [jnp.exp2(peak - biggest) for peak, _, _ in parts]
        total = sum(part[1] * factor for part, factor in zip(parts, factors))
        weighted = sum(part[2] * factor for part, factor in zip(parts, factors))
        inverse = 1.0 / total
        return [factor * inverse for factor in factors], weighted * inverse

    def gradients(pair, slot, factors, delta):
        rows = rows_of(slot)
        probs = e_ref[pair, rows] * factors[slot]
        score_grad = (probs * (dp_ref[pair, rows] - delta)).astype(jnp.bfloat16)
        ds_ref[pair, rows] = score_grad
        key_terms = jnp.dot(score_grad, pair_of(q_ref, pair), preferred_element_type=jnp.float32)
        value_terms = jnp.dot(
            probs.astype(jnp.bfloat16), pair_of(g_ref, pair), preferred_element_type=jnp.float32
        )
        if pair > 0:
            key_terms += acc_ref[rows, :head_dim]
            value_terms += acc_ref[rows, head_dim:]
        if pair < pairs - 1:
            acc_ref[rows, :head_dim] = key_terms
            acc_ref[rows, head_dim:] = value_terms
        else:
            out = near_out_ref if slot < chips else far_out_ref
            place = rows_of(slot % chips)
            out[place, :head_dim] = (key_terms * scale).astype(out.dtype)
            out[place, head_dim:] = value_terms.astype(out.dtype)

    def query_grad(pair):
        query_t = jnp.dot(kt_ref[...], ds_ref[pair], preferred_element_type=jnp.float32)
        for half in range(2):
            lo = (2 * pair + half) * head_dim
            dq_ref[:, lo : lo + head_dim] = (
                query_t[:, half * local_rows : (half + 1) * local_rows].T * scale
            ).astype(dq_ref.dtype)

    held = None
    for pair in range(pairs + 1):
        parts = []
        if pair < pairs:
            products(pair, 0)
        for slot in range(blocks):
            if pair < pairs and slot + 1 < blocks:
                products(pair, slot + 1)
            if pair < pairs:
                parts.append(exponentials(pair, slot))
            if pair > 0:
                gradients(pair - 1, slot, *held)
            if pair > 1 and slot == 1:
                query_grad(pair - 2)
        if pair < pairs:
            held = combined(parts)
    query_grad(pairs - 1)


def attend_back(tick, group_order, queries, q_stack, g_stack, kv_arrays):
    local_rows, model = queries.shape[2:]
    width = kv_arrays[0].shape[1]
    key_rows = sum(array.shape[0] for array in kv_arrays)
    head_dim = width // 2
    pairs = model // head_dim // 2
    in_vmem = pl.BlockSpec(memory_space=pltpu.VMEM)
    tile = (pairs, key_rows, 2 * local_rows)

    def kernel(*refs):
        tick_kernel(tick, len(kv_arrays), *refs)

    return pl.pallas_call(
        kernel,
        out_shape=(
            jax.ShapeDtypeStruct((local_rows, model), jnp.bfloat16),
            jax.ShapeDtypeStruct((key_rows // 2, width), jnp.float32),
            jax.ShapeDtypeStruct((key_rows // 2, width), jnp.bfloat16),
        ),
        in_specs=[pl.BlockSpec(memory_space=pltpu.SMEM), *[in_vmem] * (2 + len(kv_arrays))],
        out_specs=(in_vmem, in_vmem, in_vmem),
        scratch_shapes=[
            pltpu.VMEM(tile, jnp.float32),
            pltpu.VMEM(tile, jnp.float32),
            pltpu.VMEM(tile, jnp.float32),
            pltpu.VMEM(tile, jnp.bfloat16),
            pltpu.VMEM((key_rows, width), jnp.float32),
            pltpu.VMEM((head_dim, key_rows), jnp.bfloat16),
        ],
        compiler_params=pltpu.CompilerParams(vmem_limit_bytes=44 * 2**20),
        cost_estimate=pl.CostEstimate(
            flops=40 * model * key_rows * local_rows,
            bytes_accessed=6 * local_rows * model + 5 * key_rows * width,
            transcendentals=model // head_dim * key_rows * local_rows,
        ),
    )(group_order, q_stack, g_stack, *kv_arrays)


def other_core(block):
    return lax.ppermute(block, "core", [(0, 1), (1, 0)])


def across_chips(block, k):
    return lax.ppermute(block, "z", [(chip, chip ^ k) for chip in range(lax.axis_size("z"))])


def section_swap(block, first):
    sections = lax.axis_size("section")
    route = []
    for low in range(first, sections, 2):
        high = (low + 1) % sections
        route += [(low, high), (high, low)]
    return lax.ppermute(block, "section", route)


def body(
    queries,
    out_grad,
    keys,
    values,
    entering_keys,
    entering_values,
    key_grads_in,
    value_grads_in,
    group_order,
):
    local_rows, head_dim = keys.shape[1:]
    width = 2 * head_dim
    chips = lax.axis_size("z")
    sections = lax.axis_size("section")
    section = lax.axis_index("section")

    own_pair = jnp.concatenate([keys[0], values[0]], axis=1)
    entering_pair = jnp.concatenate([entering_keys, entering_values], axis=1)
    leaving_pair = jnp.where(section == 0, entering_pair, own_pair)

    partners = range(chips - 1, 0, -1)
    near = [across_chips(own_pair, k) for k in partners][::-1]
    own_far = other_core(own_pair)
    next_pair = lax.ppermute(
        leaving_pair, "section", [(i, (i - 1) % sections) for i in range(sections)]
    )
    stacks = stacked_heads(queries, out_grad, head_dim)
    near, next_pair, stacks = lax.optimization_barrier((near, next_pair, stacks))
    far = [own_far] + [other_core(block) for block in near]
    next_near = [across_chips(next_pair, k) for k in partners][::-1]
    first_query, near_terms, far_terms = attend_back(
        0, group_order, queries, *stacks, [own_pair, *near, *far]
    )
    far_terms, next_near = lax.optimization_barrier((far_terms, [next_pair, *next_near]))
    next_kv = [*next_near, other_core(jnp.concatenate(next_near, axis=0))]

    def chip_sums(near_terms, far_terms):
        sums = near_terms + other_core(far_terms).astype(jnp.float32)
        sums = sums.reshape(chips, local_rows, width)
        return sums[0], [sums[k].astype(jnp.bfloat16) for k in range(1, chips)]

    def reduced(own_sum, leaving):
        for k in partners:
            own_sum = own_sum + across_chips(leaving[k - 1], k).astype(jnp.float32)
        return own_sum

    own_sum, leaving = chip_sums(near_terms, far_terms)
    stacks, leaving = lax.optimization_barrier((stacks, leaving))
    first_acc = jnp.concatenate([key_grads_in[0], value_grads_in[0]], axis=1) + reduced(
        own_sum, leaving
    )
    second_query, near_terms, far_terms = attend_back(1, group_order, queries, *stacks, next_kv)
    first_acc, far_terms = lax.optimization_barrier((first_acc, far_terms))
    early_acc = section_swap(first_acc, 0)
    own_sum, leaving = chip_sums(near_terms, far_terms)
    late_acc, leaving = lax.optimization_barrier((first_acc.astype(jnp.bfloat16), leaving))
    own_sum, queries_both = lax.optimization_barrier((own_sum, (first_query, second_query)))
    second_acc = reduced(own_sum, leaving)
    late_acc = section_swap(late_acc, 1).astype(jnp.float32)
    moved_acc = jnp.where(section % 2 == 0, early_acc, late_acc)
    second_acc = second_acc + jnp.where(section == sections - 1, 0.0, moved_acc)
    query_grads = jnp.stack(queries_both, axis=0)[:, None]
    key_grads = jnp.stack([first_acc[:, :head_dim], second_acc[:, :head_dim]], axis=0)[:, None]
    value_grads = jnp.stack([first_acc[:, head_dim:], second_acc[:, head_dim:]], axis=0)[:, None]
    return (query_grads, key_grads, value_grads)


def solution(mesh):
    sections, ctx_count = mesh.shape["section"], mesh.shape["ctx"]
    chip_mesh = jax.sharding.Mesh(
        mesh.devices.reshape(sections, ctx_count // 2, 2), ("section", "z", "core")
    )
    tokens = ("z", "core")
    return jax.shard_map(
        body,
        mesh=chip_mesh,
        in_specs=(
            P(None, "section", tokens, None),
            P(None, "section", tokens, None),
            P("section", tokens, None),
            P("section", tokens, None),
            P(tokens, None),
            P(tokens, None),
            P("section", tokens, None),
            P("section", tokens, None),
            P(),
        ),
        out_specs=(
            P(None, "section", tokens, None),
            P(None, "section", tokens, None),
            P(None, "section", tokens, None),
        ),
        check_vma=False,
    )
```

time: 46.7 us -> 46.5 us (level)
  other arithmetic: 1.81 us -> 2.65 us
  waiting for transfers between devices: 4.78 us -> 4.31 us
    unnamed x1 -> x2, other arithmetic: 0.72 us -> 1.56 us
    ppermute x12, waiting for transfers between devices: 3.14 us -> 2.6 us  [across_chips(): lax.ppermute(block, 'z', [(chip, chip ^ k) for chip in range(lax.axis_siz...]
    ppermute x8 -> x7, starting transfers between devices: 1.36 us -> 1.23 us  [other_core(): return lax.ppermute(block, 'core', [(0, 1), (1, 0)])]
    ppermute x8 -> x7, waiting for transfers between devices: 0.88 us -> 0.95 us  [other_core(): return lax.ppermute(block, 'core', [(0, 1), (1, 0)])]
  transfers between devices with their start and end apart: 23 -> 22, of which waited for: 4 -> 6; matrix products, arithmetic and copies ran while one was open for 0% -> 2% of each run, Pallas kernels for 21% -> 20%
where the time goes in v5:
time: 46.5 us; the launch traced here: 46.2 us
  starting transfers between devices  27.1 us (58%)
  Pallas kernels  9.21 us (20%)
  waiting for transfers between devices  4.31 us (9%)
  other arithmetic  2.65 us (6%)
  local copies, waits for them, and re-layouts  2.16 us (5%)
  between operations  0.84 us (2%)
    ppermute x12, starting transfers between devices, across_chips(): lax.ppermute(block, 'z', [(chip, chip ^ k) for chip in range(lax.axis_siz...  19 us
    pallas_call x2, Pallas kernels, attend_back(): pl.pallas_call(kernel, out_shape=(jax.ShapeDtypeStruct((local_rows, model...  9.03 us
    ppermute x2, starting transfers between devices, section_swap(): return lax.ppermute(block, 'section', route)  4.21 us
    ppermute x1, starting transfers between devices, body(): lax.ppermute(leaving_pair, 'section', [(i, (i - 1) % sections) for i in r...  2.67 us
    ppermute x12, waiting for transfers between devices, across_chips(): lax.ppermute(block, 'z', [(chip, chip ^ k) for chip in range(lax.axis_siz...  2.6 us
    unnamed x10, local copies, waits for them, and re-layouts  2.1 us
    unnamed x2, other arithmetic  1.56 us
    ppermute x7, starting transfers between devices, other_core(): return lax.ppermute(block, 'core', [(0, 1), (1, 0)])  1.23 us
  transfers between devices with their start and end apart: 22, of which 6 were waited for; matrix products, arithmetic and copies ran while one was open for 2% of the time, Pallas kernels for 20%

profile of v5, /device:TPU:0, one launch (start us, length us, event | category | flops | bytes accessed | tf_op | source)
XLA Modules:
  0.0 46.2 jit_solution(8934401775752103505)
XLA Ops:
  0.6 0.8 %maximum_select_fusion = (bf16[128,256]{1,0:T(8,128)(2,1)S(1)}, bf16[128,256]{1,0:T(8,128)(2,1)S(1)}) fusion(bf16[128,128]{1,0:T(8,128)(2,1)} %param.14, bf16[128,128]{1,0:T(8,128)(2,1)} %param.13, pred[]{:T(512)S(6)} %eq.11, bf16[128,128]{1,0:T(8,128)(2,1)} %bitcast.30, bf16[128,128]{1,0:T(8,128)(2,1)} %bitcast.31), kind=kLoop, calls=%fused_computation.14 | loop fusion | flops 294912 | bytes 262145 | tf_op jit(solution)/shard_map/jit(_where)/select_n | solution.py:237
  1.5 3.1 %collective-permute-start = (bf16[128,256]{1,0:T(8,128)(2,1)S(1)}, bf16[128,256]{1,0:T(8,128)(2,1)S(1)}, u32[]{:S(2)}, u32[]{:S(2)}) collective-permute-start(bf16[128,256]{1,0:T(8,128)(2,1)S(1)} %get-tuple-element.87.refs_3_), channel_id=1, source_target_pairs={{0,2},{2,0},{4,6},{6,4},{1,3},{3,1},{5,7},{7,5},{8,10},{10,8},{12,... | collective-permute-start | bytes 196616 | tf_op jit(solution)/shard_map/ppermute | solution.py:206
  4.6 2.6 %collective-permute-start.1 = (bf16[128,256]{1,0:T(8,128)(2,1)S(1)}, bf16[128,256]{1,0:T(8,128)(2,1)S(1)}, u32[]{:S(2)}, u32[]{:S(2)}) collective-permute-start(bf16[128,256]{1,0:T(8,128)(2,1)S(1)} %get-tuple-element.87.refs_3_), channel_id=1, source_target_pairs={{0,4},{2,6},{4,0},{6,2},{1,5},{3,7},{5,1},{7,3},{8,12},{10,14},{12... | collective-permute-start | bytes 196616 | tf_op jit(solution)/shard_map/ppermute | solution.py:206
  7.2 2.7 %collective-permute-start.3 = (bf16[128,256]{1,0:T(8,128)(2,1)S(1)}, bf16[128,256]{1,0:T(8,128)(2,1)S(1)}, u32[]{:S(2)}, u32[]{:S(2)}) collective-permute-start(bf16[128,256]{1,0:T(8,128)(2,1)S(1)} %get-tuple-element.86), channel_id=1, source_target_pairs={{0,24},{8,0},{16,8},{24,16},{1,25},{9,1},{17,9},{25,17},{2,26},{10... | collective-permute-start | bytes 196616 | tf_op jit(solution)/shard_map/ppermute | solution.py:242
  9.8 1.0 %copy-done = bf16[2,1,128,1024]{3,2,1,0:T(8,128)(2,1)S(1)} copy-done((bf16[2,1,128,1024]{3,2,1,0:T(8,128)(2,1)S(1)}, bf16[2,1,128,1024]{3,2,1,0:T(8,128)(2,1)}, u32[]{:S(2)}) %copy-start) | copy-done | bytes 524312
  10.9 1.0 %copy-done.1 = bf16[2,1,128,1024]{3,2,1,0:T(8,128)(2,1)S(1)} copy-done((bf16[2,1,128,1024]{3,2,1,0:T(8,128)(2,1)S(1)}, bf16[2,1,128,1024]{3,2,1,0:T(8,128)(2,1)}, u32[]{:S(2)}) %copy-start.1) | copy-done | bytes 524312
  12.1 1.1 %collective-permute-done.2.refs_6_ = bf16[128,256]{1,0:T(8,128)(2,1)S(1)} collective-permute-done((bf16[128,256]{1,0:T(8,128)(2,1)S(1)}, bf16[128,256]{1,0:T(8,128)(2,1)S(1)}, u32[]{:S(2)}, u32[]{:S(2)}) %collective-permute-start.2) | collective-permute-done | bytes 65568 | tf_op jit(solution)/shard_map/ppermute | solution.py:206
  13.2 0.5 %collective-permute-start.6 = (bf16[128,256]{1,0:T(8,128)(2,1)S(1)}, bf16[128,256]{1,0:T(8,128)(2,1)S(1)}, u32[]{:S(2)}, u32[]{:S(2)}) collective-permute-start(bf16[128,256]{1,0:T(8,128)(2,1)S(1)} %collective-permute-done.1.refs_5_), channel_id=1, source_target_pairs={{0,1},{1,0},{2,3},{3,2},{4,5},{5,4},{6,7},{7,6},{8,9},{9,8},{10,11... | collective-permute-start | bytes 196616 | tf_op jit(solution)/shard_map/ppermute | solution.py:202
  13.8 3.0 %collective-permute-start.10 = (bf16[128,256]{1,0:T(8,128)(2,1)S(1)}, bf16[128,256]{1,0:T(8,128)(2,1)S(1)}, u32[]{:S(2)}, u32[]{:S(2)}) collective-permute-start(bf16[128,256]{1,0:T(8,128)(2,1)S(1)} %collective-permute-done.3.refs_3_), channel_id=1, source_target_pairs={{0,6},{2,4},{4,2},{6,0},{1,7},{3,5},{5,3},{7,1},{8,14},{10,12},{12... | collective-permute-start | bytes 196616 | tf_op jit(solution)/shard_map/ppermute | solution.py:206
  16.9 1.4 %collective-permute-start.9 = (bf16[128,256]{1,0:T(8,128)(2,1)S(1)}, bf16[128,256]{1,0:T(8,128)(2,1)S(1)}, u32[]{:S(2)}, u32[]{:S(2)}) collective-permute-start(bf16[128,256]{1,0:T(8,128)(2,1)S(1)} %collective-permute-done.3.refs_3_), channel_id=1, source_target_pairs={{0,4},{2,6},{4,0},{6,2},{1,5},{3,7},{5,1},{7,3},{8,12},{10,14},{12... | collective-permute-start | bytes 196616 | tf_op jit(solution)/shard_map/ppermute | solution.py:206
  18.2 4.5 %shard_map.113 = (bf16[128,1024]{1,0:T(8,128)(2,1)S(1)}, f32[512,256]{1,0:T(8,128)S(1)}, bf16[512,256]{1,0:T(8,128)(2,1)S(1)}) custom-call(s32[8]{0:T(128)S(1)} %copy-done.2, bf16[2048,128]{1,0:T(8,128)(2,1)S(1)} %get-tuple-element.47.refs_1_, bf16[2048,128]{1,0:T(8,128)(2,1)S(1)} %get-tuple-element.48.refs_2_, ...), custom_call_target="tpu_custom_call" | custom-call | flops 5368709120 | bytes 2097152 | tf_op jit(solution)/shard_map/pallas_call | solution.py:175
  22.9 0.6 %collective-permute-start.12 = (bf16[512,256]{1,0:T(8,128)(2,1)S(1)}, bf16[512,256]{1,0:T(8,128)(2,1)S(1)}, u32[]{:S(2)}, u32[]{:S(2)}) collective-permute-start(bf16[512,256]{1,0:T(8,128)(2,1)S(1)} %pad_maximum_fusion), channel_id=1, source_target_pairs={{0,1},{1,0},{2,3},{3,2},{4,5},{5,4},{6,7},{7,6},{8,9},{9,8},{10,11... | collective-permute-start | bytes 786440 | tf_op jit(solution)/shard_map/ppermute | solution.py:202
  23.5 0.9 %collective-permute-done.11 = bf16[512,256]{1,0:T(8,128)(2,1)S(1)} collective-permute-done((bf16[512,256]{1,0:T(8,128)(2,1)S(1)}, bf16[512,256]{1,0:T(8,128)(2,1)S(1)}, u32[]{:S(2)}, u32[]{:S(2)}) %collective-permute-start.11) | collective-permute-done | bytes 262176 | tf_op jit(solution)/shard_map/ppermute | solution.py:202
  24.5 3.1 %collective-permute-start.13 = (bf16[128,256]{1,0:T(8,128)(2,1)S(1)}, bf16[128,256]{1,0:T(8,128)(2,1)S(1)}, u32[]{:S(2)}, u32[]{:S(2)}) collective-permute-start(bf16[128,256]{1,0:T(8,128)(2,1)S(1)} %get-tuple-element.54), channel_id=1, source_target_pairs={{0,6},{2,4},{4,2},{6,0},{1,7},{3,5},{5,3},{7,1},{8,14},{10,12},{12... | collective-permute-start | bytes 196616 | tf_op jit(solution)/shard_map/ppermute | solution.py:206
  27.6 1.4 %collective-permute-start.15 = (bf16[128,256]{1,0:T(8,128)(2,1)S(1)}, bf16[128,256]{1,0:T(8,128)(2,1)S(1)}, u32[]{:S(2)}, u32[]{:S(2)}) collective-permute-start(bf16[128,256]{1,0:T(8,128)(2,1)S(1)} %get-tuple-element.56), channel_id=1, source_target_pairs={{0,2},{2,0},{4,6},{6,4},{1,3},{3,1},{5,7},{7,5},{8,10},{10,8},{12,... | collective-permute-start | bytes 196616 | tf_op jit(solution)/shard_map/ppermute | solution.py:206
  29.0 4.5 %shard_map.114 = (bf16[128,1024]{1,0:T(8,128)(2,1)S(1)}, f32[512,256]{1,0:T(8,128)S(1)}, bf16[512,256]{1,0:T(8,128)(2,1)S(1)}) custom-call(s32[8]{0:T(128)S(1)} %copy-done.2, bf16[2048,128]{1,0:T(8,128)(2,1)S(1)} %get-tuple-element.47.refs_1_, bf16[2048,128]{1,0:T(8,128)(2,1)S(1)} %get-tuple-element.48.refs_2_, ...), custom_call_target="tpu_custom_call" | custom-call | flops 5368709120 | bytes 2097152 | tf_op jit(solution)/shard_map/pallas_call | solution.py:175
  33.8 1.9 %collective-permute-start.20 = (f32[128,256]{1,0:T(8,128)S(1)}, f32[128,256]{1,0:T(8,128)S(1)}, u32[]{:S(2)}, u32[]{:S(2)}) collective-permute-start(f32[128,256]{1,0:T(8,128)S(1)} %fusion.2), channel_id=1, source_target_pairs={{0,8},{8,0},{16,24},{24,16},{1,9},{9,1},{17,25},{25,17},{2,10},{10... | collective-permute-start | bytes 393224 | tf_op jit(solution)/shard_map/ppermute | solution.py:215
  35.8 2.5 %collective-permute-start.17 = (bf16[128,256]{1,0:T(8,128)(2,1)S(1)}, bf16[128,256]{1,0:T(8,128)(2,1)S(1)}, u32[]{:S(2)}, u32[]{:S(2)}) collective-permute-start(bf16[128,256]{1,0:T(8,128)(2,1)S(1)} %get-tuple-element.65), channel_id=1, source_target_pairs={{0,6},{2,4},{4,2},{6,0},{1,7},{3,5},{5,3},{7,1},{8,14},{10,12},{12... | collective-permute-start | bytes 196616 | tf_op jit(solution)/shard_map/ppermute | solution.py:206
  38.3 1.9 %collective-permute-start.19 = (bf16[128,256]{1,0:T(8,128)(2,1)S(1)}, bf16[128,256]{1,0:T(8,128)(2,1)S(1)}, u32[]{:S(2)}, u32[]{:S(2)}) collective-permute-start(bf16[128,256]{1,0:T(8,128)(2,1)S(1)} %get-tuple-element.67), channel_id=1, source_target_pairs={{0,2},{2,0},{4,6},{6,4},{1,3},{3,1},{5,7},{7,5},{8,10},{10,8},{12,... | collective-permute-start | bytes 196616 | tf_op jit(solution)/shard_map/ppermute | solution.py:206
  40.3 2.4 %collective-permute-start.21 = (bf16[128,256]{1,0:T(8,128)(2,1)S(1)}, bf16[128,256]{1,0:T(8,128)(2,1)S(1)}, u32[]{:S(2)}, u32[]{:S(2)}) collective-permute-start(bf16[128,256]{1,0:T(8,128)(2,1)S(1)} %convert_element_type.41), channel_id=1, source_target_pairs={{8,16},{16,8},{24,0},{0,24},{9,17},{17,9},{25,1},{1,25},{10,18},{1... | collective-permute-start | bytes 196616 | tf_op jit(solution)/shard_map/ppermute | solution.py:215
  42.6 0.8 %maximum_bitcast_fusion = bf16[2,1,128,1024]{3,2,1,0:T(8,128)(2,1)} fusion(bf16[1,128,1024]{2,1,0:T(8,128)(2,1)S(1)} %bitcast.27, bf16[1,128,1024]{2,1,0:T(8,128)(2,1)S(1)} %bitcast.26), kind=kLoop, calls=%fused_computation | loop fusion | flops 262144 | bytes 1048576
  43.5 1.2 %collective-permute-done.18 = bf16[128,256]{1,0:T(8,128)(2,1)S(1)} collective-permute-done((bf16[128,256]{1,0:T(8,128)(2,1)S(1)}, bf16[128,256]{1,0:T(8,128)(2,1)S(1)}, u32[]{:S(2)}, u32[]{:S(2)}) %collective-permute-start.18) | collective-permute-done | bytes 65568 | tf_op jit(solution)/shard_map/ppermute | solution.py:206
  44.7 0.7 %collective-permute-done.21 = bf16[128,256]{1,0:T(8,128)(2,1)S(1)} collective-permute-done((bf16[128,256]{1,0:T(8,128)(2,1)S(1)}, bf16[128,256]{1,0:T(8,128)(2,1)S(1)}, u32[]{:S(2)}, u32[]{:S(2)}) %collective-permute-start.21) | collective-permute-done | bytes 65568 | tf_op jit(solution)/shard_map/ppermute | solution.py:215
  45.5 0.7 %maximum_bitcast_fusion.1 = (f32[2,1,128,128]{3,2,1,0:T(8,128)}, f32[2,1,128,128]{3,2,1,0:T(8,128)}) fusion(f32[1,128,128]{2,1,0:T(8,128)S(1)} %get-tuple-element.85, f32[1,128,128]{2,1,0:T(8,128)S(1)} %get-tuple-element.83, f32[1,128,128]{2,1,0:T(8,128)S(1)} %get-tuple-element.84, f32[1,128,128]{2,1,0:T(8,128)S(1)} %get-tuple-element.82), kind=kLoop, calls=%fused_computation.8 | loop fusion | flops 65536 | bytes 524288
  (47 shorter events, 1.0 us)
Async XLA Ops:
  1.5 10.6 %collective-permute-start = (bf16[128,256]{1,0:T(8,128)(2,1)S(1)}, bf16[128,256]{1,0:T(8,128)(2,1)S(1)}, u32[]{:S(2)}, u32[]{:S(2)}) collective-permute-start(bf16[128,256]{1,0:T(8,128)(2,1)S(1)} %get-tuple-element.87.refs_3_), channel_id=1, source_target_pairs={{0,2},{2,0},{4,6},{6,4},{1,3},{3,1},{5,7},{7,5},{8,10},{10,8},{12,... | collective-permute-start | bytes 196616 | tf_op jit(solution)/shard_map/ppermute | solution.py:206
  4.6 7.5 %collective-permute-start.1 = (bf16[128,256]{1,0:T(8,128)(2,1)S(1)}, bf16[128,256]{1,0:T(8,128)(2,1)S(1)}, u32[]{:S(2)}, u32[]{:S(2)}) collective-permute-start(bf16[128,256]{1,0:T(8,128)(2,1)S(1)} %get-tuple-element.87.refs_3_), channel_id=1, source_target_pairs={{0,4},{2,6},{4,0},{6,2},{1,5},{3,7},{5,1},{7,3},{8,12},{10,14},{12... | collective-permute-start | bytes 196616 | tf_op jit(solution)/shard_map/ppermute | solution.py:206
  7.2 6.1 %collective-permute-start.2 = (bf16[128,256]{1,0:T(8,128)(2,1)S(1)}, bf16[128,256]{1,0:T(8,128)(2,1)S(1)}, u32[]{:S(2)}, u32[]{:S(2)}) collective-permute-start(bf16[128,256]{1,0:T(8,128)(2,1)S(1)} %get-tuple-element.87.refs_3_), channel_id=1, source_target_pairs={{0,6},{2,4},{4,2},{6,0},{1,7},{3,5},{5,3},{7,1},{8,14},{10,12},{12... | collective-permute-start | bytes 196616 | tf_op jit(solution)/shard_map/ppermute | solution.py:206
  7.2 6.1 %collective-permute-start.3 = (bf16[128,256]{1,0:T(8,128)(2,1)S(1)}, bf16[128,256]{1,0:T(8,128)(2,1)S(1)}, u32[]{:S(2)}, u32[]{:S(2)}) collective-permute-start(bf16[128,256]{1,0:T(8,128)(2,1)S(1)} %get-tuple-element.86), channel_id=1, source_target_pairs={{0,24},{8,0},{16,8},{24,16},{1,25},{9,1},{17,9},{25,17},{2,26},{10... | collective-permute-start | bytes 196616 | tf_op jit(solution)/shard_map/ppermute | solution.py:242
  9.8 7.0 %collective-permute-start.4 = (bf16[128,256]{1,0:T(8,128)(2,1)S(1)}, bf16[128,256]{1,0:T(8,128)(2,1)S(1)}, u32[]{:S(2)}, u32[]{:S(2)}) collective-permute-start(bf16[128,256]{1,0:T(8,128)(2,1)S(1)} %get-tuple-element.87.refs_3_), channel_id=1, source_target_pairs={{0,1},{1,0},{2,3},{3,2},{4,5},{5,4},{6,7},{7,6},{8,9},{9,8},{10,11... | collective-permute-start | bytes 196616 | tf_op jit(solution)/shard_map/ppermute | solution.py:202
  13.2 3.6 %collective-permute-start.5 = (bf16[128,256]{1,0:T(8,128)(2,1)S(1)}, bf16[128,256]{1,0:T(8,128)(2,1)S(1)}, u32[]{:S(2)}, u32[]{:S(2)}) collective-permute-start(bf16[128,256]{1,0:T(8,128)(2,1)S(1)} %collective-permute-done.refs_4_), channel_id=1, source_target_pairs={{0,1},{1,0},{2,3},{3,2},{4,5},{5,4},{6,7},{7,6},{8,9},{9,8},{10,11... | collective-permute-start | bytes 196616 | tf_op jit(solution)/shard_map/ppermute | solution.py:202
  13.2 5.0 %collective-permute-start.6 = (bf16[128,256]{1,0:T(8,128)(2,1)S(1)}, bf16[128,256]{1,0:T(8,128)(2,1)S(1)}, u32[]{:S(2)}, u32[]{:S(2)}) collective-permute-start(bf16[128,256]{1,0:T(8,128)(2,1)S(1)} %collective-permute-done.1.refs_5_), channel_id=1, source_target_pairs={{0,1},{1,0},{2,3},{3,2},{4,5},{5,4},{6,7},{7,6},{8,9},{9,8},{10,11... | collective-permute-start | bytes 196616 | tf_op jit(solution)/shard_map/ppermute | solution.py:202
  13.7 4.5 %collective-permute-start.7 = (bf16[128,256]{1,0:T(8,128)(2,1)S(1)}, bf16[128,256]{1,0:T(8,128)(2,1)S(1)}, u32[]{:S(2)}, u32[]{:S(2)}) collective-permute-start(bf16[128,256]{1,0:T(8,128)(2,1)S(1)} %collective-permute-done.2.refs_6_), channel_id=1, source_target_pairs={{0,1},{1,0},{2,3},{3,2},{4,5},{5,4},{6,7},{7,6},{8,9},{9,8},{10,11... | collective-permute-start | bytes 196616 | tf_op jit(solution)/shard_map/ppermute | solution.py:202
  13.8 8.9 %collective-permute-start.10 = (bf16[128,256]{1,0:T(8,128)(2,1)S(1)}, bf16[128,256]{1,0:T(8,128)(2,1)S(1)}, u32[]{:S(2)}, u32[]{:S(2)}) collective-permute-start(bf16[128,256]{1,0:T(8,128)(2,1)S(1)} %collective-permute-done.3.refs_3_), channel_id=1, source_target_pairs={{0,6},{2,4},{4,2},{6,0},{1,7},{3,5},{5,3},{7,1},{8,14},{10,12},{12... | collective-permute-start | bytes 196616 | tf_op jit(solution)/shard_map/ppermute | solution.py:206
  16.8 5.9 %collective-permute-start.8 = (bf16[128,256]{1,0:T(8,128)(2,1)S(1)}, bf16[128,256]{1,0:T(8,128)(2,1)S(1)}, u32[]{:S(2)}, u32[]{:S(2)}) collective-permute-start(bf16[128,256]{1,0:T(8,128)(2,1)S(1)} %collective-permute-done.3.refs_3_), channel_id=1, source_target_pairs={{0,2},{2,0},{4,6},{6,4},{1,3},{3,1},{5,7},{7,5},{8,10},{10,8},{12,... | collective-permute-start | bytes 196616 | tf_op jit(solution)/shard_map/ppermute | solution.py:206
  16.9 6.0 %collective-permute-start.9 = (bf16[128,256]{1,0:T(8,128)(2,1)S(1)}, bf16[128,256]{1,0:T(8,128)(2,1)S(1)}, u32[]{:S(2)}, u32[]{:S(2)}) collective-permute-start(bf16[128,256]{1,0:T(8,128)(2,1)S(1)} %collective-permute-done.3.refs_3_), channel_id=1, source_target_pairs={{0,4},{2,6},{4,0},{6,2},{1,5},{3,7},{5,1},{7,3},{8,12},{10,14},{12... | collective-permute-start | bytes 196616 | tf_op jit(solution)/shard_map/ppermute | solution.py:206
  22.9 1.5 %collective-permute-start.11 = (bf16[512,256]{1,0:T(8,128)(2,1)S(1)}, bf16[512,256]{1,0:T(8,128)(2,1)S(1)}, u32[]{:S(2)}, u32[]{:S(2)}) collective-permute-start(bf16[512,256]{1,0:T(8,128)(2,1)S(1)} %get-tuple-element.46), channel_id=1, source_target_pairs={{0,1},{1,0},{2,3},{3,2},{4,5},{5,4},{6,7},{7,6},{8,9},{9,8},{10,11... | collective-permute-start | bytes 786440 | tf_op jit(solution)/shard_map/ppermute | solution.py:202
  22.9 6.1 %collective-permute-start.12 = (bf16[512,256]{1,0:T(8,128)(2,1)S(1)}, bf16[512,256]{1,0:T(8,128)(2,1)S(1)}, u32[]{:S(2)}, u32[]{:S(2)}) collective-permute-start(bf16[512,256]{1,0:T(8,128)(2,1)S(1)} %pad_maximum_fusion), channel_id=1, source_target_pairs={{0,1},{1,0},{2,3},{3,2},{4,5},{5,4},{6,7},{7,6},{8,9},{9,8},{10,11... | collective-permute-start | bytes 786440 | tf_op jit(solution)/shard_map/ppermute | solution.py:202
  24.5 9.2 %copy-start.3 = (f32[1,128,128]{2,1,0:T(8,128)S(1)}, f32[1,128,128]{2,1,0:T(8,128)}, u32[]{:S(2)}) copy-start(f32[1,128,128]{2,1,0:T(8,128)} %param.16) | copy-start | bytes 196612
  24.5 9.2 %copy-start.4 = (f32[1,128,128]{2,1,0:T(8,128)S(1)}, f32[1,128,128]{2,1,0:T(8,128)}, u32[]{:S(2)}) copy-start(f32[1,128,128]{2,1,0:T(8,128)} %param.15) | copy-start | bytes 196612
  24.5 9.0 %collective-permute-start.13 = (bf16[128,256]{1,0:T(8,128)(2,1)S(1)}, bf16[128,256]{1,0:T(8,128)(2,1)S(1)}, u32[]{:S(2)}, u32[]{:S(2)}) collective-permute-start(bf16[128,256]{1,0:T(8,128)(2,1)S(1)} %get-tuple-element.54), channel_id=1, source_target_pairs={{0,6},{2,4},{4,2},{6,0},{1,7},{3,5},{5,3},{7,1},{8,14},{10,12},{12... | collective-permute-start | bytes 196616 | tf_op jit(solution)/shard_map/ppermute | solution.py:206
  27.6 6.1 %collective-permute-start.14 = (bf16[128,256]{1,0:T(8,128)(2,1)S(1)}, bf16[128,256]{1,0:T(8,128)(2,1)S(1)}, u32[]{:S(2)}, u32[]{:S(2)}) collective-permute-start(bf16[128,256]{1,0:T(8,128)(2,1)S(1)} %get-tuple-element.55), channel_id=1, source_target_pairs={{0,4},{2,6},{4,0},{6,2},{1,5},{3,7},{5,1},{7,3},{8,12},{10,14},{12... | collective-permute-start | bytes 196616 | tf_op jit(solution)/shard_map/ppermute | solution.py:206
  27.6 6.1 %collective-permute-start.15 = (bf16[128,256]{1,0:T(8,128)(2,1)S(1)}, bf16[128,256]{1,0:T(8,128)(2,1)S(1)}, u32[]{:S(2)}, u32[]{:S(2)}) collective-permute-start(bf16[128,256]{1,0:T(8,128)(2,1)S(1)} %get-tuple-element.56), channel_id=1, source_target_pairs={{0,2},{2,0},{4,6},{6,4},{1,3},{3,1},{5,7},{7,5},{8,10},{10,8},{12,... | collective-permute-start | bytes 196616 | tf_op jit(solution)/shard_map/ppermute | solution.py:206
  33.7 2.0 %collective-permute-start.16 = (bf16[512,256]{1,0:T(8,128)(2,1)S(1)}, bf16[512,256]{1,0:T(8,128)(2,1)S(1)}, u32[]{:S(2)}, u32[]{:S(2)}) collective-permute-start(bf16[512,256]{1,0:T(8,128)(2,1)S(1)} %get-tuple-element.58), channel_id=1, source_target_pairs={{0,1},{1,0},{2,3},{3,2},{4,5},{5,4},{6,7},{7,6},{8,9},{9,8},{10,11... | collective-permute-start | bytes 786440 | tf_op jit(solution)/shard_map/ppermute | solution.py:202
  33.8 9.6 %collective-permute-start.20 = (f32[128,256]{1,0:T(8,128)S(1)}, f32[128,256]{1,0:T(8,128)S(1)}, u32[]{:S(2)}, u32[]{:S(2)}) collective-permute-start(f32[128,256]{1,0:T(8,128)S(1)} %fusion.2), channel_id=1, source_target_pairs={{0,8},{8,0},{16,24},{24,16},{1,9},{9,1},{17,25},{25,17},{2,10},{10... | collective-permute-start | bytes 393224 | tf_op jit(solution)/shard_map/ppermute | solution.py:215
  35.8 7.7 %collective-permute-start.17 = (bf16[128,256]{1,0:T(8,128)(2,1)S(1)}, bf16[128,256]{1,0:T(8,128)(2,1)S(1)}, u32[]{:S(2)}, u32[]{:S(2)}) collective-permute-start(bf16[128,256]{1,0:T(8,128)(2,1)S(1)} %get-tuple-element.65), channel_id=1, source_target_pairs={{0,6},{2,4},{4,2},{6,0},{1,7},{3,5},{5,3},{7,1},{8,14},{10,12},{12... | collective-permute-start | bytes 196616 | tf_op jit(solution)/shard_map/ppermute | solution.py:206
  38.3 6.4 %collective-permute-start.18 = (bf16[128,256]{1,0:T(8,128)(2,1)S(1)}, bf16[128,256]{1,0:T(8,128)(2,1)S(1)}, u32[]{:S(2)}, u32[]{:S(2)}) collective-permute-start(bf16[128,256]{1,0:T(8,128)(2,1)S(1)} %get-tuple-element.66), channel_id=1, source_target_pairs={{0,4},{2,6},{4,0},{6,2},{1,5},{3,7},{5,1},{7,3},{8,12},{10,14},{12... | collective-permute-start | bytes 196616 | tf_op jit(solution)/shard_map/ppermute | solution.py:206
  38.3 6.4 %collective-permute-start.19 = (bf16[128,256]{1,0:T(8,128)(2,1)S(1)}, bf16[128,256]{1,0:T(8,128)(2,1)S(1)}, u32[]{:S(2)}, u32[]{:S(2)}) collective-permute-start(bf16[128,256]{1,0:T(8,128)(2,1)S(1)} %get-tuple-element.67), channel_id=1, source_target_pairs={{0,2},{2,0},{4,6},{6,4},{1,3},{3,1},{5,7},{7,5},{8,10},{10,8},{12,... | collective-permute-start | bytes 196616 | tf_op jit(solution)/shard_map/ppermute | solution.py:206
  40.3 5.2 %collective-permute-start.21 = (bf16[128,256]{1,0:T(8,128)(2,1)S(1)}, bf16[128,256]{1,0:T(8,128)(2,1)S(1)}, u32[]{:S(2)}, u32[]{:S(2)}) collective-permute-start(bf16[128,256]{1,0:T(8,128)(2,1)S(1)} %convert_element_type.41), channel_id=1, source_target_pairs={{8,16},{16,8},{24,0},{0,24},{9,17},{17,9},{25,1},{1,25},{10,18},{1... | collective-permute-start | bytes 196616 | tf_op jit(solution)/shard_map/ppermute | solution.py:215
  (3 other events, 7.1 us)

commit v6 on v5

--- a/solution.py
+++ b/solution.py
@@ -8,10 +8,15 @@
 from jax.sharding import PartitionSpec as P
 
 MASK_FILL = -1e30
+STRIP = 32
 CONTRACT_LAST = (((1,), (1,)), ((), ()))
 
 
-def stack_kernel(q_ref, g_ref, q_out_ref, g_out_ref):
+def block_places(chips):
+    return [(k, same) for same in (True, False) for k in range(chips)]
+
+
+def stack_kernel(order_ref, q_ref, g_ref, q_out_ref, g_out_ref, cap_ref):
     ticks, _, local_rows, model = q_ref.shape
     head_dim = q_out_ref.shape[1]
     heads = model // head_dim
@@ -21,27 +26,36 @@
             cols = pl.ds(head * head_dim, head_dim)
             q_out_ref[rows, :] = q_ref[tick, 0, :, cols]
             g_out_ref[rows, :] = g_ref[tick, 0, :, cols]
-
-
-def stacked_heads(queries, out_grad, head_dim):
+    chip, core = lax.axis_index("z"), lax.axis_index("core")
+    own_group = order_ref[2 * chip + core]
+    for slot, (k, same) in enumerate(block_places(cap_ref.shape[0] // 16)):
+        source = 2 * jnp.bitwise_xor(chip, k) + (core if same else 1 - core)
+        cap = jnp.where(order_ref[source] <= own_group, -MASK_FILL, MASK_FILL)
+        cap_ref[slot * 8 : (slot + 1) * 8, :] = jnp.full((8, cap_ref.shape[1]), cap, jnp.float32)
+
+
+def stacked_heads(group_order, queries, out_grad, head_dim):
     rows = queries.size // head_dim
     in_vmem = pl.BlockSpec(memory_space=pltpu.VMEM)
+    stack = jax.ShapeDtypeStruct((rows, head_dim), queries.dtype)
+    caps = jax.ShapeDtypeStruct((8 * group_order.size, 2 * queries.shape[2]), jnp.float32)
     return pl.pallas_call(
         stack_kernel,
-        out_shape=(jax.ShapeDtypeStruct((rows, head_dim), queries.dtype),) * 2,
-        in_specs=[in_vmem, in_vmem],
-        out_specs=(in_vmem, in_vmem),
+        out_shape=(stack, stack, caps),
+        in_specs=[pl.BlockSpec(memory_space=pltpu.SMEM), in_vmem, in_vmem],
+        out_specs=(in_vmem, in_vmem, in_vmem),
         compiler_params=pltpu.CompilerParams(vmem_limit_bytes=8 * 2**20),
         cost_estimate=pl.CostEstimate(
             flops=queries.size, bytes_accessed=8 * queries.size, transcendentals=0
         ),
-    )(queries, out_grad)
+    )(group_order, queries, out_grad)
 
 
 def tick_kernel(tick, arrays, *refs):
-    order_ref, q_ref, g_ref = refs[:3]
+    q_ref, g_ref, cap_ref = refs[:3]
     outs = refs[3 + arrays :]
-    dq_ref, near_out_ref, far_out_ref, s_ref, e_ref, dp_ref, ds_ref, acc_ref, kt_ref = outs
+    dq_ref, near_out_ref, far_out_ref, s_ref, e_ref, dp_ref, *more = outs
+    p_ref, ds_ref, acc_ref, kt_ref = more
     local_rows, model = dq_ref.shape
     head_dim = near_out_ref.shape[1] // 2
     half_rows = near_out_ref.shape[0]
@@ -58,15 +72,6 @@
     scale = 1.0 / math.sqrt(head_dim)
     exp_scale = scale * math.log2(math.e)
 
-    core = lax.axis_index("core")
-    chip = lax.axis_index("z")
-    own_group = order_ref[2 * chip + core]
-
-    def allowed(slot):
-        source = jnp.bitwise_xor(chip, slot % chips)
-        parity = core if slot < chips else 1 - core
-        return order_ref[2 * source + parity] < own_group
-
     for slot in range(blocks):
         kt_ref[:, slot * local_rows : (slot + 1) * local_rows] = kv_refs[slot][:, :head_dim].T
 
@@ -85,22 +90,40 @@
                 preferred_element_type=jnp.float32,
             )
 
+    def strips(slot):
+        first = slot * local_rows
+        return [slice(row, row + STRIP) for row in range(first, first + local_rows, STRIP)]
+
+    def folded(strip, combine):
+        return combine(strip.reshape(STRIP // 8, 8, width), axis=0)
+
     def exponentials(pair, slot):
-        scores = s_ref[pair, rows_of(slot)]
-        if slot == 0:
-            key_row = lax.broadcasted_iota(jnp.int32, (local_rows, width), 0)
-            query_row = lax.rem(
-                lax.broadcasted_iota(jnp.int32, (local_rows, width), 1), local_rows
-            )
-            scores = jnp.where(key_row <= query_row, scores, MASK_FILL)
-        peak = jnp.max(scores, axis=0, keepdims=True) * exp_scale
-        expo = jnp.exp2(scores * exp_scale - peak)
-        e_ref[pair, rows_of(slot)] = expo
-        total = jnp.sum(expo, axis=0, keepdims=True)
-        weighted = jnp.sum(expo * dp_ref[pair, rows_of(slot)], axis=0, keepdims=True)
+        top = jnp.full((8, width), MASK_FILL, jnp.float32)
+        for rows in strips(slot):
+            scores = s_ref[pair, rows]
+            if slot == 0:
+                key_row = rows.start + lax.broadcasted_iota(jnp.int32, (STRIP, width), 0)
+                query_row = lax.rem(
+                    lax.broadcasted_iota(jnp.int32, (STRIP, width), 1), local_rows
+                )
+                scores = jnp.where(key_row <= query_row, scores, MASK_FILL)
+                s_ref[pair, rows] = scores
+            top = jnp.maximum(top, folded(scores, jnp.max))
+        peak = jnp.max(top, axis=0, keepdims=True) * exp_scale
+        total = jnp.zeros((8, width), jnp.float32)
+        weighted = jnp.zeros((8, width), jnp.float32)
+        for rows in strips(slot):
+            expo = jnp.exp2(s_ref[pair, rows] * exp_scale - peak)
+            e_ref[pair, rows] = expo
+            total += folded(expo, jnp.sum)
+            weighted += folded(expo * dp_ref[pair, rows], jnp.sum)
         if slot > 0:
-            peak = jnp.where(allowed(slot), peak, MASK_FILL)
-        return peak, total, weighted
+            peak = jnp.minimum(peak, cap_ref[8 * slot : 8 * slot + 1, :])
+        return (
+            peak,
+            jnp.sum(total, axis=0, keepdims=True),
+            jnp.sum(weighted, axis=0, keepdims=True),
+        )
 
     def combined(parts):
         biggest = parts[0][0]
@@ -113,13 +136,16 @@
         return [factor * inverse for factor in factors], weighted * inverse
 
     def gradients(pair, slot, factors, delta):
+        for rows in strips(slot):
+            probs = e_ref[pair, rows] * factors[slot]
+            p_ref[pair, rows] = probs.astype(jnp.bfloat16)
+            ds_ref[pair, rows] = (probs * (dp_ref[pair, rows] - delta)).astype(jnp.bfloat16)
         rows = rows_of(slot)
-        probs = e_ref[pair, rows] * factors[slot]
-        score_grad = (probs * (dp_ref[pair, rows] - delta)).astype(jnp.bfloat16)
-        ds_ref[pair, rows] = score_grad
-        key_terms = jnp.dot(score_grad, pair_of(q_ref, pair), preferred_element_type=jnp.float32)
+        key_terms = jnp.dot(
+            ds_ref[pair, rows], pair_of(q_ref, pair), preferred_element_type=jnp.float32
+        )
         value_terms = jnp.dot(
-            probs.astype(jnp.bfloat16), pair_of(g_ref, pair), preferred_element_type=jnp.float32
+            p_ref[pair, rows], pair_of(g_ref, pair), preferred_element_type=jnp.float32
         )
         if pair > 0:
             key_terms += acc_ref[rows, :head_dim]
@@ -160,7 +186,7 @@
     query_grad(pairs - 1)
 
 
-def attend_back(tick, group_order, queries, q_stack, g_stack, kv_arrays):
+def attend_back(tick, queries, stacks, kv_arrays):
     local_rows, model = queries.shape[2:]
     width = kv_arrays[0].shape[1]
     key_rows = sum(array.shape[0] for array in kv_arrays)
@@ -179,12 +205,13 @@
             jax.ShapeDtypeStruct((key_rows // 2, width), jnp.float32),
             jax.ShapeDtypeStruct((key_rows // 2, width), jnp.bfloat16),
         ),
-        in_specs=[pl.BlockSpec(memory_space=pltpu.SMEM), *[in_vmem] * (2 + len(kv_arrays))],
+        in_specs=[in_vmem] * (3 + len(kv_arrays)),
         out_specs=(in_vmem, in_vmem, in_vmem),
         scratch_shapes=[
             pltpu.VMEM(tile, jnp.float32),
             pltpu.VMEM(tile, jnp.float32),
             pltpu.VMEM(tile, jnp.float32),
+            pltpu.VMEM(tile, jnp.bfloat16),
             pltpu.VMEM(tile, jnp.bfloat16),
             pltpu.VMEM((key_rows, width), jnp.float32),
             pltpu.VMEM((head_dim, key_rows), jnp.bfloat16),
@@ -195,7 +222,7 @@
             bytes_accessed=6 * local_rows * model + 5 * key_rows * width,
             transcendentals=model // head_dim * key_rows * local_rows,
         ),
-    )(group_order, q_stack, g_stack, *kv_arrays)
+    )(*stacks, *kv_arrays)
 
 
 def other_core(block):
@@ -242,13 +269,11 @@
     next_pair = lax.ppermute(
         leaving_pair, "section", [(i, (i - 1) % sections) for i in range(sections)]
     )
-    stacks = stacked_heads(queries, out_grad, head_dim)
+    stacks = stacked_heads(group_order, queries, out_grad, head_dim)
     near, next_pair, stacks = lax.optimization_barrier((near, next_pair, stacks))
     far = [own_far] + [other_core(block) for block in near]
     next_near = [across_chips(next_pair, k) for k in partners][::-1]
-    first_query, near_terms, far_terms = attend_back(
-        0, group_order, queries, *stacks, [own_pair, *near, *far]
-    )
+    first_query, near_terms, far_terms = attend_back(0, queries, stacks, [own_pair, *near, *far])
     far_terms, next_near = lax.optimization_barrier((far_terms, [next_pair, *next_near]))
     next_kv = [*next_near, other_core(jnp.concatenate(next_near, axis=0))]
 
@@ -267,7 +292,7 @@
     first_acc = jnp.concatenate([key_grads_in[0], value_grads_in[0]], axis=1) + reduced(
         own_sum, leaving
     )
-    second_query, near_terms, far_terms = attend_back(1, group_order, queries, *stacks, next_kv)
+    second_query, near_terms, far_terms = attend_back(1, queries, stacks, next_kv)
     first_acc, far_terms = lax.optimization_barrier((first_acc, far_terms))
     early_acc = section_swap(first_acc, 0)
     own_sum, leaving = chip_sums(near_terms, far_terms)

time: 46.5 us -> 46.7 us (level)
  waiting for transfers between devices: 4.31 us -> 6.48 us
  starting transfers between devices: 27.1 us -> 25.9 us
  Pallas kernels: 9.21 us -> 8.35 us
    ppermute x12, waiting for transfers between devices: 2.6 us -> 4.34 us  [across_chips(): lax.ppermute(block, 'z', [(chip, chip ^ k) for chip in range(lax.axis_siz...]
    pallas_call x2, Pallas kernels: 9.03 us -> 7.61 us  [attend_back(): pl.pallas_call(kernel, out_shape=(jax.ShapeDtypeStruct((local_rows, model...]
    ppermute x2, starting transfers between devices: 4.21 us -> 3.1 us  [section_swap(): return lax.ppermute(block, 'section', route)]
    pallas_call x1, Pallas kernels: 0.18 us -> 0.74 us  [stacked_heads(): pl.pallas_call(stack_kernel, out_shape=(stack, stack, caps), in_specs=[pl...]
  transfers between devices with their start and end apart: 22 -> 22, of which waited for: 6 -> 8; matrix products, arithmetic and copies ran while one was open for 2% -> 2% of each run, Pallas kernels for 20% -> 18%
where the time goes in v6:
time: 46.7 us; the launch traced here: 46.4 us
  starting transfers between devices  25.9 us (55%)
  Pallas kernels  8.35 us (18%)
  waiting for transfers between devices  6.48 us (14%)
  other arithmetic  2.64 us (6%)
  local copies, waits for them, and re-layouts  2.16 us (5%)
  between operations  0.83 us (2%)
    ppermute x12, starting transfers between devices, across_chips(): lax.ppermute(block, 'z', [(chip, chip ^ k) for chip in range(lax.axis_siz...  19 us
    pallas_call x2, Pallas kernels, attend_back(): pl.pallas_call(kernel, out_shape=(jax.ShapeDtypeStruct((local_rows, model...  7.61 us
    ppermute x12, waiting for transfers between devices, across_chips(): lax.ppermute(block, 'z', [(chip, chip ^ k) for chip in range(lax.axis_siz...  4.34 us
    ppermute x2, starting transfers between devices, section_swap(): return lax.ppermute(block, 'section', route)  3.1 us
    ppermute x1, starting transfers between devices, body(): lax.ppermute(leaving_pair, 'section', [(i, (i - 1) % sections) for i in r...  2.67 us
    unnamed x10, local copies, waits for them, and re-layouts  2.1 us
    unnamed x2, other arithmetic  1.56 us
    ppermute x7, waiting for transfers between devices, other_core(): return lax.ppermute(block, 'core', [(0, 1), (1, 0)])  1.33 us
  transfers between devices with their start and end apart: 22, of which 8 were waited for; matrix products, arithmetic and copies ran while one was open for 2% of the time, Pallas kernels for 18%

profile of v6, /device:TPU:0, one launch (start us, length us, event | category | flops | bytes accessed | tf_op | source)
XLA Modules:
  0.0 46.4 jit_solution(10778590900264767115)
XLA Ops:
  0.6 0.8 %maximum_select_fusion = (bf16[128,256]{1,0:T(8,128)(2,1)S(1)}, bf16[128,256]{1,0:T(8,128)(2,1)S(1)}) fusion(bf16[128,128]{1,0:T(8,128)(2,1)} %param.14, bf16[128,128]{1,0:T(8,128)(2,1)} %param.13, pred[]{:T(512)S(6)} %eq.11, bf16[128,128]{1,0:T(8,128)(2,1)} %bitcast.30, bf16[128,128]{1,0:T(8,128)(2,1)} %bitcast.31), kind=kLoop, calls=%fused_computation.14 | loop fusion | flops 294912 | bytes 262145 | tf_op jit(solution)/shard_map/jit(_where)/select_n | solution.py:264
  1.5 3.1 %collective-permute-start = (bf16[128,256]{1,0:T(8,128)(2,1)S(1)}, bf16[128,256]{1,0:T(8,128)(2,1)S(1)}, u32[]{:S(2)}, u32[]{:S(2)}) collective-permute-start(bf16[128,256]{1,0:T(8,128)(2,1)S(1)} %get-tuple-element.93.refs_3_), channel_id=1, source_target_pairs={{0,2},{2,0},{4,6},{6,4},{1,3},{3,1},{5,7},{7,5},{8,10},{10,8},{12,... | collective-permute-start | bytes 196616 | tf_op jit(solution)/shard_map/ppermute | solution.py:233
  4.6 2.6 %collective-permute-start.1 = (bf16[128,256]{1,0:T(8,128)(2,1)S(1)}, bf16[128,256]{1,0:T(8,128)(2,1)S(1)}, u32[]{:S(2)}, u32[]{:S(2)}) collective-permute-start(bf16[128,256]{1,0:T(8,128)(2,1)S(1)} %get-tuple-element.93.refs_3_), channel_id=1, source_target_pairs={{0,4},{2,6},{4,0},{6,2},{1,5},{3,7},{5,1},{7,3},{8,12},{10,14},{12... | collective-permute-start | bytes 196616 | tf_op jit(solution)/shard_map/ppermute | solution.py:233
  7.2 2.7 %collective-permute-start.3 = (bf16[128,256]{1,0:T(8,128)(2,1)S(1)}, bf16[128,256]{1,0:T(8,128)(2,1)S(1)}, u32[]{:S(2)}, u32[]{:S(2)}) collective-permute-start(bf16[128,256]{1,0:T(8,128)(2,1)S(1)} %get-tuple-element.92), channel_id=1, source_target_pairs={{0,24},{8,0},{16,8},{24,16},{1,25},{9,1},{17,9},{25,17},{2,26},{10... | collective-permute-start | bytes 196616 | tf_op jit(solution)/shard_map/ppermute | solution.py:269
  9.8 1.0 %copy-done = bf16[2,1,128,1024]{3,2,1,0:T(8,128)(2,1)S(1)} copy-done((bf16[2,1,128,1024]{3,2,1,0:T(8,128)(2,1)S(1)}, bf16[2,1,128,1024]{3,2,1,0:T(8,128)(2,1)}, u32[]{:S(2)}) %copy-start) | copy-done | bytes 524312
  10.9 1.0 %copy-done.1 = bf16[2,1,128,1024]{3,2,1,0:T(8,128)(2,1)S(1)} copy-done((bf16[2,1,128,1024]{3,2,1,0:T(8,128)(2,1)S(1)}, bf16[2,1,128,1024]{3,2,1,0:T(8,128)(2,1)}, u32[]{:S(2)}) %copy-start.1) | copy-done | bytes 524312
  11.9 0.7 %shard_map.112 = (bf16[2048,128]{1,0:T(8,128)(2,1)S(1)}, bf16[2048,128]{1,0:T(8,128)(2,1)S(1)}, f32[64,256]{1,0:T(8,128)S(1)}) custom-call(s32[8]{0:T(128)S(1)} %copy-done.2, bf16[2,1,128,1024]{3,2,1,0:T(8,128)(2,1)S(1)} %copy-done, bf16[2,1,128,1024]{3,2,1,0:T(8,128)(2,1)S(1)} %copy-done.1), custom_call_target="tpu_custom_call" | custom-call | flops 262144 | bytes 2097152 | tf_op jit(solution)/shard_map/pallas_call | solution.py:42
  13.8 3.6 %collective-permute-start.10 = (bf16[128,256]{1,0:T(8,128)(2,1)S(1)}, bf16[128,256]{1,0:T(8,128)(2,1)S(1)}, u32[]{:S(2)}, u32[]{:S(2)}) collective-permute-start(bf16[128,256]{1,0:T(8,128)(2,1)S(1)} %collective-permute-done.3.refs_3_), channel_id=1, source_target_pairs={{0,6},{2,4},{4,2},{6,0},{1,7},{3,5},{5,3},{7,1},{8,14},{10,12},{12... | collective-permute-start | bytes 196616 | tf_op jit(solution)/shard_map/ppermute | solution.py:233
  17.4 0.8 %collective-permute-start.9 = (bf16[128,256]{1,0:T(8,128)(2,1)S(1)}, bf16[128,256]{1,0:T(8,128)(2,1)S(1)}, u32[]{:S(2)}, u32[]{:S(2)}) collective-permute-start(bf16[128,256]{1,0:T(8,128)(2,1)S(1)} %collective-permute-done.3.refs_3_), channel_id=1, source_target_pairs={{0,4},{2,6},{4,0},{6,2},{1,5},{3,7},{5,1},{7,3},{8,12},{10,14},{12... | collective-permute-start | bytes 196616 | tf_op jit(solution)/shard_map/ppermute | solution.py:233
  18.2 3.8 %shard_map.113 = (bf16[128,1024]{1,0:T(8,128)(2,1)S(1)}, f32[512,256]{1,0:T(8,128)S(1)}, bf16[512,256]{1,0:T(8,128)(2,1)S(1)}) custom-call(bf16[2048,128]{1,0:T(8,128)(2,1)S(1)} %get-tuple-element.52.refs_0_, bf16[2048,128]{1,0:T(8,128)(2,1)S(1)} %get-tuple-element.53.refs_1_, f32[64,256]{1,0:T(8,128)S(1)} %get-tuple-element.54.refs_2_, ...), custom_call_target="tpu_custom_call" | custom-call | flops 5368709120 | bytes 2097152 | tf_op jit(solution)/shard_map/pallas_call | solution.py:201
  22.3 1.0 %collective-permute-done.9.refs_5_ = bf16[128,256]{1,0:T(8,128)(2,1)S(1)} collective-permute-done((bf16[128,256]{1,0:T(8,128)(2,1)S(1)}, bf16[128,256]{1,0:T(8,128)(2,1)S(1)}, u32[]{:S(2)}, u32[]{:S(2)}) %collective-permute-start.9) | collective-permute-done | bytes 65568 | tf_op jit(solution)/shard_map/ppermute | solution.py:233
  23.9 0.9 %collective-permute-done.11 = bf16[512,256]{1,0:T(8,128)(2,1)S(1)} collective-permute-done((bf16[512,256]{1,0:T(8,128)(2,1)S(1)}, bf16[512,256]{1,0:T(8,128)(2,1)S(1)}, u32[]{:S(2)}, u32[]{:S(2)}) %collective-permute-start.11) | collective-permute-done | bytes 262176 | tf_op jit(solution)/shard_map/ppermute | solution.py:229
  24.9 2.5 %collective-permute-start.13 = (bf16[128,256]{1,0:T(8,128)(2,1)S(1)}, bf16[128,256]{1,0:T(8,128)(2,1)S(1)}, u32[]{:S(2)}, u32[]{:S(2)}) collective-permute-start(bf16[128,256]{1,0:T(8,128)(2,1)S(1)} %get-tuple-element.60), channel_id=1, source_target_pairs={{0,6},{2,4},{4,2},{6,0},{1,7},{3,5},{5,3},{7,1},{8,14},{10,12},{12... | collective-permute-start | bytes 196616 | tf_op jit(solution)/shard_map/ppermute | solution.py:233
  27.8 1.6 %collective-permute-start.15 = (bf16[128,256]{1,0:T(8,128)(2,1)S(1)}, bf16[128,256]{1,0:T(8,128)(2,1)S(1)}, u32[]{:S(2)}, u32[]{:S(2)}) collective-permute-start(bf16[128,256]{1,0:T(8,128)(2,1)S(1)} %get-tuple-element.62), channel_id=1, source_target_pairs={{0,2},{2,0},{4,6},{6,4},{1,3},{3,1},{5,7},{7,5},{8,10},{10,8},{12,... | collective-permute-start | bytes 196616 | tf_op jit(solution)/shard_map/ppermute | solution.py:233
  29.4 3.8 %shard_map.114 = (bf16[128,1024]{1,0:T(8,128)(2,1)S(1)}, f32[512,256]{1,0:T(8,128)S(1)}, bf16[512,256]{1,0:T(8,128)(2,1)S(1)}) custom-call(bf16[2048,128]{1,0:T(8,128)(2,1)S(1)} %get-tuple-element.52.refs_0_, bf16[2048,128]{1,0:T(8,128)(2,1)S(1)} %get-tuple-element.53.refs_1_, f32[64,256]{1,0:T(8,128)S(1)} %get-tuple-element.54.refs_2_, ...), custom_call_target="tpu_custom_call" | custom-call | flops 5368709120 | bytes 2097152 | tf_op jit(solution)/shard_map/pallas_call | solution.py:201
  33.2 1.0 %collective-permute-done.14 = bf16[128,256]{1,0:T(8,128)(2,1)S(1)} collective-permute-done((bf16[128,256]{1,0:T(8,128)(2,1)S(1)}, bf16[128,256]{1,0:T(8,128)(2,1)S(1)}, u32[]{:S(2)}, u32[]{:S(2)}) %collective-permute-start.14) | collective-permute-done | bytes 65568 | tf_op jit(solution)/shard_map/ppermute | solution.py:233
  34.4 1.1 %collective-permute-start.20 = (f32[128,256]{1,0:T(8,128)S(1)}, f32[128,256]{1,0:T(8,128)S(1)}, u32[]{:S(2)}, u32[]{:S(2)}) collective-permute-start(f32[128,256]{1,0:T(8,128)S(1)} %fusion.2), channel_id=1, source_target_pairs={{0,8},{8,0},{16,24},{24,16},{1,9},{9,1},{17,25},{25,17},{2,10},{10... | collective-permute-start | bytes 393224 | tf_op jit(solution)/shard_map/ppermute | solution.py:242
  36.0 2.1 %collective-permute-start.17 = (bf16[128,256]{1,0:T(8,128)(2,1)S(1)}, bf16[128,256]{1,0:T(8,128)(2,1)S(1)}, u32[]{:S(2)}, u32[]{:S(2)}) collective-permute-start(bf16[128,256]{1,0:T(8,128)(2,1)S(1)} %get-tuple-element.71), channel_id=1, source_target_pairs={{0,6},{2,4},{4,2},{6,0},{1,7},{3,5},{5,3},{7,1},{8,14},{10,12},{12... | collective-permute-start | bytes 196616 | tf_op jit(solution)/shard_map/ppermute | solution.py:233
  38.1 2.3 %collective-permute-start.19 = (bf16[128,256]{1,0:T(8,128)(2,1)S(1)}, bf16[128,256]{1,0:T(8,128)(2,1)S(1)}, u32[]{:S(2)}, u32[]{:S(2)}) collective-permute-start(bf16[128,256]{1,0:T(8,128)(2,1)S(1)} %get-tuple-element.73), channel_id=1, source_target_pairs={{0,2},{2,0},{4,6},{6,4},{1,3},{3,1},{5,7},{7,5},{8,10},{10,8},{12,... | collective-permute-start | bytes 196616 | tf_op jit(solution)/shard_map/ppermute | solution.py:233
  40.4 2.0 %collective-permute-start.21 = (bf16[128,256]{1,0:T(8,128)(2,1)S(1)}, bf16[128,256]{1,0:T(8,128)(2,1)S(1)}, u32[]{:S(2)}, u32[]{:S(2)}) collective-permute-start(bf16[128,256]{1,0:T(8,128)(2,1)S(1)} %convert_element_type.41), channel_id=1, source_target_pairs={{8,16},{16,8},{24,0},{0,24},{9,17},{17,9},{25,1},{1,25},{10,18},{1... | collective-permute-start | bytes 196616 | tf_op jit(solution)/shard_map/ppermute | solution.py:242
  42.4 0.8 %maximum_bitcast_fusion = bf16[2,1,128,1024]{3,2,1,0:T(8,128)(2,1)} fusion(bf16[1,128,1024]{2,1,0:T(8,128)(2,1)S(1)} %bitcast.27, bf16[1,128,1024]{2,1,0:T(8,128)(2,1)S(1)} %bitcast.26), kind=kLoop, calls=%fused_computation | loop fusion | flops 262144 | bytes 1048576
  43.3 1.5 %collective-permute-done.18 = bf16[128,256]{1,0:T(8,128)(2,1)S(1)} collective-permute-done((bf16[128,256]{1,0:T(8,128)(2,1)S(1)}, bf16[128,256]{1,0:T(8,128)(2,1)S(1)}, u32[]{:S(2)}, u32[]{:S(2)}) %collective-permute-start.18) | collective-permute-done | bytes 65568 | tf_op jit(solution)/shard_map/ppermute | solution.py:233
  44.8 0.8 %collective-permute-done.21 = bf16[128,256]{1,0:T(8,128)(2,1)S(1)} collective-permute-done((bf16[128,256]{1,0:T(8,128)(2,1)S(1)}, bf16[128,256]{1,0:T(8,128)(2,1)S(1)}, u32[]{:S(2)}, u32[]{:S(2)}) %collective-permute-start.21) | collective-permute-done | bytes 65568 | tf_op jit(solution)/shard_map/ppermute | solution.py:242
  45.7 0.7 %maximum_bitcast_fusion.1 = (f32[2,1,128,128]{3,2,1,0:T(8,128)}, f32[2,1,128,128]{3,2,1,0:T(8,128)}) fusion(f32[1,128,128]{2,1,0:T(8,128)S(1)} %get-tuple-element.91, f32[1,128,128]{2,1,0:T(8,128)S(1)} %get-tuple-element.89, f32[1,128,128]{2,1,0:T(8,128)S(1)} %get-tuple-element.90, f32[1,128,128]{2,1,0:T(8,128)S(1)} %get-tuple-element.88), kind=kLoop, calls=%fused_computation.8 | loop fusion | flops 65536 | bytes 524288
  (47 shorter events, 3.1 us)
Async XLA Ops:
  1.5 11.2 %collective-permute-start = (bf16[128,256]{1,0:T(8,128)(2,1)S(1)}, bf16[128,256]{1,0:T(8,128)(2,1)S(1)}, u32[]{:S(2)}, u32[]{:S(2)}) collective-permute-start(bf16[128,256]{1,0:T(8,128)(2,1)S(1)} %get-tuple-element.93.refs_3_), channel_id=1, source_target_pairs={{0,2},{2,0},{4,6},{6,4},{1,3},{3,1},{5,7},{7,5},{8,10},{10,8},{12,... | collective-permute-start | bytes 196616 | tf_op jit(solution)/shard_map/ppermute | solution.py:233
  4.6 8.1 %collective-permute-start.1 = (bf16[128,256]{1,0:T(8,128)(2,1)S(1)}, bf16[128,256]{1,0:T(8,128)(2,1)S(1)}, u32[]{:S(2)}, u32[]{:S(2)}) collective-permute-start(bf16[128,256]{1,0:T(8,128)(2,1)S(1)} %get-tuple-element.93.refs_3_), channel_id=1, source_target_pairs={{0,4},{2,6},{4,0},{6,2},{1,5},{3,7},{5,1},{7,3},{8,12},{10,14},{12... | collective-permute-start | bytes 196616 | tf_op jit(solution)/shard_map/ppermute | solution.py:233
  7.2 6.1 %collective-permute-start.2 = (bf16[128,256]{1,0:T(8,128)(2,1)S(1)}, bf16[128,256]{1,0:T(8,128)(2,1)S(1)}, u32[]{:S(2)}, u32[]{:S(2)}) collective-permute-start(bf16[128,256]{1,0:T(8,128)(2,1)S(1)} %get-tuple-element.93.refs_3_), channel_id=1, source_target_pairs={{0,6},{2,4},{4,2},{6,0},{1,7},{3,5},{5,3},{7,1},{8,14},{10,12},{12... | collective-permute-start | bytes 196616 | tf_op jit(solution)/shard_map/ppermute | solution.py:233
  7.2 6.1 %collective-permute-start.3 = (bf16[128,256]{1,0:T(8,128)(2,1)S(1)}, bf16[128,256]{1,0:T(8,128)(2,1)S(1)}, u32[]{:S(2)}, u32[]{:S(2)}) collective-permute-start(bf16[128,256]{1,0:T(8,128)(2,1)S(1)} %get-tuple-element.92), channel_id=1, source_target_pairs={{0,24},{8,0},{16,8},{24,16},{1,25},{9,1},{17,9},{25,17},{2,26},{10... | collective-permute-start | bytes 196616 | tf_op jit(solution)/shard_map/ppermute | solution.py:269
  9.8 7.6 %collective-permute-start.4 = (bf16[128,256]{1,0:T(8,128)(2,1)S(1)}, bf16[128,256]{1,0:T(8,128)(2,1)S(1)}, u32[]{:S(2)}, u32[]{:S(2)}) collective-permute-start(bf16[128,256]{1,0:T(8,128)(2,1)S(1)} %get-tuple-element.93.refs_3_), channel_id=1, source_target_pairs={{0,1},{1,0},{2,3},{3,2},{4,5},{5,4},{6,7},{7,6},{8,9},{9,8},{10,11... | collective-permute-start | bytes 196616 | tf_op jit(solution)/shard_map/ppermute | solution.py:229
  13.2 4.2 %collective-permute-start.5 = (bf16[128,256]{1,0:T(8,128)(2,1)S(1)}, bf16[128,256]{1,0:T(8,128)(2,1)S(1)}, u32[]{:S(2)}, u32[]{:S(2)}) collective-permute-start(bf16[128,256]{1,0:T(8,128)(2,1)S(1)} %collective-permute-done.refs_4_), channel_id=1, source_target_pairs={{0,1},{1,0},{2,3},{3,2},{4,5},{5,4},{6,7},{7,6},{8,9},{9,8},{10,11... | collective-permute-start | bytes 196616 | tf_op jit(solution)/shard_map/ppermute | solution.py:229
  13.3 4.9 %collective-permute-start.6 = (bf16[128,256]{1,0:T(8,128)(2,1)S(1)}, bf16[128,256]{1,0:T(8,128)(2,1)S(1)}, u32[]{:S(2)}, u32[]{:S(2)}) collective-permute-start(bf16[128,256]{1,0:T(8,128)(2,1)S(1)} %collective-permute-done.1.refs_5_), channel_id=1, source_target_pairs={{0,1},{1,0},{2,3},{3,2},{4,5},{5,4},{6,7},{7,6},{8,9},{9,8},{10,11... | collective-permute-start | bytes 196616 | tf_op jit(solution)/shard_map/ppermute | solution.py:229
  13.8 4.4 %collective-permute-start.7 = (bf16[128,256]{1,0:T(8,128)(2,1)S(1)}, bf16[128,256]{1,0:T(8,128)(2,1)S(1)}, u32[]{:S(2)}, u32[]{:S(2)}) collective-permute-start(bf16[128,256]{1,0:T(8,128)(2,1)S(1)} %collective-permute-done.2.refs_6_), channel_id=1, source_target_pairs={{0,1},{1,0},{2,3},{3,2},{4,5},{5,4},{6,7},{7,6},{8,9},{9,8},{10,11... | collective-permute-start | bytes 196616 | tf_op jit(solution)/shard_map/ppermute | solution.py:229
  13.8 8.2 %collective-permute-start.10 = (bf16[128,256]{1,0:T(8,128)(2,1)S(1)}, bf16[128,256]{1,0:T(8,128)(2,1)S(1)}, u32[]{:S(2)}, u32[]{:S(2)}) collective-permute-start(bf16[128,256]{1,0:T(8,128)(2,1)S(1)} %collective-permute-done.3.refs_3_), channel_id=1, source_target_pairs={{0,6},{2,4},{4,2},{6,0},{1,7},{3,5},{5,3},{7,1},{8,14},{10,12},{12... | collective-permute-start | bytes 196616 | tf_op jit(solution)/shard_map/ppermute | solution.py:233
  17.4 4.9 %collective-permute-start.8 = (bf16[128,256]{1,0:T(8,128)(2,1)S(1)}, bf16[128,256]{1,0:T(8,128)(2,1)S(1)}, u32[]{:S(2)}, u32[]{:S(2)}) collective-permute-start(bf16[128,256]{1,0:T(8,128)(2,1)S(1)} %collective-permute-done.3.refs_3_), channel_id=1, source_target_pairs={{0,2},{2,0},{4,6},{6,4},{1,3},{3,1},{5,7},{7,5},{8,10},{10,8},{12,... | collective-permute-start | bytes 196616 | tf_op jit(solution)/shard_map/ppermute | solution.py:233
  17.4 5.9 %collective-permute-start.9 = (bf16[128,256]{1,0:T(8,128)(2,1)S(1)}, bf16[128,256]{1,0:T(8,128)(2,1)S(1)}, u32[]{:S(2)}, u32[]{:S(2)}) collective-permute-start(bf16[128,256]{1,0:T(8,128)(2,1)S(1)} %collective-permute-done.3.refs_3_), channel_id=1, source_target_pairs={{0,4},{2,6},{4,0},{6,2},{1,5},{3,7},{5,1},{7,3},{8,12},{10,14},{12... | collective-permute-start | bytes 196616 | tf_op jit(solution)/shard_map/ppermute | solution.py:233
  23.3 1.5 %collective-permute-start.11 = (bf16[512,256]{1,0:T(8,128)(2,1)S(1)}, bf16[512,256]{1,0:T(8,128)(2,1)S(1)}, u32[]{:S(2)}, u32[]{:S(2)}) collective-permute-start(bf16[512,256]{1,0:T(8,128)(2,1)S(1)} %get-tuple-element.51), channel_id=1, source_target_pairs={{0,1},{1,0},{2,3},{3,2},{4,5},{5,4},{6,7},{7,6},{8,9},{9,8},{10,11... | collective-permute-start | bytes 786440 | tf_op jit(solution)/shard_map/ppermute | solution.py:229
  23.3 6.1 %collective-permute-start.12 = (bf16[512,256]{1,0:T(8,128)(2,1)S(1)}, bf16[512,256]{1,0:T(8,128)(2,1)S(1)}, u32[]{:S(2)}, u32[]{:S(2)}) collective-permute-start(bf16[512,256]{1,0:T(8,128)(2,1)S(1)} %pad_maximum_fusion), channel_id=1, source_target_pairs={{0,1},{1,0},{2,3},{3,2},{4,5},{5,4},{6,7},{7,6},{8,9},{9,8},{10,11... | collective-permute-start | bytes 786440 | tf_op jit(solution)/shard_map/ppermute | solution.py:229
  24.9 9.3 %copy-start.3 = (f32[1,128,128]{2,1,0:T(8,128)S(1)}, f32[1,128,128]{2,1,0:T(8,128)}, u32[]{:S(2)}) copy-start(f32[1,128,128]{2,1,0:T(8,128)} %param.16) | copy-start | bytes 196612
  24.9 9.3 %copy-start.4 = (f32[1,128,128]{2,1,0:T(8,128)S(1)}, f32[1,128,128]{2,1,0:T(8,128)}, u32[]{:S(2)}) copy-start(f32[1,128,128]{2,1,0:T(8,128)} %param.15) | copy-start | bytes 196612
  24.9 8.3 %collective-permute-start.13 = (bf16[128,256]{1,0:T(8,128)(2,1)S(1)}, bf16[128,256]{1,0:T(8,128)(2,1)S(1)}, u32[]{:S(2)}, u32[]{:S(2)}) collective-permute-start(bf16[128,256]{1,0:T(8,128)(2,1)S(1)} %get-tuple-element.60), channel_id=1, source_target_pairs={{0,6},{2,4},{4,2},{6,0},{1,7},{3,5},{5,3},{7,1},{8,14},{10,12},{12... | collective-permute-start | bytes 196616 | tf_op jit(solution)/shard_map/ppermute | solution.py:233
  27.4 6.8 %collective-permute-start.14 = (bf16[128,256]{1,0:T(8,128)(2,1)S(1)}, bf16[128,256]{1,0:T(8,128)(2,1)S(1)}, u32[]{:S(2)}, u32[]{:S(2)}) collective-permute-start(bf16[128,256]{1,0:T(8,128)(2,1)S(1)} %get-tuple-element.61), channel_id=1, source_target_pairs={{0,4},{2,6},{4,0},{6,2},{1,5},{3,7},{5,1},{7,3},{8,12},{10,14},{12... | collective-permute-start | bytes 196616 | tf_op jit(solution)/shard_map/ppermute | solution.py:233
  27.8 6.5 %collective-permute-start.15 = (bf16[128,256]{1,0:T(8,128)(2,1)S(1)}, bf16[128,256]{1,0:T(8,128)(2,1)S(1)}, u32[]{:S(2)}, u32[]{:S(2)}) collective-permute-start(bf16[128,256]{1,0:T(8,128)(2,1)S(1)} %get-tuple-element.62), channel_id=1, source_target_pairs={{0,2},{2,0},{4,6},{6,4},{1,3},{3,1},{5,7},{7,5},{8,10},{10,8},{12,... | collective-permute-start | bytes 196616 | tf_op jit(solution)/shard_map/ppermute | solution.py:233
  34.3 1.6 %collective-permute-start.16 = (bf16[512,256]{1,0:T(8,128)(2,1)S(1)}, bf16[512,256]{1,0:T(8,128)(2,1)S(1)}, u32[]{:S(2)}, u32[]{:S(2)}) collective-permute-start(bf16[512,256]{1,0:T(8,128)(2,1)S(1)} %get-tuple-element.64), channel_id=1, source_target_pairs={{0,1},{1,0},{2,3},{3,2},{4,5},{5,4},{6,7},{7,6},{8,9},{9,8},{10,11... | collective-permute-start | bytes 786440 | tf_op jit(solution)/shard_map/ppermute | solution.py:229
  34.4 8.9 %collective-permute-start.20 = (f32[128,256]{1,0:T(8,128)S(1)}, f32[128,256]{1,0:T(8,128)S(1)}, u32[]{:S(2)}, u32[]{:S(2)}) collective-permute-start(f32[128,256]{1,0:T(8,128)S(1)} %fusion.2), channel_id=1, source_target_pairs={{0,8},{8,0},{16,24},{24,16},{1,9},{9,1},{17,25},{25,17},{2,10},{10... | collective-permute-start | bytes 393224 | tf_op jit(solution)/shard_map/ppermute | solution.py:242
  36.0 7.3 %collective-permute-start.17 = (bf16[128,256]{1,0:T(8,128)(2,1)S(1)}, bf16[128,256]{1,0:T(8,128)(2,1)S(1)}, u32[]{:S(2)}, u32[]{:S(2)}) collective-permute-start(bf16[128,256]{1,0:T(8,128)(2,1)S(1)} %get-tuple-element.71), channel_id=1, source_target_pairs={{0,6},{2,4},{4,2},{6,0},{1,7},{3,5},{5,3},{7,1},{8,14},{10,12},{12... | collective-permute-start | bytes 196616 | tf_op jit(solution)/shard_map/ppermute | solution.py:233
  38.1 6.7 %collective-permute-start.18 = (bf16[128,256]{1,0:T(8,128)(2,1)S(1)}, bf16[128,256]{1,0:T(8,128)(2,1)S(1)}, u32[]{:S(2)}, u32[]{:S(2)}) collective-permute-start(bf16[128,256]{1,0:T(8,128)(2,1)S(1)} %get-tuple-element.72), channel_id=1, source_target_pairs={{0,4},{2,6},{4,0},{6,2},{1,5},{3,7},{5,1},{7,3},{8,12},{10,14},{12... | collective-permute-start | bytes 196616 | tf_op jit(solution)/shard_map/ppermute | solution.py:233
  38.1 6.7 %collective-permute-start.19 = (bf16[128,256]{1,0:T(8,128)(2,1)S(1)}, bf16[128,256]{1,0:T(8,128)(2,1)S(1)}, u32[]{:S(2)}, u32[]{:S(2)}) collective-permute-start(bf16[128,256]{1,0:T(8,128)(2,1)S(1)} %get-tuple-element.73), channel_id=1, source_target_pairs={{0,2},{2,0},{4,6},{6,4},{1,3},{3,1},{5,7},{7,5},{8,10},{10,8},{12,... | collective-permute-start | bytes 196616 | tf_op jit(solution)/shard_map/ppermute | solution.py:233
  40.4 5.2 %collective-permute-start.21 = (bf16[128,256]{1,0:T(8,128)(2,1)S(1)}, bf16[128,256]{1,0:T(8,128)(2,1)S(1)}, u32[]{:S(2)}, u32[]{:S(2)}) collective-permute-start(bf16[128,256]{1,0:T(8,128)(2,1)S(1)} %convert_element_type.41), channel_id=1, source_target_pairs={{8,16},{16,8},{24,0},{0,24},{9,17},{17,9},{25,1},{1,25},{10,18},{1... | collective-permute-start | bytes 196616 | tf_op jit(solution)/shard_map/ppermute | solution.py:242
  (3 other events, 10.4 us)

commit v7 on v6

--- a/solution.py
+++ b/solution.py
@@ -277,8 +277,8 @@
     far_terms, next_near = lax.optimization_barrier((far_terms, [next_pair, *next_near]))
     next_kv = [*next_near, other_core(jnp.concatenate(next_near, axis=0))]
 
-    def chip_sums(near_terms, far_terms):
-        sums = near_terms + other_core(far_terms).astype(jnp.float32)
+    def chip_sums(near_terms, received):
+        sums = near_terms + received.astype(jnp.float32)
         sums = sums.reshape(chips, local_rows, width)
         return sums[0], [sums[k].astype(jnp.bfloat16) for k in range(1, chips)]
 
@@ -287,21 +287,24 @@
             own_sum = own_sum + across_chips(leaving[k - 1], k).astype(jnp.float32)
         return own_sum
 
-    own_sum, leaving = chip_sums(near_terms, far_terms)
+    own_sum, leaving = chip_sums(near_terms, other_core(far_terms))
     stacks, leaving = lax.optimization_barrier((stacks, leaving))
     first_acc = jnp.concatenate([key_grads_in[0], value_grads_in[0]], axis=1) + reduced(
         own_sum, leaving
     )
     second_query, near_terms, far_terms = attend_back(1, queries, stacks, next_kv)
-    first_acc, far_terms = lax.optimization_barrier((first_acc, far_terms))
-    early_acc = section_swap(first_acc, 0)
-    own_sum, leaving = chip_sums(near_terms, far_terms)
-    late_acc, leaving = lax.optimization_barrier((first_acc.astype(jnp.bfloat16), leaving))
+    received = other_core(far_terms)
+    first_acc, received = lax.optimization_barrier((first_acc, received))
+    own_sum, leaving = chip_sums(near_terms, received)
+    is_odd = section % 2 == 1
+    late_acc = first_acc.astype(jnp.bfloat16)
+    odd_acc = jnp.where(is_odd, late_acc, 0)
+    even_acc = jnp.where(is_odd | (section == 0), 0, late_acc)
+    odd_acc, even_acc, leaving = lax.optimization_barrier((odd_acc, even_acc, leaving))
     own_sum, queries_both = lax.optimization_barrier((own_sum, (first_query, second_query)))
     second_acc = reduced(own_sum, leaving)
-    late_acc = section_swap(late_acc, 1).astype(jnp.float32)
-    moved_acc = jnp.where(section % 2 == 0, early_acc, late_acc)
-    second_acc = second_acc + jnp.where(section == sections - 1, 0.0, moved_acc)
+    second_acc = second_acc + section_swap(odd_acc, 0).astype(jnp.float32)
+    second_acc = second_acc + section_swap(even_acc, 1).astype(jnp.float32)
     query_grads = jnp.stack(queries_both, axis=0)[:, None]
     key_grads = jnp.stack([first_acc[:, :head_dim], second_acc[:, :head_dim]], axis=0)[:, None]
     value_grads = jnp.stack([first_acc[:, head_dim:], second_acc[:, head_dim:]], axis=0)[:, None]

time: 46.7 us -> 47.8 us (1.024)
  waiting for transfers between devices: 6.48 us -> 7.31 us
  other arithmetic: 2.64 us -> 3.28 us
    ppermute x2, waiting for transfers between devices: 0.81 us -> 2.33 us  [section_swap(): return lax.ppermute(block, 'section', route)]
    ppermute x12, waiting for transfers between devices: 4.34 us -> 3.5 us  [across_chips(): lax.ppermute(block, 'z', [(chip, chip ^ k) for chip in range(lax.axis_siz...]
    unnamed x2 -> x3, other arithmetic: 1.56 us -> 2.18 us
  transfers between devices with their start and end apart: 22 -> 22, of which waited for: 8 -> 9; matrix products, arithmetic and copies ran while one was open for 2% -> 2% of each run, Pallas kernels for 18% -> 18%
where the time goes in v7:
time: 47.8 us; the launch traced here: 47.5 us
  starting transfers between devices  25.6 us (54%)
  Pallas kernels  8.36 us (17%)
  waiting for transfers between devices  7.31 us (15%)
  other arithmetic  3.28 us (7%)
  local copies, waits for them, and re-layouts  2.14 us (4%)
  between operations  0.82 us (2%)
    ppermute x12, starting transfers between devices, across_chips(): lax.ppermute(block, 'z', [(chip, chip ^ k) for chip in range(lax.axis_siz...  19 us
    pallas_call x2, Pallas kernels, attend_back(): pl.pallas_call(kernel, out_shape=(jax.ShapeDtypeStruct((local_rows, model...  7.62 us
    ppermute x12, waiting for transfers between devices, across_chips(): lax.ppermute(block, 'z', [(chip, chip ^ k) for chip in range(lax.axis_siz...  3.5 us
    ppermute x2, starting transfers between devices, section_swap(): return lax.ppermute(block, 'section', route)  2.73 us
    ppermute x1, starting transfers between devices, body(): lax.ppermute(leaving_pair, 'section', [(i, (i - 1) % sections) for i in r...  2.67 us
    ppermute x2, waiting for transfers between devices, section_swap(): return lax.ppermute(block, 'section', route)  2.33 us
    unnamed x3, other arithmetic  2.18 us
    unnamed x10, local copies, waits for them, and re-layouts  2.1 us
  transfers between devices with their start and end apart: 22, of which 9 were waited for; matrix products, arithmetic and copies ran while one was open for 2% of the time, Pallas kernels for 18%

profile of v7, /device:TPU:0, one launch (start us, length us, event | category | flops | bytes accessed | tf_op | source)
XLA Modules:
  0.0 47.5 jit_solution(12706636639197836297)
XLA Ops:
  0.6 0.8 %maximum_select_fusion = (bf16[128,256]{1,0:T(8,128)(2,1)S(1)}, bf16[128,256]{1,0:T(8,128)(2,1)S(1)}) fusion(bf16[128,128]{1,0:T(8,128)(2,1)} %param.14, bf16[128,128]{1,0:T(8,128)(2,1)} %param.13, pred[]{:T(512)S(6)} %eq.9, bf16[128,128]{1,0:T(8,128)(2,1)} %bitcast.30, bf16[128,128]{1,0:T(8,128)(2,1)} %bitcast.31), kind=kLoop, calls=%fused_computation.14 | loop fusion | flops 294912 | bytes 262145 | tf_op jit(solution)/shard_map/jit(_where)/select_n | solution.py:264
  1.5 3.1 %collective-permute-start = (bf16[128,256]{1,0:T(8,128)(2,1)S(1)}, bf16[128,256]{1,0:T(8,128)(2,1)S(1)}, u32[]{:S(2)}, u32[]{:S(2)}) collective-permute-start(bf16[128,256]{1,0:T(8,128)(2,1)S(1)} %get-tuple-element.97.refs_3_), channel_id=1, source_target_pairs={{0,2},{2,0},{4,6},{6,4},{1,3},{3,1},{5,7},{7,5},{8,10},{10,8},{12,... | collective-permute-start | bytes 196616 | tf_op jit(solution)/shard_map/ppermute | solution.py:233
  4.6 2.6 %collective-permute-start.1 = (bf16[128,256]{1,0:T(8,128)(2,1)S(1)}, bf16[128,256]{1,0:T(8,128)(2,1)S(1)}, u32[]{:S(2)}, u32[]{:S(2)}) collective-permute-start(bf16[128,256]{1,0:T(8,128)(2,1)S(1)} %get-tuple-element.97.refs_3_), channel_id=1, source_target_pairs={{0,4},{2,6},{4,0},{6,2},{1,5},{3,7},{5,1},{7,3},{8,12},{10,14},{12... | collective-permute-start | bytes 196616 | tf_op jit(solution)/shard_map/ppermute | solution.py:233
  7.2 2.7 %collective-permute-start.3 = (bf16[128,256]{1,0:T(8,128)(2,1)S(1)}, bf16[128,256]{1,0:T(8,128)(2,1)S(1)}, u32[]{:S(2)}, u32[]{:S(2)}) collective-permute-start(bf16[128,256]{1,0:T(8,128)(2,1)S(1)} %get-tuple-element.96), channel_id=1, source_target_pairs={{0,24},{8,0},{16,8},{24,16},{1,25},{9,1},{17,9},{25,17},{2,26},{10... | collective-permute-start | bytes 196616 | tf_op jit(solution)/shard_map/ppermute | solution.py:269
  9.8 1.0 %copy-done = bf16[2,1,128,1024]{3,2,1,0:T(8,128)(2,1)S(1)} copy-done((bf16[2,1,128,1024]{3,2,1,0:T(8,128)(2,1)S(1)}, bf16[2,1,128,1024]{3,2,1,0:T(8,128)(2,1)}, u32[]{:S(2)}) %copy-start) | copy-done | bytes 524312
  10.9 1.0 %copy-done.1 = bf16[2,1,128,1024]{3,2,1,0:T(8,128)(2,1)S(1)} copy-done((bf16[2,1,128,1024]{3,2,1,0:T(8,128)(2,1)S(1)}, bf16[2,1,128,1024]{3,2,1,0:T(8,128)(2,1)}, u32[]{:S(2)}) %copy-start.1) | copy-done | bytes 524312
  11.9 0.7 %shard_map.112 = (bf16[2048,128]{1,0:T(8,128)(2,1)S(1)}, bf16[2048,128]{1,0:T(8,128)(2,1)S(1)}, f32[64,256]{1,0:T(8,128)S(1)}) custom-call(s32[8]{0:T(128)S(1)} %copy-done.2, bf16[2,1,128,1024]{3,2,1,0:T(8,128)(2,1)S(1)} %copy-done, bf16[2,1,128,1024]{3,2,1,0:T(8,128)(2,1)S(1)} %copy-done.1), custom_call_target="tpu_custom_call" | custom-call | flops 262144 | bytes 2097152 | tf_op jit(solution)/shard_map/pallas_call | solution.py:42
  13.8 3.6 %collective-permute-start.10 = (bf16[128,256]{1,0:T(8,128)(2,1)S(1)}, bf16[128,256]{1,0:T(8,128)(2,1)S(1)}, u32[]{:S(2)}, u32[]{:S(2)}) collective-permute-start(bf16[128,256]{1,0:T(8,128)(2,1)S(1)} %collective-permute-done.3.refs_3_), channel_id=1, source_target_pairs={{0,6},{2,4},{4,2},{6,0},{1,7},{3,5},{5,3},{7,1},{8,14},{10,12},{12... | collective-permute-start | bytes 196616 | tf_op jit(solution)/shard_map/ppermute | solution.py:233
  17.4 0.8 %collective-permute-start.9 = (bf16[128,256]{1,0:T(8,128)(2,1)S(1)}, bf16[128,256]{1,0:T(8,128)(2,1)S(1)}, u32[]{:S(2)}, u32[]{:S(2)}) collective-permute-start(bf16[128,256]{1,0:T(8,128)(2,1)S(1)} %collective-permute-done.3.refs_3_), channel_id=1, source_target_pairs={{0,4},{2,6},{4,0},{6,2},{1,5},{3,7},{5,1},{7,3},{8,12},{10,14},{12... | collective-permute-start | bytes 196616 | tf_op jit(solution)/shard_map/ppermute | solution.py:233
  18.2 3.8 %shard_map.113 = (bf16[128,1024]{1,0:T(8,128)(2,1)S(1)}, f32[512,256]{1,0:T(8,128)S(1)}, bf16[512,256]{1,0:T(8,128)(2,1)S(1)}) custom-call(bf16[2048,128]{1,0:T(8,128)(2,1)S(1)} %get-tuple-element.53.refs_0_, bf16[2048,128]{1,0:T(8,128)(2,1)S(1)} %get-tuple-element.54.refs_1_, f32[64,256]{1,0:T(8,128)S(1)} %get-tuple-element.55.refs_2_, ...), custom_call_target="tpu_custom_call" | custom-call | flops 5368709120 | bytes 2097152 | tf_op jit(solution)/shard_map/pallas_call | solution.py:201
  22.3 1.0 %collective-permute-done.9.refs_5_ = bf16[128,256]{1,0:T(8,128)(2,1)S(1)} collective-permute-done((bf16[128,256]{1,0:T(8,128)(2,1)S(1)}, bf16[128,256]{1,0:T(8,128)(2,1)S(1)}, u32[]{:S(2)}, u32[]{:S(2)}) %collective-permute-start.9) | collective-permute-done | bytes 65568 | tf_op jit(solution)/shard_map/ppermute | solution.py:233
  23.9 0.9 %collective-permute-done.11 = bf16[512,256]{1,0:T(8,128)(2,1)S(1)} collective-permute-done((bf16[512,256]{1,0:T(8,128)(2,1)S(1)}, bf16[512,256]{1,0:T(8,128)(2,1)S(1)}, u32[]{:S(2)}, u32[]{:S(2)}) %collective-permute-start.11) | collective-permute-done | bytes 262176 | tf_op jit(solution)/shard_map/ppermute | solution.py:229
  24.9 2.5 %collective-permute-start.13 = (bf16[128,256]{1,0:T(8,128)(2,1)S(1)}, bf16[128,256]{1,0:T(8,128)(2,1)S(1)}, u32[]{:S(2)}, u32[]{:S(2)}) collective-permute-start(bf16[128,256]{1,0:T(8,128)(2,1)S(1)} %get-tuple-element.61), channel_id=1, source_target_pairs={{0,6},{2,4},{4,2},{6,0},{1,7},{3,5},{5,3},{7,1},{8,14},{10,12},{12... | collective-permute-start | bytes 196616 | tf_op jit(solution)/shard_map/ppermute | solution.py:233
  27.8 1.6 %collective-permute-start.15 = (bf16[128,256]{1,0:T(8,128)(2,1)S(1)}, bf16[128,256]{1,0:T(8,128)(2,1)S(1)}, u32[]{:S(2)}, u32[]{:S(2)}) collective-permute-start(bf16[128,256]{1,0:T(8,128)(2,1)S(1)} %get-tuple-element.63), channel_id=1, source_target_pairs={{0,2},{2,0},{4,6},{6,4},{1,3},{3,1},{5,7},{7,5},{8,10},{10,8},{12,... | collective-permute-start | bytes 196616 | tf_op jit(solution)/shard_map/ppermute | solution.py:233
  29.4 3.8 %shard_map.114 = (bf16[128,1024]{1,0:T(8,128)(2,1)S(1)}, f32[512,256]{1,0:T(8,128)S(1)}, bf16[512,256]{1,0:T(8,128)(2,1)S(1)}) custom-call(bf16[2048,128]{1,0:T(8,128)(2,1)S(1)} %get-tuple-element.53.refs_0_, bf16[2048,128]{1,0:T(8,128)(2,1)S(1)} %get-tuple-element.54.refs_1_, f32[64,256]{1,0:T(8,128)S(1)} %get-tuple-element.55.refs_2_, ...), custom_call_target="tpu_custom_call" | custom-call | flops 5368709120 | bytes 2097152 | tf_op jit(solution)/shard_map/pallas_call | solution.py:201
  33.3 0.9 %collective-permute-done.14 = bf16[128,256]{1,0:T(8,128)(2,1)S(1)} collective-permute-done((bf16[128,256]{1,0:T(8,128)(2,1)S(1)}, bf16[128,256]{1,0:T(8,128)(2,1)S(1)}, u32[]{:S(2)}, u32[]{:S(2)}) %collective-permute-start.14) | collective-permute-done | bytes 65568 | tf_op jit(solution)/shard_map/ppermute | solution.py:233
  34.9 2.5 %collective-permute-start.17 = (bf16[128,256]{1,0:T(8,128)(2,1)S(1)}, bf16[128,256]{1,0:T(8,128)(2,1)S(1)}, u32[]{:S(2)}, u32[]{:S(2)}) collective-permute-start(bf16[128,256]{1,0:T(8,128)(2,1)S(1)} %get-tuple-element.72), channel_id=1, source_target_pairs={{0,6},{2,4},{4,2},{6,0},{1,7},{3,5},{5,3},{7,1},{8,14},{10,12},{12... | collective-permute-start | bytes 196616 | tf_op jit(solution)/shard_map/ppermute | solution.py:233
  37.4 2.0 %collective-permute-start.19 = (bf16[128,256]{1,0:T(8,128)(2,1)S(1)}, bf16[128,256]{1,0:T(8,128)(2,1)S(1)}, u32[]{:S(2)}, u32[]{:S(2)}) collective-permute-start(bf16[128,256]{1,0:T(8,128)(2,1)S(1)} %get-tuple-element.74), channel_id=1, source_target_pairs={{0,2},{2,0},{4,6},{6,4},{1,3},{3,1},{5,7},{7,5},{8,10},{10,8},{12,... | collective-permute-start | bytes 196616 | tf_op jit(solution)/shard_map/ppermute | solution.py:233
  39.4 1.5 %collective-permute-start.20 = (bf16[128,256]{1,0:T(8,128)(2,1)S(1)}, bf16[128,256]{1,0:T(8,128)(2,1)S(1)}, u32[]{:S(2)}, u32[]{:S(2)}) collective-permute-start(bf16[128,256]{1,0:T(8,128)(2,1)S(1)} %get-tuple-element.75), channel_id=1, source_target_pairs={{0,8},{8,0},{16,24},{24,16},{1,9},{9,1},{17,25},{25,17},{2,10},{10... | collective-permute-start | bytes 196616 | tf_op jit(solution)/shard_map/ppermute | solution.py:242
  40.9 1.2 %collective-permute-start.21 = (bf16[128,256]{1,0:T(8,128)(2,1)S(1)}, bf16[128,256]{1,0:T(8,128)(2,1)S(1)}, u32[]{:S(2)}, u32[]{:S(2)}) collective-permute-start(bf16[128,256]{1,0:T(8,128)(2,1)S(1)} %get-tuple-element.76), channel_id=1, source_target_pairs={{8,16},{16,8},{24,0},{0,24},{9,17},{17,9},{25,1},{1,25},{10,18},{1... | collective-permute-start | bytes 196616 | tf_op jit(solution)/shard_map/ppermute | solution.py:242
  42.1 0.8 %maximum_bitcast_fusion = bf16[2,1,128,1024]{3,2,1,0:T(8,128)(2,1)} fusion(bf16[1,128,1024]{2,1,0:T(8,128)(2,1)S(1)} %bitcast.27, bf16[1,128,1024]{2,1,0:T(8,128)(2,1)S(1)} %bitcast.26), kind=kLoop, calls=%fused_computation | loop fusion | flops 262144 | bytes 1048576
  43.0 0.8 %collective-permute-done.18 = bf16[128,256]{1,0:T(8,128)(2,1)S(1)} collective-permute-done((bf16[128,256]{1,0:T(8,128)(2,1)S(1)}, bf16[128,256]{1,0:T(8,128)(2,1)S(1)}, u32[]{:S(2)}, u32[]{:S(2)}) %collective-permute-start.18) | collective-permute-done | bytes 65568 | tf_op jit(solution)/shard_map/ppermute | solution.py:233
  43.9 2.2 %collective-permute-done.21 = bf16[128,256]{1,0:T(8,128)(2,1)S(1)} collective-permute-done((bf16[128,256]{1,0:T(8,128)(2,1)S(1)}, bf16[128,256]{1,0:T(8,128)(2,1)S(1)}, u32[]{:S(2)}, u32[]{:S(2)}) %collective-permute-start.21) | collective-permute-done | bytes 65568 | tf_op jit(solution)/shard_map/ppermute | solution.py:242
  46.1 0.7 %maximum_bitcast_fusion.2 = f32[2,1,128,128]{3,2,1,0:T(8,128)} fusion(f32[1,128,128]{2,1,0:T(8,128)S(1)} %get-tuple-element.92, f32[1,128,128]{2,1,0:T(8,128)S(1)} %get-tuple-element.90), kind=kLoop, calls=%fused_computation.9 | loop fusion | flops 32768 | bytes 262144
  (47 shorter events, 4.1 us)
Async XLA Ops:
  1.5 8.4 %copy-start.2 = (s32[8]{0:T(128)S(1)}, s32[8]{0:T(128)}, u32[]{:S(2)}) copy-start(s32[8]{0:T(128)} %order_ref.1) | copy-start | bytes 100
  1.5 11.2 %collective-permute-start = (bf16[128,256]{1,0:T(8,128)(2,1)S(1)}, bf16[128,256]{1,0:T(8,128)(2,1)S(1)}, u32[]{:S(2)}, u32[]{:S(2)}) collective-permute-start(bf16[128,256]{1,0:T(8,128)(2,1)S(1)} %get-tuple-element.97.refs_3_), channel_id=1, source_target_pairs={{0,2},{2,0},{4,6},{6,4},{1,3},{3,1},{5,7},{7,5},{8,10},{10,8},{12,... | collective-permute-start | bytes 196616 | tf_op jit(solution)/shard_map/ppermute | solution.py:233
  4.6 8.1 %collective-permute-start.1 = (bf16[128,256]{1,0:T(8,128)(2,1)S(1)}, bf16[128,256]{1,0:T(8,128)(2,1)S(1)}, u32[]{:S(2)}, u32[]{:S(2)}) collective-permute-start(bf16[128,256]{1,0:T(8,128)(2,1)S(1)} %get-tuple-element.97.refs_3_), channel_id=1, source_target_pairs={{0,4},{2,6},{4,0},{6,2},{1,5},{3,7},{5,1},{7,3},{8,12},{10,14},{12... | collective-permute-start | bytes 196616 | tf_op jit(solution)/shard_map/ppermute | solution.py:233
  7.2 6.1 %collective-permute-start.2 = (bf16[128,256]{1,0:T(8,128)(2,1)S(1)}, bf16[128,256]{1,0:T(8,128)(2,1)S(1)}, u32[]{:S(2)}, u32[]{:S(2)}) collective-permute-start(bf16[128,256]{1,0:T(8,128)(2,1)S(1)} %get-tuple-element.97.refs_3_), channel_id=1, source_target_pairs={{0,6},{2,4},{4,2},{6,0},{1,7},{3,5},{5,3},{7,1},{8,14},{10,12},{12... | collective-permute-start | bytes 196616 | tf_op jit(solution)/shard_map/ppermute | solution.py:233
  7.2 6.1 %collective-permute-start.3 = (bf16[128,256]{1,0:T(8,128)(2,1)S(1)}, bf16[128,256]{1,0:T(8,128)(2,1)S(1)}, u32[]{:S(2)}, u32[]{:S(2)}) collective-permute-start(bf16[128,256]{1,0:T(8,128)(2,1)S(1)} %get-tuple-element.96), channel_id=1, source_target_pairs={{0,24},{8,0},{16,8},{24,16},{1,25},{9,1},{17,9},{25,17},{2,26},{10... | collective-permute-start | bytes 196616 | tf_op jit(solution)/shard_map/ppermute | solution.py:269
  9.8 7.6 %collective-permute-start.4 = (bf16[128,256]{1,0:T(8,128)(2,1)S(1)}, bf16[128,256]{1,0:T(8,128)(2,1)S(1)}, u32[]{:S(2)}, u32[]{:S(2)}) collective-permute-start(bf16[128,256]{1,0:T(8,128)(2,1)S(1)} %get-tuple-element.97.refs_3_), channel_id=1, source_target_pairs={{0,1},{1,0},{2,3},{3,2},{4,5},{5,4},{6,7},{7,6},{8,9},{9,8},{10,11... | collective-permute-start | bytes 196616 | tf_op jit(solution)/shard_map/ppermute | solution.py:229
  13.2 4.2 %collective-permute-start.5 = (bf16[128,256]{1,0:T(8,128)(2,1)S(1)}, bf16[128,256]{1,0:T(8,128)(2,1)S(1)}, u32[]{:S(2)}, u32[]{:S(2)}) collective-permute-start(bf16[128,256]{1,0:T(8,128)(2,1)S(1)} %collective-permute-done.refs_4_), channel_id=1, source_target_pairs={{0,1},{1,0},{2,3},{3,2},{4,5},{5,4},{6,7},{7,6},{8,9},{9,8},{10,11... | collective-permute-start | bytes 196616 | tf_op jit(solution)/shard_map/ppermute | solution.py:229
  13.3 4.9 %collective-permute-start.6 = (bf16[128,256]{1,0:T(8,128)(2,1)S(1)}, bf16[128,256]{1,0:T(8,128)(2,1)S(1)}, u32[]{:S(2)}, u32[]{:S(2)}) collective-permute-start(bf16[128,256]{1,0:T(8,128)(2,1)S(1)} %collective-permute-done.1.refs_5_), channel_id=1, source_target_pairs={{0,1},{1,0},{2,3},{3,2},{4,5},{5,4},{6,7},{7,6},{8,9},{9,8},{10,11... | collective-permute-start | bytes 196616 | tf_op jit(solution)/shard_map/ppermute | solution.py:229
  13.8 4.4 %collective-permute-start.7 = (bf16[128,256]{1,0:T(8,128)(2,1)S(1)}, bf16[128,256]{1,0:T(8,128)(2,1)S(1)}, u32[]{:S(2)}, u32[]{:S(2)}) collective-permute-start(bf16[128,256]{1,0:T(8,128)(2,1)S(1)} %collective-permute-done.2.refs_6_), channel_id=1, source_target_pairs={{0,1},{1,0},{2,3},{3,2},{4,5},{5,4},{6,7},{7,6},{8,9},{9,8},{10,11... | collective-permute-start | bytes 196616 | tf_op jit(solution)/shard_map/ppermute | solution.py:229
  13.8 8.2 %collective-permute-start.10 = (bf16[128,256]{1,0:T(8,128)(2,1)S(1)}, bf16[128,256]{1,0:T(8,128)(2,1)S(1)}, u32[]{:S(2)}, u32[]{:S(2)}) collective-permute-start(bf16[128,256]{1,0:T(8,128)(2,1)S(1)} %collective-permute-done.3.refs_3_), channel_id=1, source_target_pairs={{0,6},{2,4},{4,2},{6,0},{1,7},{3,5},{5,3},{7,1},{8,14},{10,12},{12... | collective-permute-start | bytes 196616 | tf_op jit(solution)/shard_map/ppermute | solution.py:233
  17.4 4.9 %collective-permute-start.8 = (bf16[128,256]{1,0:T(8,128)(2,1)S(1)}, bf16[128,256]{1,0:T(8,128)(2,1)S(1)}, u32[]{:S(2)}, u32[]{:S(2)}) collective-permute-start(bf16[128,256]{1,0:T(8,128)(2,1)S(1)} %collective-permute-done.3.refs_3_), channel_id=1, source_target_pairs={{0,2},{2,0},{4,6},{6,4},{1,3},{3,1},{5,7},{7,5},{8,10},{10,8},{12,... | collective-permute-start | bytes 196616 | tf_op jit(solution)/shard_map/ppermute | solution.py:233
  17.4 5.9 %collective-permute-start.9 = (bf16[128,256]{1,0:T(8,128)(2,1)S(1)}, bf16[128,256]{1,0:T(8,128)(2,1)S(1)}, u32[]{:S(2)}, u32[]{:S(2)}) collective-permute-start(bf16[128,256]{1,0:T(8,128)(2,1)S(1)} %collective-permute-done.3.refs_3_), channel_id=1, source_target_pairs={{0,4},{2,6},{4,0},{6,2},{1,5},{3,7},{5,1},{7,3},{8,12},{10,14},{12... | collective-permute-start | bytes 196616 | tf_op jit(solution)/shard_map/ppermute | solution.py:233
  23.3 1.5 %collective-permute-start.11 = (bf16[512,256]{1,0:T(8,128)(2,1)S(1)}, bf16[512,256]{1,0:T(8,128)(2,1)S(1)}, u32[]{:S(2)}, u32[]{:S(2)}) collective-permute-start(bf16[512,256]{1,0:T(8,128)(2,1)S(1)} %get-tuple-element.52), channel_id=1, source_target_pairs={{0,1},{1,0},{2,3},{3,2},{4,5},{5,4},{6,7},{7,6},{8,9},{9,8},{10,11... | collective-permute-start | bytes 786440 | tf_op jit(solution)/shard_map/ppermute | solution.py:229
  23.3 6.1 %collective-permute-start.12 = (bf16[512,256]{1,0:T(8,128)(2,1)S(1)}, bf16[512,256]{1,0:T(8,128)(2,1)S(1)}, u32[]{:S(2)}, u32[]{:S(2)}) collective-permute-start(bf16[512,256]{1,0:T(8,128)(2,1)S(1)} %pad_maximum_fusion), channel_id=1, source_target_pairs={{0,1},{1,0},{2,3},{3,2},{4,5},{5,4},{6,7},{7,6},{8,9},{9,8},{10,11... | collective-permute-start | bytes 786440 | tf_op jit(solution)/shard_map/ppermute | solution.py:229
  24.9 8.4 %collective-permute-start.13 = (bf16[128,256]{1,0:T(8,128)(2,1)S(1)}, bf16[128,256]{1,0:T(8,128)(2,1)S(1)}, u32[]{:S(2)}, u32[]{:S(2)}) collective-permute-start(bf16[128,256]{1,0:T(8,128)(2,1)S(1)} %get-tuple-element.61), channel_id=1, source_target_pairs={{0,6},{2,4},{4,2},{6,0},{1,7},{3,5},{5,3},{7,1},{8,14},{10,12},{12... | collective-permute-start | bytes 196616 | tf_op jit(solution)/shard_map/ppermute | solution.py:233
  27.4 6.8 %collective-permute-start.14 = (bf16[128,256]{1,0:T(8,128)(2,1)S(1)}, bf16[128,256]{1,0:T(8,128)(2,1)S(1)}, u32[]{:S(2)}, u32[]{:S(2)}) collective-permute-start(bf16[128,256]{1,0:T(8,128)(2,1)S(1)} %get-tuple-element.62), channel_id=1, source_target_pairs={{0,4},{2,6},{4,0},{6,2},{1,5},{3,7},{5,1},{7,3},{8,12},{10,14},{12... | collective-permute-start | bytes 196616 | tf_op jit(solution)/shard_map/ppermute | solution.py:233
  27.8 6.5 %collective-permute-start.15 = (bf16[128,256]{1,0:T(8,128)(2,1)S(1)}, bf16[128,256]{1,0:T(8,128)(2,1)S(1)}, u32[]{:S(2)}, u32[]{:S(2)}) collective-permute-start(bf16[128,256]{1,0:T(8,128)(2,1)S(1)} %get-tuple-element.63), channel_id=1, source_target_pairs={{0,2},{2,0},{4,6},{6,4},{1,3},{3,1},{5,7},{7,5},{8,10},{10,8},{12,... | collective-permute-start | bytes 196616 | tf_op jit(solution)/shard_map/ppermute | solution.py:233
  29.4 4.8 %copy-start.4 = (f32[1,128,128]{2,1,0:T(8,128)S(1)}, f32[1,128,128]{2,1,0:T(8,128)}, u32[]{:S(2)}) copy-start(f32[1,128,128]{2,1,0:T(8,128)} %param.15) | copy-start | bytes 196612
  33.2 1.6 %collective-permute-start.16 = (bf16[512,256]{1,0:T(8,128)(2,1)S(1)}, bf16[512,256]{1,0:T(8,128)(2,1)S(1)}, u32[]{:S(2)}, u32[]{:S(2)}) collective-permute-start(bf16[512,256]{1,0:T(8,128)(2,1)S(1)} %get-tuple-element.64), channel_id=1, source_target_pairs={{0,1},{1,0},{2,3},{3,2},{4,5},{5,4},{6,7},{7,6},{8,9},{9,8},{10,11... | collective-permute-start | bytes 786440 | tf_op jit(solution)/shard_map/ppermute | solution.py:229
  34.9 8.0 %collective-permute-start.17 = (bf16[128,256]{1,0:T(8,128)(2,1)S(1)}, bf16[128,256]{1,0:T(8,128)(2,1)S(1)}, u32[]{:S(2)}, u32[]{:S(2)}) collective-permute-start(bf16[128,256]{1,0:T(8,128)(2,1)S(1)} %get-tuple-element.72), channel_id=1, source_target_pairs={{0,6},{2,4},{4,2},{6,0},{1,7},{3,5},{5,3},{7,1},{8,14},{10,12},{12... | collective-permute-start | bytes 196616 | tf_op jit(solution)/shard_map/ppermute | solution.py:233
  37.4 6.3 %collective-permute-start.18 = (bf16[128,256]{1,0:T(8,128)(2,1)S(1)}, bf16[128,256]{1,0:T(8,128)(2,1)S(1)}, u32[]{:S(2)}, u32[]{:S(2)}) collective-permute-start(bf16[128,256]{1,0:T(8,128)(2,1)S(1)} %get-tuple-element.73), channel_id=1, source_target_pairs={{0,4},{2,6},{4,0},{6,2},{1,5},{3,7},{5,1},{7,3},{8,12},{10,14},{12... | collective-permute-start | bytes 196616 | tf_op jit(solution)/shard_map/ppermute | solution.py:233
  37.4 6.3 %collective-permute-start.19 = (bf16[128,256]{1,0:T(8,128)(2,1)S(1)}, bf16[128,256]{1,0:T(8,128)(2,1)S(1)}, u32[]{:S(2)}, u32[]{:S(2)}) collective-permute-start(bf16[128,256]{1,0:T(8,128)(2,1)S(1)} %get-tuple-element.74), channel_id=1, source_target_pairs={{0,2},{2,0},{4,6},{6,4},{1,3},{3,1},{5,7},{7,5},{8,10},{10,8},{12,... | collective-permute-start | bytes 196616 | tf_op jit(solution)/shard_map/ppermute | solution.py:233
  39.4 4.5 %collective-permute-start.20 = (bf16[128,256]{1,0:T(8,128)(2,1)S(1)}, bf16[128,256]{1,0:T(8,128)(2,1)S(1)}, u32[]{:S(2)}, u32[]{:S(2)}) collective-permute-start(bf16[128,256]{1,0:T(8,128)(2,1)S(1)} %get-tuple-element.75), channel_id=1, source_target_pairs={{0,8},{8,0},{16,24},{24,16},{1,9},{9,1},{17,25},{25,17},{2,10},{10... | collective-permute-start | bytes 196616 | tf_op jit(solution)/shard_map/ppermute | solution.py:242
  40.9 5.2 %collective-permute-start.21 = (bf16[128,256]{1,0:T(8,128)(2,1)S(1)}, bf16[128,256]{1,0:T(8,128)(2,1)S(1)}, u32[]{:S(2)}, u32[]{:S(2)}) collective-permute-start(bf16[128,256]{1,0:T(8,128)(2,1)S(1)} %get-tuple-element.76), channel_id=1, source_target_pairs={{8,16},{16,8},{24,0},{0,24},{9,17},{17,9},{25,1},{1,25},{10,18},{1... | collective-permute-start | bytes 196616 | tf_op jit(solution)/shard_map/ppermute | solution.py:242
  (3 other events, 6.9 us)

commit v8 on v7

--- a/solution.py
+++ b/solution.py
@@ -225,6 +225,48 @@
     )(*stacks, *kv_arrays)
 
 
+def finish_kernel(first_ref, own_ref, *refs):
+    key_ref, value_ref, held, copy_sem = refs[-4:]
+    head_dim = key_ref.shape[3]
+    copies = []
+    for tick in range(2):
+        total = (first_ref if tick == 0 else own_ref)[...]
+        if tick == 1:
+            for ref in refs[:-4]:
+                total = total + ref[...].astype(jnp.float32)
+        for half, out in enumerate((key_ref, value_ref)):
+            held[tick, half] = total[:, half * head_dim : (half + 1) * head_dim]
+            copy = pltpu.make_async_copy(
+                held.at[tick, half], out.at[tick, 0], copy_sem.at[2 * tick + half]
+            )
+            copy.start()
+            copies.append(copy)
+    for copy in copies:
+        copy.wait()
+
+
+def finished(first_acc, own_sum, blocks):
+    rows, width = first_acc.shape
+    head_dim = width // 2
+    in_vmem = pl.BlockSpec(memory_space=pltpu.VMEM)
+    return pl.pallas_call(
+        finish_kernel,
+        out_shape=(jax.ShapeDtypeStruct((2, 1, rows, head_dim), jnp.float32),) * 2,
+        in_specs=[in_vmem] * (2 + len(blocks)),
+        out_specs=(pl.BlockSpec(memory_space=pl.ANY),) * 2,
+        scratch_shapes=[
+            pltpu.VMEM((2, 2, rows, head_dim), jnp.float32),
+            pltpu.SemaphoreType.DMA((4,)),
+        ],
+        compiler_params=pltpu.CompilerParams(vmem_limit_bytes=8 * 2**20),
+        cost_estimate=pl.CostEstimate(
+            flops=len(blocks) * first_acc.size,
+            bytes_accessed=16 * first_acc.size,
+            transcendentals=0,
+        ),
+    )(first_acc, own_sum, *blocks)
+
+
 def other_core(block):
     return lax.ppermute(block, "core", [(0, 1), (1, 0)])
 
@@ -302,12 +344,11 @@
     even_acc = jnp.where(is_odd | (section == 0), 0, late_acc)
     odd_acc, even_acc, leaving = lax.optimization_barrier((odd_acc, even_acc, leaving))
     own_sum, queries_both = lax.optimization_barrier((own_sum, (first_query, second_query)))
-    second_acc = reduced(own_sum, leaving)
-    second_acc = second_acc + section_swap(odd_acc, 0).astype(jnp.float32)
-    second_acc = second_acc + section_swap(even_acc, 1).astype(jnp.float32)
+    arrived = [across_chips(leaving[k - 1], k) for k in partners]
+    arrived.insert(-1, section_swap(even_acc, 1))
+    arrived.append(section_swap(odd_acc, 0))
+    key_grads, value_grads = finished(first_acc, own_sum, arrived)
     query_grads = jnp.stack(queries_both, axis=0)[:, None]
-    key_grads = jnp.stack([first_acc[:, :head_dim], second_acc[:, :head_dim]], axis=0)[:, None]
-    value_grads = jnp.stack([first_acc[:, head_dim:], second_acc[:, head_dim:]], axis=0)[:, None]
     return (query_grads, key_grads, value_grads)
 
 

time: 47.8 us -> 47.1 us (0.985)
  other arithmetic: 3.28 us -> 1.89 us
  Pallas kernels: 8.36 us -> 9.09 us
    unnamed x3 -> x1, other arithmetic: 2.18 us -> 0.84 us
    ppermute x12, waiting for transfers between devices: 3.5 us -> 4.48 us  [across_chips(): lax.ppermute(block, 'z', [(chip, chip ^ k) for chip in range(lax.axis_siz...]
    ppermute x2, waiting for transfers between devices: 2.33 us -> 1.41 us  [section_swap(): return lax.ppermute(block, 'section', route)]
    ppermute x12, starting transfers between devices: 19 us -> 19.7 us  [across_chips(): lax.ppermute(block, 'z', [(chip, chip ^ k) for chip in range(lax.axis_siz...]
    ppermute x2, starting transfers between devices: 2.73 us -> 1.97 us  [section_swap(): return lax.ppermute(block, 'section', route)]
    pallas_call x0 -> x1, Pallas kernels: none -> 0.73 us  [finished(): pl.pallas_call(finish_kernel, out_shape=(jax.ShapeDtypeStruct((2, 1, rows...]
where the time goes in v8:
time: 47.1 us; the launch traced here: 46.8 us
  starting transfers between devices  25.6 us (54%)
  Pallas kernels  9.09 us (19%)
  waiting for transfers between devices  7.37 us (16%)
  local copies, waits for them, and re-layouts  2.12 us (5%)
  other arithmetic  1.89 us (4%)
  between operations  0.8 us (2%)
    ppermute x12, starting transfers between devices, across_chips(): lax.ppermute(block, 'z', [(chip, chip ^ k) for chip in range(lax.axis_siz...  19.7 us
    pallas_call x2, Pallas kernels, attend_back(): pl.pallas_call(kernel, out_shape=(jax.ShapeDtypeStruct((local_rows, model...  7.62 us
    ppermute x12, waiting for transfers between devices, across_chips(): lax.ppermute(block, 'z', [(chip, chip ^ k) for chip in range(lax.axis_siz...  4.48 us
    ppermute x1, starting transfers between devices, body(): lax.ppermute(leaving_pair, 'section', [(i, (i - 1) % sections) for i in r...  2.67 us
    unnamed x10, local copies, waits for them, and re-layouts  2.1 us
    ppermute x2, starting transfers between devices, section_swap(): return lax.ppermute(block, 'section', route)  1.97 us
    ppermute x7, waiting for transfers between devices, other_core(): return lax.ppermute(block, 'core', [(0, 1), (1, 0)])  1.48 us
    ppermute x2, waiting for transfers between devices, section_swap(): return lax.ppermute(block, 'section', route)  1.41 us
  transfers between devices with their start and end apart: 22, of which 9 were waited for; matrix products, arithmetic and copies ran while one was open for 2% of the time, Pallas kernels for 18%

profile of v8, /device:TPU:0, one launch (start us, length us, event | category | flops | bytes accessed | tf_op | source)
XLA Modules:
  0.0 46.8 jit_solution(1294895788050444297)
XLA Ops:
  0.6 0.8 %maximum_select_fusion = (bf16[128,256]{1,0:T(8,128)(2,1)S(1)}, bf16[128,256]{1,0:T(8,128)(2,1)S(1)}) fusion(bf16[128,128]{1,0:T(8,128)(2,1)} %param.14, bf16[128,128]{1,0:T(8,128)(2,1)} %param.13, pred[]{:T(512)S(6)} %eq.9, bf16[128,128]{1,0:T(8,128)(2,1)} %bitcast.14, bf16[128,128]{1,0:T(8,128)(2,1)} %bitcast.15), kind=kLoop, calls=%fused_computation.9 | loop fusion | flops 294912 | bytes 262145 | tf_op jit(solution)/shard_map/jit(_where)/select_n | solution.py:306
  1.5 3.1 %collective-permute-start = (bf16[128,256]{1,0:T(8,128)(2,1)S(1)}, bf16[128,256]{1,0:T(8,128)(2,1)S(1)}, u32[]{:S(2)}, u32[]{:S(2)}) collective-permute-start(bf16[128,256]{1,0:T(8,128)(2,1)S(1)} %get-tuple-element.97.refs_3_), channel_id=1, source_target_pairs={{0,2},{2,0},{4,6},{6,4},{1,3},{3,1},{5,7},{7,5},{8,10},{10,8},{12,... | collective-permute-start | bytes 196616 | tf_op jit(solution)/shard_map/ppermute | solution.py:275
  4.6 2.6 %collective-permute-start.1 = (bf16[128,256]{1,0:T(8,128)(2,1)S(1)}, bf16[128,256]{1,0:T(8,128)(2,1)S(1)}, u32[]{:S(2)}, u32[]{:S(2)}) collective-permute-start(bf16[128,256]{1,0:T(8,128)(2,1)S(1)} %get-tuple-element.97.refs_3_), channel_id=1, source_target_pairs={{0,4},{2,6},{4,0},{6,2},{1,5},{3,7},{5,1},{7,3},{8,12},{10,14},{12... | collective-permute-start | bytes 196616 | tf_op jit(solution)/shard_map/ppermute | solution.py:275
  7.2 2.7 %collective-permute-start.3 = (bf16[128,256]{1,0:T(8,128)(2,1)S(1)}, bf16[128,256]{1,0:T(8,128)(2,1)S(1)}, u32[]{:S(2)}, u32[]{:S(2)}) collective-permute-start(bf16[128,256]{1,0:T(8,128)(2,1)S(1)} %get-tuple-element.96), channel_id=1, source_target_pairs={{0,24},{8,0},{16,8},{24,16},{1,25},{9,1},{17,9},{25,17},{2,26},{10... | collective-permute-start | bytes 196616 | tf_op jit(solution)/shard_map/ppermute | solution.py:311
  9.8 1.0 %copy-done = bf16[2,1,128,1024]{3,2,1,0:T(8,128)(2,1)S(1)} copy-done((bf16[2,1,128,1024]{3,2,1,0:T(8,128)(2,1)S(1)}, bf16[2,1,128,1024]{3,2,1,0:T(8,128)(2,1)}, u32[]{:S(2)}) %copy-start) | copy-done | bytes 524312
  10.9 1.0 %copy-done.1 = bf16[2,1,128,1024]{3,2,1,0:T(8,128)(2,1)S(1)} copy-done((bf16[2,1,128,1024]{3,2,1,0:T(8,128)(2,1)S(1)}, bf16[2,1,128,1024]{3,2,1,0:T(8,128)(2,1)}, u32[]{:S(2)}) %copy-start.1) | copy-done | bytes 524312
  11.9 0.7 %shard_map.112 = (bf16[2048,128]{1,0:T(8,128)(2,1)S(1)}, bf16[2048,128]{1,0:T(8,128)(2,1)S(1)}, f32[64,256]{1,0:T(8,128)S(1)}) custom-call(s32[8]{0:T(128)S(1)} %copy-done.2, bf16[2,1,128,1024]{3,2,1,0:T(8,128)(2,1)S(1)} %copy-done, bf16[2,1,128,1024]{3,2,1,0:T(8,128)(2,1)S(1)} %copy-done.1), custom_call_target="tpu_custom_call" | custom-call | flops 262144 | bytes 2097152 | tf_op jit(solution)/shard_map/pallas_call | solution.py:42
  13.8 3.6 %collective-permute-start.10 = (bf16[128,256]{1,0:T(8,128)(2,1)S(1)}, bf16[128,256]{1,0:T(8,128)(2,1)S(1)}, u32[]{:S(2)}, u32[]{:S(2)}) collective-permute-start(bf16[128,256]{1,0:T(8,128)(2,1)S(1)} %collective-permute-done.3.refs_3_), channel_id=1, source_target_pairs={{0,6},{2,4},{4,2},{6,0},{1,7},{3,5},{5,3},{7,1},{8,14},{10,12},{12... | collective-permute-start | bytes 196616 | tf_op jit(solution)/shard_map/ppermute | solution.py:275
  17.4 0.8 %collective-permute-start.9 = (bf16[128,256]{1,0:T(8,128)(2,1)S(1)}, bf16[128,256]{1,0:T(8,128)(2,1)S(1)}, u32[]{:S(2)}, u32[]{:S(2)}) collective-permute-start(bf16[128,256]{1,0:T(8,128)(2,1)S(1)} %collective-permute-done.3.refs_3_), channel_id=1, source_target_pairs={{0,4},{2,6},{4,0},{6,2},{1,5},{3,7},{5,1},{7,3},{8,12},{10,14},{12... | collective-permute-start | bytes 196616 | tf_op jit(solution)/shard_map/ppermute | solution.py:275
  18.2 3.8 %shard_map.113 = (bf16[128,1024]{1,0:T(8,128)(2,1)S(1)}, f32[512,256]{1,0:T(8,128)S(1)}, bf16[512,256]{1,0:T(8,128)(2,1)S(1)}) custom-call(bf16[2048,128]{1,0:T(8,128)(2,1)S(1)} %get-tuple-element.55.refs_0_, bf16[2048,128]{1,0:T(8,128)(2,1)S(1)} %get-tuple-element.56.refs_1_, f32[64,256]{1,0:T(8,128)S(1)} %get-tuple-element.57.refs_2_, ...), custom_call_target="tpu_custom_call" | custom-call | flops 5368709120 | bytes 2097152 | tf_op jit(solution)/shard_map/pallas_call | solution.py:201
  22.3 1.0 %collective-permute-done.9.refs_5_ = bf16[128,256]{1,0:T(8,128)(2,1)S(1)} collective-permute-done((bf16[128,256]{1,0:T(8,128)(2,1)S(1)}, bf16[128,256]{1,0:T(8,128)(2,1)S(1)}, u32[]{:S(2)}, u32[]{:S(2)}) %collective-permute-start.9) | collective-permute-done | bytes 65568 | tf_op jit(solution)/shard_map/ppermute | solution.py:275
  23.9 0.9 %collective-permute-done.11 = bf16[512,256]{1,0:T(8,128)(2,1)S(1)} collective-permute-done((bf16[512,256]{1,0:T(8,128)(2,1)S(1)}, bf16[512,256]{1,0:T(8,128)(2,1)S(1)}, u32[]{:S(2)}, u32[]{:S(2)}) %collective-permute-start.11) | collective-permute-done | bytes 262176 | tf_op jit(solution)/shard_map/ppermute | solution.py:271
  24.9 2.5 %collective-permute-start.13 = (bf16[128,256]{1,0:T(8,128)(2,1)S(1)}, bf16[128,256]{1,0:T(8,128)(2,1)S(1)}, u32[]{:S(2)}, u32[]{:S(2)}) collective-permute-start(bf16[128,256]{1,0:T(8,128)(2,1)S(1)} %get-tuple-element.63), channel_id=1, source_target_pairs={{0,6},{2,4},{4,2},{6,0},{1,7},{3,5},{5,3},{7,1},{8,14},{10,12},{12... | collective-permute-start | bytes 196616 | tf_op jit(solution)/shard_map/ppermute | solution.py:275
  27.8 1.6 %collective-permute-start.15 = (bf16[128,256]{1,0:T(8,128)(2,1)S(1)}, bf16[128,256]{1,0:T(8,128)(2,1)S(1)}, u32[]{:S(2)}, u32[]{:S(2)}) collective-permute-start(bf16[128,256]{1,0:T(8,128)(2,1)S(1)} %get-tuple-element.65), channel_id=1, source_target_pairs={{0,2},{2,0},{4,6},{6,4},{1,3},{3,1},{5,7},{7,5},{8,10},{10,8},{12,... | collective-permute-start | bytes 196616 | tf_op jit(solution)/shard_map/ppermute | solution.py:275
  29.4 3.8 %shard_map.114 = (bf16[128,1024]{1,0:T(8,128)(2,1)S(1)}, f32[512,256]{1,0:T(8,128)S(1)}, bf16[512,256]{1,0:T(8,128)(2,1)S(1)}) custom-call(bf16[2048,128]{1,0:T(8,128)(2,1)S(1)} %get-tuple-element.55.refs_0_, bf16[2048,128]{1,0:T(8,128)(2,1)S(1)} %get-tuple-element.56.refs_1_, f32[64,256]{1,0:T(8,128)S(1)} %get-tuple-element.57.refs_2_, ...), custom_call_target="tpu_custom_call" | custom-call | flops 5368709120 | bytes 2097152 | tf_op jit(solution)/shard_map/pallas_call | solution.py:201
  33.3 0.9 %collective-permute-done.14 = bf16[128,256]{1,0:T(8,128)(2,1)S(1)} collective-permute-done((bf16[128,256]{1,0:T(8,128)(2,1)S(1)}, bf16[128,256]{1,0:T(8,128)(2,1)S(1)}, u32[]{:S(2)}, u32[]{:S(2)}) %collective-permute-start.14) | collective-permute-done | bytes 65568 | tf_op jit(solution)/shard_map/ppermute | solution.py:275
  34.9 2.5 %collective-permute-start.17 = (bf16[128,256]{1,0:T(8,128)(2,1)S(1)}, bf16[128,256]{1,0:T(8,128)(2,1)S(1)}, u32[]{:S(2)}, u32[]{:S(2)}) collective-permute-start(bf16[128,256]{1,0:T(8,128)(2,1)S(1)} %get-tuple-element.74), channel_id=1, source_target_pairs={{0,6},{2,4},{4,2},{6,0},{1,7},{3,5},{5,3},{7,1},{8,14},{10,12},{12... | collective-permute-start | bytes 196616 | tf_op jit(solution)/shard_map/ppermute | solution.py:275
  37.4 1.7 %collective-permute-start.19 = (bf16[128,256]{1,0:T(8,128)(2,1)S(1)}, bf16[128,256]{1,0:T(8,128)(2,1)S(1)}, u32[]{:S(2)}, u32[]{:S(2)}) collective-permute-start(bf16[128,256]{1,0:T(8,128)(2,1)S(1)} %get-tuple-element.76), channel_id=1, source_target_pairs={{8,16},{16,8},{24,0},{0,24},{9,17},{17,9},{25,1},{1,25},{10,18},{1... | collective-permute-start | bytes 196616 | tf_op jit(solution)/shard_map/ppermute | solution.py:284
  39.1 2.7 %collective-permute-start.20 = (bf16[128,256]{1,0:T(8,128)(2,1)S(1)}, bf16[128,256]{1,0:T(8,128)(2,1)S(1)}, u32[]{:S(2)}, u32[]{:S(2)}) collective-permute-start(bf16[128,256]{1,0:T(8,128)(2,1)S(1)} %get-tuple-element.77), channel_id=1, source_target_pairs={{0,2},{2,0},{4,6},{6,4},{1,3},{3,1},{5,7},{7,5},{8,10},{10,8},{12,... | collective-permute-start | bytes 196616 | tf_op jit(solution)/shard_map/ppermute | solution.py:275
  42.1 0.8 %maximum_bitcast_fusion = bf16[2,1,128,1024]{3,2,1,0:T(8,128)(2,1)} fusion(bf16[1,128,1024]{2,1,0:T(8,128)(2,1)S(1)} %bitcast.11, bf16[1,128,1024]{2,1,0:T(8,128)(2,1)S(1)} %bitcast.10), kind=kLoop, calls=%fused_computation | loop fusion | flops 262144 | bytes 1048576
  42.9 0.9 %collective-permute-done.18.refs_1_ = bf16[128,256]{1,0:T(8,128)(2,1)S(1)} collective-permute-done((bf16[128,256]{1,0:T(8,128)(2,1)S(1)}, bf16[128,256]{1,0:T(8,128)(2,1)S(1)}, u32[]{:S(2)}, u32[]{:S(2)}) %collective-permute-start.18) | collective-permute-done | bytes 65568 | tf_op jit(solution)/shard_map/ppermute | solution.py:275
  43.8 0.9 %collective-permute-done.20.refs_3_ = bf16[128,256]{1,0:T(8,128)(2,1)S(1)} collective-permute-done((bf16[128,256]{1,0:T(8,128)(2,1)S(1)}, bf16[128,256]{1,0:T(8,128)(2,1)S(1)}, u32[]{:S(2)}, u32[]{:S(2)}) %collective-permute-start.20) | collective-permute-done | bytes 65568 | tf_op jit(solution)/shard_map/ppermute | solution.py:275
  44.7 1.4 %collective-permute-done.21.refs_4_ = bf16[128,256]{1,0:T(8,128)(2,1)S(1)} collective-permute-done((bf16[128,256]{1,0:T(8,128)(2,1)S(1)}, bf16[128,256]{1,0:T(8,128)(2,1)S(1)}, u32[]{:S(2)}, u32[]{:S(2)}) %collective-permute-start.21) | collective-permute-done | bytes 65568 | tf_op jit(solution)/shard_map/ppermute | solution.py:284
  46.1 0.7 %shard_map.115 = (f32[2,1,128,128]{3,2,1,0:T(8,128)}, f32[2,1,128,128]{3,2,1,0:T(8,128)}) custom-call(f32[128,256]{1,0:T(8,128)S(1)} %fusion.2.first_ref, f32[128,256]{1,0:T(8,128)S(1)} %slice.50.own_ref, bf16[128,256]{1,0:T(8,128)(2,1)S(1)} %collective-permute-done.17.refs_0_, bf16[128,256]{1,0:T(8,128)(2,1)S(1)} %collective-permute-done.18.refs_1_, ...), custom_call_target="tpu_custom_call" | custom-call | flops 163840 | bytes 524288 | tf_op jit(solution)/shard_map/pallas_call | solution.py:252
  (43 shorter events, 3.4 us)
Async XLA Ops:
  1.5 8.4 %copy-start.2 = (s32[8]{0:T(128)S(1)}, s32[8]{0:T(128)}, u32[]{:S(2)}) copy-start(s32[8]{0:T(128)} %order_ref.1) | copy-start | bytes 100
  1.5 11.2 %collective-permute-start = (bf16[128,256]{1,0:T(8,128)(2,1)S(1)}, bf16[128,256]{1,0:T(8,128)(2,1)S(1)}, u32[]{:S(2)}, u32[]{:S(2)}) collective-permute-start(bf16[128,256]{1,0:T(8,128)(2,1)S(1)} %get-tuple-element.97.refs_3_), channel_id=1, source_target_pairs={{0,2},{2,0},{4,6},{6,4},{1,3},{3,1},{5,7},{7,5},{8,10},{10,8},{12,... | collective-permute-start | bytes 196616 | tf_op jit(solution)/shard_map/ppermute | solution.py:275
  4.6 8.1 %collective-permute-start.1 = (bf16[128,256]{1,0:T(8,128)(2,1)S(1)}, bf16[128,256]{1,0:T(8,128)(2,1)S(1)}, u32[]{:S(2)}, u32[]{:S(2)}) collective-permute-start(bf16[128,256]{1,0:T(8,128)(2,1)S(1)} %get-tuple-element.97.refs_3_), channel_id=1, source_target_pairs={{0,4},{2,6},{4,0},{6,2},{1,5},{3,7},{5,1},{7,3},{8,12},{10,14},{12... | collective-permute-start | bytes 196616 | tf_op jit(solution)/shard_map/ppermute | solution.py:275
  7.2 6.1 %collective-permute-start.2 = (bf16[128,256]{1,0:T(8,128)(2,1)S(1)}, bf16[128,256]{1,0:T(8,128)(2,1)S(1)}, u32[]{:S(2)}, u32[]{:S(2)}) collective-permute-start(bf16[128,256]{1,0:T(8,128)(2,1)S(1)} %get-tuple-element.97.refs_3_), channel_id=1, source_target_pairs={{0,6},{2,4},{4,2},{6,0},{1,7},{3,5},{5,3},{7,1},{8,14},{10,12},{12... | collective-permute-start | bytes 196616 | tf_op jit(solution)/shard_map/ppermute | solution.py:275
  7.2 6.1 %collective-permute-start.3 = (bf16[128,256]{1,0:T(8,128)(2,1)S(1)}, bf16[128,256]{1,0:T(8,128)(2,1)S(1)}, u32[]{:S(2)}, u32[]{:S(2)}) collective-permute-start(bf16[128,256]{1,0:T(8,128)(2,1)S(1)} %get-tuple-element.96), channel_id=1, source_target_pairs={{0,24},{8,0},{16,8},{24,16},{1,25},{9,1},{17,9},{25,17},{2,26},{10... | collective-permute-start | bytes 196616 | tf_op jit(solution)/shard_map/ppermute | solution.py:311
  9.8 7.6 %collective-permute-start.4 = (bf16[128,256]{1,0:T(8,128)(2,1)S(1)}, bf16[128,256]{1,0:T(8,128)(2,1)S(1)}, u32[]{:S(2)}, u32[]{:S(2)}) collective-permute-start(bf16[128,256]{1,0:T(8,128)(2,1)S(1)} %get-tuple-element.97.refs_3_), channel_id=1, source_target_pairs={{0,1},{1,0},{2,3},{3,2},{4,5},{5,4},{6,7},{7,6},{8,9},{9,8},{10,11... | collective-permute-start | bytes 196616 | tf_op jit(solution)/shard_map/ppermute | solution.py:271
  13.2 4.2 %collective-permute-start.5 = (bf16[128,256]{1,0:T(8,128)(2,1)S(1)}, bf16[128,256]{1,0:T(8,128)(2,1)S(1)}, u32[]{:S(2)}, u32[]{:S(2)}) collective-permute-start(bf16[128,256]{1,0:T(8,128)(2,1)S(1)} %collective-permute-done.refs_4_), channel_id=1, source_target_pairs={{0,1},{1,0},{2,3},{3,2},{4,5},{5,4},{6,7},{7,6},{8,9},{9,8},{10,11... | collective-permute-start | bytes 196616 | tf_op jit(solution)/shard_map/ppermute | solution.py:271
  13.3 4.9 %collective-permute-start.6 = (bf16[128,256]{1,0:T(8,128)(2,1)S(1)}, bf16[128,256]{1,0:T(8,128)(2,1)S(1)}, u32[]{:S(2)}, u32[]{:S(2)}) collective-permute-start(bf16[128,256]{1,0:T(8,128)(2,1)S(1)} %collective-permute-done.1.refs_5_), channel_id=1, source_target_pairs={{0,1},{1,0},{2,3},{3,2},{4,5},{5,4},{6,7},{7,6},{8,9},{9,8},{10,11... | collective-permute-start | bytes 196616 | tf_op jit(solution)/shard_map/ppermute | solution.py:271
  13.8 4.4 %collective-permute-start.7 = (bf16[128,256]{1,0:T(8,128)(2,1)S(1)}, bf16[128,256]{1,0:T(8,128)(2,1)S(1)}, u32[]{:S(2)}, u32[]{:S(2)}) collective-permute-start(bf16[128,256]{1,0:T(8,128)(2,1)S(1)} %collective-permute-done.2.refs_6_), channel_id=1, source_target_pairs={{0,1},{1,0},{2,3},{3,2},{4,5},{5,4},{6,7},{7,6},{8,9},{9,8},{10,11... | collective-permute-start | bytes 196616 | tf_op jit(solution)/shard_map/ppermute | solution.py:271
  13.8 8.2 %collective-permute-start.10 = (bf16[128,256]{1,0:T(8,128)(2,1)S(1)}, bf16[128,256]{1,0:T(8,128)(2,1)S(1)}, u32[]{:S(2)}, u32[]{:S(2)}) collective-permute-start(bf16[128,256]{1,0:T(8,128)(2,1)S(1)} %collective-permute-done.3.refs_3_), channel_id=1, source_target_pairs={{0,6},{2,4},{4,2},{6,0},{1,7},{3,5},{5,3},{7,1},{8,14},{10,12},{12... | collective-permute-start | bytes 196616 | tf_op jit(solution)/shard_map/ppermute | solution.py:275
  17.4 4.9 %collective-permute-start.8 = (bf16[128,256]{1,0:T(8,128)(2,1)S(1)}, bf16[128,256]{1,0:T(8,128)(2,1)S(1)}, u32[]{:S(2)}, u32[]{:S(2)}) collective-permute-start(bf16[128,256]{1,0:T(8,128)(2,1)S(1)} %collective-permute-done.3.refs_3_), channel_id=1, source_target_pairs={{0,2},{2,0},{4,6},{6,4},{1,3},{3,1},{5,7},{7,5},{8,10},{10,8},{12,... | collective-permute-start | bytes 196616 | tf_op jit(solution)/shard_map/ppermute | solution.py:275
  17.4 5.9 %collective-permute-start.9 = (bf16[128,256]{1,0:T(8,128)(2,1)S(1)}, bf16[128,256]{1,0:T(8,128)(2,1)S(1)}, u32[]{:S(2)}, u32[]{:S(2)}) collective-permute-start(bf16[128,256]{1,0:T(8,128)(2,1)S(1)} %collective-permute-done.3.refs_3_), channel_id=1, source_target_pairs={{0,4},{2,6},{4,0},{6,2},{1,5},{3,7},{5,1},{7,3},{8,12},{10,14},{12... | collective-permute-start | bytes 196616 | tf_op jit(solution)/shard_map/ppermute | solution.py:275
  23.3 1.5 %collective-permute-start.11 = (bf16[512,256]{1,0:T(8,128)(2,1)S(1)}, bf16[512,256]{1,0:T(8,128)(2,1)S(1)}, u32[]{:S(2)}, u32[]{:S(2)}) collective-permute-start(bf16[512,256]{1,0:T(8,128)(2,1)S(1)} %get-tuple-element.54), channel_id=1, source_target_pairs={{0,1},{1,0},{2,3},{3,2},{4,5},{5,4},{6,7},{7,6},{8,9},{9,8},{10,11... | collective-permute-start | bytes 786440 | tf_op jit(solution)/shard_map/ppermute | solution.py:271
  23.3 6.1 %collective-permute-start.12 = (bf16[512,256]{1,0:T(8,128)(2,1)S(1)}, bf16[512,256]{1,0:T(8,128)(2,1)S(1)}, u32[]{:S(2)}, u32[]{:S(2)}) collective-permute-start(bf16[512,256]{1,0:T(8,128)(2,1)S(1)} %pad_maximum_fusion), channel_id=1, source_target_pairs={{0,1},{1,0},{2,3},{3,2},{4,5},{5,4},{6,7},{7,6},{8,9},{9,8},{10,11... | collective-permute-start | bytes 786440 | tf_op jit(solution)/shard_map/ppermute | solution.py:271
  24.9 8.4 %collective-permute-start.13 = (bf16[128,256]{1,0:T(8,128)(2,1)S(1)}, bf16[128,256]{1,0:T(8,128)(2,1)S(1)}, u32[]{:S(2)}, u32[]{:S(2)}) collective-permute-start(bf16[128,256]{1,0:T(8,128)(2,1)S(1)} %get-tuple-element.63), channel_id=1, source_target_pairs={{0,6},{2,4},{4,2},{6,0},{1,7},{3,5},{5,3},{7,1},{8,14},{10,12},{12... | collective-permute-start | bytes 196616 | tf_op jit(solution)/shard_map/ppermute | solution.py:275
  27.4 6.8 %collective-permute-start.14 = (bf16[128,256]{1,0:T(8,128)(2,1)S(1)}, bf16[128,256]{1,0:T(8,128)(2,1)S(1)}, u32[]{:S(2)}, u32[]{:S(2)}) collective-permute-start(bf16[128,256]{1,0:T(8,128)(2,1)S(1)} %get-tuple-element.64), channel_id=1, source_target_pairs={{0,4},{2,6},{4,0},{6,2},{1,5},{3,7},{5,1},{7,3},{8,12},{10,14},{12... | collective-permute-start | bytes 196616 | tf_op jit(solution)/shard_map/ppermute | solution.py:275
  27.8 6.5 %collective-permute-start.15 = (bf16[128,256]{1,0:T(8,128)(2,1)S(1)}, bf16[128,256]{1,0:T(8,128)(2,1)S(1)}, u32[]{:S(2)}, u32[]{:S(2)}) collective-permute-start(bf16[128,256]{1,0:T(8,128)(2,1)S(1)} %get-tuple-element.65), channel_id=1, source_target_pairs={{0,2},{2,0},{4,6},{6,4},{1,3},{3,1},{5,7},{7,5},{8,10},{10,8},{12,... | collective-permute-start | bytes 196616 | tf_op jit(solution)/shard_map/ppermute | solution.py:275
  29.4 4.8 %copy-start.4 = (f32[1,128,128]{2,1,0:T(8,128)S(1)}, f32[1,128,128]{2,1,0:T(8,128)}, u32[]{:S(2)}) copy-start(f32[1,128,128]{2,1,0:T(8,128)} %param.15) | copy-start | bytes 196612
  33.2 1.6 %collective-permute-start.16 = (bf16[512,256]{1,0:T(8,128)(2,1)S(1)}, bf16[512,256]{1,0:T(8,128)(2,1)S(1)}, u32[]{:S(2)}, u32[]{:S(2)}) collective-permute-start(bf16[512,256]{1,0:T(8,128)(2,1)S(1)} %get-tuple-element.66), channel_id=1, source_target_pairs={{0,1},{1,0},{2,3},{3,2},{4,5},{5,4},{6,7},{7,6},{8,9},{9,8},{10,11... | collective-permute-start | bytes 786440 | tf_op jit(solution)/shard_map/ppermute | solution.py:271
  34.9 8.0 %collective-permute-start.17 = (bf16[128,256]{1,0:T(8,128)(2,1)S(1)}, bf16[128,256]{1,0:T(8,128)(2,1)S(1)}, u32[]{:S(2)}, u32[]{:S(2)}) collective-permute-start(bf16[128,256]{1,0:T(8,128)(2,1)S(1)} %get-tuple-element.74), channel_id=1, source_target_pairs={{0,6},{2,4},{4,2},{6,0},{1,7},{3,5},{5,3},{7,1},{8,14},{10,12},{12... | collective-permute-start | bytes 196616 | tf_op jit(solution)/shard_map/ppermute | solution.py:275
  37.4 6.4 %collective-permute-start.18 = (bf16[128,256]{1,0:T(8,128)(2,1)S(1)}, bf16[128,256]{1,0:T(8,128)(2,1)S(1)}, u32[]{:S(2)}, u32[]{:S(2)}) collective-permute-start(bf16[128,256]{1,0:T(8,128)(2,1)S(1)} %get-tuple-element.75), channel_id=1, source_target_pairs={{0,4},{2,6},{4,0},{6,2},{1,5},{3,7},{5,1},{7,3},{8,12},{10,14},{12... | collective-permute-start | bytes 196616 | tf_op jit(solution)/shard_map/ppermute | solution.py:275
  37.4 6.4 %collective-permute-start.19 = (bf16[128,256]{1,0:T(8,128)(2,1)S(1)}, bf16[128,256]{1,0:T(8,128)(2,1)S(1)}, u32[]{:S(2)}, u32[]{:S(2)}) collective-permute-start(bf16[128,256]{1,0:T(8,128)(2,1)S(1)} %get-tuple-element.76), channel_id=1, source_target_pairs={{8,16},{16,8},{24,0},{0,24},{9,17},{17,9},{25,1},{1,25},{10,18},{1... | collective-permute-start | bytes 196616 | tf_op jit(solution)/shard_map/ppermute | solution.py:284
  39.1 5.6 %collective-permute-start.20 = (bf16[128,256]{1,0:T(8,128)(2,1)S(1)}, bf16[128,256]{1,0:T(8,128)(2,1)S(1)}, u32[]{:S(2)}, u32[]{:S(2)}) collective-permute-start(bf16[128,256]{1,0:T(8,128)(2,1)S(1)} %get-tuple-element.77), channel_id=1, source_target_pairs={{0,2},{2,0},{4,6},{6,4},{1,3},{3,1},{5,7},{7,5},{8,10},{10,8},{12,... | collective-permute-start | bytes 196616 | tf_op jit(solution)/shard_map/ppermute | solution.py:275
  41.8 4.3 %collective-permute-start.21 = (bf16[128,256]{1,0:T(8,128)(2,1)S(1)}, bf16[128,256]{1,0:T(8,128)(2,1)S(1)}, u32[]{:S(2)}, u32[]{:S(2)}) collective-permute-start(bf16[128,256]{1,0:T(8,128)(2,1)S(1)} %get-tuple-element.78), channel_id=1, source_target_pairs={{0,8},{8,0},{16,24},{24,16},{1,9},{9,1},{17,25},{25,17},{2,10},{10... | collective-permute-start | bytes 196616 | tf_op jit(solution)/shard_map/ppermute | solution.py:284
  (3 other events, 6.9 us)

commit v9 on v6

--- a/solution.py
+++ b/solution.py
@@ -274,7 +274,11 @@
     far = [own_far] + [other_core(block) for block in near]
     next_near = [across_chips(next_pair, k) for k in partners][::-1]
     first_query, near_terms, far_terms = attend_back(0, queries, stacks, [own_pair, *near, *far])
-    far_terms, next_near = lax.optimization_barrier((far_terms, [next_pair, *next_near]))
+    *others, farthest = next_near
+    far_terms, others, farthest, next_pair = lax.optimization_barrier(
+        (far_terms, others[::-1], farthest, next_pair)
+    )
+    next_near = [next_pair, *others[::-1], farthest]
     next_kv = [*next_near, other_core(jnp.concatenate(next_near, axis=0))]
 
     def chip_sums(near_terms, far_terms):
@@ -294,13 +298,13 @@
     )
     second_query, near_terms, far_terms = attend_back(1, queries, stacks, next_kv)
     first_acc, far_terms = lax.optimization_barrier((first_acc, far_terms))
-    early_acc = section_swap(first_acc, 0)
+    early_acc = section_swap(first_acc, 1)
     own_sum, leaving = chip_sums(near_terms, far_terms)
     late_acc, leaving = lax.optimization_barrier((first_acc.astype(jnp.bfloat16), leaving))
     own_sum, queries_both = lax.optimization_barrier((own_sum, (first_query, second_query)))
     second_acc = reduced(own_sum, leaving)
-    late_acc = section_swap(late_acc, 1).astype(jnp.float32)
-    moved_acc = jnp.where(section % 2 == 0, early_acc, late_acc)
+    late_acc = section_swap(late_acc, 0).astype(jnp.float32)
+    moved_acc = jnp.where(section % 2 == 0, late_acc, early_acc)
     second_acc = second_acc + jnp.where(section == sections - 1, 0.0, moved_acc)
     query_grads = jnp.stack(queries_both, axis=0)[:, None]
     key_grads = jnp.stack([first_acc[:, :head_dim], second_acc[:, :head_dim]], axis=0)[:, None]

time: 46.7 us -> 46.4 us (level)
    ppermute x12, waiting for transfers between devices: 4.34 us -> 5.69 us  [across_chips(): lax.ppermute(block, 'z', [(chip, chip ^ k) for chip in range(lax.axis_siz...]
    ppermute x2, waiting for transfers between devices: 0.81 us -> 0.01 us  [section_swap(): return lax.ppermute(block, 'section', route)]
  transfers between devices with their start and end apart: 22 -> 22, of which waited for: 8 -> 7; matrix products, arithmetic and copies ran while one was open for 2% -> 2% of each run, Pallas kernels for 18% -> 18%
where the time goes in v9:
time: 46.4 us; the launch traced here: 46.1 us
  starting transfers between devices  25.5 us (55%)
  Pallas kernels  8.34 us (18%)
  waiting for transfers between devices  6.65 us (14%)
  other arithmetic  2.65 us (6%)
  local copies, waits for them, and re-layouts  2.16 us (5%)
  between operations  0.84 us (2%)
    ppermute x12, starting transfers between devices, across_chips(): lax.ppermute(block, 'z', [(chip, chip ^ k) for chip in range(lax.axis_siz...  19 us
    pallas_call x2, Pallas kernels, attend_back(): pl.pallas_call(kernel, out_shape=(jax.ShapeDtypeStruct((local_rows, model...  7.61 us
    ppermute x12, waiting for transfers between devices, across_chips(): lax.ppermute(block, 'z', [(chip, chip ^ k) for chip in range(lax.axis_siz...  5.69 us
    ppermute x1, starting transfers between devices, body(): lax.ppermute(leaving_pair, 'section', [(i, (i - 1) % sections) for i in r...  2.67 us
    ppermute x2, starting transfers between devices, section_swap(): return lax.ppermute(block, 'section', route)  2.66 us
    unnamed x10, local copies, waits for them, and re-layouts  2.1 us
    unnamed x2, other arithmetic  1.56 us
    ppermute x7, starting transfers between devices, other_core(): return lax.ppermute(block, 'core', [(0, 1), (1, 0)])  1.2 us
  transfers between devices with their start and end apart: 22, of which 7 were waited for; matrix products, arithmetic and copies ran while one was open for 2% of the time, Pallas kernels for 18%

profile of v9, /device:TPU:0, one launch (start us, length us, event | category | flops | bytes accessed | tf_op | source)
XLA Modules:
  0.0 46.1 jit_solution(4163459403713721714)
XLA Ops:
  0.6 0.8 %maximum_select_fusion = (bf16[128,256]{1,0:T(8,128)(2,1)S(1)}, bf16[128,256]{1,0:T(8,128)(2,1)S(1)}) fusion(bf16[128,128]{1,0:T(8,128)(2,1)} %param.14, bf16[128,128]{1,0:T(8,128)(2,1)} %param.13, pred[]{:T(512)S(6)} %eq.11, bf16[128,128]{1,0:T(8,128)(2,1)} %bitcast.30, bf16[128,128]{1,0:T(8,128)(2,1)} %bitcast.31), kind=kLoop, calls=%fused_computation.14 | loop fusion | flops 294912 | bytes 262145 | tf_op jit(solution)/shard_map/jit(_where)/select_n | solution.py:264
  1.5 3.1 %collective-permute-start = (bf16[128,256]{1,0:T(8,128)(2,1)S(1)}, bf16[128,256]{1,0:T(8,128)(2,1)S(1)}, u32[]{:S(2)}, u32[]{:S(2)}) collective-permute-start(bf16[128,256]{1,0:T(8,128)(2,1)S(1)} %get-tuple-element.93.refs_3_), channel_id=1, source_target_pairs={{0,2},{2,0},{4,6},{6,4},{1,3},{3,1},{5,7},{7,5},{8,10},{10,8},{12,... | collective-permute-start | bytes 196616 | tf_op jit(solution)/shard_map/ppermute | solution.py:233
  4.6 2.6 %collective-permute-start.1 = (bf16[128,256]{1,0:T(8,128)(2,1)S(1)}, bf16[128,256]{1,0:T(8,128)(2,1)S(1)}, u32[]{:S(2)}, u32[]{:S(2)}) collective-permute-start(bf16[128,256]{1,0:T(8,128)(2,1)S(1)} %get-tuple-element.93.refs_3_), channel_id=1, source_target_pairs={{0,4},{2,6},{4,0},{6,2},{1,5},{3,7},{5,1},{7,3},{8,12},{10,14},{12... | collective-permute-start | bytes 196616 | tf_op jit(solution)/shard_map/ppermute | solution.py:233
  7.2 2.7 %collective-permute-start.3 = (bf16[128,256]{1,0:T(8,128)(2,1)S(1)}, bf16[128,256]{1,0:T(8,128)(2,1)S(1)}, u32[]{:S(2)}, u32[]{:S(2)}) collective-permute-start(bf16[128,256]{1,0:T(8,128)(2,1)S(1)} %get-tuple-element.92), channel_id=1, source_target_pairs={{0,24},{8,0},{16,8},{24,16},{1,25},{9,1},{17,9},{25,17},{2,26},{10... | collective-permute-start | bytes 196616 | tf_op jit(solution)/shard_map/ppermute | solution.py:269
  9.8 1.0 %copy-done = bf16[2,1,128,1024]{3,2,1,0:T(8,128)(2,1)S(1)} copy-done((bf16[2,1,128,1024]{3,2,1,0:T(8,128)(2,1)S(1)}, bf16[2,1,128,1024]{3,2,1,0:T(8,128)(2,1)}, u32[]{:S(2)}) %copy-start) | copy-done | bytes 524312
  10.9 1.0 %copy-done.1 = bf16[2,1,128,1024]{3,2,1,0:T(8,128)(2,1)S(1)} copy-done((bf16[2,1,128,1024]{3,2,1,0:T(8,128)(2,1)S(1)}, bf16[2,1,128,1024]{3,2,1,0:T(8,128)(2,1)}, u32[]{:S(2)}) %copy-start.1) | copy-done | bytes 524312
  11.9 0.7 %shard_map.112 = (bf16[2048,128]{1,0:T(8,128)(2,1)S(1)}, bf16[2048,128]{1,0:T(8,128)(2,1)S(1)}, f32[64,256]{1,0:T(8,128)S(1)}) custom-call(s32[8]{0:T(128)S(1)} %copy-done.2, bf16[2,1,128,1024]{3,2,1,0:T(8,128)(2,1)S(1)} %copy-done, bf16[2,1,128,1024]{3,2,1,0:T(8,128)(2,1)S(1)} %copy-done.1), custom_call_target="tpu_custom_call" | custom-call | flops 262144 | bytes 2097152 | tf_op jit(solution)/shard_map/pallas_call | solution.py:42
  13.8 3.6 %collective-permute-start.10 = (bf16[128,256]{1,0:T(8,128)(2,1)S(1)}, bf16[128,256]{1,0:T(8,128)(2,1)S(1)}, u32[]{:S(2)}, u32[]{:S(2)}) collective-permute-start(bf16[128,256]{1,0:T(8,128)(2,1)S(1)} %collective-permute-done.3.refs_3_), channel_id=1, source_target_pairs={{0,6},{2,4},{4,2},{6,0},{1,7},{3,5},{5,3},{7,1},{8,14},{10,12},{12... | collective-permute-start | bytes 196616 | tf_op jit(solution)/shard_map/ppermute | solution.py:233
  17.4 0.8 %collective-permute-start.9 = (bf16[128,256]{1,0:T(8,128)(2,1)S(1)}, bf16[128,256]{1,0:T(8,128)(2,1)S(1)}, u32[]{:S(2)}, u32[]{:S(2)}) collective-permute-start(bf16[128,256]{1,0:T(8,128)(2,1)S(1)} %collective-permute-done.3.refs_3_), channel_id=1, source_target_pairs={{0,2},{2,0},{4,6},{6,4},{1,3},{3,1},{5,7},{7,5},{8,10},{10,8},{12,... | collective-permute-start | bytes 196616 | tf_op jit(solution)/shard_map/ppermute | solution.py:233
  18.2 3.8 %shard_map.113 = (bf16[128,1024]{1,0:T(8,128)(2,1)S(1)}, f32[512,256]{1,0:T(8,128)S(1)}, bf16[512,256]{1,0:T(8,128)(2,1)S(1)}) custom-call(bf16[2048,128]{1,0:T(8,128)(2,1)S(1)} %get-tuple-element.52.refs_0_, bf16[2048,128]{1,0:T(8,128)(2,1)S(1)} %get-tuple-element.53.refs_1_, f32[64,256]{1,0:T(8,128)S(1)} %get-tuple-element.54.refs_2_, ...), custom_call_target="tpu_custom_call" | custom-call | flops 5368709120 | bytes 2097152 | tf_op jit(solution)/shard_map/pallas_call | solution.py:201
  22.0 1.0 %collective-permute-done.8.refs_5_ = bf16[128,256]{1,0:T(8,128)(2,1)S(1)} collective-permute-done((bf16[128,256]{1,0:T(8,128)(2,1)S(1)}, bf16[128,256]{1,0:T(8,128)(2,1)S(1)}, u32[]{:S(2)}, u32[]{:S(2)}) %collective-permute-start.8) | collective-permute-done | bytes 65568 | tf_op jit(solution)/shard_map/ppermute | solution.py:233
  23.1 0.6 %collective-permute-start.12 = (bf16[512,256]{1,0:T(8,128)(2,1)S(1)}, bf16[512,256]{1,0:T(8,128)(2,1)S(1)}, u32[]{:S(2)}, u32[]{:S(2)}) collective-permute-start(bf16[512,256]{1,0:T(8,128)(2,1)S(1)} %pad_maximum_fusion), channel_id=1, source_target_pairs={{0,1},{1,0},{2,3},{3,2},{4,5},{5,4},{6,7},{7,6},{8,9},{9,8},{10,11... | collective-permute-start | bytes 786440 | tf_op jit(solution)/shard_map/ppermute | solution.py:229
  23.7 0.9 %collective-permute-done.11 = bf16[512,256]{1,0:T(8,128)(2,1)S(1)} collective-permute-done((bf16[512,256]{1,0:T(8,128)(2,1)S(1)}, bf16[512,256]{1,0:T(8,128)(2,1)S(1)}, u32[]{:S(2)}, u32[]{:S(2)}) %collective-permute-start.11) | collective-permute-done | bytes 262176 | tf_op jit(solution)/shard_map/ppermute | solution.py:229
  24.8 2.7 %collective-permute-start.13 = (bf16[128,256]{1,0:T(8,128)(2,1)S(1)}, bf16[128,256]{1,0:T(8,128)(2,1)S(1)}, u32[]{:S(2)}, u32[]{:S(2)}) collective-permute-start(bf16[128,256]{1,0:T(8,128)(2,1)S(1)} %get-tuple-element.60), channel_id=1, source_target_pairs={{0,6},{2,4},{4,2},{6,0},{1,7},{3,5},{5,3},{7,1},{8,14},{10,12},{12... | collective-permute-start | bytes 196616 | tf_op jit(solution)/shard_map/ppermute | solution.py:233
  27.5 1.7 %collective-permute-start.15 = (bf16[128,256]{1,0:T(8,128)(2,1)S(1)}, bf16[128,256]{1,0:T(8,128)(2,1)S(1)}, u32[]{:S(2)}, u32[]{:S(2)}) collective-permute-start(bf16[128,256]{1,0:T(8,128)(2,1)S(1)} %get-tuple-element.62), channel_id=1, source_target_pairs={{0,2},{2,0},{4,6},{6,4},{1,3},{3,1},{5,7},{7,5},{8,10},{10,8},{12,... | collective-permute-start | bytes 196616 | tf_op jit(solution)/shard_map/ppermute | solution.py:233
  29.2 3.8 %shard_map.114 = (bf16[128,1024]{1,0:T(8,128)(2,1)S(1)}, f32[512,256]{1,0:T(8,128)S(1)}, bf16[512,256]{1,0:T(8,128)(2,1)S(1)}) custom-call(bf16[2048,128]{1,0:T(8,128)(2,1)S(1)} %get-tuple-element.52.refs_0_, bf16[2048,128]{1,0:T(8,128)(2,1)S(1)} %get-tuple-element.53.refs_1_, f32[64,256]{1,0:T(8,128)S(1)} %get-tuple-element.54.refs_2_, ...), custom_call_target="tpu_custom_call" | custom-call | flops 5368709120 | bytes 2097152 | tf_op jit(solution)/shard_map/pallas_call | solution.py:201
  33.0 0.9 %collective-permute-done.14 = bf16[128,256]{1,0:T(8,128)(2,1)S(1)} collective-permute-done((bf16[128,256]{1,0:T(8,128)(2,1)S(1)}, bf16[128,256]{1,0:T(8,128)(2,1)S(1)}, u32[]{:S(2)}, u32[]{:S(2)}) %collective-permute-start.14) | collective-permute-done | bytes 65568 | tf_op jit(solution)/shard_map/ppermute | solution.py:233
  34.1 2.2 %collective-permute-start.21 = (f32[128,256]{1,0:T(8,128)S(1)}, f32[128,256]{1,0:T(8,128)S(1)}, u32[]{:S(2)}, u32[]{:S(2)}) collective-permute-start(f32[128,256]{1,0:T(8,128)S(1)} %fusion.2), channel_id=1, source_target_pairs={{8,16},{16,8},{24,0},{0,24},{9,17},{17,9},{25,1},{1,25},{10,18},{1... | collective-permute-start | bytes 393224 | tf_op jit(solution)/shard_map/ppermute | solution.py:242
  36.5 2.4 %collective-permute-start.17 = (bf16[128,256]{1,0:T(8,128)(2,1)S(1)}, bf16[128,256]{1,0:T(8,128)(2,1)S(1)}, u32[]{:S(2)}, u32[]{:S(2)}) collective-permute-start(bf16[128,256]{1,0:T(8,128)(2,1)S(1)} %get-tuple-element.71), channel_id=1, source_target_pairs={{0,6},{2,4},{4,2},{6,0},{1,7},{3,5},{5,3},{7,1},{8,14},{10,12},{12... | collective-permute-start | bytes 196616 | tf_op jit(solution)/shard_map/ppermute | solution.py:233
  38.8 2.1 %collective-permute-start.19 = (bf16[128,256]{1,0:T(8,128)(2,1)S(1)}, bf16[128,256]{1,0:T(8,128)(2,1)S(1)}, u32[]{:S(2)}, u32[]{:S(2)}) collective-permute-start(bf16[128,256]{1,0:T(8,128)(2,1)S(1)} %get-tuple-element.73), channel_id=1, source_target_pairs={{0,2},{2,0},{4,6},{6,4},{1,3},{3,1},{5,7},{7,5},{8,10},{10,8},{12,... | collective-permute-start | bytes 196616 | tf_op jit(solution)/shard_map/ppermute | solution.py:233
  41.4 0.8 %maximum_bitcast_fusion = bf16[2,1,128,1024]{3,2,1,0:T(8,128)(2,1)} fusion(bf16[1,128,1024]{2,1,0:T(8,128)(2,1)S(1)} %bitcast.27, bf16[1,128,1024]{2,1,0:T(8,128)(2,1)S(1)} %bitcast.26), kind=kLoop, calls=%fused_computation | loop fusion | flops 262144 | bytes 1048576
  42.2 1.1 %collective-permute-done.17 = bf16[128,256]{1,0:T(8,128)(2,1)S(1)} collective-permute-done((bf16[128,256]{1,0:T(8,128)(2,1)S(1)}, bf16[128,256]{1,0:T(8,128)(2,1)S(1)}, u32[]{:S(2)}, u32[]{:S(2)}) %collective-permute-start.17) | collective-permute-done | bytes 65568 | tf_op jit(solution)/shard_map/ppermute | solution.py:233
  43.3 2.0 %collective-permute-done.18 = bf16[128,256]{1,0:T(8,128)(2,1)S(1)} collective-permute-done((bf16[128,256]{1,0:T(8,128)(2,1)S(1)}, bf16[128,256]{1,0:T(8,128)(2,1)S(1)}, u32[]{:S(2)}, u32[]{:S(2)}) %collective-permute-start.18) | collective-permute-done | bytes 65568 | tf_op jit(solution)/shard_map/ppermute | solution.py:233
  45.4 0.7 %maximum_bitcast_fusion.1 = (f32[2,1,128,128]{3,2,1,0:T(8,128)}, f32[2,1,128,128]{3,2,1,0:T(8,128)}) fusion(f32[1,128,128]{2,1,0:T(8,128)S(1)} %get-tuple-element.91, f32[1,128,128]{2,1,0:T(8,128)S(1)} %get-tuple-element.89, f32[1,128,128]{2,1,0:T(8,128)S(1)} %get-tuple-element.90, f32[1,128,128]{2,1,0:T(8,128)S(1)} %get-tuple-element.88), kind=kLoop, calls=%fused_computation.8 | loop fusion | flops 65536 | bytes 524288
  (47 shorter events, 2.2 us)
Async XLA Ops:
  1.5 11.2 %collective-permute-start = (bf16[128,256]{1,0:T(8,128)(2,1)S(1)}, bf16[128,256]{1,0:T(8,128)(2,1)S(1)}, u32[]{:S(2)}, u32[]{:S(2)}) collective-permute-start(bf16[128,256]{1,0:T(8,128)(2,1)S(1)} %get-tuple-element.93.refs_3_), channel_id=1, source_target_pairs={{0,2},{2,0},{4,6},{6,4},{1,3},{3,1},{5,7},{7,5},{8,10},{10,8},{12,... | collective-permute-start | bytes 196616 | tf_op jit(solution)/shard_map/ppermute | solution.py:233
  4.6 8.1 %collective-permute-start.1 = (bf16[128,256]{1,0:T(8,128)(2,1)S(1)}, bf16[128,256]{1,0:T(8,128)(2,1)S(1)}, u32[]{:S(2)}, u32[]{:S(2)}) collective-permute-start(bf16[128,256]{1,0:T(8,128)(2,1)S(1)} %get-tuple-element.93.refs_3_), channel_id=1, source_target_pairs={{0,4},{2,6},{4,0},{6,2},{1,5},{3,7},{5,1},{7,3},{8,12},{10,14},{12... | collective-permute-start | bytes 196616 | tf_op jit(solution)/shard_map/ppermute | solution.py:233
  7.2 6.1 %collective-permute-start.2 = (bf16[128,256]{1,0:T(8,128)(2,1)S(1)}, bf16[128,256]{1,0:T(8,128)(2,1)S(1)}, u32[]{:S(2)}, u32[]{:S(2)}) collective-permute-start(bf16[128,256]{1,0:T(8,128)(2,1)S(1)} %get-tuple-element.93.refs_3_), channel_id=1, source_target_pairs={{0,6},{2,4},{4,2},{6,0},{1,7},{3,5},{5,3},{7,1},{8,14},{10,12},{12... | collective-permute-start | bytes 196616 | tf_op jit(solution)/shard_map/ppermute | solution.py:233
  7.2 6.1 %collective-permute-start.3 = (bf16[128,256]{1,0:T(8,128)(2,1)S(1)}, bf16[128,256]{1,0:T(8,128)(2,1)S(1)}, u32[]{:S(2)}, u32[]{:S(2)}) collective-permute-start(bf16[128,256]{1,0:T(8,128)(2,1)S(1)} %get-tuple-element.92), channel_id=1, source_target_pairs={{0,24},{8,0},{16,8},{24,16},{1,25},{9,1},{17,9},{25,17},{2,26},{10... | collective-permute-start | bytes 196616 | tf_op jit(solution)/shard_map/ppermute | solution.py:269
  9.8 7.6 %collective-permute-start.4 = (bf16[128,256]{1,0:T(8,128)(2,1)S(1)}, bf16[128,256]{1,0:T(8,128)(2,1)S(1)}, u32[]{:S(2)}, u32[]{:S(2)}) collective-permute-start(bf16[128,256]{1,0:T(8,128)(2,1)S(1)} %get-tuple-element.93.refs_3_), channel_id=1, source_target_pairs={{0,1},{1,0},{2,3},{3,2},{4,5},{5,4},{6,7},{7,6},{8,9},{9,8},{10,11... | collective-permute-start | bytes 196616 | tf_op jit(solution)/shard_map/ppermute | solution.py:229
  13.2 4.2 %collective-permute-start.5 = (bf16[128,256]{1,0:T(8,128)(2,1)S(1)}, bf16[128,256]{1,0:T(8,128)(2,1)S(1)}, u32[]{:S(2)}, u32[]{:S(2)}) collective-permute-start(bf16[128,256]{1,0:T(8,128)(2,1)S(1)} %collective-permute-done.refs_4_), channel_id=1, source_target_pairs={{0,1},{1,0},{2,3},{3,2},{4,5},{5,4},{6,7},{7,6},{8,9},{9,8},{10,11... | collective-permute-start | bytes 196616 | tf_op jit(solution)/shard_map/ppermute | solution.py:229
  13.3 4.9 %collective-permute-start.6 = (bf16[128,256]{1,0:T(8,128)(2,1)S(1)}, bf16[128,256]{1,0:T(8,128)(2,1)S(1)}, u32[]{:S(2)}, u32[]{:S(2)}) collective-permute-start(bf16[128,256]{1,0:T(8,128)(2,1)S(1)} %collective-permute-done.1.refs_5_), channel_id=1, source_target_pairs={{0,1},{1,0},{2,3},{3,2},{4,5},{5,4},{6,7},{7,6},{8,9},{9,8},{10,11... | collective-permute-start | bytes 196616 | tf_op jit(solution)/shard_map/ppermute | solution.py:229
  13.8 4.4 %collective-permute-start.7 = (bf16[128,256]{1,0:T(8,128)(2,1)S(1)}, bf16[128,256]{1,0:T(8,128)(2,1)S(1)}, u32[]{:S(2)}, u32[]{:S(2)}) collective-permute-start(bf16[128,256]{1,0:T(8,128)(2,1)S(1)} %collective-permute-done.2.refs_6_), channel_id=1, source_target_pairs={{0,1},{1,0},{2,3},{3,2},{4,5},{5,4},{6,7},{7,6},{8,9},{9,8},{10,11... | collective-permute-start | bytes 196616 | tf_op jit(solution)/shard_map/ppermute | solution.py:229
  13.8 8.2 %collective-permute-start.10 = (bf16[128,256]{1,0:T(8,128)(2,1)S(1)}, bf16[128,256]{1,0:T(8,128)(2,1)S(1)}, u32[]{:S(2)}, u32[]{:S(2)}) collective-permute-start(bf16[128,256]{1,0:T(8,128)(2,1)S(1)} %collective-permute-done.3.refs_3_), channel_id=1, source_target_pairs={{0,6},{2,4},{4,2},{6,0},{1,7},{3,5},{5,3},{7,1},{8,14},{10,12},{12... | collective-permute-start | bytes 196616 | tf_op jit(solution)/shard_map/ppermute | solution.py:233
  17.4 5.6 %collective-permute-start.8 = (bf16[128,256]{1,0:T(8,128)(2,1)S(1)}, bf16[128,256]{1,0:T(8,128)(2,1)S(1)}, u32[]{:S(2)}, u32[]{:S(2)}) collective-permute-start(bf16[128,256]{1,0:T(8,128)(2,1)S(1)} %collective-permute-done.3.refs_3_), channel_id=1, source_target_pairs={{0,4},{2,6},{4,0},{6,2},{1,5},{3,7},{5,1},{7,3},{8,12},{10,14},{12... | collective-permute-start | bytes 196616 | tf_op jit(solution)/shard_map/ppermute | solution.py:233
  17.4 5.7 %collective-permute-start.9 = (bf16[128,256]{1,0:T(8,128)(2,1)S(1)}, bf16[128,256]{1,0:T(8,128)(2,1)S(1)}, u32[]{:S(2)}, u32[]{:S(2)}) collective-permute-start(bf16[128,256]{1,0:T(8,128)(2,1)S(1)} %collective-permute-done.3.refs_3_), channel_id=1, source_target_pairs={{0,2},{2,0},{4,6},{6,4},{1,3},{3,1},{5,7},{7,5},{8,10},{10,8},{12,... | collective-permute-start | bytes 196616 | tf_op jit(solution)/shard_map/ppermute | solution.py:233
  23.1 1.5 %collective-permute-start.11 = (bf16[512,256]{1,0:T(8,128)(2,1)S(1)}, bf16[512,256]{1,0:T(8,128)(2,1)S(1)}, u32[]{:S(2)}, u32[]{:S(2)}) collective-permute-start(bf16[512,256]{1,0:T(8,128)(2,1)S(1)} %get-tuple-element.51), channel_id=1, source_target_pairs={{0,1},{1,0},{2,3},{3,2},{4,5},{5,4},{6,7},{7,6},{8,9},{9,8},{10,11... | collective-permute-start | bytes 786440 | tf_op jit(solution)/shard_map/ppermute | solution.py:229
  23.1 6.1 %collective-permute-start.12 = (bf16[512,256]{1,0:T(8,128)(2,1)S(1)}, bf16[512,256]{1,0:T(8,128)(2,1)S(1)}, u32[]{:S(2)}, u32[]{:S(2)}) collective-permute-start(bf16[512,256]{1,0:T(8,128)(2,1)S(1)} %pad_maximum_fusion), channel_id=1, source_target_pairs={{0,1},{1,0},{2,3},{3,2},{4,5},{5,4},{6,7},{7,6},{8,9},{9,8},{10,11... | collective-permute-start | bytes 786440 | tf_op jit(solution)/shard_map/ppermute | solution.py:229
  24.7 9.2 %copy-start.3 = (f32[1,128,128]{2,1,0:T(8,128)S(1)}, f32[1,128,128]{2,1,0:T(8,128)}, u32[]{:S(2)}) copy-start(f32[1,128,128]{2,1,0:T(8,128)} %param.16) | copy-start | bytes 196612
  24.8 9.2 %copy-start.4 = (f32[1,128,128]{2,1,0:T(8,128)S(1)}, f32[1,128,128]{2,1,0:T(8,128)}, u32[]{:S(2)}) copy-start(f32[1,128,128]{2,1,0:T(8,128)} %param.15) | copy-start | bytes 196612
  24.8 8.3 %collective-permute-start.13 = (bf16[128,256]{1,0:T(8,128)(2,1)S(1)}, bf16[128,256]{1,0:T(8,128)(2,1)S(1)}, u32[]{:S(2)}, u32[]{:S(2)}) collective-permute-start(bf16[128,256]{1,0:T(8,128)(2,1)S(1)} %get-tuple-element.60), channel_id=1, source_target_pairs={{0,6},{2,4},{4,2},{6,0},{1,7},{3,5},{5,3},{7,1},{8,14},{10,12},{12... | collective-permute-start | bytes 196616 | tf_op jit(solution)/shard_map/ppermute | solution.py:233
  27.4 6.5 %collective-permute-start.14 = (bf16[128,256]{1,0:T(8,128)(2,1)S(1)}, bf16[128,256]{1,0:T(8,128)(2,1)S(1)}, u32[]{:S(2)}, u32[]{:S(2)}) collective-permute-start(bf16[128,256]{1,0:T(8,128)(2,1)S(1)} %get-tuple-element.61), channel_id=1, source_target_pairs={{0,4},{2,6},{4,0},{6,2},{1,5},{3,7},{5,1},{7,3},{8,12},{10,14},{12... | collective-permute-start | bytes 196616 | tf_op jit(solution)/shard_map/ppermute | solution.py:233
  27.5 6.5 %collective-permute-start.15 = (bf16[128,256]{1,0:T(8,128)(2,1)S(1)}, bf16[128,256]{1,0:T(8,128)(2,1)S(1)}, u32[]{:S(2)}, u32[]{:S(2)}) collective-permute-start(bf16[128,256]{1,0:T(8,128)(2,1)S(1)} %get-tuple-element.62), channel_id=1, source_target_pairs={{0,2},{2,0},{4,6},{6,4},{1,3},{3,1},{5,7},{7,5},{8,10},{10,8},{12,... | collective-permute-start | bytes 196616 | tf_op jit(solution)/shard_map/ppermute | solution.py:233
  34.0 2.3 %collective-permute-start.16 = (bf16[512,256]{1,0:T(8,128)(2,1)S(1)}, bf16[512,256]{1,0:T(8,128)(2,1)S(1)}, u32[]{:S(2)}, u32[]{:S(2)}) collective-permute-start(bf16[512,256]{1,0:T(8,128)(2,1)S(1)} %get-tuple-element.64), channel_id=1, source_target_pairs={{0,1},{1,0},{2,3},{3,2},{4,5},{5,4},{6,7},{7,6},{8,9},{9,8},{10,11... | collective-permute-start | bytes 786440 | tf_op jit(solution)/shard_map/ppermute | solution.py:229
  34.1 8.1 %collective-permute-start.21 = (f32[128,256]{1,0:T(8,128)S(1)}, f32[128,256]{1,0:T(8,128)S(1)}, u32[]{:S(2)}, u32[]{:S(2)}) collective-permute-start(f32[128,256]{1,0:T(8,128)S(1)} %fusion.2), channel_id=1, source_target_pairs={{8,16},{16,8},{24,0},{0,24},{9,17},{17,9},{25,1},{1,25},{10,18},{1... | collective-permute-start | bytes 393224 | tf_op jit(solution)/shard_map/ppermute | solution.py:242
  36.5 6.9 %collective-permute-start.17 = (bf16[128,256]{1,0:T(8,128)(2,1)S(1)}, bf16[128,256]{1,0:T(8,128)(2,1)S(1)}, u32[]{:S(2)}, u32[]{:S(2)}) collective-permute-start(bf16[128,256]{1,0:T(8,128)(2,1)S(1)} %get-tuple-element.71), channel_id=1, source_target_pairs={{0,6},{2,4},{4,2},{6,0},{1,7},{3,5},{5,3},{7,1},{8,14},{10,12},{12... | collective-permute-start | bytes 196616 | tf_op jit(solution)/shard_map/ppermute | solution.py:233
  38.8 6.5 %collective-permute-start.18 = (bf16[128,256]{1,0:T(8,128)(2,1)S(1)}, bf16[128,256]{1,0:T(8,128)(2,1)S(1)}, u32[]{:S(2)}, u32[]{:S(2)}) collective-permute-start(bf16[128,256]{1,0:T(8,128)(2,1)S(1)} %get-tuple-element.72), channel_id=1, source_target_pairs={{0,4},{2,6},{4,0},{6,2},{1,5},{3,7},{5,1},{7,3},{8,12},{10,14},{12... | collective-permute-start | bytes 196616 | tf_op jit(solution)/shard_map/ppermute | solution.py:233
  38.8 6.5 %collective-permute-start.19 = (bf16[128,256]{1,0:T(8,128)(2,1)S(1)}, bf16[128,256]{1,0:T(8,128)(2,1)S(1)}, u32[]{:S(2)}, u32[]{:S(2)}) collective-permute-start(bf16[128,256]{1,0:T(8,128)(2,1)S(1)} %get-tuple-element.73), channel_id=1, source_target_pairs={{0,2},{2,0},{4,6},{6,4},{1,3},{3,1},{5,7},{7,5},{8,10},{10,8},{12,... | collective-permute-start | bytes 196616 | tf_op jit(solution)/shard_map/ppermute | solution.py:233
  40.9 4.4 %collective-permute-start.20 = (bf16[128,256]{1,0:T(8,128)(2,1)S(1)}, bf16[128,256]{1,0:T(8,128)(2,1)S(1)}, u32[]{:S(2)}, u32[]{:S(2)}) collective-permute-start(bf16[128,256]{1,0:T(8,128)(2,1)S(1)} %convert_element_type.41), channel_id=1, source_target_pairs={{0,8},{8,0},{16,24},{24,16},{1,9},{9,1},{17,25},{25,17},{2,10},{10... | collective-permute-start | bytes 196616 | tf_op jit(solution)/shard_map/ppermute | solution.py:242
  (3 other events, 10.4 us)

commit v10 on v8

--- a/solution.py
+++ b/solution.py
@@ -316,7 +316,11 @@
     far = [own_far] + [other_core(block) for block in near]
     next_near = [across_chips(next_pair, k) for k in partners][::-1]
     first_query, near_terms, far_terms = attend_back(0, queries, stacks, [own_pair, *near, *far])
-    far_terms, next_near = lax.optimization_barrier((far_terms, [next_pair, *next_near]))
+    *others, farthest = next_near
+    far_terms, others, farthest, next_pair = lax.optimization_barrier(
+        (far_terms, others[::-1], farthest, next_pair)
+    )
+    next_near = [next_pair, *others[::-1], farthest]
     next_kv = [*next_near, other_core(jnp.concatenate(next_near, axis=0))]
 
     def chip_sums(near_terms, received):
@@ -345,7 +349,7 @@
     odd_acc, even_acc, leaving = lax.optimization_barrier((odd_acc, even_acc, leaving))
     own_sum, queries_both = lax.optimization_barrier((own_sum, (first_query, second_query)))
     arrived = [across_chips(leaving[k - 1], k) for k in partners]
-    arrived.insert(-1, section_swap(even_acc, 1))
+    arrived.append(section_swap(even_acc, 1))
     arrived.append(section_swap(odd_acc, 0))
     key_grads, value_grads = finished(first_acc, own_sum, arrived)
     query_grads = jnp.stack(queries_both, axis=0)[:, None]

time: 47.1 us -> 46.7 us (level)
    ppermute x12, waiting for transfers between devices: 4.48 us -> 3.21 us  [across_chips(): lax.ppermute(block, 'z', [(chip, chip ^ k) for chip in range(lax.axis_siz...]
    ppermute x2, starting transfers between devices: 1.97 us -> 2.75 us  [section_swap(): return lax.ppermute(block, 'section', route)]
    ppermute x12, starting transfers between devices: 19.7 us -> 19 us  [across_chips(): lax.ppermute(block, 'z', [(chip, chip ^ k) for chip in range(lax.axis_siz...]
    ppermute x2, waiting for transfers between devices: 1.41 us -> 2.13 us  [section_swap(): return lax.ppermute(block, 'section', route)]
where the time goes in v10:
time: 46.7 us; the launch traced here: 46.4 us
  starting transfers between devices  25.6 us (55%)
  Pallas kernels  9.08 us (19%)
  waiting for transfers between devices  6.91 us (15%)
  local copies, waits for them, and re-layouts  2.12 us (5%)
  other arithmetic  1.89 us (4%)
  between operations  0.8 us (2%)
    ppermute x12, starting transfers between devices, across_chips(): lax.ppermute(block, 'z', [(chip, chip ^ k) for chip in range(lax.axis_siz...  19 us
    pallas_call x2, Pallas kernels, attend_back(): pl.pallas_call(kernel, out_shape=(jax.ShapeDtypeStruct((local_rows, model...  7.62 us
    ppermute x12, waiting for transfers between devices, across_chips(): lax.ppermute(block, 'z', [(chip, chip ^ k) for chip in range(lax.axis_siz...  3.21 us
    ppermute x2, starting transfers between devices, section_swap(): return lax.ppermute(block, 'section', route)  2.75 us
    ppermute x1, starting transfers between devices, body(): lax.ppermute(leaving_pair, 'section', [(i, (i - 1) % sections) for i in r...  2.67 us
    ppermute x2, waiting for transfers between devices, section_swap(): return lax.ppermute(block, 'section', route)  2.13 us
    unnamed x10, local copies, waits for them, and re-layouts  2.1 us
    ppermute x7, waiting for transfers between devices, other_core(): return lax.ppermute(block, 'core', [(0, 1), (1, 0)])  1.57 us
  transfers between devices with their start and end apart: 22, of which 9 were waited for; matrix products, arithmetic and copies ran while one was open for 2% of the time, Pallas kernels for 18%

profile of v10, /device:TPU:0, one launch (start us, length us, event | category | flops | bytes accessed | tf_op | source)
XLA Modules:
  0.0 46.4 jit_solution(11935896483799618331)
XLA Ops:
  0.6 0.8 %maximum_select_fusion = (bf16[128,256]{1,0:T(8,128)(2,1)S(1)}, bf16[128,256]{1,0:T(8,128)(2,1)S(1)}) fusion(bf16[128,128]{1,0:T(8,128)(2,1)} %param.14, bf16[128,128]{1,0:T(8,128)(2,1)} %param.13, pred[]{:T(512)S(6)} %eq.9, bf16[128,128]{1,0:T(8,128)(2,1)} %bitcast.14, bf16[128,128]{1,0:T(8,128)(2,1)} %bitcast.15), kind=kLoop, calls=%fused_computation.9 | loop fusion | flops 294912 | bytes 262145 | tf_op jit(solution)/shard_map/jit(_where)/select_n | solution.py:306
  1.5 3.1 %collective-permute-start = (bf16[128,256]{1,0:T(8,128)(2,1)S(1)}, bf16[128,256]{1,0:T(8,128)(2,1)S(1)}, u32[]{:S(2)}, u32[]{:S(2)}) collective-permute-start(bf16[128,256]{1,0:T(8,128)(2,1)S(1)} %get-tuple-element.97.refs_3_), channel_id=1, source_target_pairs={{0,2},{2,0},{4,6},{6,4},{1,3},{3,1},{5,7},{7,5},{8,10},{10,8},{12,... | collective-permute-start | bytes 196616 | tf_op jit(solution)/shard_map/ppermute | solution.py:275
  4.6 2.6 %collective-permute-start.1 = (bf16[128,256]{1,0:T(8,128)(2,1)S(1)}, bf16[128,256]{1,0:T(8,128)(2,1)S(1)}, u32[]{:S(2)}, u32[]{:S(2)}) collective-permute-start(bf16[128,256]{1,0:T(8,128)(2,1)S(1)} %get-tuple-element.97.refs_3_), channel_id=1, source_target_pairs={{0,4},{2,6},{4,0},{6,2},{1,5},{3,7},{5,1},{7,3},{8,12},{10,14},{12... | collective-permute-start | bytes 196616 | tf_op jit(solution)/shard_map/ppermute | solution.py:275
  7.2 2.7 %collective-permute-start.3 = (bf16[128,256]{1,0:T(8,128)(2,1)S(1)}, bf16[128,256]{1,0:T(8,128)(2,1)S(1)}, u32[]{:S(2)}, u32[]{:S(2)}) collective-permute-start(bf16[128,256]{1,0:T(8,128)(2,1)S(1)} %get-tuple-element.96), channel_id=1, source_target_pairs={{0,24},{8,0},{16,8},{24,16},{1,25},{9,1},{17,9},{25,17},{2,26},{10... | collective-permute-start | bytes 196616 | tf_op jit(solution)/shard_map/ppermute | solution.py:311
  9.8 1.0 %copy-done = bf16[2,1,128,1024]{3,2,1,0:T(8,128)(2,1)S(1)} copy-done((bf16[2,1,128,1024]{3,2,1,0:T(8,128)(2,1)S(1)}, bf16[2,1,128,1024]{3,2,1,0:T(8,128)(2,1)}, u32[]{:S(2)}) %copy-start) | copy-done | bytes 524312
  10.9 1.0 %copy-done.1 = bf16[2,1,128,1024]{3,2,1,0:T(8,128)(2,1)S(1)} copy-done((bf16[2,1,128,1024]{3,2,1,0:T(8,128)(2,1)S(1)}, bf16[2,1,128,1024]{3,2,1,0:T(8,128)(2,1)}, u32[]{:S(2)}) %copy-start.1) | copy-done | bytes 524312
  11.9 0.7 %shard_map.112 = (bf16[2048,128]{1,0:T(8,128)(2,1)S(1)}, bf16[2048,128]{1,0:T(8,128)(2,1)S(1)}, f32[64,256]{1,0:T(8,128)S(1)}) custom-call(s32[8]{0:T(128)S(1)} %copy-done.2, bf16[2,1,128,1024]{3,2,1,0:T(8,128)(2,1)S(1)} %copy-done, bf16[2,1,128,1024]{3,2,1,0:T(8,128)(2,1)S(1)} %copy-done.1), custom_call_target="tpu_custom_call" | custom-call | flops 262144 | bytes 2097152 | tf_op jit(solution)/shard_map/pallas_call | solution.py:42
  13.8 3.6 %collective-permute-start.10 = (bf16[128,256]{1,0:T(8,128)(2,1)S(1)}, bf16[128,256]{1,0:T(8,128)(2,1)S(1)}, u32[]{:S(2)}, u32[]{:S(2)}) collective-permute-start(bf16[128,256]{1,0:T(8,128)(2,1)S(1)} %collective-permute-done.3.refs_3_), channel_id=1, source_target_pairs={{0,6},{2,4},{4,2},{6,0},{1,7},{3,5},{5,3},{7,1},{8,14},{10,12},{12... | collective-permute-start | bytes 196616 | tf_op jit(solution)/shard_map/ppermute | solution.py:275
  17.4 0.8 %collective-permute-start.9 = (bf16[128,256]{1,0:T(8,128)(2,1)S(1)}, bf16[128,256]{1,0:T(8,128)(2,1)S(1)}, u32[]{:S(2)}, u32[]{:S(2)}) collective-permute-start(bf16[128,256]{1,0:T(8,128)(2,1)S(1)} %collective-permute-done.3.refs_3_), channel_id=1, source_target_pairs={{0,2},{2,0},{4,6},{6,4},{1,3},{3,1},{5,7},{7,5},{8,10},{10,8},{12,... | collective-permute-start | bytes 196616 | tf_op jit(solution)/shard_map/ppermute | solution.py:275
  18.2 3.8 %shard_map.113 = (bf16[128,1024]{1,0:T(8,128)(2,1)S(1)}, f32[512,256]{1,0:T(8,128)S(1)}, bf16[512,256]{1,0:T(8,128)(2,1)S(1)}) custom-call(bf16[2048,128]{1,0:T(8,128)(2,1)S(1)} %get-tuple-element.55.refs_0_, bf16[2048,128]{1,0:T(8,128)(2,1)S(1)} %get-tuple-element.56.refs_1_, f32[64,256]{1,0:T(8,128)S(1)} %get-tuple-element.57.refs_2_, ...), custom_call_target="tpu_custom_call" | custom-call | flops 5368709120 | bytes 2097152 | tf_op jit(solution)/shard_map/pallas_call | solution.py:201
  22.0 0.9 %collective-permute-done.8.refs_5_ = bf16[128,256]{1,0:T(8,128)(2,1)S(1)} collective-permute-done((bf16[128,256]{1,0:T(8,128)(2,1)S(1)}, bf16[128,256]{1,0:T(8,128)(2,1)S(1)}, u32[]{:S(2)}, u32[]{:S(2)}) %collective-permute-start.8) | collective-permute-done | bytes 65568 | tf_op jit(solution)/shard_map/ppermute | solution.py:275
  23.7 0.9 %collective-permute-done.11 = bf16[512,256]{1,0:T(8,128)(2,1)S(1)} collective-permute-done((bf16[512,256]{1,0:T(8,128)(2,1)S(1)}, bf16[512,256]{1,0:T(8,128)(2,1)S(1)}, u32[]{:S(2)}, u32[]{:S(2)}) %collective-permute-start.11) | collective-permute-done | bytes 262176 | tf_op jit(solution)/shard_map/ppermute | solution.py:271
  24.7 2.7 %collective-permute-start.13 = (bf16[128,256]{1,0:T(8,128)(2,1)S(1)}, bf16[128,256]{1,0:T(8,128)(2,1)S(1)}, u32[]{:S(2)}, u32[]{:S(2)}) collective-permute-start(bf16[128,256]{1,0:T(8,128)(2,1)S(1)} %get-tuple-element.63), channel_id=1, source_target_pairs={{0,6},{2,4},{4,2},{6,0},{1,7},{3,5},{5,3},{7,1},{8,14},{10,12},{12... | collective-permute-start | bytes 196616 | tf_op jit(solution)/shard_map/ppermute | solution.py:275
  27.5 1.7 %collective-permute-start.15 = (bf16[128,256]{1,0:T(8,128)(2,1)S(1)}, bf16[128,256]{1,0:T(8,128)(2,1)S(1)}, u32[]{:S(2)}, u32[]{:S(2)}) collective-permute-start(bf16[128,256]{1,0:T(8,128)(2,1)S(1)} %get-tuple-element.65), channel_id=1, source_target_pairs={{0,2},{2,0},{4,6},{6,4},{1,3},{3,1},{5,7},{7,5},{8,10},{10,8},{12,... | collective-permute-start | bytes 196616 | tf_op jit(solution)/shard_map/ppermute | solution.py:275
  29.2 3.8 %shard_map.114 = (bf16[128,1024]{1,0:T(8,128)(2,1)S(1)}, f32[512,256]{1,0:T(8,128)S(1)}, bf16[512,256]{1,0:T(8,128)(2,1)S(1)}) custom-call(bf16[2048,128]{1,0:T(8,128)(2,1)S(1)} %get-tuple-element.55.refs_0_, bf16[2048,128]{1,0:T(8,128)(2,1)S(1)} %get-tuple-element.56.refs_1_, f32[64,256]{1,0:T(8,128)S(1)} %get-tuple-element.57.refs_2_, ...), custom_call_target="tpu_custom_call" | custom-call | flops 5368709120 | bytes 2097152 | tf_op jit(solution)/shard_map/pallas_call | solution.py:201
  33.1 0.8 %collective-permute-done.14 = bf16[128,256]{1,0:T(8,128)(2,1)S(1)} collective-permute-done((bf16[128,256]{1,0:T(8,128)(2,1)S(1)}, bf16[128,256]{1,0:T(8,128)(2,1)S(1)}, u32[]{:S(2)}, u32[]{:S(2)}) %collective-permute-start.14) | collective-permute-done | bytes 65568 | tf_op jit(solution)/shard_map/ppermute | solution.py:275
  34.7 2.7 %collective-permute-start.17 = (bf16[128,256]{1,0:T(8,128)(2,1)S(1)}, bf16[128,256]{1,0:T(8,128)(2,1)S(1)}, u32[]{:S(2)}, u32[]{:S(2)}) collective-permute-start(bf16[128,256]{1,0:T(8,128)(2,1)S(1)} %get-tuple-element.74), channel_id=1, source_target_pairs={{0,6},{2,4},{4,2},{6,0},{1,7},{3,5},{5,3},{7,1},{8,14},{10,12},{12... | collective-permute-start | bytes 196616 | tf_op jit(solution)/shard_map/ppermute | solution.py:275
  37.4 1.8 %collective-permute-start.19 = (bf16[128,256]{1,0:T(8,128)(2,1)S(1)}, bf16[128,256]{1,0:T(8,128)(2,1)S(1)}, u32[]{:S(2)}, u32[]{:S(2)}) collective-permute-start(bf16[128,256]{1,0:T(8,128)(2,1)S(1)} %get-tuple-element.76), channel_id=1, source_target_pairs={{0,2},{2,0},{4,6},{6,4},{1,3},{3,1},{5,7},{7,5},{8,10},{10,8},{12,... | collective-permute-start | bytes 196616 | tf_op jit(solution)/shard_map/ppermute | solution.py:275
  39.2 2.2 %collective-permute-start.20 = (bf16[128,256]{1,0:T(8,128)(2,1)S(1)}, bf16[128,256]{1,0:T(8,128)(2,1)S(1)}, u32[]{:S(2)}, u32[]{:S(2)}) collective-permute-start(bf16[128,256]{1,0:T(8,128)(2,1)S(1)} %get-tuple-element.77), channel_id=1, source_target_pairs={{8,16},{16,8},{24,0},{0,24},{9,17},{17,9},{25,1},{1,25},{10,18},{1... | collective-permute-start | bytes 196616 | tf_op jit(solution)/shard_map/ppermute | solution.py:284
  41.9 0.8 %maximum_bitcast_fusion = bf16[2,1,128,1024]{3,2,1,0:T(8,128)(2,1)} fusion(bf16[1,128,1024]{2,1,0:T(8,128)(2,1)S(1)} %bitcast.11, bf16[1,128,1024]{2,1,0:T(8,128)(2,1)S(1)} %bitcast.10), kind=kLoop, calls=%fused_computation | loop fusion | flops 262144 | bytes 1048576
  42.8 0.7 %collective-permute-done.18.refs_1_ = bf16[128,256]{1,0:T(8,128)(2,1)S(1)} collective-permute-done((bf16[128,256]{1,0:T(8,128)(2,1)S(1)}, bf16[128,256]{1,0:T(8,128)(2,1)S(1)}, u32[]{:S(2)}, u32[]{:S(2)}) %collective-permute-start.18) | collective-permute-done | bytes 65568 | tf_op jit(solution)/shard_map/ppermute | solution.py:275
  43.5 0.8 %collective-permute-done.20.refs_3_ = bf16[128,256]{1,0:T(8,128)(2,1)S(1)} collective-permute-done((bf16[128,256]{1,0:T(8,128)(2,1)S(1)}, bf16[128,256]{1,0:T(8,128)(2,1)S(1)}, u32[]{:S(2)}, u32[]{:S(2)}) %collective-permute-start.20) | collective-permute-done | bytes 65568 | tf_op jit(solution)/shard_map/ppermute | solution.py:284
  44.3 1.3 %collective-permute-done.21.refs_4_ = bf16[128,256]{1,0:T(8,128)(2,1)S(1)} collective-permute-done((bf16[128,256]{1,0:T(8,128)(2,1)S(1)}, bf16[128,256]{1,0:T(8,128)(2,1)S(1)}, u32[]{:S(2)}, u32[]{:S(2)}) %collective-permute-start.21) | collective-permute-done | bytes 65568 | tf_op jit(solution)/shard_map/ppermute | solution.py:284
  45.7 0.7 %shard_map.115 = (f32[2,1,128,128]{3,2,1,0:T(8,128)}, f32[2,1,128,128]{3,2,1,0:T(8,128)}) custom-call(f32[128,256]{1,0:T(8,128)S(1)} %fusion.2.first_ref, f32[128,256]{1,0:T(8,128)S(1)} %slice.50.own_ref, bf16[128,256]{1,0:T(8,128)(2,1)S(1)} %collective-permute-done.17.refs_0_, bf16[128,256]{1,0:T(8,128)(2,1)S(1)} %collective-permute-done.18.refs_1_, ...), custom_call_target="tpu_custom_call" | custom-call | flops 163840 | bytes 524288 | tf_op jit(solution)/shard_map/pallas_call | solution.py:252
  (43 shorter events, 3.4 us)
Async XLA Ops:
  1.5 8.4 %copy-start.2 = (s32[8]{0:T(128)S(1)}, s32[8]{0:T(128)}, u32[]{:S(2)}) copy-start(s32[8]{0:T(128)} %order_ref.1) | copy-start | bytes 100
  1.5 11.2 %collective-permute-start = (bf16[128,256]{1,0:T(8,128)(2,1)S(1)}, bf16[128,256]{1,0:T(8,128)(2,1)S(1)}, u32[]{:S(2)}, u32[]{:S(2)}) collective-permute-start(bf16[128,256]{1,0:T(8,128)(2,1)S(1)} %get-tuple-element.97.refs_3_), channel_id=1, source_target_pairs={{0,2},{2,0},{4,6},{6,4},{1,3},{3,1},{5,7},{7,5},{8,10},{10,8},{12,... | collective-permute-start | bytes 196616 | tf_op jit(solution)/shard_map/ppermute | solution.py:275
  4.6 8.1 %collective-permute-start.1 = (bf16[128,256]{1,0:T(8,128)(2,1)S(1)}, bf16[128,256]{1,0:T(8,128)(2,1)S(1)}, u32[]{:S(2)}, u32[]{:S(2)}) collective-permute-start(bf16[128,256]{1,0:T(8,128)(2,1)S(1)} %get-tuple-element.97.refs_3_), channel_id=1, source_target_pairs={{0,4},{2,6},{4,0},{6,2},{1,5},{3,7},{5,1},{7,3},{8,12},{10,14},{12... | collective-permute-start | bytes 196616 | tf_op jit(solution)/shard_map/ppermute | solution.py:275
  7.2 6.1 %collective-permute-start.2 = (bf16[128,256]{1,0:T(8,128)(2,1)S(1)}, bf16[128,256]{1,0:T(8,128)(2,1)S(1)}, u32[]{:S(2)}, u32[]{:S(2)}) collective-permute-start(bf16[128,256]{1,0:T(8,128)(2,1)S(1)} %get-tuple-element.97.refs_3_), channel_id=1, source_target_pairs={{0,6},{2,4},{4,2},{6,0},{1,7},{3,5},{5,3},{7,1},{8,14},{10,12},{12... | collective-permute-start | bytes 196616 | tf_op jit(solution)/shard_map/ppermute | solution.py:275
  7.2 6.1 %collective-permute-start.3 = (bf16[128,256]{1,0:T(8,128)(2,1)S(1)}, bf16[128,256]{1,0:T(8,128)(2,1)S(1)}, u32[]{:S(2)}, u32[]{:S(2)}) collective-permute-start(bf16[128,256]{1,0:T(8,128)(2,1)S(1)} %get-tuple-element.96), channel_id=1, source_target_pairs={{0,24},{8,0},{16,8},{24,16},{1,25},{9,1},{17,9},{25,17},{2,26},{10... | collective-permute-start | bytes 196616 | tf_op jit(solution)/shard_map/ppermute | solution.py:311
  9.8 7.6 %collective-permute-start.4 = (bf16[128,256]{1,0:T(8,128)(2,1)S(1)}, bf16[128,256]{1,0:T(8,128)(2,1)S(1)}, u32[]{:S(2)}, u32[]{:S(2)}) collective-permute-start(bf16[128,256]{1,0:T(8,128)(2,1)S(1)} %get-tuple-element.97.refs_3_), channel_id=1, source_target_pairs={{0,1},{1,0},{2,3},{3,2},{4,5},{5,4},{6,7},{7,6},{8,9},{9,8},{10,11... | collective-permute-start | bytes 196616 | tf_op jit(solution)/shard_map/ppermute | solution.py:271
  13.2 4.2 %collective-permute-start.5 = (bf16[128,256]{1,0:T(8,128)(2,1)S(1)}, bf16[128,256]{1,0:T(8,128)(2,1)S(1)}, u32[]{:S(2)}, u32[]{:S(2)}) collective-permute-start(bf16[128,256]{1,0:T(8,128)(2,1)S(1)} %collective-permute-done.refs_4_), channel_id=1, source_target_pairs={{0,1},{1,0},{2,3},{3,2},{4,5},{5,4},{6,7},{7,6},{8,9},{9,8},{10,11... | collective-permute-start | bytes 196616 | tf_op jit(solution)/shard_map/ppermute | solution.py:271
  13.3 4.9 %collective-permute-start.6 = (bf16[128,256]{1,0:T(8,128)(2,1)S(1)}, bf16[128,256]{1,0:T(8,128)(2,1)S(1)}, u32[]{:S(2)}, u32[]{:S(2)}) collective-permute-start(bf16[128,256]{1,0:T(8,128)(2,1)S(1)} %collective-permute-done.1.refs_5_), channel_id=1, source_target_pairs={{0,1},{1,0},{2,3},{3,2},{4,5},{5,4},{6,7},{7,6},{8,9},{9,8},{10,11... | collective-permute-start | bytes 196616 | tf_op jit(solution)/shard_map/ppermute | solution.py:271
  13.8 4.4 %collective-permute-start.7 = (bf16[128,256]{1,0:T(8,128)(2,1)S(1)}, bf16[128,256]{1,0:T(8,128)(2,1)S(1)}, u32[]{:S(2)}, u32[]{:S(2)}) collective-permute-start(bf16[128,256]{1,0:T(8,128)(2,1)S(1)} %collective-permute-done.2.refs_6_), channel_id=1, source_target_pairs={{0,1},{1,0},{2,3},{3,2},{4,5},{5,4},{6,7},{7,6},{8,9},{9,8},{10,11... | collective-permute-start | bytes 196616 | tf_op jit(solution)/shard_map/ppermute | solution.py:271
  13.8 8.2 %collective-permute-start.10 = (bf16[128,256]{1,0:T(8,128)(2,1)S(1)}, bf16[128,256]{1,0:T(8,128)(2,1)S(1)}, u32[]{:S(2)}, u32[]{:S(2)}) collective-permute-start(bf16[128,256]{1,0:T(8,128)(2,1)S(1)} %collective-permute-done.3.refs_3_), channel_id=1, source_target_pairs={{0,6},{2,4},{4,2},{6,0},{1,7},{3,5},{5,3},{7,1},{8,14},{10,12},{12... | collective-permute-start | bytes 196616 | tf_op jit(solution)/shard_map/ppermute | solution.py:275
  17.4 5.6 %collective-permute-start.8 = (bf16[128,256]{1,0:T(8,128)(2,1)S(1)}, bf16[128,256]{1,0:T(8,128)(2,1)S(1)}, u32[]{:S(2)}, u32[]{:S(2)}) collective-permute-start(bf16[128,256]{1,0:T(8,128)(2,1)S(1)} %collective-permute-done.3.refs_3_), channel_id=1, source_target_pairs={{0,4},{2,6},{4,0},{6,2},{1,5},{3,7},{5,1},{7,3},{8,12},{10,14},{12... | collective-permute-start | bytes 196616 | tf_op jit(solution)/shard_map/ppermute | solution.py:275
  17.4 5.7 %collective-permute-start.9 = (bf16[128,256]{1,0:T(8,128)(2,1)S(1)}, bf16[128,256]{1,0:T(8,128)(2,1)S(1)}, u32[]{:S(2)}, u32[]{:S(2)}) collective-permute-start(bf16[128,256]{1,0:T(8,128)(2,1)S(1)} %collective-permute-done.3.refs_3_), channel_id=1, source_target_pairs={{0,2},{2,0},{4,6},{6,4},{1,3},{3,1},{5,7},{7,5},{8,10},{10,8},{12,... | collective-permute-start | bytes 196616 | tf_op jit(solution)/shard_map/ppermute | solution.py:275
  23.1 1.5 %collective-permute-start.11 = (bf16[512,256]{1,0:T(8,128)(2,1)S(1)}, bf16[512,256]{1,0:T(8,128)(2,1)S(1)}, u32[]{:S(2)}, u32[]{:S(2)}) collective-permute-start(bf16[512,256]{1,0:T(8,128)(2,1)S(1)} %get-tuple-element.54), channel_id=1, source_target_pairs={{0,1},{1,0},{2,3},{3,2},{4,5},{5,4},{6,7},{7,6},{8,9},{9,8},{10,11... | collective-permute-start | bytes 786440 | tf_op jit(solution)/shard_map/ppermute | solution.py:271
  23.1 6.1 %collective-permute-start.12 = (bf16[512,256]{1,0:T(8,128)(2,1)S(1)}, bf16[512,256]{1,0:T(8,128)(2,1)S(1)}, u32[]{:S(2)}, u32[]{:S(2)}) collective-permute-start(bf16[512,256]{1,0:T(8,128)(2,1)S(1)} %pad_maximum_fusion), channel_id=1, source_target_pairs={{0,1},{1,0},{2,3},{3,2},{4,5},{5,4},{6,7},{7,6},{8,9},{9,8},{10,11... | collective-permute-start | bytes 786440 | tf_op jit(solution)/shard_map/ppermute | solution.py:271
  24.7 8.4 %collective-permute-start.13 = (bf16[128,256]{1,0:T(8,128)(2,1)S(1)}, bf16[128,256]{1,0:T(8,128)(2,1)S(1)}, u32[]{:S(2)}, u32[]{:S(2)}) collective-permute-start(bf16[128,256]{1,0:T(8,128)(2,1)S(1)} %get-tuple-element.63), channel_id=1, source_target_pairs={{0,6},{2,4},{4,2},{6,0},{1,7},{3,5},{5,3},{7,1},{8,14},{10,12},{12... | collective-permute-start | bytes 196616 | tf_op jit(solution)/shard_map/ppermute | solution.py:275
  27.4 6.5 %collective-permute-start.14 = (bf16[128,256]{1,0:T(8,128)(2,1)S(1)}, bf16[128,256]{1,0:T(8,128)(2,1)S(1)}, u32[]{:S(2)}, u32[]{:S(2)}) collective-permute-start(bf16[128,256]{1,0:T(8,128)(2,1)S(1)} %get-tuple-element.64), channel_id=1, source_target_pairs={{0,4},{2,6},{4,0},{6,2},{1,5},{3,7},{5,1},{7,3},{8,12},{10,14},{12... | collective-permute-start | bytes 196616 | tf_op jit(solution)/shard_map/ppermute | solution.py:275
  27.5 6.5 %collective-permute-start.15 = (bf16[128,256]{1,0:T(8,128)(2,1)S(1)}, bf16[128,256]{1,0:T(8,128)(2,1)S(1)}, u32[]{:S(2)}, u32[]{:S(2)}) collective-permute-start(bf16[128,256]{1,0:T(8,128)(2,1)S(1)} %get-tuple-element.65), channel_id=1, source_target_pairs={{0,2},{2,0},{4,6},{6,4},{1,3},{3,1},{5,7},{7,5},{8,10},{10,8},{12,... | collective-permute-start | bytes 196616 | tf_op jit(solution)/shard_map/ppermute | solution.py:275
  29.2 4.7 %copy-start.4 = (f32[1,128,128]{2,1,0:T(8,128)S(1)}, f32[1,128,128]{2,1,0:T(8,128)}, u32[]{:S(2)}) copy-start(f32[1,128,128]{2,1,0:T(8,128)} %param.15) | copy-start | bytes 196612
  33.0 1.6 %collective-permute-start.16 = (bf16[512,256]{1,0:T(8,128)(2,1)S(1)}, bf16[512,256]{1,0:T(8,128)(2,1)S(1)}, u32[]{:S(2)}, u32[]{:S(2)}) collective-permute-start(bf16[512,256]{1,0:T(8,128)(2,1)S(1)} %get-tuple-element.66), channel_id=1, source_target_pairs={{0,1},{1,0},{2,3},{3,2},{4,5},{5,4},{6,7},{7,6},{8,9},{9,8},{10,11... | collective-permute-start | bytes 786440 | tf_op jit(solution)/shard_map/ppermute | solution.py:271
  34.7 8.1 %collective-permute-start.17 = (bf16[128,256]{1,0:T(8,128)(2,1)S(1)}, bf16[128,256]{1,0:T(8,128)(2,1)S(1)}, u32[]{:S(2)}, u32[]{:S(2)}) collective-permute-start(bf16[128,256]{1,0:T(8,128)(2,1)S(1)} %get-tuple-element.74), channel_id=1, source_target_pairs={{0,6},{2,4},{4,2},{6,0},{1,7},{3,5},{5,3},{7,1},{8,14},{10,12},{12... | collective-permute-start | bytes 196616 | tf_op jit(solution)/shard_map/ppermute | solution.py:275
  37.4 6.1 %collective-permute-start.18 = (bf16[128,256]{1,0:T(8,128)(2,1)S(1)}, bf16[128,256]{1,0:T(8,128)(2,1)S(1)}, u32[]{:S(2)}, u32[]{:S(2)}) collective-permute-start(bf16[128,256]{1,0:T(8,128)(2,1)S(1)} %get-tuple-element.75), channel_id=1, source_target_pairs={{0,4},{2,6},{4,0},{6,2},{1,5},{3,7},{5,1},{7,3},{8,12},{10,14},{12... | collective-permute-start | bytes 196616 | tf_op jit(solution)/shard_map/ppermute | solution.py:275
  37.4 6.1 %collective-permute-start.19 = (bf16[128,256]{1,0:T(8,128)(2,1)S(1)}, bf16[128,256]{1,0:T(8,128)(2,1)S(1)}, u32[]{:S(2)}, u32[]{:S(2)}) collective-permute-start(bf16[128,256]{1,0:T(8,128)(2,1)S(1)} %get-tuple-element.76), channel_id=1, source_target_pairs={{0,2},{2,0},{4,6},{6,4},{1,3},{3,1},{5,7},{7,5},{8,10},{10,8},{12,... | collective-permute-start | bytes 196616 | tf_op jit(solution)/shard_map/ppermute | solution.py:275
  39.2 5.2 %collective-permute-start.20 = (bf16[128,256]{1,0:T(8,128)(2,1)S(1)}, bf16[128,256]{1,0:T(8,128)(2,1)S(1)}, u32[]{:S(2)}, u32[]{:S(2)}) collective-permute-start(bf16[128,256]{1,0:T(8,128)(2,1)S(1)} %get-tuple-element.77), channel_id=1, source_target_pairs={{8,16},{16,8},{24,0},{0,24},{9,17},{17,9},{25,1},{1,25},{10,18},{1... | collective-permute-start | bytes 196616 | tf_op jit(solution)/shard_map/ppermute | solution.py:284
  41.4 4.3 %collective-permute-start.21 = (bf16[128,256]{1,0:T(8,128)(2,1)S(1)}, bf16[128,256]{1,0:T(8,128)(2,1)S(1)}, u32[]{:S(2)}, u32[]{:S(2)}) collective-permute-start(bf16[128,256]{1,0:T(8,128)(2,1)S(1)} %get-tuple-element.78), channel_id=1, source_target_pairs={{0,8},{8,0},{16,24},{24,16},{1,9},{9,1},{17,25},{25,17},{2,10},{10... | collective-permute-start | bytes 196616 | tf_op jit(solution)/shard_map/ppermute | solution.py:284
  (3 other events, 6.8 us)
